TPU v7x, 32 devices: a whole 2x2x4 slice. The times are simulated.
32 devices in a mesh: groups: 2 (over x), cell: 16 (over z, y, core), gene: 1.
Axes of the slice: x: 2, y: 2, z: 4, core: 2. Of those that a mesh axis runs over, the one named last changes fastest.
Arguments:
- expression: bfloat16 [2048, 30720], P(('groups', 'cell'), 'gene'), parts along dimension 0, may hold values from -6 to 6
- start_basis: bfloat16 [61440, 64], P(('groups', 'gene', 'cell')), parts along dimension 0, may hold values from -0.03125 to 0.03125
Outputs:
- basis_out: float32 [61440, 64], P(('groups', 'gene', 'cell')), parts along dimension 0
There are 2 independent parts, one for each index of `groups`. A program takes and returns all parts, laid end to end along the dimension named above; each array names one. Nothing has to cross between parts.
All inputs are finite; a program needn't handle non-finite values.
Results may differ from a plain program's by a relative error of at most 0.006.
Values may be sent and summed in bfloat16 or wider, within the bound.
No kernel may reach another device: no remote copies, remote signals or barrier semaphores. Data moves between devices by JAX's collectives and lax.ppermute only.
A program may use at most 64 MiB of HBM per device.

v0:
```python
import math

import jax
import jax.numpy as jnp
from jax import lax
from jax.sharding import PartitionSpec as P

GENES = 30720
ITERS = 2


def factor_of(loading):
    local_gram = lax.dot_general(
        loading,
        loading,
        (((0,), (0,)), ((), ())),
        precision=lax.Precision.HIGHEST,
        preferred_element_type=jnp.float32,
    )
    gram = lax.psum(local_gram, ("cell", "gene"))
    return jnp.linalg.cholesky(gram)


def apply_factor(rows, lower):
    return jax.scipy.linalg.solve_triangular(lower, rows.T, lower=True).T


def transposed_product(left, right):
    return lax.dot_general(
        left, right, (((0,), (0,)), ((), ())), preferred_element_type=jnp.float32
    )


def scores_of(partial_value):
    return lax.psum(partial_value, "gene").astype(jnp.bfloat16)


def on_device(expression, start_basis):
    ortho = jnp.zeros(start_basis.shape, jnp.float32)
    basis = start_basis
    for step in range(ITERS):
        partial_value = jnp.dot(
            expression,
            lax.all_gather(basis, "cell", axis=0, tiled=True),
            preferred_element_type=jnp.float32,
        )
        image = scores_of(partial_value)
        loading = lax.psum_scatter(
            transposed_product(expression, image), "cell", scatter_dimension=0, tiled=True
        )
        lower = factor_of(loading)
        ortho = apply_factor(loading, lower)
        basis = ortho.astype(jnp.bfloat16)
    return ortho * math.sqrt(GENES)


def solution(mesh):
    placed = (P(("groups", "cell"), "gene"), P(("groups", "gene", "cell"), None))
    return jax.shard_map(
        on_device,
        mesh=mesh,
        in_specs=placed,
        out_specs=P(("groups", "gene", "cell"), None),
        check_vma=False,
    )
```

profile of v0, /device:TPU:0, one launch (start us, length us, event | category | flops | bytes accessed | tf_op | source)
XLA Modules:
  0.0 480.3 jit_solution(8556086764871783882)
XLA Ops:
  6.5 0.0 all-gather.3.cloned.1.call-start
  6.5 0.7 all-gather.3.cloned.1.call-update
  7.3 0.0 reduce-scatter.3.cloned.1.call-start
  7.3 54.3 %all-gather.3.cloned.1.call-done = bf16[30720,64]{0,1:T(8,128)(2,1)} async-done(((bf16[1920,64]{0,1:T(8,128)(2,1)}), bf16[30720,64]{0,1:T(8,128)(2,1)}) %all-gather.3.cloned.1.call-update) | async-done | bytes 3932176 | tf_op jit(solution)/shard_map/all_gather | solution.py:44
  61.6 11.9 %convolution_bitcast_fusion.1 = f32[30720,64]{0,1:T(8,128)} fusion(bf16[64,30720]{1,0:T(8,128)(2,1)} %param.5, bf16[30720,64]{0,1:T(8,128)(2,1)} %all-gather.3.cloned.1.call-done), kind=kOutput, calls=%fused_computation.1 | convolution fusion | flops 503320576 | bytes 15728640 | tf_op jit(solution)/shard_map/dot_general | solution.py:29
  73.5 0.0 reduce-scatter.3.cloned.1.call-update
  73.5 0.0 all-gather.5.cloned.1.call-start
  73.6 94.3 %reduce-scatter.3.cloned.1.call-done = f32[1920,64]{0,1:T(8,128)} async-done(((f32[30720,64]{0,1:T(8,128)}), f32[1920,64]{0,1:T(8,128)}) %reduce-scatter.3.cloned.1.call-update) | async-done | bytes 491536 | tf_op jit(solution)/shard_map/reduce_scatter | solution.py:48
  167.9 1.8 fusion.12
  169.7 60.1 %psum.14 = f32[64,64]{0,1:T(8,128)S(1)} all-reduce(f32[64,64]{0,1:T(8,128)S(1)} %fusion.12), channel_id=1, replica_groups=mesh['groups'=2,'cell'=16,'gene'=1] {'cell','gene'}, use_global_device_ids=true, to_apply=%region_1.0 | all-reduce | flops 4096 | bytes 32768 | tf_op jit(solution)/shard_map/psum | solution.py:20
  229.8 0.1 copy.4
  229.9 5.9 %cholesky.44 = f32[64,64]{1,0:T(8,128)S(1)} custom-call(f32[64,64]{1,0:T(8,128)S(1)} %fusion.9), custom_call_target="Cholesky" | custom-call | tf_op jit(solution)/shard_map/jit(cholesky)/cholesky | solution.py:21
  235.8 0.6 compare_reduce_fusion.1
  236.4 0.7 fusion.4
  237.1 4.9 %custom-call.6 = f32[1,64,64]{1,2,0:T(8,128)S(1)} custom-call(f32[1,64,64]{2,1,0:T(8,128)S(1)} %fusion.4), custom_call_target="InvertDiagBlocksLowerTriangular" | custom-call | tf_op jit(solution)/shard_map/jit(_solve_triangular)/triangular_solve | solution.py:25
  242.0 2.3 fusion.1
  244.3 0.0 all-gather.5.cloned.1.call-update
  244.4 0.0 reduce-scatter.5.cloned.1.call-start
  244.4 46.6 %all-gather.5.cloned.1.call-done = bf16[30720,64]{0,1:T(8,128)(2,1)} async-done(((bf16[1920,64]{0,1:T(8,128)(2,1)}), bf16[30720,64]{0,1:T(8,128)(2,1)}) %all-gather.5.cloned.1.call-update) | async-done | bytes 3932176 | tf_op jit(solution)/shard_map/all_gather | solution.py:44
  291.0 11.8 %convolution_bitcast_fusion = f32[30720,64]{0,1:T(8,128)} fusion(bf16[64,30720]{1,0:T(8,128)(2,1)} %param.5, bf16[30720,64]{0,1:T(8,128)(2,1)} %all-gather.5.cloned.1.call-done), kind=kOutput, calls=%fused_computation | convolution fusion | flops 503320576 | bytes 15728640 | tf_op jit(solution)/shard_map/dot_general | solution.py:29
  302.8 0.0 reduce-scatter.5.cloned.1.call-update
  302.9 94.4 %reduce-scatter.5.cloned.1.call-done = f32[1920,64]{0,1:T(8,128)} async-done(((f32[30720,64]{0,1:T(8,128)}), f32[1920,64]{0,1:T(8,128)}) %reduce-scatter.5.cloned.1.call-update) | async-done | bytes 491536 | tf_op jit(solution)/shard_map/reduce_scatter | solution.py:48
  397.2 1.8 fusion.13
  399.0 60.1 %psum.15 = f32[64,64]{0,1:T(8,128)S(1)} all-reduce(f32[64,64]{0,1:T(8,128)S(1)} %fusion.13), channel_id=1, replica_groups=mesh['groups'=2,'cell'=16,'gene'=1] {'cell','gene'}, use_global_device_ids=true, to_apply=%region_5.0 | all-reduce | flops 4096 | bytes 32768 | tf_op jit(solution)/shard_map/psum | solution.py:20
  459.2 0.1 copy.6
  459.2 5.8 %cholesky.55 = f32[64,64]{1,0:T(8,128)S(1)} custom-call(f32[64,64]{1,0:T(8,128)S(1)} %fusion.7), custom_call_target="Cholesky" | custom-call | tf_op jit(solution)/shard_map/jit(cholesky)/cholesky | solution.py:21
  465.1 0.6 compare_reduce_fusion
  465.8 0.7 fusion.5
  466.4 4.9 %custom-call.7 = f32[1,64,64]{1,2,0:T(8,128)S(1)} custom-call(f32[1,64,64]{2,1,0:T(8,128)S(1)} %fusion.5), custom_call_target="InvertDiagBlocksLowerTriangular" | custom-call | tf_op jit(solution)/shard_map/jit(_solve_triangular)/triangular_solve | solution.py:25
  471.3 2.4 fusion
  (4 shorter events, 0.1 us)
Async XLA Ops:
  6.5 55.1 %all-gather.3.cloned.1.call-start = ((), (), s32[]{:S(2)}) async-start(), calls=%async_computation.2 | async-start | bytes 4177920 | tf_op jit(solution)/shard_map/all_gather | solution.py:44
  7.3 160.7 %reduce-scatter.3.cloned.1.call-start = ((), (), s32[]{:S(2)}) async-start(), calls=%async_computation.3 | async-start | bytes 8355840 | tf_op jit(solution)/shard_map/reduce_scatter | solution.py:48
  73.5 217.5 %all-gather.5.cloned.1.call-start = ((), (), s32[]{:S(2)}) async-start(), calls=%async_computation.4 | async-start | bytes 4177920 | tf_op jit(solution)/shard_map/all_gather | solution.py:44
  244.4 152.9 %reduce-scatter.5.cloned.1.call-start = ((), (), s32[]{:S(2)}) async-start(), calls=%async_computation.5 | async-start | bytes 8355840 | tf_op jit(solution)/shard_map/reduce_scatter | solution.py:48
Sparse Core Ops, SparseCore 0:
  9.7 51.9 all-gather.2
  73.7 94.2 reduce-scatter.2
  244.5 46.4 all-gather.4
  303.0 94.2 reduce-scatter.4
where the time goes:
time: 481 us; the launch traced here: 480 us
  waiting for transfers between devices  290 us (60%)
  blocking collectives  120 us (25%)
  matrix products  32 us (7%)
  other arithmetic  24.2 us (5%)
  between operations  13.2 us (3%)
    reduce_scatter x2, waiting for transfers between devices, on_device(): lax.psum_scatter(transposed_product(expression, image), 'cell', scatter_d...  189 us
    psum x2, blocking collectives, factor_of(): gram = lax.psum(local_gram, ('cell', 'gene'))  120 us
    all_gather x2, waiting for transfers between devices, on_device(): lax.all_gather(basis, 'cell', axis=0, tiled=True)  101 us
    dot_general x2, matrix products, transposed_product(): lax.dot_general(left, right, (((0,), (0,)), ((), ())), preferred_element_...  23.7 us
    another operation x6, other arithmetic, factor_of(): return jnp.linalg.cholesky(gram)  13 us
    another operation x4, other arithmetic, apply_factor(): return jax.scipy.linalg.solve_triangular(lower, rows.T, lower=True).T  11.1 us
  transfers between devices with their start and end apart: 4, of which 4 were waited for; matrix products, arithmetic and copies ran while one was open for 0% of the time, Pallas kernels for 0%

commit v1 on v0

v1 whole, which is shorter than its diff:
```python
import functools
import math

import jax
import jax.numpy as jnp
from jax import lax
from jax.experimental import pallas as pl
from jax.experimental.pallas import tpu as pltpu
from jax.sharding import PartitionSpec as P

GENES = 30720
ITERS = 2
PARTS = 2
GROUP = 8
BIG = pltpu.CompilerParams(vmem_limit_bytes=32 * 2**20)
VMEM = pl.BlockSpec(memory_space=pltpu.VMEM)
HIGHEST = lax.Precision.HIGHEST
f32, bf16 = jnp.float32, jnp.bfloat16


def nn(a, b, precision=None):
    return lax.dot_general(a, b, (((1,), (0,)), ((), ())), precision=precision, preferred_element_type=f32)


def nt(a, b, precision=None):
    return lax.dot_general(a, b, (((1,), (1,)), ((), ())), precision=precision, preferred_element_type=f32)


def struct(shape, dtype):
    return jax.ShapeDtypeStruct(shape, dtype)


def cost(flops, bytes_accessed):
    return pl.CostEstimate(flops=flops, bytes_accessed=bytes_accessed, transcendentals=0)


def pack_kernel(width, ids, matrix, *refs):
    outs, sem = refs[:-1], refs[-1]
    copies = []
    for k, out in enumerate(outs):
        for j in range(2):
            start = pl.multiple_of(ids[2 * k + j] * width, 128)
            copies.append(pltpu.make_async_copy(
                matrix.at[:, pl.ds(start, width)], out.at[:, pl.ds(j * width, width)], sem.at[2 * k + j]))
    for copy in copies:
        copy.start()
    for copy in copies:
        copy.wait()


def pack(matrix, ids, width):
    rows, count = matrix.shape[0], ids.shape[0] // 2
    anywhere = pl.BlockSpec(memory_space=pl.ANY)
    return pl.pallas_call(
        functools.partial(pack_kernel, width),
        in_specs=[pl.BlockSpec(memory_space=pltpu.SMEM), anywhere],
        out_specs=[anywhere] * count,
        out_shape=[struct((rows, 2 * width), matrix.dtype)] * count,
        scratch_shapes=[pltpu.SemaphoreType.DMA((2 * count,))],
        cost_estimate=cost(0, 8 * rows * count * width),
    )(ids, matrix)


def slot_specs(blocks, rows, width):
    specs = []
    for j in blocks:
        specs.append(pl.BlockSpec((rows, width), functools.partial(lambda j, s, ids: (0, ids[j]), j)))
        specs += [pl.BlockSpec((rows, width), functools.partial(lambda j, s, ids: (0, j), j))] * (GROUP - 1)
    return specs


def whole_spec(shape):
    return pl.BlockSpec(shape, lambda s, ids: (0,) * len(shape))


def prefetched(kernel, ids, args, in_specs, outs, estimate):
    return pl.pallas_call(
        kernel,
        grid_spec=pltpu.PrefetchScalarGridSpec(
            num_scalar_prefetch=1, grid=(1,), in_specs=in_specs,
            out_specs=[whole_spec(x.shape) for x in outs],
        ),
        out_shape=outs,
        compiler_params=BIG,
        cost_estimate=estimate,
    )(ids, *args)


def scores_kernel(counts, carried, ids, *refs):
    refs = list(refs)
    slots = [[refs.pop(0) for _ in range(GROUP)] for _ in counts]
    pieces = [[refs.pop(0) for _ in range(count)] for count in counts]
    carry = [refs.pop(0) for _ in range(2)] if carried else None
    for odd in range(2):
        total = carry[odd][...] if carried else 0.0
        for block, parts in zip(slots, pieces):
            basis = jnp.concatenate([ref[...] for ref in parts], axis=0) if len(parts) > 1 else parts[0][...]
            total = total + jnp.concatenate([nt(basis, ref[...]) for ref in block[odd::2]], axis=1)
        refs[odd][...] = total


def scores(slots, ids, blocks, pieces, carry):
    rows, width = slots[0].shape[0], pieces[0][0].shape[1]
    rank = sum(x.shape[0] for x in pieces[0])
    outs = [struct((rank, rows * GROUP // 2), f32)] * 2
    args = list(slots) * len(blocks) + [x for parts in pieces for x in parts] + list(carry or ())
    specs = slot_specs(blocks, rows, width) + [whole_spec(x.shape) for x in args[len(blocks) * GROUP:]]
    estimate = cost(2 * rank * rows * width * GROUP * len(blocks), 2 * rows * width * GROUP * len(blocks))
    kernel = functools.partial(scores_kernel, [len(parts) for parts in pieces], carry is not None)
    return prefetched(kernel, ids, args, specs, outs, estimate)


def image_kernel(normalised, *refs):
    value, mates = refs[0][...], [ref[...] for ref in refs[1:4]]
    size = value.shape[1] // (GROUP // 2)

    def turned(x, mask):
        return jnp.concatenate([x[:, (j ^ mask) * size:((j ^ mask) + 1) * size] for j in range(GROUP // 2)], axis=1)

    value = (value + turned(mates[0], 1)) + (turned(mates[1], 2) + turned(mates[2], 3))
    if normalised:
        value = nn(refs[4][...], value, HIGHEST)
    refs[-1][...] = value.astype(bf16)


def image_of(value, mates, inverse):
    args = [value, *mates] + ([] if inverse is None else [inverse])
    return pl.pallas_call(
        functools.partial(image_kernel, inverse is not None),
        in_specs=[VMEM] * len(args), out_specs=VMEM, out_shape=struct(value.shape, bf16),
        compiler_params=BIG, cost_estimate=cost(12 * value.size * value.shape[0], 16 * value.size),
    )(*args)


def terms_kernel(ids, *refs):
    slots, images, outs = refs[:GROUP], refs[GROUP:GROUP + 2], refs[GROUP + 2:]
    total = 0.0
    for odd in range(2):
        stacked = jnp.concatenate([ref[...] for ref in slots[odd::2]], axis=0)
        total = total + nn(images[odd][...], stacked)
    step = total.shape[0] // len(outs)
    for part, out in enumerate(outs):
        out[...] = total[part * step:(part + 1) * step].astype(out.dtype)


def terms(slots, ids, block, images, width, parts, dtype):
    rows, rank = slots[0].shape[0], images[0].shape[0]
    args = list(slots) + list(images)
    specs = slot_specs([block], rows, width) + [whole_spec(x.shape) for x in images]
    outs = [struct((rank // parts, width), dtype)] * parts
    estimate = cost(2 * rank * rows * width * GROUP, 2 * rows * width * GROUP)
    return prefetched(terms_kernel, ids, args, specs, outs, estimate)


def fold_kernel(count, with_gram, received, own, *refs):
    before, outs = refs[:count], refs[count:]
    value = own[...] + received[...].astype(f32)
    outs[0][...] = value.astype(outs[0].dtype)
    if not with_gram:
        outs[1][...] = value
        return
    if count:
        value = jnp.concatenate([ref[...] for ref in before] + [value], axis=0)
    outs[1][...] = nt(value, value, HIGHEST)


def fold(received, own, before, dtype, gram):
    rank = own.shape[0] * (1 + len(before))
    second = struct((rank, rank), f32) if gram else struct(own.shape, f32)
    return pl.pallas_call(
        functools.partial(fold_kernel, len(before), gram),
        in_specs=[VMEM] * (2 + len(before)), out_specs=[VMEM] * 2,
        out_shape=[struct(own.shape, dtype), second],
        compiler_params=BIG, cost_estimate=cost(12 * rank * own.size, 12 * own.size),
    )(received, own, *before)


def inverse_factor(gram):
    size = gram.shape[0]
    row = lax.broadcasted_iota(jnp.int32, (size, size), 0)
    column = lax.broadcasted_iota(jnp.int32, (size, size), 1)
    both = jnp.concatenate([gram, jnp.where(row == column, 1.0, 0.0).astype(f32)], axis=1)
    blocks = [both[8 * b:8 * b + 8] for b in range(size // 8)]
    inner = lax.broadcasted_iota(jnp.int32, (8, 2 * size), 0)
    done = []
    for j in range(size):
        b, i = divmod(j, 8)
        root = lax.rsqrt(blocks[b][i:i + 1, j:j + 1])
        pivot = blocks[b][i:i + 1] * root
        done.append(pivot)
        for k in range(b, size // 8):
            factor = jnp.broadcast_to(blocks[k][:, j:j + 1] * root, (8, 2 * size))
            if k == b:
                factor = jnp.where(inner > i, factor, 0.0)
            blocks[k] = blocks[k] - factor * pivot
    return jnp.concatenate(done, axis=0)[:, size:]


def factor_kernel(gram, out):
    out[...] = inverse_factor(gram[...])


def factor_call(gram):
    return pl.pallas_call(
        factor_kernel, in_specs=[VMEM], out_specs=VMEM, out_shape=struct(gram.shape, f32),
        cost_estimate=pl.CostEstimate(flops=20_000_000, bytes_accessed=32768, transcendentals=64),
    )(gram)


def output_kernel(scale, gram, loading, out):
    out[...] = nn(inverse_factor(gram[...]), loading[...], HIGHEST) * scale


def output_call(gram, loading):
    return pl.pallas_call(
        functools.partial(output_kernel, math.sqrt(GENES)),
        in_specs=[VMEM, VMEM], out_specs=VMEM, out_shape=struct(loading.shape, f32),
        compiler_params=pltpu.CompilerParams(vmem_limit_bytes=24 * 2**20),
    )(gram, loading)


def mate(value, cells, mask):
    return lax.ppermute(value, "cell", [(i, i ^ mask) for i in range(cells)])


def total_over_cells(value, cells):
    for low in range(0, cells.bit_length() - 1, 2):
        one, two = 1 << low, 2 << low
        value = (value + mate(value, cells, one)) + (mate(value, cells, two) + mate(value, cells, one | two))
    return value


def square_program(cells, expression, start_basis):
    width, rank = start_basis.shape
    index = lax.axis_index("cell").astype(jnp.int32)
    masks = jnp.arange(1, GROUP, dtype=jnp.int32)
    wanted = index ^ masks
    packs = pack(expression, jnp.stack([wanted, wanted ^ GROUP], axis=1).reshape(-1), width)
    ids = jnp.stack([index, index ^ GROUP])
    basis = start_basis.T
    basis_mate = [mate(basis, cells, GROUP)]
    received = {k: mate(packs[k - 1], cells, k) for k in (2, 4, 3, 5, 6, 7, 1)}
    slots = [expression] + [received[k] for k in range(1, GROUP)]
    step = rank // PARTS

    def summed_image(even, odd, inverse):
        even = even + mate(odd, cells, 1)
        image = image_of(even, [mate(even, cells, mask) for mask in (2, 4, 6)], inverse)
        return image, mate(image, cells, 1)

    even, odd = scores(slots, ids, (0, 1), [[basis], basis_mate], None)
    images = summed_image(even, odd, None)

    for iteration in range(1, ITERS):
        sent = terms(slots, ids, 1, images, width, PARTS, bf16)
        arrived = [mate(x, cells, GROUP) for x in sent]
        own = terms(slots, ids, 0, images, width, PARTS, f32)
        rounded, exact = [], []
        for part in range(PARTS - 1):
            rows, kept = fold(arrived[part], own[part], [], bf16, False)
            rounded.append(rows)
            exact.append(kept)
        rows, gram = fold(arrived[-1], own[-1], exact, bf16, True)
        rounded.append(rows)
        others = [mate(x, cells, GROUP) for x in rounded]
        inverse = factor_call(total_over_cells(gram, cells))
        carry = scores(slots, ids, (0,), [rounded], None)
        even, odd = scores(slots, ids, (1,), [others], carry)
        images = summed_image(even, odd, inverse)

    (sent,) = terms(slots, ids, 1, images, width, 1, bf16)
    arrived = mate(sent, cells, GROUP)
    (own,) = terms(slots, ids, 0, images, width, 1, f32)
    loading, gram = fold(arrived, own, [], f32, True)
    return output_call(total_over_cells(gram, cells), loading).T


def plain_program(expression, start_basis):
    basis = start_basis
    for _ in range(ITERS):
        whole = lax.all_gather(basis, "cell", axis=0, tiled=True)
        partial = jnp.dot(expression, whole, preferred_element_type=f32)
        image = lax.psum(partial, "gene").astype(bf16)
        partial = lax.dot_general(expression, image, (((0,), (0,)), ((), ())), preferred_element_type=f32)
        loading = lax.psum_scatter(partial, "cell", scatter_dimension=0, tiled=True)
        gram = lax.dot_general(loading, loading, (((0,), (0,)), ((), ())), precision=HIGHEST, preferred_element_type=f32)
        lower = jnp.linalg.cholesky(lax.psum(gram, ("cell", "gene")))
        ortho = jax.scipy.linalg.solve_triangular(lower, loading.T, lower=True).T
        basis = ortho.astype(bf16)
    return ortho * math.sqrt(GENES)


def solution(mesh):
    cells, genes = mesh.shape["cell"], mesh.shape["gene"]

    def on_device(expression, start_basis):
        width, rank = start_basis.shape
        fits = genes == 1 and cells == 2 * GROUP and width % 128 == 0 and rank == 64
        if fits and expression.shape[0] % 16 == 0:
            return square_program(cells, expression, start_basis)
        return plain_program(expression, start_basis)

    return jax.shard_map(
        on_device,
        mesh=mesh,
        in_specs=(P(("groups", "cell"), "gene"), P(("groups", "gene", "cell"), None)),
        out_specs=P(("groups", "gene", "cell"), None),
        check_vma=False,
    )
```

time: 481 us -> 264 us (0.55)
  waiting for transfers between devices: 290 us -> 86.2 us
  Pallas kernels: 0 us -> 131 us
  blocking collectives: 120 us -> 0 us
  starting transfers between devices: 0.12 us -> 37.6 us
  matrix products: 32 us -> 0 us
  other arithmetic: 24.2 us -> 0.77 us
  between operations: 13.2 us -> 0.18 us
  local copies, waits for them, and re-layouts: 0.15 us -> 8.26 us
    reduce_scatter x2 -> x0, waiting for transfers between devices: 189 us -> none  [on_device(): lax.psum_scatter(transposed_product(expression, image), 'cell', scatter_d...]
    pallas_call x0 -> x15, Pallas kernels: none -> 131 us  [the longest x1 106 us: pack(): pl.pallas_call(functools.partial(pack_kernel, width), in_specs=[pl.BlockS...]
    psum x2 -> x0, blocking collectives: 120 us -> none  [factor_of(): gram = lax.psum(local_gram, ('cell', 'gene'))]
    all_gather x2 -> x0, waiting for transfers between devices: 101 us -> none  [on_device(): lax.all_gather(basis, 'cell', axis=0, tiled=True)]
    ppermute x0 -> x35, waiting for transfers between devices: none -> 86.2 us  [mate(): return lax.ppermute(value, 'cell', [(i, i ^ mask) for i in range(cells)])]
    ppermute x0 -> x35, starting transfers between devices: none -> 37.6 us  [mate(): return lax.ppermute(value, 'cell', [(i, i ^ mask) for i in range(cells)])]
    dot_general x4 -> x0, matrix products: 27.3 us -> none  [the longest x2 23.7 us: transposed_product(): lax.dot_general(left, right, (((0,), (0,)), ((), ())), preferred_element_...]
    another operation x10 -> x2, other arithmetic: 24.2 us -> 0.09 us  [the longest x1 0.07 us: square_program(): ids = jnp.stack([index, index ^ GROUP])]
  transfers between devices with their start and end apart: 4 -> 35, of which waited for: 4 -> 19; matrix products, arithmetic and copies ran while one was open for 0% -> 0% of each run, Pallas kernels for 0% -> 4%
where the time goes in v1:
time: 264 us
  Pallas kernels  131 us (50%)
  waiting for transfers between devices  86.2 us (33%)
  starting transfers between devices  37.6 us (14%)
  local copies, waits for them, and re-layouts  8.26 us (3%)
    pallas_call x1, Pallas kernels, pack(): pl.pallas_call(functools.partial(pack_kernel, width), in_specs=[pl.BlockS...  106 us
    ppermute x35, waiting for transfers between devices, mate(): return lax.ppermute(value, 'cell', [(i, i ^ mask) for i in range(cells)])  86.2 us
    ppermute x35, starting transfers between devices, mate(): return lax.ppermute(value, 'cell', [(i, i ^ mask) for i in range(cells)])  37.6 us
    pallas_call x7, Pallas kernels, prefetched(): pl.pallas_call(kernel, grid_spec=pltpu.PrefetchScalarGridSpec(num_scalar_...  8.49 us
    unnamed x16, local copies, waits for them, and re-layouts  7.56 us
    pallas_call x1, Pallas kernels, factor_call(): pl.pallas_call(factor_kernel, in_specs=[VMEM], out_specs=VMEM, out_shape=...  6.82 us
    pallas_call x1, Pallas kernels, output_call(): pl.pallas_call(functools.partial(output_kernel, math.sqrt(GENES)), in_spe...  6.74 us
  transfers between devices with their start and end apart: 35, of which 19 were waited for; matrix products, arithmetic and copies ran while one was open for 0% of the time, Pallas kernels for 4%

profile of v1, /device:TPU:0, one launch (start us, length us, event | category | flops | bytes accessed | tf_op | source)
XLA Modules:
  0.0 263.6 jit_solution(5412690253153398700)
XLA Ops:
  0.7 106.1 %shard_map.28 = (bf16[64,3840]{1,0:T(8,128)(2,1)}, bf16[64,3840]{1,0:T(8,128)(2,1)}, bf16[64,3840]{1,0:T(8,128)(2,1)}, bf16[64,3840]{1,0:T(8,128)(2,1)}, bf16[64...) custom-call(s32[14]{0:T(128)} %reshape.17.ids, bf16[64,30720]{1,0:T(8,128)(2,1)} %refs_0_.13), custom_call_target="tpu_custom_call" | custom-call | bytes 6881280 | tf_op jit(solution)/shard_map/pallas_call | solution.py:54
  107.4 2.6 collective-permute-start.1
  110.0 2.6 collective-permute-start.7
  112.6 1.6 collective-permute-start.3
  114.1 10.1 %collective-permute-done.7.refs_17_ = bf16[64,1920]{1,0:T(8,128)(2,1)S(1)} collective-permute-done((bf16[64,1920]{1,0:T(8,128)(2,1)S(1)}, bf16[64,1920]{1,0:T(8,128)(2,1)S(1)}, u32[]{:S(2)}, u32[]{:S(2)}) %collective-permute-start.7) | collective-permute-done | bytes 245792 | tf_op jit(solution)/shard_map/ppermute | solution.py:223
  126.1 1.9 collective-permute-start.6
  128.0 4.2 %collective-permute-done.2.refs_3_.refs_11_ = bf16[64,3840]{1,0:T(8,128)(2,1)S(1)} collective-permute-done((bf16[64,3840]{1,0:T(8,128)(2,1)}, bf16[64,3840]{1,0:T(8,128)(2,1)S(1)}, u32[]{:S(2)}, u32[]{:S(2)}) %collective-permute-start.2) | collective-permute-done | bytes 491552 | tf_op jit(solution)/shard_map/ppermute | solution.py:223
  132.3 8.7 %collective-permute-done.4.refs_5_.refs_13_ = bf16[64,3840]{1,0:T(8,128)(2,1)S(1)} collective-permute-done((bf16[64,3840]{1,0:T(8,128)(2,1)}, bf16[64,3840]{1,0:T(8,128)(2,1)S(1)}, u32[]{:S(2)}, u32[]{:S(2)}) %collective-permute-start.4) | collective-permute-done | bytes 491552 | tf_op jit(solution)/shard_map/ppermute | solution.py:223
  140.9 11.9 %collective-permute-done.5.refs_6_.refs_14_ = bf16[64,3840]{1,0:T(8,128)(2,1)S(1)} collective-permute-done((bf16[64,3840]{1,0:T(8,128)(2,1)}, bf16[64,3840]{1,0:T(8,128)(2,1)S(1)}, u32[]{:S(2)}, u32[]{:S(2)}) %collective-permute-start.5) | collective-permute-done | bytes 491552 | tf_op jit(solution)/shard_map/ppermute | solution.py:223
  152.9 10.0 %collective-permute-done.6.refs_7_.refs_15_ = bf16[64,3840]{1,0:T(8,128)(2,1)S(1)} collective-permute-done((bf16[64,3840]{1,0:T(8,128)(2,1)}, bf16[64,3840]{1,0:T(8,128)(2,1)S(1)}, u32[]{:S(2)}, u32[]{:S(2)}) %collective-permute-start.6) | collective-permute-done | bytes 491552 | tf_op jit(solution)/shard_map/ppermute | solution.py:223
  162.9 2.1 copy-done
  166.9 1.9 shard_map.29
  170.4 1.8 collective-permute-start.10
  172.2 1.5 collective-permute-start.9
  173.7 2.3 collective-permute-done.11.refs_3_
  180.0 2.1 collective-permute-start.15
  183.0 7.5 %collective-permute-done.13.received = bf16[32,1920]{1,0:T(8,128)(2,1)S(1)} collective-permute-done((bf16[32,1920]{1,0:T(8,128)(2,1)S(1)}, bf16[32,1920]{1,0:T(8,128)(2,1)S(1)}, u32[]{:S(2)}, u32[]{:S(2)}) %collective-permute-start.13) | collective-permute-done | bytes 122912 | tf_op jit(solution)/shard_map/ppermute | solution.py:223
  190.5 2.5 collective-permute-done.15.received
  193.7 2.9 %collective-permute-start.14 = (bf16[32,1920]{1,0:T(8,128)(2,1)S(1)}, bf16[32,1920]{1,0:T(8,128)(2,1)S(1)}, u32[]{:S(2)}, u32[]{:S(2)}) collective-permute-start(bf16[32,1920]{1,0:T(8,128)(2,1)S(1)} %get-tuple-element.39.refs_8_), channel_id=1, source_target_pairs={{0,8},{1,9},{2,10},{3,11},{4,12},{5,13},{6,14},{7,15},{8,0},{9,1},... | collective-permute-start | bytes 368648 | tf_op jit(solution)/shard_map/ppermute | solution.py:223
  199.8 4.7 %collective-permute-done.16.refs_9_ = bf16[32,1920]{1,0:T(8,128)(2,1)S(1)} collective-permute-done((bf16[32,1920]{1,0:T(8,128)(2,1)S(1)}, bf16[32,1920]{1,0:T(8,128)(2,1)S(1)}, u32[]{:S(2)}, u32[]{:S(2)}) %collective-permute-start.16) | collective-permute-done | bytes 122912 | tf_op jit(solution)/shard_map/ppermute | solution.py:223
  204.6 2.6 collective-permute-done.14.refs_8_
  208.6 1.9 collective-permute-start.26
  210.5 2.5 collective-permute-start.24
  213.9 2.0 collective-permute-start.19
  217.2 6.8 %shard_map.37.refs_4_ = f32[64,64]{1,0:T(8,128)} custom-call(f32[64,64]{1,0:T(8,128)} %add_add_fusion.2.gram), custom_call_target="tpu_custom_call" | custom-call | flops 20000000 | bytes 32768 | tf_op jit(solution)/shard_map/pallas_call | solution.py:204
  227.3 2.1 copy-done.2
  232.5 12.1 %collective-permute-done.28.received = bf16[64,1920]{1,0:T(8,128)(2,1)S(1)} collective-permute-done((bf16[64,1920]{1,0:T(8,128)(2,1)S(1)}, bf16[64,1920]{1,0:T(8,128)(2,1)S(1)}, u32[]{:S(2)}, u32[]{:S(2)}) %collective-permute-start.28) | collective-permute-done | bytes 245792 | tf_op jit(solution)/shard_map/ppermute | solution.py:223
  247.2 1.8 collective-permute-done.31
  250.0 1.8 collective-permute-start.34
  251.9 2.6 collective-permute-start.32
  254.5 1.6 collective-permute-done.34
  256.9 6.7 %shard_map.42 = f32[64,1920]{1,0:T(8,128)} custom-call(f32[64,64]{1,0:T(8,128)S(1)} %add_add_fusion.gram, f32[64,1920]{1,0:T(8,128)S(1)} %get-tuple-element.50.loading), custom_call_target="tpu_custom_call" | custom-call | tf_op jit(solution)/shard_map/pallas_call | solution.py:215
  (80 shorter events, 29.8 us)
Async XLA Ops:
  106.8 18.4 %collective-permute-start = (bf16[64,3840]{1,0:T(8,128)(2,1)}, bf16[64,3840]{1,0:T(8,128)(2,1)S(1)}, u32[]{:S(2)}, u32[]{:S(2)}) collective-permute-start(bf16[64,3840]{1,0:T(8,128)(2,1)} %get-tuple-element.28), channel_id=1, source_target_pairs={{0,1},{1,0},{2,3},{3,2},{4,5},{5,4},{6,7},{7,6},{8,9},{9,8},{10,11... | collective-permute-start | bytes 1474568 | tf_op jit(solution)/shard_map/ppermute | solution.py:223
  107.4 18.7 %collective-permute-start.1 = (bf16[64,3840]{1,0:T(8,128)(2,1)}, bf16[64,3840]{1,0:T(8,128)(2,1)S(1)}, u32[]{:S(2)}, u32[]{:S(2)}) collective-permute-start(bf16[64,3840]{1,0:T(8,128)(2,1)} %get-tuple-element.29), channel_id=1, source_target_pairs={{0,2},{1,3},{2,0},{3,1},{4,6},{5,7},{6,4},{7,5},{8,10},{9,11},{10,... | collective-permute-start | bytes 1474568 | tf_op jit(solution)/shard_map/ppermute | solution.py:223
  110.0 14.3 %collective-permute-start.7 = (bf16[64,1920]{1,0:T(8,128)(2,1)S(1)}, bf16[64,1920]{1,0:T(8,128)(2,1)S(1)}, u32[]{:S(2)}, u32[]{:S(2)}) collective-permute-start(bf16[64,1920]{1,0:T(8,128)(2,1)S(1)} %bitcast.4), channel_id=1, source_target_pairs={{0,8},{1,9},{2,10},{3,11},{4,12},{5,13},{6,14},{7,15},{8,0},{9,1},... | collective-permute-start | bytes 737288 | tf_op jit(solution)/shard_map/ppermute | solution.py:223
  112.5 19.7 %collective-permute-start.2 = (bf16[64,3840]{1,0:T(8,128)(2,1)}, bf16[64,3840]{1,0:T(8,128)(2,1)S(1)}, u32[]{:S(2)}, u32[]{:S(2)}) collective-permute-start(bf16[64,3840]{1,0:T(8,128)(2,1)} %get-tuple-element.30), channel_id=1, source_target_pairs={{0,3},{1,2},{2,1},{3,0},{4,7},{5,6},{6,5},{7,4},{8,11},{9,10},{10,... | collective-permute-start | bytes 1474568 | tf_op jit(solution)/shard_map/ppermute | solution.py:223
  112.6 19.7 %collective-permute-start.3 = (bf16[64,3840]{1,0:T(8,128)(2,1)}, bf16[64,3840]{1,0:T(8,128)(2,1)S(1)}, u32[]{:S(2)}, u32[]{:S(2)}) collective-permute-start(bf16[64,3840]{1,0:T(8,128)(2,1)} %get-tuple-element.31), channel_id=1, source_target_pairs={{0,4},{1,5},{2,6},{3,7},{4,0},{5,1},{6,2},{7,3},{8,12},{9,13},{10,... | collective-permute-start | bytes 1474568 | tf_op jit(solution)/shard_map/ppermute | solution.py:223
  125.0 16.0 %collective-permute-start.4 = (bf16[64,3840]{1,0:T(8,128)(2,1)}, bf16[64,3840]{1,0:T(8,128)(2,1)S(1)}, u32[]{:S(2)}, u32[]{:S(2)}) collective-permute-start(bf16[64,3840]{1,0:T(8,128)(2,1)} %get-tuple-element.32), channel_id=1, source_target_pairs={{0,5},{1,4},{2,7},{3,6},{4,1},{5,0},{6,3},{7,2},{8,13},{9,12},{10,... | collective-permute-start | bytes 1474568 | tf_op jit(solution)/shard_map/ppermute | solution.py:223
  125.2 27.7 %collective-permute-start.5 = (bf16[64,3840]{1,0:T(8,128)(2,1)}, bf16[64,3840]{1,0:T(8,128)(2,1)S(1)}, u32[]{:S(2)}, u32[]{:S(2)}) collective-permute-start(bf16[64,3840]{1,0:T(8,128)(2,1)} %get-tuple-element.33), channel_id=1, source_target_pairs={{0,6},{1,7},{2,4},{3,5},{4,2},{5,3},{6,0},{7,1},{8,14},{9,15},{10,... | collective-permute-start | bytes 1474568 | tf_op jit(solution)/shard_map/ppermute | solution.py:223
  126.1 36.8 %collective-permute-start.6 = (bf16[64,3840]{1,0:T(8,128)(2,1)}, bf16[64,3840]{1,0:T(8,128)(2,1)S(1)}, u32[]{:S(2)}, u32[]{:S(2)}) collective-permute-start(bf16[64,3840]{1,0:T(8,128)(2,1)} %get-tuple-element.34), channel_id=1, source_target_pairs={{0,7},{1,6},{2,5},{3,4},{4,3},{5,2},{6,1},{7,0},{8,15},{9,14},{10,... | collective-permute-start | bytes 1474568 | tf_op jit(solution)/shard_map/ppermute | solution.py:223
  170.1 5.8 %collective-permute-start.11 = (f32[64,256]{1,0:T(8,128)S(1)}, f32[64,256]{1,0:T(8,128)S(1)}, u32[]{:S(2)}, u32[]{:S(2)}) collective-permute-start(f32[64,256]{1,0:T(8,128)S(1)} %add.57.refs_0_), channel_id=1, source_target_pairs={{0,6},{1,7},{2,4},{3,5},{4,2},{5,3},{6,0},{7,1},{8,14},{9,15},{10,... | collective-permute-start | bytes 196616 | tf_op jit(solution)/shard_map/ppermute | solution.py:223
  170.4 5.6 %collective-permute-start.10 = (f32[64,256]{1,0:T(8,128)S(1)}, f32[64,256]{1,0:T(8,128)S(1)}, u32[]{:S(2)}, u32[]{:S(2)}) collective-permute-start(f32[64,256]{1,0:T(8,128)S(1)} %add.57.refs_0_), channel_id=1, source_target_pairs={{0,4},{1,5},{2,6},{3,7},{4,0},{5,1},{6,2},{7,3},{8,12},{9,13},{10,... | collective-permute-start | bytes 196616 | tf_op jit(solution)/shard_map/ppermute | solution.py:223
  172.2 4.4 %collective-permute-start.9 = (f32[64,256]{1,0:T(8,128)S(1)}, f32[64,256]{1,0:T(8,128)S(1)}, u32[]{:S(2)}, u32[]{:S(2)}) collective-permute-start(f32[64,256]{1,0:T(8,128)S(1)} %add.57.refs_0_), channel_id=1, source_target_pairs={{0,2},{1,3},{2,0},{3,1},{4,6},{5,7},{6,4},{7,5},{8,10},{9,11},{10,... | collective-permute-start | bytes 196616 | tf_op jit(solution)/shard_map/ppermute | solution.py:223
  179.0 11.5 %collective-permute-start.13 = (bf16[32,1920]{1,0:T(8,128)(2,1)S(1)}, bf16[32,1920]{1,0:T(8,128)(2,1)S(1)}, u32[]{:S(2)}, u32[]{:S(2)}) collective-permute-start(bf16[32,1920]{1,0:T(8,128)(2,1)S(1)} %get-tuple-element.37), channel_id=1, source_target_pairs={{0,8},{1,9},{2,10},{3,11},{4,12},{5,13},{6,14},{7,15},{8,0},{9,1},... | collective-permute-start | bytes 368648 | tf_op jit(solution)/shard_map/ppermute | solution.py:223
  180.0 13.1 %collective-permute-start.15 = (bf16[32,1920]{1,0:T(8,128)(2,1)S(1)}, bf16[32,1920]{1,0:T(8,128)(2,1)S(1)}, u32[]{:S(2)}, u32[]{:S(2)}) collective-permute-start(bf16[32,1920]{1,0:T(8,128)(2,1)S(1)} %get-tuple-element.40), channel_id=1, source_target_pairs={{0,8},{1,9},{2,10},{3,11},{4,12},{5,13},{6,14},{7,15},{8,0},{9,1},... | collective-permute-start | bytes 368648 | tf_op jit(solution)/shard_map/ppermute | solution.py:223
  193.6 10.9 %collective-permute-start.16 = (bf16[32,1920]{1,0:T(8,128)(2,1)S(1)}, bf16[32,1920]{1,0:T(8,128)(2,1)S(1)}, u32[]{:S(2)}, u32[]{:S(2)}) collective-permute-start(bf16[32,1920]{1,0:T(8,128)(2,1)S(1)} %get-tuple-element.43.refs_9_), channel_id=1, source_target_pairs={{0,8},{1,9},{2,10},{3,11},{4,12},{5,13},{6,14},{7,15},{8,0},{9,1},... | collective-permute-start | bytes 368648 | tf_op jit(solution)/shard_map/ppermute | solution.py:223
  193.7 13.4 %collective-permute-start.14 = (bf16[32,1920]{1,0:T(8,128)(2,1)S(1)}, bf16[32,1920]{1,0:T(8,128)(2,1)S(1)}, u32[]{:S(2)}, u32[]{:S(2)}) collective-permute-start(bf16[32,1920]{1,0:T(8,128)(2,1)S(1)} %get-tuple-element.39.refs_8_), channel_id=1, source_target_pairs={{0,8},{1,9},{2,10},{3,11},{4,12},{5,13},{6,14},{7,15},{8,0},{9,1},... | collective-permute-start | bytes 368648 | tf_op jit(solution)/shard_map/ppermute | solution.py:223
  196.6 11.9 %collective-permute-start.23 = (f32[64,64]{1,0:T(8,128)S(1)}, f32[64,64]{1,0:T(8,128)S(1)}, u32[]{:S(2)}, u32[]{:S(2)}) collective-permute-start(f32[64,64]{1,0:T(8,128)S(1)} %get-tuple-element.48), channel_id=1, source_target_pairs={{0,3},{1,2},{2,1},{3,0},{4,7},{5,6},{6,5},{7,4},{8,11},{9,10},{10,... | collective-permute-start | bytes 49160 | tf_op jit(solution)/shard_map/ppermute | solution.py:223
  197.0 11.5 %collective-permute-start.22 = (f32[64,64]{1,0:T(8,128)S(1)}, f32[64,64]{1,0:T(8,128)S(1)}, u32[]{:S(2)}, u32[]{:S(2)}) collective-permute-start(f32[64,64]{1,0:T(8,128)S(1)} %get-tuple-element.48), channel_id=1, source_target_pairs={{0,2},{1,3},{2,0},{3,1},{4,6},{5,7},{6,4},{7,5},{8,10},{9,11},{10,... | collective-permute-start | bytes 49160 | tf_op jit(solution)/shard_map/ppermute | solution.py:223
  198.0 10.6 %collective-permute-start.21 = (f32[64,64]{1,0:T(8,128)S(1)}, f32[64,64]{1,0:T(8,128)S(1)}, u32[]{:S(2)}, u32[]{:S(2)}) collective-permute-start(f32[64,64]{1,0:T(8,128)S(1)} %get-tuple-element.48), channel_id=1, source_target_pairs={{0,1},{1,0},{2,3},{3,2},{4,5},{5,4},{6,7},{7,6},{8,9},{9,8},{10,11... | collective-permute-start | bytes 49160 | tf_op jit(solution)/shard_map/ppermute | solution.py:223
  208.4 4.6 %collective-permute-start.17 = (f32[64,256]{1,0:T(8,128)S(1)}, f32[64,256]{1,0:T(8,128)S(1)}, u32[]{:S(2)}, u32[]{:S(2)}) collective-permute-start(f32[64,256]{1,0:T(8,128)S(1)} %get-tuple-element.47), channel_id=1, source_target_pairs={{0,1},{1,0},{2,3},{3,2},{4,5},{5,4},{6,7},{7,6},{8,9},{9,8},{10,11... | collective-permute-start | bytes 196616 | tf_op jit(solution)/shard_map/ppermute | solution.py:223
  208.6 7.4 %collective-permute-start.26 = (f32[64,64]{1,0:T(8,128)S(1)}, f32[64,64]{1,0:T(8,128)S(1)}, u32[]{:S(2)}, u32[]{:S(2)}) collective-permute-start(f32[64,64]{1,0:T(8,128)S(1)} %add_add_fusion.3), channel_id=1, source_target_pairs={{0,12},{1,13},{2,14},{3,15},{4,8},{5,9},{6,10},{7,11},{8,4},{9,5},... | collective-permute-start | bytes 49160 | tf_op jit(solution)/shard_map/ppermute | solution.py:223
  210.5 6.1 %collective-permute-start.25 = (f32[64,64]{1,0:T(8,128)S(1)}, f32[64,64]{1,0:T(8,128)S(1)}, u32[]{:S(2)}, u32[]{:S(2)}) collective-permute-start(f32[64,64]{1,0:T(8,128)S(1)} %add_add_fusion.3), channel_id=1, source_target_pairs={{0,8},{1,9},{2,10},{3,11},{4,12},{5,13},{6,14},{7,15},{8,0},{9,1},... | collective-permute-start | bytes 49160 | tf_op jit(solution)/shard_map/ppermute | solution.py:223
  210.5 6.1 %collective-permute-start.24 = (f32[64,64]{1,0:T(8,128)S(1)}, f32[64,64]{1,0:T(8,128)S(1)}, u32[]{:S(2)}, u32[]{:S(2)}) collective-permute-start(f32[64,64]{1,0:T(8,128)S(1)} %add_add_fusion.3), channel_id=1, source_target_pairs={{0,4},{1,5},{2,6},{3,7},{4,0},{5,1},{6,2},{7,3},{8,12},{9,13},{10,... | collective-permute-start | bytes 49160 | tf_op jit(solution)/shard_map/ppermute | solution.py:223
  213.0 11.0 %collective-permute-start.20 = (f32[64,256]{1,0:T(8,128)S(1)}, f32[64,256]{1,0:T(8,128)}, u32[]{:S(2)}, u32[]{:S(2)}) collective-permute-start(f32[64,256]{1,0:T(8,128)S(1)} %add.58.refs_0_), channel_id=1, source_target_pairs={{0,6},{1,7},{2,4},{3,5},{4,2},{5,3},{6,0},{7,1},{8,14},{9,15},{10,... | collective-permute-start | bytes 196616 | tf_op jit(solution)/shard_map/ppermute | solution.py:223
  213.9 10.1 %collective-permute-start.19 = (f32[64,256]{1,0:T(8,128)S(1)}, f32[64,256]{1,0:T(8,128)}, u32[]{:S(2)}, u32[]{:S(2)}) collective-permute-start(f32[64,256]{1,0:T(8,128)S(1)} %add.58.refs_0_), channel_id=1, source_target_pairs={{0,4},{1,5},{2,6},{3,7},{4,0},{5,1},{6,2},{7,3},{8,12},{9,13},{10,... | collective-permute-start | bytes 196616 | tf_op jit(solution)/shard_map/ppermute | solution.py:223
  216.0 8.1 %collective-permute-start.18 = (f32[64,256]{1,0:T(8,128)S(1)}, f32[64,256]{1,0:T(8,128)}, u32[]{:S(2)}, u32[]{:S(2)}) collective-permute-start(f32[64,256]{1,0:T(8,128)S(1)} %add.58.refs_0_), channel_id=1, source_target_pairs={{0,2},{1,3},{2,0},{3,1},{4,6},{5,7},{6,4},{7,5},{8,10},{9,11},{10,... | collective-permute-start | bytes 196616 | tf_op jit(solution)/shard_map/ppermute | solution.py:223
  230.4 14.2 %collective-permute-start.28 = (bf16[64,1920]{1,0:T(8,128)(2,1)S(1)}, bf16[64,1920]{1,0:T(8,128)(2,1)S(1)}, u32[]{:S(2)}, u32[]{:S(2)}) collective-permute-start(bf16[64,1920]{1,0:T(8,128)(2,1)S(1)} %shard_map.39), channel_id=1, source_target_pairs={{0,8},{1,9},{2,10},{3,11},{4,12},{5,13},{6,14},{7,15},{8,0},{9,1},... | collective-permute-start | bytes 737288 | tf_op jit(solution)/shard_map/ppermute | solution.py:223
  245.2 3.7 %collective-permute-start.31 = (f32[64,64]{1,0:T(8,128)S(1)}, f32[64,64]{1,0:T(8,128)S(1)}, u32[]{:S(2)}, u32[]{:S(2)}) collective-permute-start(f32[64,64]{1,0:T(8,128)S(1)} %get-tuple-element.49), channel_id=1, source_target_pairs={{0,3},{1,2},{2,1},{3,0},{4,7},{5,6},{6,5},{7,4},{8,11},{9,10},{10,... | collective-permute-start | bytes 49160 | tf_op jit(solution)/shard_map/ppermute | solution.py:223
  246.1 3.9 %collective-permute-start.30 = (f32[64,64]{1,0:T(8,128)S(1)}, f32[64,64]{1,0:T(8,128)S(1)}, u32[]{:S(2)}, u32[]{:S(2)}) collective-permute-start(f32[64,64]{1,0:T(8,128)S(1)} %get-tuple-element.49), channel_id=1, source_target_pairs={{0,2},{1,3},{2,0},{3,1},{4,6},{5,7},{6,4},{7,5},{8,10},{9,11},{10,... | collective-permute-start | bytes 49160 | tf_op jit(solution)/shard_map/ppermute | solution.py:223
  246.8 3.2 %collective-permute-start.29 = (f32[64,64]{1,0:T(8,128)S(1)}, f32[64,64]{1,0:T(8,128)S(1)}, u32[]{:S(2)}, u32[]{:S(2)}) collective-permute-start(f32[64,64]{1,0:T(8,128)S(1)} %get-tuple-element.49), channel_id=1, source_target_pairs={{0,1},{1,0},{2,3},{3,2},{4,5},{5,4},{6,7},{7,6},{8,9},{9,8},{10,11... | collective-permute-start | bytes 49160 | tf_op jit(solution)/shard_map/ppermute | solution.py:223
  250.0 6.0 %collective-permute-start.34 = (f32[64,64]{1,0:T(8,128)S(1)}, f32[64,64]{1,0:T(8,128)S(1)}, u32[]{:S(2)}, u32[]{:S(2)}) collective-permute-start(f32[64,64]{1,0:T(8,128)S(1)} %add_add_fusion.1), channel_id=1, source_target_pairs={{0,12},{1,13},{2,14},{3,15},{4,8},{5,9},{6,10},{7,11},{8,4},{9,5},... | collective-permute-start | bytes 49160 | tf_op jit(solution)/shard_map/ppermute | solution.py:223
  251.9 5.0 %collective-permute-start.33 = (f32[64,64]{1,0:T(8,128)S(1)}, f32[64,64]{1,0:T(8,128)S(1)}, u32[]{:S(2)}, u32[]{:S(2)}) collective-permute-start(f32[64,64]{1,0:T(8,128)S(1)} %add_add_fusion.1), channel_id=1, source_target_pairs={{0,8},{1,9},{2,10},{3,11},{4,12},{5,13},{6,14},{7,15},{8,0},{9,1},... | collective-permute-start | bytes 49160 | tf_op jit(solution)/shard_map/ppermute | solution.py:223
  251.9 5.0 %collective-permute-start.32 = (f32[64,64]{1,0:T(8,128)S(1)}, f32[64,64]{1,0:T(8,128)S(1)}, u32[]{:S(2)}, u32[]{:S(2)}) collective-permute-start(f32[64,64]{1,0:T(8,128)S(1)} %add_add_fusion.1), channel_id=1, source_target_pairs={{0,4},{1,5},{2,6},{3,7},{4,0},{5,1},{6,2},{7,3},{8,12},{9,13},{10,... | collective-permute-start | bytes 49160 | tf_op jit(solution)/shard_map/ppermute | solution.py:223
  (11 other events, 132.5 us)

commit v2 on v1

--- a/solution.py
+++ b/solution.py
@@ -12,7 +12,8 @@
 ITERS = 2
 PARTS = 2
 GROUP = 8
-BIG = pltpu.CompilerParams(vmem_limit_bytes=32 * 2**20)
+BIG = pltpu.CompilerParams(vmem_limit_bytes=16 * 2**20)
+SMALL = pltpu.CompilerParams(vmem_limit_bytes=4 * 2**20)
 VMEM = pl.BlockSpec(memory_space=pltpu.VMEM)
 HIGHEST = lax.Precision.HIGHEST
 f32, bf16 = jnp.float32, jnp.bfloat16
@@ -34,80 +35,52 @@
     return pl.CostEstimate(flops=flops, bytes_accessed=bytes_accessed, transcendentals=0)
 
 
-def pack_kernel(width, ids, matrix, *refs):
-    outs, sem = refs[:-1], refs[-1]
-    copies = []
-    for k, out in enumerate(outs):
-        for j in range(2):
-            start = pl.multiple_of(ids[2 * k + j] * width, 128)
-            copies.append(pltpu.make_async_copy(
-                matrix.at[:, pl.ds(start, width)], out.at[:, pl.ds(j * width, width)], sem.at[2 * k + j]))
-    for copy in copies:
-        copy.start()
-    for copy in copies:
-        copy.wait()
+def pack_kernel(ids, first, second, out):
+    width = first.shape[1]
+    out[:, :width] = first[...]
+    out[:, width:] = second[...]
 
 
 def pack(matrix, ids, width):
-    rows, count = matrix.shape[0], ids.shape[0] // 2
-    anywhere = pl.BlockSpec(memory_space=pl.ANY)
-    return pl.pallas_call(
-        functools.partial(pack_kernel, width),
-        in_specs=[pl.BlockSpec(memory_space=pltpu.SMEM), anywhere],
-        out_specs=[anywhere] * count,
-        out_shape=[struct((rows, 2 * width), matrix.dtype)] * count,
-        scratch_shapes=[pltpu.SemaphoreType.DMA((2 * count,))],
-        cost_estimate=cost(0, 8 * rows * count * width),
-    )(ids, matrix)
-
-
-def slot_specs(blocks, rows, width):
-    specs = []
-    for j in blocks:
-        specs.append(pl.BlockSpec((rows, width), functools.partial(lambda j, s, ids: (0, ids[j]), j)))
-        specs += [pl.BlockSpec((rows, width), functools.partial(lambda j, s, ids: (0, j), j))] * (GROUP - 1)
-    return specs
-
-
-def whole_spec(shape):
-    return pl.BlockSpec(shape, lambda s, ids: (0,) * len(shape))
-
-
-def prefetched(kernel, ids, args, in_specs, outs, estimate):
-    return pl.pallas_call(
-        kernel,
+    rows = matrix.shape[0]
+    return pl.pallas_call(
+        pack_kernel,
         grid_spec=pltpu.PrefetchScalarGridSpec(
-            num_scalar_prefetch=1, grid=(1,), in_specs=in_specs,
-            out_specs=[whole_spec(x.shape) for x in outs],
+            num_scalar_prefetch=1, grid=(1,),
+            in_specs=[pl.BlockSpec((rows, width), lambda s, ids: (0, ids[0])),
+                      pl.BlockSpec((rows, width), lambda s, ids: (0, ids[1]))],
+            out_specs=pl.BlockSpec((rows, 2 * width), lambda s, ids: (0, 0)),
         ),
-        out_shape=outs,
-        compiler_params=BIG,
-        cost_estimate=estimate,
-    )(ids, *args)
-
-
-def scores_kernel(counts, carried, ids, *refs):
-    refs = list(refs)
-    slots = [[refs.pop(0) for _ in range(GROUP)] for _ in counts]
-    pieces = [[refs.pop(0) for _ in range(count)] for count in counts]
-    carry = [refs.pop(0) for _ in range(2)] if carried else None
-    for odd in range(2):
-        total = carry[odd][...] if carried else 0.0
-        for block, parts in zip(slots, pieces):
-            basis = jnp.concatenate([ref[...] for ref in parts], axis=0) if len(parts) > 1 else parts[0][...]
-            total = total + jnp.concatenate([nt(basis, ref[...]) for ref in block[odd::2]], axis=1)
-        refs[odd][...] = total
-
-
-def scores(slots, ids, blocks, pieces, carry):
-    rows, width = slots[0].shape[0], pieces[0][0].shape[1]
-    rank = sum(x.shape[0] for x in pieces[0])
-    outs = [struct((rank, rows * GROUP // 2), f32)] * 2
-    args = list(slots) * len(blocks) + [x for parts in pieces for x in parts] + list(carry or ())
-    specs = slot_specs(blocks, rows, width) + [whole_spec(x.shape) for x in args[len(blocks) * GROUP:]]
-    estimate = cost(2 * rank * rows * width * GROUP * len(blocks), 2 * rows * width * GROUP * len(blocks))
-    kernel = functools.partial(scores_kernel, [len(parts) for parts in pieces], carry is not None)
-    return prefetched(kernel, ids, args, specs, outs, estimate)
+        out_shape=struct((rows, 2 * width), matrix.dtype),
+        compiler_params=SMALL,
+        cost_estimate=cost(0, 8 * rows * width),
+    )(ids, matrix, matrix)
+
+
+def call(kernel, args, outs, estimate):
+    return pl.pallas_call(
+        kernel, in_specs=[VMEM] * len(args), out_specs=[VMEM] * len(outs), out_shape=outs,
+        compiler_params=BIG, cost_estimate=estimate,
+    )(*args)
+
+
+def stacked(slots, block, width):
+    return jnp.concatenate([ref[:, block * width:(block + 1) * width] for ref in slots], axis=0)
+
+
+def scores_kernel(count, own, other, *refs):
+    width = own.shape[1]
+    slots, before, out = refs[:count], refs[count:-1], refs[-1]
+    total = nt(own[...], stacked(slots, 0, width)) + nt(other[...], stacked(slots, 1, width))
+    out[...] = jnp.concatenate([ref[...] for ref in before] + [total], axis=0) if before else total
+
+
+def scores(slots, own, other, before):
+    rank, width = own.shape
+    cells = slots[0].shape[0] * len(slots)
+    outs = [struct((rank + sum(x.shape[0] for x in before), cells), f32)]
+    return call(functools.partial(scores_kernel, len(slots)), [own, other, *slots, *before], outs,
+                cost(4 * rank * cells * width, 4 * cells * width))[0]
 
 
 def image_kernel(normalised, *refs):
@@ -132,24 +105,22 @@
     )(*args)
 
 
-def terms_kernel(ids, *refs):
+def terms_kernel(block, *refs):
     slots, images, outs = refs[:GROUP], refs[GROUP:GROUP + 2], refs[GROUP + 2:]
-    total = 0.0
-    for odd in range(2):
-        stacked = jnp.concatenate([ref[...] for ref in slots[odd::2]], axis=0)
-        total = total + nn(images[odd][...], stacked)
+    width = outs[0].shape[1]
+    total = nn(images[0][...], stacked(slots[0::2], block, width))
+    total = total + nn(images[1][...], stacked(slots[1::2], block, width))
     step = total.shape[0] // len(outs)
     for part, out in enumerate(outs):
         out[...] = total[part * step:(part + 1) * step].astype(out.dtype)
 
 
-def terms(slots, ids, block, images, width, parts, dtype):
-    rows, rank = slots[0].shape[0], images[0].shape[0]
-    args = list(slots) + list(images)
-    specs = slot_specs([block], rows, width) + [whole_spec(x.shape) for x in images]
+def terms(slots, block, images, parts, dtype):
+    rank, width = images[0].shape[0], slots[0].shape[1] // 2
     outs = [struct((rank // parts, width), dtype)] * parts
-    estimate = cost(2 * rank * rows * width * GROUP, 2 * rows * width * GROUP)
-    return prefetched(terms_kernel, ids, args, specs, outs, estimate)
+    cells = slots[0].shape[0] * GROUP
+    return call(functools.partial(terms_kernel, block), [*slots, *images], outs,
+                cost(2 * rank * cells * width, 2 * cells * width))
 
 
 def fold_kernel(count, with_gram, received, own, *refs):
@@ -215,7 +186,7 @@
     return pl.pallas_call(
         functools.partial(output_kernel, math.sqrt(GENES)),
         in_specs=[VMEM, VMEM], out_specs=VMEM, out_shape=struct(loading.shape, f32),
-        compiler_params=pltpu.CompilerParams(vmem_limit_bytes=24 * 2**20),
+        compiler_params=pltpu.CompilerParams(vmem_limit_bytes=16 * 2**20),
     )(gram, loading)
 
 
@@ -233,14 +204,10 @@
 def square_program(cells, expression, start_basis):
     width, rank = start_basis.shape
     index = lax.axis_index("cell").astype(jnp.int32)
-    masks = jnp.arange(1, GROUP, dtype=jnp.int32)
-    wanted = index ^ masks
-    packs = pack(expression, jnp.stack([wanted, wanted ^ GROUP], axis=1).reshape(-1), width)
-    ids = jnp.stack([index, index ^ GROUP])
-    basis = start_basis.T
-    basis_mate = [mate(basis, cells, GROUP)]
-    received = {k: mate(packs[k - 1], cells, k) for k in (2, 4, 3, 5, 6, 7, 1)}
-    slots = [expression] + [received[k] for k in range(1, GROUP)]
+    slots = [None] * GROUP
+    for k in (3, 5, 7, 1, 2, 4, 6, 0):
+        packed = pack(expression, jnp.stack([index ^ k, index ^ k ^ GROUP]), width)
+        slots[k] = mate(packed, cells, k) if k else packed
     step = rank // PARTS
 
     def summed_image(even, odd, inverse):
@@ -248,30 +215,34 @@
         image = image_of(even, [mate(even, cells, mask) for mask in (2, 4, 6)], inverse)
         return image, mate(image, cells, 1)
 
-    even, odd = scores(slots, ids, (0, 1), [[basis], basis_mate], None)
+    basis = start_basis.T
+    basis_mate = mate(basis, cells, GROUP)
+    odd = scores(slots[1::2], basis, basis_mate, [])
+    even = scores(slots[0::2], basis, basis_mate, [])
     images = summed_image(even, odd, None)
 
     for iteration in range(1, ITERS):
-        sent = terms(slots, ids, 1, images, width, PARTS, bf16)
-        arrived = [mate(x, cells, GROUP) for x in sent]
-        own = terms(slots, ids, 0, images, width, PARTS, f32)
-        rounded, exact = [], []
-        for part in range(PARTS - 1):
-            rows, kept = fold(arrived[part], own[part], [], bf16, False)
+        sent = terms(slots, 1, images, PARTS, bf16)
+        own = terms(slots, 0, images, PARTS, f32)
+        exact, rounded = [], []
+        for part in range(PARTS):
+            last = part == PARTS - 1
+            rows, kept = fold(mate(sent[part], cells, GROUP), own[part], exact if last else [], bf16, last)
             rounded.append(rows)
             exact.append(kept)
-        rows, gram = fold(arrived[-1], own[-1], exact, bf16, True)
-        rounded.append(rows)
-        others = [mate(x, cells, GROUP) for x in rounded]
-        inverse = factor_call(total_over_cells(gram, cells))
-        carry = scores(slots, ids, (0,), [rounded], None)
-        even, odd = scores(slots, ids, (1,), [others], carry)
-        images = summed_image(even, odd, inverse)
-
-    (sent,) = terms(slots, ids, 1, images, width, 1, bf16)
-    arrived = mate(sent, cells, GROUP)
-    (own,) = terms(slots, ids, 0, images, width, 1, f32)
-    loading, gram = fold(arrived, own, [], f32, True)
+        inverse = factor_call(total_over_cells(exact.pop(), cells))
+        odd, even = [], []
+        for rows in rounded:
+            other = mate(rows, cells, GROUP)
+            if len(odd) == PARTS - 1:
+                other, inverse = lax.optimization_barrier((other, inverse))
+            odd.append(scores(slots[1::2], rows, other, odd))
+            even.append(scores(slots[0::2], rows, other, even))
+        images = summed_image(even[-1], odd[-1], inverse)
+
+    (sent,) = terms(slots, 1, images, 1, bf16)
+    (own,) = terms(slots, 0, images, 1, f32)
+    loading, gram = fold(mate(sent, cells, GROUP), own, [], f32, True)
     return output_call(total_over_cells(gram, cells), loading).T
 
 

time: 264 us -> 158 us (0.60)
  Pallas kernels: 131 us -> 40.7 us
  waiting for transfers between devices: 86.2 us -> 61.4 us
  local copies, waits for them, and re-layouts: 8.26 us -> 13.6 us
    pallas_call x8 -> x18, Pallas kernels: 115 us -> 24.6 us  [the longest x10 15.1 us: call(): pl.pallas_call(kernel, in_specs=[VMEM] * len(args), out_specs=[VMEM] * le...]
    ppermute x35, waiting for transfers between devices: 86.2 us -> 61.4 us  [mate(): return lax.ppermute(value, 'cell', [(i, i ^ mask) for i in range(cells)])]
    unnamed x16 -> x24, local copies, waits for them, and re-layouts: 7.56 us -> 13.6 us
  transfers between devices with their start and end apart: 35 -> 35, of which waited for: 19 -> 22; matrix products, arithmetic and copies ran while one was open for 0% -> 1% of each run, Pallas kernels for 4% -> 16%
where the time goes in v2:
time: 158 us; the launch traced here: 157 us
  waiting for transfers between devices  61.4 us (39%)
  Pallas kernels  40.7 us (26%)
  starting transfers between devices  40 us (25%)
  local copies, waits for them, and re-layouts  13.6 us (9%)
    ppermute x35, waiting for transfers between devices, mate(): return lax.ppermute(value, 'cell', [(i, i ^ mask) for i in range(cells)])  61.4 us
    ppermute x35, starting transfers between devices, mate(): return lax.ppermute(value, 'cell', [(i, i ^ mask) for i in range(cells)])  40 us
    pallas_call x10, Pallas kernels, call(): pl.pallas_call(kernel, in_specs=[VMEM] * len(args), out_specs=[VMEM] * le...  15.1 us
    unnamed x24, local copies, waits for them, and re-layouts  13.6 us
    pallas_call x8, Pallas kernels, pack(): pl.pallas_call(pack_kernel, grid_spec=pltpu.PrefetchScalarGridSpec(num_sc...  9.42 us
    pallas_call x1, Pallas kernels, factor_call(): pl.pallas_call(factor_kernel, in_specs=[VMEM], out_specs=VMEM, out_shape=...  6.8 us
    pallas_call x1, Pallas kernels, output_call(): pl.pallas_call(functools.partial(output_kernel, math.sqrt(GENES)), in_spe...  6.74 us
  transfers between devices with their start and end apart: 35, of which 22 were waited for; matrix products, arithmetic and copies ran while one was open for 1% of the time, Pallas kernels for 16%

profile of v2, /device:TPU:0, one launch (start us, length us, event | category | flops | bytes accessed | tf_op | source)
XLA Modules:
  0.0 157.1 jit_solution(7642167149730821518)
XLA Ops:
  0.0 4.0 %collective-permute-start.7 = (bf16[64,1920]{1,0:T(8,128)(2,1)}, bf16[64,1920]{1,0:T(8,128)(2,1)S(1)}, u32[]{:S(2)}, u32[]{:S(2)}) collective-permute-start(bf16[64,1920]{1,0:T(8,128)(2,1)} %bitcast.18), channel_id=1, source_target_pairs={{0,8},{1,9},{2,10},{3,11},{4,12},{5,13},{6,14},{7,15},{8,0},{9,1},... | collective-permute-start | bytes 737288 | tf_op jit(solution)/shard_map/ppermute | solution.py:194
  4.1 2.1 %copy-done = bf16[64,30720]{1,0:T(8,128)(2,1)S(1)} copy-done((bf16[64,30720]{1,0:T(8,128)(2,1)S(1)}, bf16[64,30720]{1,0:T(8,128)(2,1)}, u32[]{:S(2)}) %copy-start) | copy-done | bytes 3932184
  6.8 1.8 %collective-permute-start.6 = (bf16[64,3840]{1,0:T(8,128)(2,1)S(1)}, bf16[64,3840]{1,0:T(8,128)(2,1)S(1)}, u32[]{:S(2)}, u32[]{:S(2)}) collective-permute-start(bf16[64,3840]{1,0:T(8,128)(2,1)S(1)} %shard_map.35), channel_id=1, source_target_pairs={{0,7},{1,6},{2,5},{3,4},{4,3},{5,2},{6,1},{7,0},{8,15},{9,14},{10,... | collective-permute-start | bytes 1474568 | tf_op jit(solution)/shard_map/ppermute | solution.py:194
  8.7 2.1 %copy-done.1 = bf16[64,30720]{1,0:T(8,128)(2,1)S(1)} copy-done((bf16[64,30720]{1,0:T(8,128)(2,1)S(1)}, bf16[64,30720]{1,0:T(8,128)(2,1)}, u32[]{:S(2)}) %copy-start.1) | copy-done | bytes 3932184
  13.2 2.1 %copy-done.2 = bf16[64,30720]{1,0:T(8,128)(2,1)S(1)} copy-done((bf16[64,30720]{1,0:T(8,128)(2,1)S(1)}, bf16[64,30720]{1,0:T(8,128)(2,1)}, u32[]{:S(2)}) %copy-start.2) | copy-done | bytes 3932184
  16.8 2.1 %copy-done.3 = bf16[64,30720]{1,0:T(8,128)(2,1)S(1)} copy-done((bf16[64,30720]{1,0:T(8,128)(2,1)S(1)}, bf16[64,30720]{1,0:T(8,128)(2,1)}, u32[]{:S(2)}) %copy-start.3) | copy-done | bytes 3932184
  21.1 2.1 %copy-done.4 = bf16[64,30720]{1,0:T(8,128)(2,1)S(1)} copy-done((bf16[64,30720]{1,0:T(8,128)(2,1)S(1)}, bf16[64,30720]{1,0:T(8,128)(2,1)}, u32[]{:S(2)}) %copy-start.4) | copy-done | bytes 3932184
  28.2 2.5 %collective-permute-start.5 = (bf16[64,3840]{1,0:T(8,128)(2,1)}, bf16[64,3840]{1,0:T(8,128)(2,1)S(1)}, u32[]{:S(2)}, u32[]{:S(2)}) collective-permute-start(bf16[64,3840]{1,0:T(8,128)(2,1)} %shard_map.34), channel_id=1, source_target_pairs={{0,6},{1,7},{2,4},{3,5},{4,2},{5,3},{6,0},{7,1},{8,14},{9,15},{10,... | collective-permute-start | bytes 1474568 | tf_op jit(solution)/shard_map/ppermute | solution.py:194
  31.7 4.4 %collective-permute-done.2.refs_1_.refs_3_ = bf16[64,3840]{1,0:T(8,128)(2,1)S(1)} collective-permute-done((bf16[64,3840]{1,0:T(8,128)(2,1)}, bf16[64,3840]{1,0:T(8,128)(2,1)S(1)}, u32[]{:S(2)}, u32[]{:S(2)}) %collective-permute-start.2) | collective-permute-done | bytes 491552 | tf_op jit(solution)/shard_map/ppermute | solution.py:194
  37.1 2.1 %copy-done.6 = bf16[64,30720]{1,0:T(8,128)(2,1)S(1)} copy-done((bf16[64,30720]{1,0:T(8,128)(2,1)S(1)}, bf16[64,30720]{1,0:T(8,128)(2,1)}, u32[]{:S(2)}) %copy-start.6) | copy-done | bytes 3932184
  39.8 7.0 %collective-permute-done.5.refs_3_.refs_6_ = bf16[64,3840]{1,0:T(8,128)(2,1)S(1)} collective-permute-done((bf16[64,3840]{1,0:T(8,128)(2,1)}, bf16[64,3840]{1,0:T(8,128)(2,1)S(1)}, u32[]{:S(2)}, u32[]{:S(2)}) %collective-permute-start.5) | collective-permute-done | bytes 491552 | tf_op jit(solution)/shard_map/ppermute | solution.py:194
  46.8 10.3 %collective-permute-done.1.refs_1_.refs_2_ = bf16[64,3840]{1,0:T(8,128)(2,1)S(1)} collective-permute-done((bf16[64,3840]{1,0:T(8,128)(2,1)}, bf16[64,3840]{1,0:T(8,128)(2,1)S(1)}, u32[]{:S(2)}, u32[]{:S(2)}) %collective-permute-start.1) | collective-permute-done | bytes 491552 | tf_op jit(solution)/shard_map/ppermute | solution.py:194
  57.1 1.7 %shard_map.36 = f32[64,256]{1,0:T(8,128)S(1)} custom-call(bf16[64,1920]{1,0:T(8,128)(2,1)S(1)} %bitcast.20, bf16[64,1920]{1,0:T(8,128)(2,1)S(1)} %copy-done.10, bf16[64,3840]{1,0:T(8,128)(2,1)S(1)} %shard_map.28.refs_0_, bf16[64,3840]{1,0:T(8,128)(2,1)S(1)} %collective-permute-done.1.refs_1_.refs_2_, ...), custom_call_target="tpu_custom_call" | custom-call | flops 125829120 | bytes 1966080 | tf_op jit(solution)/shard_map/pallas_call | solution.py:61
  58.9 2.6 %collective-permute-start.10 = (f32[64,256]{1,0:T(8,128)S(1)}, f32[64,256]{1,0:T(8,128)S(1)}, u32[]{:S(2)}, u32[]{:S(2)}) collective-permute-start(f32[64,256]{1,0:T(8,128)S(1)} %add.42.refs_0_), channel_id=1, source_target_pairs={{0,4},{1,5},{2,6},{3,7},{4,0},{5,1},{6,2},{7,3},{8,12},{9,13},{10,... | collective-permute-start | bytes 196616 | tf_op jit(solution)/shard_map/ppermute | solution.py:194
  62.4 2.3 %collective-permute-done.11.refs_3_ = f32[64,256]{1,0:T(8,128)S(1)} collective-permute-done((f32[64,256]{1,0:T(8,128)S(1)}, f32[64,256]{1,0:T(8,128)S(1)}, u32[]{:S(2)}, u32[]{:S(2)}) %collective-permute-start.11) | collective-permute-done | bytes 65568 | tf_op jit(solution)/shard_map/ppermute | solution.py:194
  69.4 2.3 %collective-permute-start.13 = (bf16[32,1920]{1,0:T(8,128)(2,1)S(1)}, bf16[32,1920]{1,0:T(8,128)(2,1)S(1)}, u32[]{:S(2)}, u32[]{:S(2)}) collective-permute-start(bf16[32,1920]{1,0:T(8,128)(2,1)S(1)} %get-tuple-element.17), channel_id=1, source_target_pairs={{0,8},{1,9},{2,10},{3,11},{4,12},{5,13},{6,14},{7,15},{8,0},{9,1},... | collective-permute-start | bytes 368648 | tf_op jit(solution)/shard_map/ppermute | solution.py:194
  73.1 6.7 %collective-permute-done.14.received = bf16[32,1920]{1,0:T(8,128)(2,1)S(1)} collective-permute-done((bf16[32,1920]{1,0:T(8,128)(2,1)S(1)}, bf16[32,1920]{1,0:T(8,128)(2,1)S(1)}, u32[]{:S(2)}, u32[]{:S(2)}) %collective-permute-start.14) | collective-permute-done | bytes 122912 | tf_op jit(solution)/shard_map/ppermute | solution.py:194
  80.5 1.9 %collective-permute-done.13.received = bf16[32,1920]{1,0:T(8,128)(2,1)S(1)} collective-permute-done((bf16[32,1920]{1,0:T(8,128)(2,1)S(1)}, bf16[32,1920]{1,0:T(8,128)(2,1)S(1)}, u32[]{:S(2)}, u32[]{:S(2)}) %collective-permute-start.13) | collective-permute-done | bytes 122912 | tf_op jit(solution)/shard_map/ppermute | solution.py:194
  87.8 2.1 %collective-permute-start.21 = (f32[64,64]{1,0:T(8,128)S(1)}, f32[64,64]{1,0:T(8,128)S(1)}, u32[]{:S(2)}, u32[]{:S(2)}) collective-permute-start(f32[64,64]{1,0:T(8,128)S(1)} %add_add_fusion.3), channel_id=1, source_target_pairs={{0,12},{1,13},{2,14},{3,15},{4,8},{5,9},{6,10},{7,11},{8,4},{9,5},... | collective-permute-start | bytes 49160 | tf_op jit(solution)/shard_map/ppermute | solution.py:194
  89.9 2.3 %collective-permute-start.19 = (f32[64,64]{1,0:T(8,128)S(1)}, f32[64,64]{1,0:T(8,128)S(1)}, u32[]{:S(2)}, u32[]{:S(2)}) collective-permute-start(f32[64,64]{1,0:T(8,128)S(1)} %add_add_fusion.3), channel_id=1, source_target_pairs={{0,4},{1,5},{2,6},{3,7},{4,0},{5,1},{6,2},{7,3},{8,12},{9,13},{10,... | collective-permute-start | bytes 49160 | tf_op jit(solution)/shard_map/ppermute | solution.py:194
  92.9 2.3 %collective-permute-start.22 = (bf16[32,1920]{1,0:T(8,128)(2,1)}, bf16[32,1920]{1,0:T(8,128)(2,1)}, u32[]{:S(2)}, u32[]{:S(2)}) collective-permute-start(bf16[32,1920]{1,0:T(8,128)(2,1)} %get-tuple-element.25.own), channel_id=1, source_target_pairs={{0,8},{1,9},{2,10},{3,11},{4,12},{5,13},{6,14},{7,15},{8,0},{9,1},... | collective-permute-start | bytes 368648 | tf_op jit(solution)/shard_map/ppermute | solution.py:194
  96.7 6.8 %shard_map.43.refs_4_ = f32[64,64]{1,0:T(8,128)} custom-call(f32[64,64]{1,0:T(8,128)} %add_add_fusion.2.gram), custom_call_target="tpu_custom_call" | custom-call | flops 20000000 | bytes 32768 | tf_op jit(solution)/shard_map/pallas_call | solution.py:175
  103.6 1.8 %collective-permute-done.22.other = bf16[32,1920]{1,0:T(8,128)(2,1)} collective-permute-done((bf16[32,1920]{1,0:T(8,128)(2,1)}, bf16[32,1920]{1,0:T(8,128)(2,1)}, u32[]{:S(2)}, u32[]{:S(2)}) %collective-permute-start.22) | collective-permute-done | bytes 122912 | tf_op jit(solution)/shard_map/ppermute | solution.py:194
  108.7 1.8 %shard_map.44.refs_4_ = f32[32,256]{1,0:T(8,128)S(1)} custom-call(bf16[32,1920]{1,0:T(8,128)(2,1)} %get-tuple-element.25.own, bf16[32,1920]{1,0:T(8,128)(2,1)} %collective-permute-done.22.other, bf16[64,3840]{1,0:T(8,128)(2,1)S(1)} %shard_map.28.refs_0_, bf16[64,3840]{1,0:T(8,128)(2,1)S(1)} %collective-permute-done.1.refs_1_.refs_2_, ...), custom_call_target="tpu_custom_call" | custom-call | flops 62914560 | bytes 1966080 | tf_op jit(solution)/shard_map/pallas_call | solution.py:61
  110.5 1.8 %shard_map.45 = f32[64,256]{1,0:T(8,128)S(1)} custom-call(bf16[32,1920]{1,0:T(8,128)(2,1)} %get-tuple-element.22.own, bf16[32,1920]{1,0:T(8,128)(2,1)} %collective-permute-done.15.other, bf16[64,3840]{1,0:T(8,128)(2,1)S(1)} %shard_map.28.refs_0_, bf16[64,3840]{1,0:T(8,128)(2,1)S(1)} %collective-permute-done.1.refs_1_.refs_2_, ...), custom_call_target="tpu_custom_call" | custom-call | flops 62914560 | bytes 1966080 | tf_op jit(solution)/shard_map/pallas_call | solution.py:61
  112.5 2.5 %collective-permute-start.25 = (f32[64,256]{1,0:T(8,128)S(1)}, f32[64,256]{1,0:T(8,128)S(1)}, u32[]{:S(2)}, u32[]{:S(2)}) collective-permute-start(f32[64,256]{1,0:T(8,128)S(1)} %add.49.refs_0_), channel_id=1, source_target_pairs={{0,4},{1,5},{2,6},{3,7},{4,0},{5,1},{6,2},{7,3},{8,12},{9,13},{10,... | collective-permute-start | bytes 196616 | tf_op jit(solution)/shard_map/ppermute | solution.py:194
  115.9 2.3 %collective-permute-done.26.refs_3_ = f32[64,256]{1,0:T(8,128)S(1)} collective-permute-done((f32[64,256]{1,0:T(8,128)S(1)}, f32[64,256]{1,0:T(8,128)S(1)}, u32[]{:S(2)}, u32[]{:S(2)}) %collective-permute-start.26) | collective-permute-done | bytes 65568 | tf_op jit(solution)/shard_map/ppermute | solution.py:194
  122.3 3.0 %collective-permute-start.28 = (bf16[64,1920]{1,0:T(8,128)(2,1)S(1)}, bf16[64,1920]{1,0:T(8,128)(2,1)S(1)}, u32[]{:S(2)}, u32[]{:S(2)}) collective-permute-start(bf16[64,1920]{1,0:T(8,128)(2,1)S(1)} %shard_map.49), channel_id=1, source_target_pairs={{0,8},{1,9},{2,10},{3,11},{4,12},{5,13},{6,14},{7,15},{8,0},{9,1},... | collective-permute-start | bytes 737288 | tf_op jit(solution)/shard_map/ppermute | solution.py:194
  126.8 10.1 %collective-permute-done.28.received = bf16[64,1920]{1,0:T(8,128)(2,1)S(1)} collective-permute-done((bf16[64,1920]{1,0:T(8,128)(2,1)S(1)}, bf16[64,1920]{1,0:T(8,128)(2,1)S(1)}, u32[]{:S(2)}, u32[]{:S(2)}) %collective-permute-start.28) | collective-permute-done | bytes 245792 | tf_op jit(solution)/shard_map/ppermute | solution.py:194
  141.8 3.8 %collective-permute-start.34 = (f32[64,64]{1,0:T(8,128)S(1)}, f32[64,64]{1,0:T(8,128)S(1)}, u32[]{:S(2)}, u32[]{:S(2)}) collective-permute-start(f32[64,64]{1,0:T(8,128)S(1)} %add_add_fusion.1), channel_id=1, source_target_pairs={{0,12},{1,13},{2,14},{3,15},{4,8},{5,9},{6,10},{7,11},{8,4},{9,5},... | collective-permute-start | bytes 49160 | tf_op jit(solution)/shard_map/ppermute | solution.py:194
  147.6 2.8 %collective-permute-done.33 = f32[64,64]{1,0:T(8,128)S(1)} collective-permute-done((f32[64,64]{1,0:T(8,128)S(1)}, f32[64,64]{1,0:T(8,128)S(1)}, u32[]{:S(2)}, u32[]{:S(2)}) %collective-permute-start.33) | collective-permute-done | bytes 16416 | tf_op jit(solution)/shard_map/ppermute | solution.py:194
  150.4 6.7 %shard_map.52 = f32[64,1920]{1,0:T(8,128)} custom-call(f32[64,64]{1,0:T(8,128)S(1)} %add_add_fusion.gram, f32[64,1920]{1,0:T(8,128)S(1)} %get-tuple-element.28.loading), custom_call_target="tpu_custom_call" | custom-call | tf_op jit(solution)/shard_map/pallas_call | solution.py:186
  (101 shorter events, 46.4 us)
Async XLA Ops:
  0.0 28.2 %collective-permute-start.7 = (bf16[64,1920]{1,0:T(8,128)(2,1)}, bf16[64,1920]{1,0:T(8,128)(2,1)S(1)}, u32[]{:S(2)}, u32[]{:S(2)}) collective-permute-start(bf16[64,1920]{1,0:T(8,128)(2,1)} %bitcast.18), channel_id=1, source_target_pairs={{0,8},{1,9},{2,10},{3,11},{4,12},{5,13},{6,14},{7,15},{8,0},{9,1},... | collective-permute-start | bytes 737288 | tf_op jit(solution)/shard_map/ppermute | solution.py:194
  6.8 23.9 %collective-permute-start.6 = (bf16[64,3840]{1,0:T(8,128)(2,1)S(1)}, bf16[64,3840]{1,0:T(8,128)(2,1)S(1)}, u32[]{:S(2)}, u32[]{:S(2)}) collective-permute-start(bf16[64,3840]{1,0:T(8,128)(2,1)S(1)} %shard_map.35), channel_id=1, source_target_pairs={{0,7},{1,6},{2,5},{3,4},{4,3},{5,2},{6,1},{7,0},{8,15},{9,14},{10,... | collective-permute-start | bytes 1474568 | tf_op jit(solution)/shard_map/ppermute | solution.py:194
  12.1 19.1 %collective-permute-start = (bf16[64,3840]{1,0:T(8,128)(2,1)}, bf16[64,3840]{1,0:T(8,128)(2,1)S(1)}, u32[]{:S(2)}, u32[]{:S(2)}) collective-permute-start(bf16[64,3840]{1,0:T(8,128)(2,1)} %shard_map.29), channel_id=1, source_target_pairs={{0,1},{1,0},{2,3},{3,2},{4,5},{5,4},{6,7},{7,6},{8,9},{9,8},{10,11... | collective-permute-start | bytes 1474568 | tf_op jit(solution)/shard_map/ppermute | solution.py:194
  16.7 19.4 %collective-permute-start.2 = (bf16[64,3840]{1,0:T(8,128)(2,1)}, bf16[64,3840]{1,0:T(8,128)(2,1)S(1)}, u32[]{:S(2)}, u32[]{:S(2)}) collective-permute-start(bf16[64,3840]{1,0:T(8,128)(2,1)} %shard_map.31), channel_id=1, source_target_pairs={{0,3},{1,2},{2,1},{3,0},{4,7},{5,6},{6,5},{7,4},{8,11},{9,10},{10,... | collective-permute-start | bytes 1474568 | tf_op jit(solution)/shard_map/ppermute | solution.py:194
  20.4 15.7 %collective-permute-start.4 = (bf16[64,3840]{1,0:T(8,128)(2,1)}, bf16[64,3840]{1,0:T(8,128)(2,1)S(1)}, u32[]{:S(2)}, u32[]{:S(2)}) collective-permute-start(bf16[64,3840]{1,0:T(8,128)(2,1)} %shard_map.33), channel_id=1, source_target_pairs={{0,5},{1,4},{2,7},{3,6},{4,1},{5,0},{6,3},{7,2},{8,13},{9,12},{10,... | collective-permute-start | bytes 1474568 | tf_op jit(solution)/shard_map/ppermute | solution.py:194
  28.2 18.6 %collective-permute-start.5 = (bf16[64,3840]{1,0:T(8,128)(2,1)}, bf16[64,3840]{1,0:T(8,128)(2,1)S(1)}, u32[]{:S(2)}, u32[]{:S(2)}) collective-permute-start(bf16[64,3840]{1,0:T(8,128)(2,1)} %shard_map.34), channel_id=1, source_target_pairs={{0,6},{1,7},{2,4},{3,5},{4,2},{5,3},{6,0},{7,1},{8,14},{9,15},{10,... | collective-permute-start | bytes 1474568 | tf_op jit(solution)/shard_map/ppermute | solution.py:194
  30.8 26.3 %collective-permute-start.1 = (bf16[64,3840]{1,0:T(8,128)(2,1)}, bf16[64,3840]{1,0:T(8,128)(2,1)S(1)}, u32[]{:S(2)}, u32[]{:S(2)}) collective-permute-start(bf16[64,3840]{1,0:T(8,128)(2,1)} %shard_map.30), channel_id=1, source_target_pairs={{0,2},{1,3},{2,0},{3,1},{4,6},{5,7},{6,4},{7,5},{8,10},{9,11},{10,... | collective-permute-start | bytes 1474568 | tf_op jit(solution)/shard_map/ppermute | solution.py:194
  31.3 25.8 %collective-permute-start.3 = (bf16[64,3840]{1,0:T(8,128)(2,1)}, bf16[64,3840]{1,0:T(8,128)(2,1)}, u32[]{:S(2)}, u32[]{:S(2)}) collective-permute-start(bf16[64,3840]{1,0:T(8,128)(2,1)} %shard_map.32), channel_id=1, source_target_pairs={{0,4},{1,5},{2,6},{3,7},{4,0},{5,1},{6,2},{7,3},{8,12},{9,13},{10,... | collective-permute-start | bytes 1474568 | tf_op jit(solution)/shard_map/ppermute | solution.py:194
  36.8 22.0 %collective-permute-start.8 = (f32[64,256]{1,0:T(8,128)S(1)}, f32[64,256]{1,0:T(8,128)S(1)}, u32[]{:S(2)}, u32[]{:S(2)}) collective-permute-start(f32[64,256]{1,0:T(8,128)S(1)} %shard_map.37), channel_id=1, source_target_pairs={{0,1},{1,0},{2,3},{3,2},{4,5},{5,4},{6,7},{7,6},{8,9},{9,8},{10,11... | collective-permute-start | bytes 196616 | tf_op jit(solution)/shard_map/ppermute | solution.py:194
  58.8 5.9 %collective-permute-start.11 = (f32[64,256]{1,0:T(8,128)S(1)}, f32[64,256]{1,0:T(8,128)S(1)}, u32[]{:S(2)}, u32[]{:S(2)}) collective-permute-start(f32[64,256]{1,0:T(8,128)S(1)} %add.42.refs_0_), channel_id=1, source_target_pairs={{0,6},{1,7},{2,4},{3,5},{4,2},{5,3},{6,0},{7,1},{8,14},{9,15},{10,... | collective-permute-start | bytes 196616 | tf_op jit(solution)/shard_map/ppermute | solution.py:194
  58.9 6.1 %collective-permute-start.10 = (f32[64,256]{1,0:T(8,128)S(1)}, f32[64,256]{1,0:T(8,128)S(1)}, u32[]{:S(2)}, u32[]{:S(2)}) collective-permute-start(f32[64,256]{1,0:T(8,128)S(1)} %add.42.refs_0_), channel_id=1, source_target_pairs={{0,4},{1,5},{2,6},{3,7},{4,0},{5,1},{6,2},{7,3},{8,12},{9,13},{10,... | collective-permute-start | bytes 196616 | tf_op jit(solution)/shard_map/ppermute | solution.py:194
  61.6 4.3 %collective-permute-start.9 = (f32[64,256]{1,0:T(8,128)S(1)}, f32[64,256]{1,0:T(8,128)S(1)}, u32[]{:S(2)}, u32[]{:S(2)}) collective-permute-start(f32[64,256]{1,0:T(8,128)S(1)} %add.42.refs_0_), channel_id=1, source_target_pairs={{0,2},{1,3},{2,0},{3,1},{4,6},{5,7},{6,4},{7,5},{8,10},{9,11},{10,... | collective-permute-start | bytes 196616 | tf_op jit(solution)/shard_map/ppermute | solution.py:194
  68.7 11.2 %collective-permute-start.14 = (bf16[32,1920]{1,0:T(8,128)(2,1)S(1)}, bf16[32,1920]{1,0:T(8,128)(2,1)S(1)}, u32[]{:S(2)}, u32[]{:S(2)}) collective-permute-start(bf16[32,1920]{1,0:T(8,128)(2,1)S(1)} %get-tuple-element.19), channel_id=1, source_target_pairs={{0,8},{1,9},{2,10},{3,11},{4,12},{5,13},{6,14},{7,15},{8,0},{9,1},... | collective-permute-start | bytes 368648 | tf_op jit(solution)/shard_map/ppermute | solution.py:194
  69.4 13.0 %collective-permute-start.13 = (bf16[32,1920]{1,0:T(8,128)(2,1)S(1)}, bf16[32,1920]{1,0:T(8,128)(2,1)S(1)}, u32[]{:S(2)}, u32[]{:S(2)}) collective-permute-start(bf16[32,1920]{1,0:T(8,128)(2,1)S(1)} %get-tuple-element.17), channel_id=1, source_target_pairs={{0,8},{1,9},{2,10},{3,11},{4,12},{5,13},{6,14},{7,15},{8,0},{9,1},... | collective-permute-start | bytes 368648 | tf_op jit(solution)/shard_map/ppermute | solution.py:194
  83.4 3.5 %collective-permute-start.18 = (f32[64,64]{1,0:T(8,128)S(1)}, f32[64,64]{1,0:T(8,128)S(1)}, u32[]{:S(2)}, u32[]{:S(2)}) collective-permute-start(f32[64,64]{1,0:T(8,128)S(1)} %get-tuple-element.23), channel_id=1, source_target_pairs={{0,3},{1,2},{2,1},{3,0},{4,7},{5,6},{6,5},{7,4},{8,11},{9,10},{10,... | collective-permute-start | bytes 49160 | tf_op jit(solution)/shard_map/ppermute | solution.py:194
  83.9 3.9 %collective-permute-start.17 = (f32[64,64]{1,0:T(8,128)S(1)}, f32[64,64]{1,0:T(8,128)S(1)}, u32[]{:S(2)}, u32[]{:S(2)}) collective-permute-start(f32[64,64]{1,0:T(8,128)S(1)} %get-tuple-element.23), channel_id=1, source_target_pairs={{0,2},{1,3},{2,0},{3,1},{4,6},{5,7},{6,4},{7,5},{8,10},{9,11},{10,... | collective-permute-start | bytes 49160 | tf_op jit(solution)/shard_map/ppermute | solution.py:194
  87.8 7.4 %collective-permute-start.21 = (f32[64,64]{1,0:T(8,128)S(1)}, f32[64,64]{1,0:T(8,128)S(1)}, u32[]{:S(2)}, u32[]{:S(2)}) collective-permute-start(f32[64,64]{1,0:T(8,128)S(1)} %add_add_fusion.3), channel_id=1, source_target_pairs={{0,12},{1,13},{2,14},{3,15},{4,8},{5,9},{6,10},{7,11},{8,4},{9,5},... | collective-permute-start | bytes 49160 | tf_op jit(solution)/shard_map/ppermute | solution.py:194
  89.9 6.2 %collective-permute-start.20 = (f32[64,64]{1,0:T(8,128)S(1)}, f32[64,64]{1,0:T(8,128)S(1)}, u32[]{:S(2)}, u32[]{:S(2)}) collective-permute-start(f32[64,64]{1,0:T(8,128)S(1)} %add_add_fusion.3), channel_id=1, source_target_pairs={{0,8},{1,9},{2,10},{3,11},{4,12},{5,13},{6,14},{7,15},{8,0},{9,1},... | collective-permute-start | bytes 49160 | tf_op jit(solution)/shard_map/ppermute | solution.py:194
  89.9 6.2 %collective-permute-start.19 = (f32[64,64]{1,0:T(8,128)S(1)}, f32[64,64]{1,0:T(8,128)S(1)}, u32[]{:S(2)}, u32[]{:S(2)}) collective-permute-start(f32[64,64]{1,0:T(8,128)S(1)} %add_add_fusion.3), channel_id=1, source_target_pairs={{0,4},{1,5},{2,6},{3,7},{4,0},{5,1},{6,2},{7,3},{8,12},{9,13},{10,... | collective-permute-start | bytes 49160 | tf_op jit(solution)/shard_map/ppermute | solution.py:194
  92.2 11.3 %collective-permute-start.15 = (bf16[32,1920]{1,0:T(8,128)(2,1)}, bf16[32,1920]{1,0:T(8,128)(2,1)}, u32[]{:S(2)}, u32[]{:S(2)}) collective-permute-start(bf16[32,1920]{1,0:T(8,128)(2,1)} %get-tuple-element.22.own), channel_id=1, source_target_pairs={{0,8},{1,9},{2,10},{3,11},{4,12},{5,13},{6,14},{7,15},{8,0},{9,1},... | collective-permute-start | bytes 368648 | tf_op jit(solution)/shard_map/ppermute | solution.py:194
  92.9 12.5 %collective-permute-start.22 = (bf16[32,1920]{1,0:T(8,128)(2,1)}, bf16[32,1920]{1,0:T(8,128)(2,1)}, u32[]{:S(2)}, u32[]{:S(2)}) collective-permute-start(bf16[32,1920]{1,0:T(8,128)(2,1)} %get-tuple-element.25.own), channel_id=1, source_target_pairs={{0,8},{1,9},{2,10},{3,11},{4,12},{5,13},{6,14},{7,15},{8,0},{9,1},... | collective-permute-start | bytes 368648 | tf_op jit(solution)/shard_map/ppermute | solution.py:194
  108.6 3.7 %collective-permute-start.23 = (f32[64,256]{1,0:T(8,128)S(1)}, f32[64,256]{1,0:T(8,128)S(1)}, u32[]{:S(2)}, u32[]{:S(2)}) collective-permute-start(f32[64,256]{1,0:T(8,128)S(1)} %shard_map.47), channel_id=1, source_target_pairs={{0,1},{1,0},{2,3},{3,2},{4,5},{5,4},{6,7},{7,6},{8,9},{9,8},{10,11... | collective-permute-start | bytes 196616 | tf_op jit(solution)/shard_map/ppermute | solution.py:194
  112.4 5.9 %collective-permute-start.26 = (f32[64,256]{1,0:T(8,128)S(1)}, f32[64,256]{1,0:T(8,128)S(1)}, u32[]{:S(2)}, u32[]{:S(2)}) collective-permute-start(f32[64,256]{1,0:T(8,128)S(1)} %add.49.refs_0_), channel_id=1, source_target_pairs={{0,6},{1,7},{2,4},{3,5},{4,2},{5,3},{6,0},{7,1},{8,14},{9,15},{10,... | collective-permute-start | bytes 196616 | tf_op jit(solution)/shard_map/ppermute | solution.py:194
  112.5 6.4 %collective-permute-start.25 = (f32[64,256]{1,0:T(8,128)S(1)}, f32[64,256]{1,0:T(8,128)S(1)}, u32[]{:S(2)}, u32[]{:S(2)}) collective-permute-start(f32[64,256]{1,0:T(8,128)S(1)} %add.49.refs_0_), channel_id=1, source_target_pairs={{0,4},{1,5},{2,6},{3,7},{4,0},{5,1},{6,2},{7,3},{8,12},{9,13},{10,... | collective-permute-start | bytes 196616 | tf_op jit(solution)/shard_map/ppermute | solution.py:194
  115.0 4.3 %collective-permute-start.24 = (f32[64,256]{1,0:T(8,128)S(1)}, f32[64,256]{1,0:T(8,128)S(1)}, u32[]{:S(2)}, u32[]{:S(2)}) collective-permute-start(f32[64,256]{1,0:T(8,128)S(1)} %add.49.refs_0_), channel_id=1, source_target_pairs={{0,2},{1,3},{2,0},{3,1},{4,6},{5,7},{6,4},{7,5},{8,10},{9,11},{10,... | collective-permute-start | bytes 196616 | tf_op jit(solution)/shard_map/ppermute | solution.py:194
  122.3 14.6 %collective-permute-start.28 = (bf16[64,1920]{1,0:T(8,128)(2,1)S(1)}, bf16[64,1920]{1,0:T(8,128)(2,1)S(1)}, u32[]{:S(2)}, u32[]{:S(2)}) collective-permute-start(bf16[64,1920]{1,0:T(8,128)(2,1)S(1)} %shard_map.49), channel_id=1, source_target_pairs={{0,8},{1,9},{2,10},{3,11},{4,12},{5,13},{6,14},{7,15},{8,0},{9,1},... | collective-permute-start | bytes 737288 | tf_op jit(solution)/shard_map/ppermute | solution.py:194
  137.5 3.6 %collective-permute-start.31 = (f32[64,64]{1,0:T(8,128)S(1)}, f32[64,64]{1,0:T(8,128)S(1)}, u32[]{:S(2)}, u32[]{:S(2)}) collective-permute-start(f32[64,64]{1,0:T(8,128)S(1)} %get-tuple-element.27), channel_id=1, source_target_pairs={{0,3},{1,2},{2,1},{3,0},{4,7},{5,6},{6,5},{7,4},{8,11},{9,10},{10,... | collective-permute-start | bytes 49160 | tf_op jit(solution)/shard_map/ppermute | solution.py:194
  137.6 4.2 %collective-permute-start.30 = (f32[64,64]{1,0:T(8,128)S(1)}, f32[64,64]{1,0:T(8,128)S(1)}, u32[]{:S(2)}, u32[]{:S(2)}) collective-permute-start(f32[64,64]{1,0:T(8,128)S(1)} %get-tuple-element.27), channel_id=1, source_target_pairs={{0,2},{1,3},{2,0},{3,1},{4,6},{5,7},{6,4},{7,5},{8,10},{9,11},{10,... | collective-permute-start | bytes 49160 | tf_op jit(solution)/shard_map/ppermute | solution.py:194
  138.8 2.9 %collective-permute-start.29 = (f32[64,64]{1,0:T(8,128)S(1)}, f32[64,64]{1,0:T(8,128)S(1)}, u32[]{:S(2)}, u32[]{:S(2)}) collective-permute-start(f32[64,64]{1,0:T(8,128)S(1)} %get-tuple-element.27), channel_id=1, source_target_pairs={{0,1},{1,0},{2,3},{3,2},{4,5},{5,4},{6,7},{7,6},{8,9},{9,8},{10,11... | collective-permute-start | bytes 49160 | tf_op jit(solution)/shard_map/ppermute | solution.py:194
  141.8 5.8 %collective-permute-start.34 = (f32[64,64]{1,0:T(8,128)S(1)}, f32[64,64]{1,0:T(8,128)S(1)}, u32[]{:S(2)}, u32[]{:S(2)}) collective-permute-start(f32[64,64]{1,0:T(8,128)S(1)} %add_add_fusion.1), channel_id=1, source_target_pairs={{0,12},{1,13},{2,14},{3,15},{4,8},{5,9},{6,10},{7,11},{8,4},{9,5},... | collective-permute-start | bytes 49160 | tf_op jit(solution)/shard_map/ppermute | solution.py:194
  145.6 4.8 %collective-permute-start.33 = (f32[64,64]{1,0:T(8,128)S(1)}, f32[64,64]{1,0:T(8,128)S(1)}, u32[]{:S(2)}, u32[]{:S(2)}) collective-permute-start(f32[64,64]{1,0:T(8,128)S(1)} %add_add_fusion.1), channel_id=1, source_target_pairs={{0,8},{1,9},{2,10},{3,11},{4,12},{5,13},{6,14},{7,15},{8,0},{9,1},... | collective-permute-start | bytes 49160 | tf_op jit(solution)/shard_map/ppermute | solution.py:194
  145.6 4.8 %collective-permute-start.32 = (f32[64,64]{1,0:T(8,128)S(1)}, f32[64,64]{1,0:T(8,128)S(1)}, u32[]{:S(2)}, u32[]{:S(2)}) collective-permute-start(f32[64,64]{1,0:T(8,128)S(1)} %add_add_fusion.1), channel_id=1, source_target_pairs={{0,4},{1,5},{2,6},{3,7},{4,0},{5,1},{6,2},{7,3},{8,12},{9,13},{10,... | collective-permute-start | bytes 49160 | tf_op jit(solution)/shard_map/ppermute | solution.py:194
  (15 other events, 86.3 us)

commit v3 on v2

v3 whole, which is shorter than its diff:
```python
import functools
import math

import jax
import jax.numpy as jnp
from jax import lax
from jax.experimental import pallas as pl
from jax.experimental.pallas import tpu as pltpu
from jax.sharding import PartitionSpec as P

GENES = 30720
ITERS = 2
GROUP = 8
BIG = pltpu.CompilerParams(vmem_limit_bytes=16 * 2**20)
VMEM = pl.BlockSpec(memory_space=pltpu.VMEM)
HIGHEST = lax.Precision.HIGHEST
f32, bf16 = jnp.float32, jnp.bfloat16


def nn(a, b, precision=None):
    return lax.dot_general(a, b, (((1,), (0,)), ((), ())), precision=precision, preferred_element_type=f32)


def nt(a, b, precision=None):
    return lax.dot_general(a, b, (((1,), (1,)), ((), ())), precision=precision, preferred_element_type=f32)


def struct(shape, dtype):
    return jax.ShapeDtypeStruct(shape, dtype)


def cost(flops, bytes_accessed):
    return pl.CostEstimate(flops=flops, bytes_accessed=bytes_accessed, transcendentals=0)


def pack_kernel(ids, matrix, *refs):
    outs, sem = refs[:-1], refs[-1]
    width = outs[0].shape[1] // 2
    copies = []
    for k, out in enumerate(outs):
        for j in range(2):
            start = pl.multiple_of(ids[2 * k + j] * width, 128)
            copies.append(pltpu.make_async_copy(
                matrix.at[:, pl.ds(start, width)], out.at[:, pl.ds(j * width, width)], sem.at[2 * k + j]))
    for copy in copies:
        copy.start()
    for copy in copies:
        copy.wait()


def pack(matrix, ids, width):
    rows, count = matrix.shape[0], ids.shape[0] // 2
    return pl.pallas_call(
        pack_kernel,
        in_specs=[pl.BlockSpec(memory_space=pltpu.SMEM), pl.BlockSpec(memory_space=pltpu.HBM)],
        out_specs=[VMEM] * count,
        out_shape=[struct((rows, 2 * width), matrix.dtype)] * count,
        scratch_shapes=[pltpu.SemaphoreType.DMA((2 * count,))],
        compiler_params=BIG,
        cost_estimate=cost(0, 8 * rows * count * width),
    )(ids, matrix)


def call(kernel, args, outs, estimate):
    return pl.pallas_call(
        kernel, in_specs=[VMEM] * len(args), out_specs=[VMEM] * len(outs), out_shape=outs,
        compiler_params=BIG, cost_estimate=estimate,
    )(*args)


def scores_kernel(block, width, basis, *refs):
    slots, before, outs = refs[:GROUP], refs[GROUP:-2], refs[-2:]
    rows = slots[0].shape[0]
    for odd in range(2):
        for pair in range(GROUP // 4):
            picked = [slots[4 * pair + odd], slots[4 * pair + 2 + odd]]
            big = jnp.concatenate([ref[:, block * width:(block + 1) * width] for ref in picked], axis=0)
            value = nt(big, basis[...]).T
            lanes = slice(2 * pair * rows, 2 * (pair + 1) * rows)
            outs[odd][:, lanes] = value + before[odd][:, lanes] if before else value


def scores(slots, block, basis, before):
    rank, width = basis.shape
    cells = slots[0].shape[0] * GROUP
    return call(functools.partial(scores_kernel, block, width), [basis, *slots, *before],
                [struct((rank, cells // 2), f32)] * 2, cost(2 * rank * cells * width, 2 * cells * width))


def image_kernel(normalised, *refs):
    value, mates = refs[0][...], [ref[...] for ref in refs[1:4]]
    size = value.shape[1] // (GROUP // 2)

    def turned(x, mask):
        return jnp.concatenate([x[:, (j ^ mask) * size:((j ^ mask) + 1) * size] for j in range(GROUP // 2)], axis=1)

    value = (value + turned(mates[0], 1)) + (turned(mates[1], 2) + turned(mates[2], 3))
    if normalised:
        value = nn(refs[4][...], value, HIGHEST)
    refs[-1][...] = value.astype(bf16)


def image_of(value, mates, inverse):
    args = [value, *mates] + ([] if inverse is None else [inverse])
    return pl.pallas_call(
        functools.partial(image_kernel, inverse is not None),
        in_specs=[VMEM] * len(args), out_specs=VMEM, out_shape=struct(value.shape, bf16),
        compiler_params=BIG, cost_estimate=cost(12 * value.size * value.shape[0], 16 * value.size),
    )(*args)


def terms_kernel(block, *refs):
    slots, images, out = refs[:GROUP], refs[GROUP:GROUP + 2], refs[-1]
    width = out.shape[1]
    chunk = width // 3 if width % 384 == 0 else width
    for start in range(0, width, chunk):
        total = 0.0
        for odd in range(2):
            lanes = slice(block * width + start, block * width + start + chunk)
            big = jnp.concatenate([ref[:, lanes] for ref in slots[odd::2]], axis=0)
            total = total + nn(images[odd][...], big)
        out[:, start:start + chunk] = total.astype(out.dtype)


def terms(slots, block, images, dtype):
    rank, width = images[0].shape[0], slots[0].shape[1] // 2
    cells = slots[0].shape[0] * GROUP
    return call(functools.partial(terms_kernel, block), [*slots, *images], [struct((rank, width), dtype)],
                cost(2 * rank * cells * width, 2 * cells * width))[0]


def fold_kernel(received, own, loading, gram):
    value = own[...] + received[...].astype(f32)
    loading[...] = value.astype(loading.dtype)
    gram[...] = nt(value, value, HIGHEST)


def fold(received, own, dtype):
    rank = own.shape[0]
    return call(fold_kernel, [received, own], [struct(own.shape, dtype), struct((rank, rank), f32)],
                cost(12 * rank * own.size, 12 * own.size))


def inverse_factor(gram):
    size = gram.shape[0]
    row = lax.broadcasted_iota(jnp.int32, (size, size), 0)
    column = lax.broadcasted_iota(jnp.int32, (size, size), 1)
    both = jnp.concatenate([gram, jnp.where(row == column, 1.0, 0.0).astype(f32)], axis=1)
    panels = size // 8
    shape = (8, 2 * size)
    blocks = [both[8 * b:8 * b + 8] for b in range(panels)]
    inner = lax.broadcasted_iota(jnp.int32, shape, 0)
    done = []
    for b in range(panels):
        columns = [
            {k: jnp.broadcast_to(blocks[k][:, 8 * b + t:8 * b + t + 1], shape) for k in range(b, panels)}
            for t in range(8)
        ]
        for t in range(8):
            root = lax.rsqrt(jnp.broadcast_to(columns[t][b][t:t + 1], shape))
            scaled = {k: x * root for k, x in columns[t].items()}
            for s in range(t + 1, 8):
                along = jnp.broadcast_to(scaled[b][s:s + 1], shape)
                for k in range(b, panels):
                    columns[s][k] = columns[s][k] - scaled[k] * along
            pivot = jnp.broadcast_to(blocks[b][t:t + 1], shape) * root
            done.append(pivot[:1])
            for k in range(b, panels):
                factor = jnp.where(inner > t, scaled[k], 0.0) if k == b else scaled[k]
                blocks[k] = blocks[k] - factor * pivot
    return jnp.concatenate(done, axis=0)[:, size:]


def factor_kernel(gram, out):
    out[...] = inverse_factor(gram[...])


def factor_call(gram):
    return pl.pallas_call(
        factor_kernel, in_specs=[VMEM], out_specs=VMEM, out_shape=struct(gram.shape, f32),
        cost_estimate=pl.CostEstimate(flops=100_000, bytes_accessed=32768, transcendentals=64),
    )(gram)


def output_kernel(scale, gram, loading, out):
    out[...] = nn(inverse_factor(gram[...]), loading[...], HIGHEST) * scale


def output_call(gram, loading):
    return pl.pallas_call(
        functools.partial(output_kernel, math.sqrt(GENES)),
        in_specs=[VMEM, VMEM], out_specs=VMEM, out_shape=struct(loading.shape, f32),
        compiler_params=pltpu.CompilerParams(vmem_limit_bytes=16 * 2**20),
    )(gram, loading)


def mate(value, cells, mask):
    return lax.ppermute(value, "cell", [(i, i ^ mask) for i in range(cells)])


def total_over_cells(value, cells):
    for low in range(0, cells.bit_length() - 1, 2):
        one, two = 1 << low, 2 << low
        value = (value + mate(value, cells, one)) + (mate(value, cells, two) + mate(value, cells, one | two))
    return value


def square_program(cells, expression, start_basis):
    width = start_basis.shape[0]
    index = lax.axis_index("cell").astype(jnp.int32)
    members = index ^ jnp.arange(GROUP, dtype=jnp.int32)
    slots = pack(expression, jnp.stack([members, members ^ GROUP], axis=1).reshape(-1), width)
    slots = [mate(x, cells, k) if k else x for k, x in enumerate(slots)]

    def image_from(basis, other, inverse):
        even, odd = scores(slots, 1, other, scores(slots, 0, basis, []))
        even = even + mate(odd, cells, 1)
        image = image_of(even, [mate(even, cells, mask) for mask in (2, 4, 6)], inverse)
        return image, mate(image, cells, 1)

    def loading_from(images, dtype):
        received = mate(terms(slots, 1, images, bf16), cells, GROUP)
        rows, gram = fold(received, terms(slots, 0, images, f32), dtype)
        return rows, total_over_cells(gram, cells)

    basis = start_basis.T
    images = image_from(basis, mate(basis, cells, GROUP), None)
    for _ in range(1, ITERS):
        rows, gram = loading_from(images, bf16)
        other, gram = lax.optimization_barrier((mate(rows, cells, GROUP), gram))
        images = image_from(rows, other, factor_call(gram))
    loading, gram = loading_from(images, f32)
    return output_call(gram, loading).T


def plain_program(expression, start_basis):
    basis = start_basis
    for _ in range(ITERS):
        whole = lax.all_gather(basis, "cell", axis=0, tiled=True)
        partial = jnp.dot(expression, whole, preferred_element_type=f32)
        image = lax.psum(partial, "gene").astype(bf16)
        partial = lax.dot_general(expression, image, (((0,), (0,)), ((), ())), preferred_element_type=f32)
        loading = lax.psum_scatter(partial, "cell", scatter_dimension=0, tiled=True)
        gram = lax.dot_general(loading, loading, (((0,), (0,)), ((), ())), precision=HIGHEST, preferred_element_type=f32)
        lower = jnp.linalg.cholesky(lax.psum(gram, ("cell", "gene")))
        ortho = jax.scipy.linalg.solve_triangular(lower, loading.T, lower=True).T
        basis = ortho.astype(bf16)
    return ortho * math.sqrt(GENES)


def solution(mesh):
    cells, genes = mesh.shape["cell"], mesh.shape["gene"]

    def on_device(expression, start_basis):
        width, rank = start_basis.shape
        fits = genes == 1 and cells == 2 * GROUP and width % 128 == 0 and rank == 64
        if fits and expression.shape[0] % 16 == 0:
            return square_program(cells, expression, start_basis)
        return plain_program(expression, start_basis)

    return jax.shard_map(
        on_device,
        mesh=mesh,
        in_specs=(P(("groups", "cell"), "gene"), P(("groups", "gene", "cell"), None)),
        out_specs=P(("groups", "gene", "cell"), None),
        check_vma=False,
    )
```

time: 158 us -> 147 us (0.930)
  waiting for transfers between devices: 61.4 us -> 91.9 us
  Pallas kernels: 40.7 us -> 14.9 us
  local copies, waits for them, and re-layouts: 13.6 us -> 4.08 us
  starting transfers between devices: 40 us -> 34.6 us
    ppermute x35 -> x33, waiting for transfers between devices: 61.4 us -> 91.9 us  [mate(): return lax.ppermute(value, 'cell', [(i, i ^ mask) for i in range(cells)])]
    pallas_call x11 -> x1, Pallas kernels: 11.7 us -> 1.52 us  [pack(): pl.pallas_call(pack_kernel, in_specs=[pl.BlockSpec(memory_space=pltpu.SME...]
    unnamed x24 -> x10, local copies, waits for them, and re-layouts: 13.6 us -> 3.91 us
    pallas_call x10, Pallas kernels: 15.1 us -> 5.71 us  [call(): pl.pallas_call(kernel, in_specs=[VMEM] * len(args), out_specs=[VMEM] * le...]
    ppermute x35 -> x33, starting transfers between devices: 40 us -> 34.6 us  [mate(): return lax.ppermute(value, 'cell', [(i, i ^ mask) for i in range(cells)])]
    pallas_call x1, Pallas kernels: 6.74 us -> 3.17 us  [output_call(): pl.pallas_call(functools.partial(output_kernel, math.sqrt(GENES)), in_spe...]
    pallas_call x1, Pallas kernels: 6.8 us -> 3.24 us  [factor_call(): pl.pallas_call(factor_kernel, in_specs=[VMEM], out_specs=VMEM, out_shape=...]
  transfers between devices with their start and end apart: 35 -> 33, of which waited for: 22 -> 21; matrix products, arithmetic and copies ran while one was open for 1% -> 0% of each run, Pallas kernels for 16% -> 4%
where the time goes in v3:
time: 147 us; the launch traced here: 146 us
  waiting for transfers between devices  91.9 us (63%)
  starting transfers between devices  34.6 us (24%)
  Pallas kernels  14.9 us (10%)
  local copies, waits for them, and re-layouts  4.08 us (3%)
    ppermute x33, waiting for transfers between devices, mate(): return lax.ppermute(value, 'cell', [(i, i ^ mask) for i in range(cells)])  91.9 us
    ppermute x33, starting transfers between devices, mate(): return lax.ppermute(value, 'cell', [(i, i ^ mask) for i in range(cells)])  34.6 us
    pallas_call x10, Pallas kernels, call(): pl.pallas_call(kernel, in_specs=[VMEM] * len(args), out_specs=[VMEM] * le...  5.71 us
    unnamed x10, local copies, waits for them, and re-layouts  3.91 us
    pallas_call x1, Pallas kernels, factor_call(): pl.pallas_call(factor_kernel, in_specs=[VMEM], out_specs=VMEM, out_shape=...  3.24 us
    pallas_call x1, Pallas kernels, output_call(): pl.pallas_call(functools.partial(output_kernel, math.sqrt(GENES)), in_spe...  3.17 us
  transfers between devices with their start and end apart: 33, of which 21 were waited for; matrix products, arithmetic and copies ran while one was open for 0% of the time, Pallas kernels for 4%

profile of v3, /device:TPU:0, one launch (start us, length us, event | category | flops | bytes accessed | tf_op | source)
XLA Modules:
  0.0 146.3 jit_solution(4989003955652241066)
XLA Ops:
  0.2 2.1 %copy-done.2 = bf16[64,30720]{1,0:T(8,128)(2,1)S(1)} copy-done((bf16[64,30720]{1,0:T(8,128)(2,1)S(1)}, bf16[64,30720]{1,0:T(8,128)(2,1)}, u32[]{:S(2)}) %copy-start.2) | copy-done | bytes 3932184
  2.3 1.5 %shard_map.28 = (bf16[64,3840]{1,0:T(8,128)(2,1)S(1)}, bf16[64,3840]{1,0:T(8,128)(2,1)S(1)}, bf16[64,3840]{1,0:T(8,128)(2,1)S(1)}, bf16[64,3840]{1,0:T(8,128)(2,...) custom-call(s32[16]{0:T(128)S(1)} %reshape.14.ids, ...), custom_call_target="tpu_custom_call" | custom-call | bytes 7864320 | tf_op jit(solution)/shard_map/pallas_call | solution.py:53
  4.4 2.6 %collective-permute-start.1 = (bf16[64,3840]{1,0:T(8,128)(2,1)S(1)}, bf16[64,3840]{1,0:T(8,128)(2,1)S(1)}, u32[]{:S(2)}, u32[]{:S(2)}) collective-permute-start(bf16[64,3840]{1,0:T(8,128)(2,1)S(1)} %get-tuple-element.29), channel_id=1, source_target_pairs={{0,2},{1,3},{2,0},{3,1},{4,6},{5,7},{6,4},{7,5},{8,10},{9,11},{10,... | collective-permute-start | bytes 1474568 | tf_op jit(solution)/shard_map/ppermute | solution.py:198
  7.0 1.8 %collective-permute-start.3 = (bf16[64,3840]{1,0:T(8,128)(2,1)S(1)}, bf16[64,3840]{1,0:T(8,128)(2,1)S(1)}, u32[]{:S(2)}, u32[]{:S(2)}) collective-permute-start(bf16[64,3840]{1,0:T(8,128)(2,1)S(1)} %get-tuple-element.31), channel_id=1, source_target_pairs={{0,4},{1,5},{2,6},{3,7},{4,0},{5,1},{6,2},{7,3},{8,12},{9,13},{10,... | collective-permute-start | bytes 1474568 | tf_op jit(solution)/shard_map/ppermute | solution.py:198
  8.8 2.6 %collective-permute-start.5 = (bf16[64,3840]{1,0:T(8,128)(2,1)S(1)}, bf16[64,3840]{1,0:T(8,128)(2,1)S(1)}, u32[]{:S(2)}, u32[]{:S(2)}) collective-permute-start(bf16[64,3840]{1,0:T(8,128)(2,1)S(1)} %get-tuple-element.33), channel_id=1, source_target_pairs={{0,6},{1,7},{2,4},{3,5},{4,2},{5,3},{6,0},{7,1},{8,14},{9,15},{10,... | collective-permute-start | bytes 1474568 | tf_op jit(solution)/shard_map/ppermute | solution.py:198
  11.5 7.6 %collective-permute-done.1.refs_2_ = bf16[64,3840]{1,0:T(8,128)(2,1)S(1)} collective-permute-done((bf16[64,3840]{1,0:T(8,128)(2,1)S(1)}, bf16[64,3840]{1,0:T(8,128)(2,1)S(1)}, u32[]{:S(2)}, u32[]{:S(2)}) %collective-permute-start.1) | collective-permute-done | bytes 491552 | tf_op jit(solution)/shard_map/ppermute | solution.py:198
  19.0 1.8 %collective-permute-start.6 = (bf16[64,3840]{1,0:T(8,128)(2,1)S(1)}, bf16[64,3840]{1,0:T(8,128)(2,1)S(1)}, u32[]{:S(2)}, u32[]{:S(2)}) collective-permute-start(bf16[64,3840]{1,0:T(8,128)(2,1)S(1)} %get-tuple-element.34), channel_id=1, source_target_pairs={{0,7},{1,6},{2,5},{3,4},{4,3},{5,2},{6,1},{7,0},{8,15},{9,14},{10,... | collective-permute-start | bytes 1474568 | tf_op jit(solution)/shard_map/ppermute | solution.py:198
  20.8 8.2 %collective-permute-done.2.refs_3_ = bf16[64,3840]{1,0:T(8,128)(2,1)S(1)} collective-permute-done((bf16[64,3840]{1,0:T(8,128)(2,1)S(1)}, bf16[64,3840]{1,0:T(8,128)(2,1)S(1)}, u32[]{:S(2)}, u32[]{:S(2)}) %collective-permute-start.2) | collective-permute-done | bytes 491552 | tf_op jit(solution)/shard_map/ppermute | solution.py:198
  29.0 2.6 %collective-permute-start.7 = (bf16[64,1920]{1,0:T(8,128)(2,1)S(1)}, bf16[64,1920]{1,0:T(8,128)(2,1)S(1)}, u32[]{:S(2)}, u32[]{:S(2)}) collective-permute-start(bf16[64,1920]{1,0:T(8,128)(2,1)S(1)} %bitcast.2), channel_id=1, source_target_pairs={{0,8},{1,9},{2,10},{3,11},{4,12},{5,13},{6,14},{7,15},{8,0},{9,1},... | collective-permute-start | bytes 737288 | tf_op jit(solution)/shard_map/ppermute | solution.py:198
  31.7 16.9 %collective-permute-done.5.refs_6_ = bf16[64,3840]{1,0:T(8,128)(2,1)S(1)} collective-permute-done((bf16[64,3840]{1,0:T(8,128)(2,1)S(1)}, bf16[64,3840]{1,0:T(8,128)(2,1)S(1)}, u32[]{:S(2)}, u32[]{:S(2)}) %collective-permute-start.5) | collective-permute-done | bytes 491552 | tf_op jit(solution)/shard_map/ppermute | solution.py:198
  48.5 9.4 %collective-permute-done.6.refs_7_ = bf16[64,3840]{1,0:T(8,128)(2,1)S(1)} collective-permute-done((bf16[64,3840]{1,0:T(8,128)(2,1)S(1)}, bf16[64,3840]{1,0:T(8,128)(2,1)S(1)}, u32[]{:S(2)}, u32[]{:S(2)}) %collective-permute-start.6) | collective-permute-done | bytes 491552 | tf_op jit(solution)/shard_map/ppermute | solution.py:198
  60.8 2.4 %collective-permute-start.11 = (f32[64,256]{1,0:T(8,128)S(1)}, f32[64,256]{1,0:T(8,128)S(1)}, u32[]{:S(2)}, u32[]{:S(2)}) collective-permute-start(f32[64,256]{1,0:T(8,128)S(1)} %add.42.refs_0_), channel_id=1, source_target_pairs={{0,6},{1,7},{2,4},{3,5},{4,2},{5,3},{6,0},{7,1},{8,14},{9,15},{10,... | collective-permute-start | bytes 196616 | tf_op jit(solution)/shard_map/ppermute | solution.py:198
  64.3 2.2 %collective-permute-done.11.refs_3_ = f32[64,256]{1,0:T(8,128)S(1)} collective-permute-done((f32[64,256]{1,0:T(8,128)S(1)}, f32[64,256]{1,0:T(8,128)S(1)}, u32[]{:S(2)}, u32[]{:S(2)}) %collective-permute-start.11) | collective-permute-done | bytes 65568 | tf_op jit(solution)/shard_map/ppermute | solution.py:198
  67.7 1.2 collective-permute-done.12.refs_9_
  69.3 1.9 %collective-permute-start.13 = (bf16[64,1920]{1,0:T(8,128)(2,1)S(1)}, bf16[64,1920]{1,0:T(8,128)(2,1)S(1)}, u32[]{:S(2)}, u32[]{:S(2)}) collective-permute-start(bf16[64,1920]{1,0:T(8,128)(2,1)S(1)} %shard_map.32), channel_id=1, source_target_pairs={{0,8},{1,9},{2,10},{3,11},{4,12},{5,13},{6,14},{7,15},{8,0},{9,1},... | collective-permute-start | bytes 737288 | tf_op jit(solution)/shard_map/ppermute | solution.py:198
  71.7 11.9 %collective-permute-done.13.received = bf16[64,1920]{1,0:T(8,128)(2,1)S(1)} collective-permute-done((bf16[64,1920]{1,0:T(8,128)(2,1)S(1)}, bf16[64,1920]{1,0:T(8,128)(2,1)S(1)}, u32[]{:S(2)}, u32[]{:S(2)}) %collective-permute-start.13) | collective-permute-done | bytes 245792 | tf_op jit(solution)/shard_map/ppermute | solution.py:198
  84.3 1.1 collective-permute-start.16
  86.1 1.5 %collective-permute-done.17 = f32[64,64]{1,0:T(8,128)S(1)} collective-permute-done((f32[64,64]{1,0:T(8,128)S(1)}, f32[64,64]{1,0:T(8,128)S(1)}, u32[]{:S(2)}, u32[]{:S(2)}) %collective-permute-start.17) | collective-permute-done | bytes 16416 | tf_op jit(solution)/shard_map/ppermute | solution.py:198
  88.5 3.5 %collective-permute-start.20 = (f32[64,64]{1,0:T(8,128)S(1)}, f32[64,64]{1,0:T(8,128)S(1)}, u32[]{:S(2)}, u32[]{:S(2)}) collective-permute-start(f32[64,64]{1,0:T(8,128)S(1)} %add_add_fusion.3), channel_id=1, source_target_pairs={{0,12},{1,13},{2,14},{3,15},{4,8},{5,9},{6,10},{7,11},{8,4},{9,5},... | collective-permute-start | bytes 49160 | tf_op jit(solution)/shard_map/ppermute | solution.py:198
  93.6 2.8 %collective-permute-done.20 = f32[64,64]{1,0:T(8,128)S(1)} collective-permute-done((f32[64,64]{1,0:T(8,128)S(1)}, f32[64,64]{1,0:T(8,128)S(1)}, u32[]{:S(2)}, u32[]{:S(2)}) %collective-permute-start.20) | collective-permute-done | bytes 16416 | tf_op jit(solution)/shard_map/ppermute | solution.py:198
  96.4 6.5 %collective-permute-done.19 = f32[64,64]{1,0:T(8,128)S(1)} collective-permute-done((f32[64,64]{1,0:T(8,128)S(1)}, f32[64,64]{1,0:T(8,128)S(1)}, u32[]{:S(2)}, u32[]{:S(2)}) %collective-permute-start.19) | collective-permute-done | bytes 16416 | tf_op jit(solution)/shard_map/ppermute | solution.py:198
  104.4 1.2 collective-permute-done.21
  106.4 1.8 %collective-permute-start.23 = (f32[64,256]{1,0:T(8,128)S(1)}, f32[64,256]{1,0:T(8,128)}, u32[]{:S(2)}, u32[]{:S(2)}) collective-permute-start(f32[64,256]{1,0:T(8,128)S(1)} %add.49.refs_0_), channel_id=1, source_target_pairs={{0,4},{1,5},{2,6},{3,7},{4,0},{5,1},{6,2},{7,3},{8,12},{9,13},{10,... | collective-permute-start | bytes 196616 | tf_op jit(solution)/shard_map/ppermute | solution.py:198
  109.2 3.2 %shard_map.37.refs_4_ = f32[64,64]{1,0:T(8,128)} custom-call(f32[64,64]{1,0:T(8,128)} %add_add_fusion.2.gram), custom_call_target="tpu_custom_call" | custom-call | flops 100000 | bytes 32768 | tf_op jit(solution)/shard_map/pallas_call | solution.py:179
  113.3 1.2 shard_map.38.refs_8_
  114.6 1.2 collective-permute-done.25.refs_9_
  117.8 13.4 %collective-permute-done.26.received = bf16[64,1920]{1,0:T(8,128)(2,1)S(1)} collective-permute-done((bf16[64,1920]{1,0:T(8,128)(2,1)S(1)}, bf16[64,1920]{1,0:T(8,128)(2,1)S(1)}, u32[]{:S(2)}, u32[]{:S(2)}) %collective-permute-start.26) | collective-permute-done | bytes 245792 | tf_op jit(solution)/shard_map/ppermute | solution.py:198
  133.7 1.6 %collective-permute-done.29 = f32[64,64]{1,0:T(8,128)S(1)} collective-permute-done((f32[64,64]{1,0:T(8,128)S(1)}, f32[64,64]{1,0:T(8,128)S(1)}, u32[]{:S(2)}, u32[]{:S(2)}) %collective-permute-start.29) | collective-permute-done | bytes 16416 | tf_op jit(solution)/shard_map/ppermute | solution.py:198
  136.4 1.6 %collective-permute-start.32 = (f32[64,64]{1,0:T(8,128)S(1)}, f32[64,64]{1,0:T(8,128)S(1)}, u32[]{:S(2)}, u32[]{:S(2)}) collective-permute-start(f32[64,64]{1,0:T(8,128)S(1)} %add_add_fusion.1), channel_id=1, source_target_pairs={{0,12},{1,13},{2,14},{3,15},{4,8},{5,9},{6,10},{7,11},{8,4},{9,5},... | collective-permute-start | bytes 49160 | tf_op jit(solution)/shard_map/ppermute | solution.py:198
  138.0 2.9 %collective-permute-start.30 = (f32[64,64]{1,0:T(8,128)S(1)}, f32[64,64]{1,0:T(8,128)S(1)}, u32[]{:S(2)}, u32[]{:S(2)}) collective-permute-start(f32[64,64]{1,0:T(8,128)S(1)} %add_add_fusion.1), channel_id=1, source_target_pairs={{0,4},{1,5},{2,6},{3,7},{4,0},{5,1},{6,2},{7,3},{8,12},{9,13},{10,... | collective-permute-start | bytes 49160 | tf_op jit(solution)/shard_map/ppermute | solution.py:198
  140.8 1.6 %collective-permute-done.32 = f32[64,64]{1,0:T(8,128)S(1)} collective-permute-done((f32[64,64]{1,0:T(8,128)S(1)}, f32[64,64]{1,0:T(8,128)S(1)}, u32[]{:S(2)}, u32[]{:S(2)}) %collective-permute-start.32) | collective-permute-done | bytes 16416 | tf_op jit(solution)/shard_map/ppermute | solution.py:198
  143.1 3.2 %shard_map.42 = f32[64,1920]{1,0:T(8,128)} custom-call(f32[64,64]{1,0:T(8,128)S(1)} %add_add_fusion.gram, f32[64,1920]{1,0:T(8,128)S(1)} %get-tuple-element.48.loading), custom_call_target="tpu_custom_call" | custom-call | tf_op jit(solution)/shard_map/pallas_call | solution.py:190
  (69 shorter events, 21.0 us)
Async XLA Ops:
  3.8 5.0 %collective-permute-start = (bf16[64,3840]{1,0:T(8,128)(2,1)S(1)}, bf16[64,3840]{1,0:T(8,128)(2,1)S(1)}, u32[]{:S(2)}, u32[]{:S(2)}) collective-permute-start(bf16[64,3840]{1,0:T(8,128)(2,1)S(1)} %get-tuple-element.28), channel_id=1, source_target_pairs={{0,1},{1,0},{2,3},{3,2},{4,5},{5,4},{6,7},{7,6},{8,9},{9,8},{10,11... | collective-permute-start | bytes 1474568 | tf_op jit(solution)/shard_map/ppermute | solution.py:198
  4.4 14.7 %collective-permute-start.1 = (bf16[64,3840]{1,0:T(8,128)(2,1)S(1)}, bf16[64,3840]{1,0:T(8,128)(2,1)S(1)}, u32[]{:S(2)}, u32[]{:S(2)}) collective-permute-start(bf16[64,3840]{1,0:T(8,128)(2,1)S(1)} %get-tuple-element.29), channel_id=1, source_target_pairs={{0,2},{1,3},{2,0},{3,1},{4,6},{5,7},{6,4},{7,5},{8,10},{9,11},{10,... | collective-permute-start | bytes 1474568 | tf_op jit(solution)/shard_map/ppermute | solution.py:198
  6.9 22.1 %collective-permute-start.2 = (bf16[64,3840]{1,0:T(8,128)(2,1)S(1)}, bf16[64,3840]{1,0:T(8,128)(2,1)S(1)}, u32[]{:S(2)}, u32[]{:S(2)}) collective-permute-start(bf16[64,3840]{1,0:T(8,128)(2,1)S(1)} %get-tuple-element.30), channel_id=1, source_target_pairs={{0,3},{1,2},{2,1},{3,0},{4,7},{5,6},{6,5},{7,4},{8,11},{9,10},{10,... | collective-permute-start | bytes 1474568 | tf_op jit(solution)/shard_map/ppermute | solution.py:198
  7.0 24.7 %collective-permute-start.3 = (bf16[64,3840]{1,0:T(8,128)(2,1)S(1)}, bf16[64,3840]{1,0:T(8,128)(2,1)S(1)}, u32[]{:S(2)}, u32[]{:S(2)}) collective-permute-start(bf16[64,3840]{1,0:T(8,128)(2,1)S(1)} %get-tuple-element.31), channel_id=1, source_target_pairs={{0,4},{1,5},{2,6},{3,7},{4,0},{5,1},{6,2},{7,3},{8,12},{9,13},{10,... | collective-permute-start | bytes 1474568 | tf_op jit(solution)/shard_map/ppermute | solution.py:198
  8.8 22.9 %collective-permute-start.4 = (bf16[64,3840]{1,0:T(8,128)(2,1)S(1)}, bf16[64,3840]{1,0:T(8,128)(2,1)S(1)}, u32[]{:S(2)}, u32[]{:S(2)}) collective-permute-start(bf16[64,3840]{1,0:T(8,128)(2,1)S(1)} %get-tuple-element.32), channel_id=1, source_target_pairs={{0,5},{1,4},{2,7},{3,6},{4,1},{5,0},{6,3},{7,2},{8,13},{9,12},{10,... | collective-permute-start | bytes 1474568 | tf_op jit(solution)/shard_map/ppermute | solution.py:198
  8.8 39.7 %collective-permute-start.5 = (bf16[64,3840]{1,0:T(8,128)(2,1)S(1)}, bf16[64,3840]{1,0:T(8,128)(2,1)S(1)}, u32[]{:S(2)}, u32[]{:S(2)}) collective-permute-start(bf16[64,3840]{1,0:T(8,128)(2,1)S(1)} %get-tuple-element.33), channel_id=1, source_target_pairs={{0,6},{1,7},{2,4},{3,5},{4,2},{5,3},{6,0},{7,1},{8,14},{9,15},{10,... | collective-permute-start | bytes 1474568 | tf_op jit(solution)/shard_map/ppermute | solution.py:198
  19.0 38.9 %collective-permute-start.6 = (bf16[64,3840]{1,0:T(8,128)(2,1)S(1)}, bf16[64,3840]{1,0:T(8,128)(2,1)S(1)}, u32[]{:S(2)}, u32[]{:S(2)}) collective-permute-start(bf16[64,3840]{1,0:T(8,128)(2,1)S(1)} %get-tuple-element.34), channel_id=1, source_target_pairs={{0,7},{1,6},{2,5},{3,4},{4,3},{5,2},{6,1},{7,0},{8,15},{9,14},{10,... | collective-permute-start | bytes 1474568 | tf_op jit(solution)/shard_map/ppermute | solution.py:198
  29.0 29.6 %collective-permute-start.7 = (bf16[64,1920]{1,0:T(8,128)(2,1)S(1)}, bf16[64,1920]{1,0:T(8,128)(2,1)S(1)}, u32[]{:S(2)}, u32[]{:S(2)}) collective-permute-start(bf16[64,1920]{1,0:T(8,128)(2,1)S(1)} %bitcast.2), channel_id=1, source_target_pairs={{0,8},{1,9},{2,10},{3,11},{4,12},{5,13},{6,14},{7,15},{8,0},{9,1},... | collective-permute-start | bytes 737288 | tf_op jit(solution)/shard_map/ppermute | solution.py:198
  59.4 1.4 collective-permute-start.8
  60.8 5.8 %collective-permute-start.11 = (f32[64,256]{1,0:T(8,128)S(1)}, f32[64,256]{1,0:T(8,128)S(1)}, u32[]{:S(2)}, u32[]{:S(2)}) collective-permute-start(f32[64,256]{1,0:T(8,128)S(1)} %add.42.refs_0_), channel_id=1, source_target_pairs={{0,6},{1,7},{2,4},{3,5},{4,2},{5,3},{6,0},{7,1},{8,14},{9,15},{10,... | collective-permute-start | bytes 196616 | tf_op jit(solution)/shard_map/ppermute | solution.py:198
  63.2 4.3 %collective-permute-start.10 = (f32[64,256]{1,0:T(8,128)S(1)}, f32[64,256]{1,0:T(8,128)S(1)}, u32[]{:S(2)}, u32[]{:S(2)}) collective-permute-start(f32[64,256]{1,0:T(8,128)S(1)} %add.42.refs_0_), channel_id=1, source_target_pairs={{0,4},{1,5},{2,6},{3,7},{4,0},{5,1},{6,2},{7,3},{8,12},{9,13},{10,... | collective-permute-start | bytes 196616 | tf_op jit(solution)/shard_map/ppermute | solution.py:198
  63.2 4.3 %collective-permute-start.9 = (f32[64,256]{1,0:T(8,128)S(1)}, f32[64,256]{1,0:T(8,128)S(1)}, u32[]{:S(2)}, u32[]{:S(2)}) collective-permute-start(f32[64,256]{1,0:T(8,128)S(1)} %add.42.refs_0_), channel_id=1, source_target_pairs={{0,2},{1,3},{2,0},{3,1},{4,6},{5,7},{6,4},{7,5},{8,10},{9,11},{10,... | collective-permute-start | bytes 196616 | tf_op jit(solution)/shard_map/ppermute | solution.py:198
  67.6 1.3 collective-permute-start.12
  69.3 14.3 %collective-permute-start.13 = (bf16[64,1920]{1,0:T(8,128)(2,1)S(1)}, bf16[64,1920]{1,0:T(8,128)(2,1)S(1)}, u32[]{:S(2)}, u32[]{:S(2)}) collective-permute-start(bf16[64,1920]{1,0:T(8,128)(2,1)S(1)} %shard_map.32), channel_id=1, source_target_pairs={{0,8},{1,9},{2,10},{3,11},{4,12},{5,13},{6,14},{7,15},{8,0},{9,1},... | collective-permute-start | bytes 737288 | tf_op jit(solution)/shard_map/ppermute | solution.py:198
  84.2 3.4 %collective-permute-start.17 = (f32[64,64]{1,0:T(8,128)S(1)}, f32[64,64]{1,0:T(8,128)S(1)}, u32[]{:S(2)}, u32[]{:S(2)}) collective-permute-start(f32[64,64]{1,0:T(8,128)S(1)} %get-tuple-element.40), channel_id=1, source_target_pairs={{0,3},{1,2},{2,1},{3,0},{4,7},{5,6},{6,5},{7,4},{8,11},{9,10},{10,... | collective-permute-start | bytes 49160 | tf_op jit(solution)/shard_map/ppermute | solution.py:198
  84.3 4.2 %collective-permute-start.16 = (f32[64,64]{1,0:T(8,128)S(1)}, f32[64,64]{1,0:T(8,128)S(1)}, u32[]{:S(2)}, u32[]{:S(2)}) collective-permute-start(f32[64,64]{1,0:T(8,128)S(1)} %get-tuple-element.40), channel_id=1, source_target_pairs={{0,2},{1,3},{2,0},{3,1},{4,6},{5,7},{6,4},{7,5},{8,10},{9,11},{10,... | collective-permute-start | bytes 49160 | tf_op jit(solution)/shard_map/ppermute | solution.py:198
  85.4 3.1 %collective-permute-start.15 = (f32[64,64]{1,0:T(8,128)S(1)}, f32[64,64]{1,0:T(8,128)S(1)}, u32[]{:S(2)}, u32[]{:S(2)}) collective-permute-start(f32[64,64]{1,0:T(8,128)S(1)} %get-tuple-element.40), channel_id=1, source_target_pairs={{0,1},{1,0},{2,3},{3,2},{4,5},{5,4},{6,7},{7,6},{8,9},{9,8},{10,11... | collective-permute-start | bytes 49160 | tf_op jit(solution)/shard_map/ppermute | solution.py:198
  86.1 17.5 %collective-permute-start.14 = (bf16[64,1920]{1,0:T(8,128)(2,1)S(1)}, bf16[64,1920]{1,0:T(8,128)(2,1)S(1)}, u32[]{:S(2)}, u32[]{:S(2)}) collective-permute-start(bf16[64,1920]{1,0:T(8,128)(2,1)S(1)} %get-tuple-element.39.basis), channel_id=1, source_target_pairs={{0,8},{1,9},{2,10},{3,11},{4,12},{5,13},{6,14},{7,15},{8,0},{9,1},... | collective-permute-start | bytes 737288 | tf_op jit(solution)/shard_map/ppermute | solution.py:198
  88.5 7.9 %collective-permute-start.20 = (f32[64,64]{1,0:T(8,128)S(1)}, f32[64,64]{1,0:T(8,128)S(1)}, u32[]{:S(2)}, u32[]{:S(2)}) collective-permute-start(f32[64,64]{1,0:T(8,128)S(1)} %add_add_fusion.3), channel_id=1, source_target_pairs={{0,12},{1,13},{2,14},{3,15},{4,8},{5,9},{6,10},{7,11},{8,4},{9,5},... | collective-permute-start | bytes 49160 | tf_op jit(solution)/shard_map/ppermute | solution.py:198
  92.0 10.9 %collective-permute-start.19 = (f32[64,64]{1,0:T(8,128)S(1)}, f32[64,64]{1,0:T(8,128)S(1)}, u32[]{:S(2)}, u32[]{:S(2)}) collective-permute-start(f32[64,64]{1,0:T(8,128)S(1)} %add_add_fusion.3), channel_id=1, source_target_pairs={{0,8},{1,9},{2,10},{3,11},{4,12},{5,13},{6,14},{7,15},{8,0},{9,1},... | collective-permute-start | bytes 49160 | tf_op jit(solution)/shard_map/ppermute | solution.py:198
  92.0 10.9 %collective-permute-start.18 = (f32[64,64]{1,0:T(8,128)S(1)}, f32[64,64]{1,0:T(8,128)S(1)}, u32[]{:S(2)}, u32[]{:S(2)}) collective-permute-start(f32[64,64]{1,0:T(8,128)S(1)} %add_add_fusion.3), channel_id=1, source_target_pairs={{0,4},{1,5},{2,6},{3,7},{4,0},{5,1},{6,2},{7,3},{8,12},{9,13},{10,... | collective-permute-start | bytes 49160 | tf_op jit(solution)/shard_map/ppermute | solution.py:198
  104.3 1.3 collective-permute-start.21
  105.6 6.8 %collective-permute-start.24 = (f32[64,256]{1,0:T(8,128)S(1)}, f32[64,256]{1,0:T(8,128)}, u32[]{:S(2)}, u32[]{:S(2)}) collective-permute-start(f32[64,256]{1,0:T(8,128)S(1)} %add.49.refs_0_), channel_id=1, source_target_pairs={{0,6},{1,7},{2,4},{3,5},{4,2},{5,3},{6,0},{7,1},{8,14},{9,15},{10,... | collective-permute-start | bytes 196616 | tf_op jit(solution)/shard_map/ppermute | solution.py:198
  106.4 6.0 %collective-permute-start.23 = (f32[64,256]{1,0:T(8,128)S(1)}, f32[64,256]{1,0:T(8,128)}, u32[]{:S(2)}, u32[]{:S(2)}) collective-permute-start(f32[64,256]{1,0:T(8,128)S(1)} %add.49.refs_0_), channel_id=1, source_target_pairs={{0,4},{1,5},{2,6},{3,7},{4,0},{5,1},{6,2},{7,3},{8,12},{9,13},{10,... | collective-permute-start | bytes 196616 | tf_op jit(solution)/shard_map/ppermute | solution.py:198
  108.2 4.4 %collective-permute-start.22 = (f32[64,256]{1,0:T(8,128)S(1)}, f32[64,256]{1,0:T(8,128)}, u32[]{:S(2)}, u32[]{:S(2)}) collective-permute-start(f32[64,256]{1,0:T(8,128)S(1)} %add.49.refs_0_), channel_id=1, source_target_pairs={{0,2},{1,3},{2,0},{3,1},{4,6},{5,7},{6,4},{7,5},{8,10},{9,11},{10,... | collective-permute-start | bytes 196616 | tf_op jit(solution)/shard_map/ppermute | solution.py:198
  117.3 13.9 %collective-permute-start.26 = (bf16[64,1920]{1,0:T(8,128)(2,1)S(1)}, bf16[64,1920]{1,0:T(8,128)(2,1)S(1)}, u32[]{:S(2)}, u32[]{:S(2)}) collective-permute-start(bf16[64,1920]{1,0:T(8,128)(2,1)S(1)} %shard_map.39), channel_id=1, source_target_pairs={{0,8},{1,9},{2,10},{3,11},{4,12},{5,13},{6,14},{7,15},{8,0},{9,1},... | collective-permute-start | bytes 737288 | tf_op jit(solution)/shard_map/ppermute | solution.py:198
  131.8 3.5 %collective-permute-start.29 = (f32[64,64]{1,0:T(8,128)S(1)}, f32[64,64]{1,0:T(8,128)S(1)}, u32[]{:S(2)}, u32[]{:S(2)}) collective-permute-start(f32[64,64]{1,0:T(8,128)S(1)} %get-tuple-element.47), channel_id=1, source_target_pairs={{0,3},{1,2},{2,1},{3,0},{4,7},{5,6},{6,5},{7,4},{8,11},{9,10},{10,... | collective-permute-start | bytes 49160 | tf_op jit(solution)/shard_map/ppermute | solution.py:198
  132.4 3.9 %collective-permute-start.28 = (f32[64,64]{1,0:T(8,128)S(1)}, f32[64,64]{1,0:T(8,128)S(1)}, u32[]{:S(2)}, u32[]{:S(2)}) collective-permute-start(f32[64,64]{1,0:T(8,128)S(1)} %get-tuple-element.47), channel_id=1, source_target_pairs={{0,2},{1,3},{2,0},{3,1},{4,6},{5,7},{6,4},{7,5},{8,10},{9,11},{10,... | collective-permute-start | bytes 49160 | tf_op jit(solution)/shard_map/ppermute | solution.py:198
  133.5 2.8 %collective-permute-start.27 = (f32[64,64]{1,0:T(8,128)S(1)}, f32[64,64]{1,0:T(8,128)S(1)}, u32[]{:S(2)}, u32[]{:S(2)}) collective-permute-start(f32[64,64]{1,0:T(8,128)S(1)} %get-tuple-element.47), channel_id=1, source_target_pairs={{0,1},{1,0},{2,3},{3,2},{4,5},{5,4},{6,7},{7,6},{8,9},{9,8},{10,11... | collective-permute-start | bytes 49160 | tf_op jit(solution)/shard_map/ppermute | solution.py:198
  136.4 6.0 %collective-permute-start.32 = (f32[64,64]{1,0:T(8,128)S(1)}, f32[64,64]{1,0:T(8,128)S(1)}, u32[]{:S(2)}, u32[]{:S(2)}) collective-permute-start(f32[64,64]{1,0:T(8,128)S(1)} %add_add_fusion.1), channel_id=1, source_target_pairs={{0,12},{1,13},{2,14},{3,15},{4,8},{5,9},{6,10},{7,11},{8,4},{9,5},... | collective-permute-start | bytes 49160 | tf_op jit(solution)/shard_map/ppermute | solution.py:198
  137.9 5.1 %collective-permute-start.31 = (f32[64,64]{1,0:T(8,128)S(1)}, f32[64,64]{1,0:T(8,128)S(1)}, u32[]{:S(2)}, u32[]{:S(2)}) collective-permute-start(f32[64,64]{1,0:T(8,128)S(1)} %add_add_fusion.1), channel_id=1, source_target_pairs={{0,8},{1,9},{2,10},{3,11},{4,12},{5,13},{6,14},{7,15},{8,0},{9,1},... | collective-permute-start | bytes 49160 | tf_op jit(solution)/shard_map/ppermute | solution.py:198
  138.0 5.1 %collective-permute-start.30 = (f32[64,64]{1,0:T(8,128)S(1)}, f32[64,64]{1,0:T(8,128)S(1)}, u32[]{:S(2)}, u32[]{:S(2)}) collective-permute-start(f32[64,64]{1,0:T(8,128)S(1)} %add_add_fusion.1), channel_id=1, source_target_pairs={{0,4},{1,5},{2,6},{3,7},{4,0},{5,1},{6,2},{7,3},{8,12},{9,13},{10,... | collective-permute-start | bytes 49160 | tf_op jit(solution)/shard_map/ppermute | solution.py:198
  (6 other events, 77.5 us)

commit v4 on v3

--- a/solution.py
+++ b/solution.py
@@ -56,7 +56,7 @@
         out_specs=[VMEM] * count,
         out_shape=[struct((rows, 2 * width), matrix.dtype)] * count,
         scratch_shapes=[pltpu.SemaphoreType.DMA((2 * count,))],
-        compiler_params=BIG,
+        compiler_params=pltpu.CompilerParams(vmem_limit_bytes=56 * 2**20),
         cost_estimate=cost(0, 8 * rows * count * width),
     )(ids, matrix)
 
@@ -87,25 +87,28 @@
                 [struct((rank, cells // 2), f32)] * 2, cost(2 * rank * cells * width, 2 * cells * width))
 
 
-def image_kernel(normalised, *refs):
-    value, mates = refs[0][...], [ref[...] for ref in refs[1:4]]
-    size = value.shape[1] // (GROUP // 2)
+def image_kernel(normalised, own, values, *refs):
+    size = values.shape[2] // 4
 
     def turned(x, mask):
-        return jnp.concatenate([x[:, (j ^ mask) * size:((j ^ mask) + 1) * size] for j in range(GROUP // 2)], axis=1)
-
-    value = (value + turned(mates[0], 1)) + (turned(mates[1], 2) + turned(mates[2], 3))
+        return jnp.concatenate([x[:, (j ^ mask) * size:((j ^ mask) + 1) * size] for j in range(4)], axis=1)
+
+    terms = [turned(values[r], r) for r in range(4)]
+    value = (terms[0] + terms[1]) + (terms[2] + terms[3])
+    for bit in range(2):
+        value = jnp.where((own[0] >> bit) & 1 == 1, turned(value, 1 << bit), value)
     if normalised:
-        value = nn(refs[4][...], value, HIGHEST)
+        value = nn(refs[0][...], value, HIGHEST)
     refs[-1][...] = value.astype(bf16)
 
 
-def image_of(value, mates, inverse):
-    args = [value, *mates] + ([] if inverse is None else [inverse])
+def image_of(own, values, inverse):
+    args = [own, values] + ([] if inverse is None else [inverse])
     return pl.pallas_call(
         functools.partial(image_kernel, inverse is not None),
-        in_specs=[VMEM] * len(args), out_specs=VMEM, out_shape=struct(value.shape, bf16),
-        compiler_params=BIG, cost_estimate=cost(12 * value.size * value.shape[0], 16 * value.size),
+        in_specs=[pl.BlockSpec(memory_space=pltpu.SMEM)] + [VMEM] * (len(args) - 1), out_specs=VMEM,
+        out_shape=struct(values.shape[1:], bf16),
+        compiler_params=BIG, cost_estimate=cost(12 * values.size, 4 * values.size),
     )(*args)
 
 
@@ -198,10 +201,16 @@
     return lax.ppermute(value, "cell", [(i, i ^ mask) for i in range(cells)])
 
 
+def from_four(value, cells, low):
+    four = [base + low * j for base in range(cells) if not base & (3 * low) for j in range(4)]
+    groups = [four[i:i + 4] for i in range(0, cells, 4)]
+    return lax.all_to_all(jnp.broadcast_to(value, (4,) + value.shape), "cell", 0, 0, axis_index_groups=groups)
+
+
 def total_over_cells(value, cells):
-    for low in range(0, cells.bit_length() - 1, 2):
-        one, two = 1 << low, 2 << low
-        value = (value + mate(value, cells, one)) + (mate(value, cells, two) + mate(value, cells, one | two))
+    for low in (4, 1):
+        x = from_four(value, cells, low)
+        value = (x[0] + x[1]) + (x[2] + x[3])
     return value
 
 
@@ -209,13 +218,17 @@
     width = start_basis.shape[0]
     index = lax.axis_index("cell").astype(jnp.int32)
     members = index ^ jnp.arange(GROUP, dtype=jnp.int32)
-    slots = pack(expression, jnp.stack([members, members ^ GROUP], axis=1).reshape(-1), width)
-    slots = [mate(x, cells, k) if k else x for k, x in enumerate(slots)]
+    packs = pack(expression, jnp.stack([members, members ^ GROUP], axis=1).reshape(-1), width)
+    slots = list(packs)
+    for k in (1, 6, 2, 4, 7, 3, 5):
+        slots[k] = mate(packs[k], cells, k)
+
+    place = ((index >> 1) & 3).reshape(1)
 
     def image_from(basis, other, inverse):
         even, odd = scores(slots, 1, other, scores(slots, 0, basis, []))
         even = even + mate(odd, cells, 1)
-        image = image_of(even, [mate(even, cells, mask) for mask in (2, 4, 6)], inverse)
+        image = image_of(place, from_four(even, cells, 2), inverse)
         return image, mate(image, cells, 1)
 
     def loading_from(images, dtype):

time: 147 us -> 187 us (1.27)
  blocking collectives: 0 us -> 23.5 us
  local copies, waits for them, and re-layouts: 4.08 us -> 18.8 us
  other arithmetic: 0.67 us -> 7.75 us
  starting transfers between devices: 34.6 us -> 28.1 us
  Pallas kernels: 14.9 us -> 21.4 us
  waiting for transfers between devices: 91.9 us -> 86.2 us
    all_to_all x0 -> x3, blocking collectives: none -> 23.5 us  [from_four(): lax.all_to_all(jnp.broadcast_to(value, (4,) + value.shape), 'cell', 0, 0,...]
    ppermute x33 -> x15, starting transfers between devices: 34.6 us -> 16.1 us  [mate(): return lax.ppermute(value, 'cell', [(i, i ^ mask) for i in range(cells)])]
    ppermute x33 -> x15, waiting for transfers between devices: 91.9 us -> 77.3 us  [mate(): return lax.ppermute(value, 'cell', [(i, i ^ mask) for i in range(cells)])]
    all_to_all x0 -> x3, starting transfers between devices: none -> 12 us  [from_four(): lax.all_to_all(jnp.broadcast_to(value, (4,) + value.shape), 'cell', 0, 0,...]
    unnamed x10 -> x32, local copies, waits for them, and re-layouts: 3.91 us -> 14.8 us
    all_to_all x0 -> x3, waiting for transfers between devices: none -> 8.88 us  [from_four(): lax.all_to_all(jnp.broadcast_to(value, (4,) + value.shape), 'cell', 0, 0,...]
    all_to_all x0 -> x4, other arithmetic: none -> 5.45 us  [from_four(): lax.all_to_all(jnp.broadcast_to(value, (4,) + value.shape), 'cell', 0, 0,...]
    pallas_call x1, Pallas kernels: 1.52 us -> 4.95 us  [pack(): pl.pallas_call(pack_kernel, in_specs=[pl.BlockSpec(memory_space=pltpu.SME...]
  transfers between devices with their start and end apart: 33 -> 18, of which waited for: 21 -> 13; matrix products, arithmetic and copies ran while one was open for 0% -> 3% of each run, Pallas kernels for 4% -> 3%
where the time goes in v4:
time: 187 us; the launch traced here: 186 us
  waiting for transfers between devices  86.2 us (46%)
  starting transfers between devices  28.1 us (15%)
  blocking collectives  23.5 us (13%)
  Pallas kernels  21.4 us (11%)
  local copies, waits for them, and re-layouts  18.8 us (10%)
  other arithmetic  7.75 us (4%)
    ppermute x15, waiting for transfers between devices, mate(): return lax.ppermute(value, 'cell', [(i, i ^ mask) for i in range(cells)])  77.3 us
    all_to_all x3, blocking collectives, from_four(): lax.all_to_all(jnp.broadcast_to(value, (4,) + value.shape), 'cell', 0, 0,...  23.5 us
    ppermute x15, starting transfers between devices, mate(): return lax.ppermute(value, 'cell', [(i, i ^ mask) for i in range(cells)])  16.1 us
    unnamed x32, local copies, waits for them, and re-layouts  14.8 us
    all_to_all x3, starting transfers between devices, from_four(): lax.all_to_all(jnp.broadcast_to(value, (4,) + value.shape), 'cell', 0, 0,...  12 us
    all_to_all x3, waiting for transfers between devices, from_four(): lax.all_to_all(jnp.broadcast_to(value, (4,) + value.shape), 'cell', 0, 0,...  8.88 us
    pallas_call x10, Pallas kernels, call(): pl.pallas_call(kernel, in_specs=[VMEM] * len(args), out_specs=[VMEM] * le...  7.64 us
    all_to_all x4, other arithmetic, from_four(): lax.all_to_all(jnp.broadcast_to(value, (4,) + value.shape), 'cell', 0, 0,...  5.45 us
  transfers between devices with their start and end apart: 18, of which 13 were waited for; matrix products, arithmetic and copies ran while one was open for 3% of the time, Pallas kernels for 3%

profile of v4, /device:TPU:0, one launch (start us, length us, event | category | flops | bytes accessed | tf_op | source)
XLA Modules:
  0.0 186.0 jit_solution(9077955288459404888)
XLA Ops:
  0.7 4.9 %shard_map.28 = (bf16[64,3840]{1,0:T(8,128)(2,1)}, bf16[64,3840]{1,0:T(8,128)(2,1)}, bf16[64,3840]{1,0:T(8,128)(2,1)}, bf16[64,3840]{1,0:T(8,128)(2,1)}, bf16[64...) custom-call(s32[16]{0:T(128)} %reshape.29.ids, ...), custom_call_target="tpu_custom_call" | custom-call | bytes 7864320 | tf_op jit(solution)/shard_map/pallas_call | solution.py:53
  6.2 2.6 %collective-permute-start.1 = (bf16[64,3840]{1,0:T(8,128)(2,1)}, bf16[64,3840]{1,0:T(8,128)(2,1)S(1)}, u32[]{:S(2)}, u32[]{:S(2)}) collective-permute-start(bf16[64,3840]{1,0:T(8,128)(2,1)} %get-tuple-element.29), channel_id=1, source_target_pairs={{0,2},{1,3},{2,0},{3,1},{4,6},{5,7},{6,4},{7,5},{8,10},{9,11},{10,... | collective-permute-start | bytes 1474568 | tf_op jit(solution)/shard_map/ppermute | solution.py:201
  8.9 1.8 collective-permute-start.3
  10.7 2.6 %collective-permute-start.5 = (bf16[64,3840]{1,0:T(8,128)(2,1)}, bf16[64,3840]{1,0:T(8,128)(2,1)S(1)}, u32[]{:S(2)}, u32[]{:S(2)}) collective-permute-start(bf16[64,3840]{1,0:T(8,128)(2,1)} %get-tuple-element.33), channel_id=1, source_target_pairs={{0,6},{1,7},{2,4},{3,5},{4,2},{5,3},{6,0},{7,1},{8,14},{9,15},{10,... | collective-permute-start | bytes 1474568 | tf_op jit(solution)/shard_map/ppermute | solution.py:201
  13.3 7.8 %collective-permute-done.1.refs_2_ = bf16[64,3840]{1,0:T(8,128)(2,1)S(1)} collective-permute-done((bf16[64,3840]{1,0:T(8,128)(2,1)}, bf16[64,3840]{1,0:T(8,128)(2,1)S(1)}, u32[]{:S(2)}, u32[]{:S(2)}) %collective-permute-start.1) | collective-permute-done | bytes 491552 | tf_op jit(solution)/shard_map/ppermute | solution.py:201
  21.1 1.8 collective-permute-start.6
  22.8 8.2 %collective-permute-done.2.refs_3_ = bf16[64,3840]{1,0:T(8,128)(2,1)S(1)} collective-permute-done((bf16[64,3840]{1,0:T(8,128)(2,1)}, bf16[64,3840]{1,0:T(8,128)(2,1)S(1)}, u32[]{:S(2)}, u32[]{:S(2)}) %collective-permute-start.2) | collective-permute-done | bytes 491552 | tf_op jit(solution)/shard_map/ppermute | solution.py:201
  31.1 2.6 %collective-permute-start.7 = (bf16[64,1920]{1,0:T(8,128)(2,1)}, bf16[64,1920]{1,0:T(8,128)(2,1)S(1)}, u32[]{:S(2)}, u32[]{:S(2)}) collective-permute-start(bf16[64,1920]{1,0:T(8,128)(2,1)} %bitcast.1.basis), channel_id=1, source_target_pairs={{0,8},{1,9},{2,10},{3,11},{4,12},{5,13},{6,14},{7,15},{8,0},{9,1},... | collective-permute-start | bytes 737288 | tf_op jit(solution)/shard_map/ppermute | solution.py:201
  33.7 16.9 %collective-permute-done.5.refs_6_ = bf16[64,3840]{1,0:T(8,128)(2,1)S(1)} collective-permute-done((bf16[64,3840]{1,0:T(8,128)(2,1)}, bf16[64,3840]{1,0:T(8,128)(2,1)S(1)}, u32[]{:S(2)}, u32[]{:S(2)}) %collective-permute-start.5) | collective-permute-done | bytes 491552 | tf_op jit(solution)/shard_map/ppermute | solution.py:201
  50.6 9.4 %collective-permute-done.6.refs_7_ = bf16[64,3840]{1,0:T(8,128)(2,1)S(1)} collective-permute-done((bf16[64,3840]{1,0:T(8,128)(2,1)}, bf16[64,3840]{1,0:T(8,128)(2,1)S(1)}, u32[]{:S(2)}, u32[]{:S(2)}) %collective-permute-start.6) | collective-permute-done | bytes 491552 | tf_op jit(solution)/shard_map/ppermute | solution.py:201
  61.2 1.7 shard_map.29
  65.8 4.1 %all-to-all-start = ((f32[4,64,256]{2,1,0:T(8,128)}), f32[4,64,256]{2,1,0:T(8,128)}, u32[]{:S(2)}, u32[]{:S(2)}) async-start(f32[4,64,256]{2,1,0:T(8,128)} %broadcast_in_dim.18), calls=%async_computation | async-start | bytes 524288 | tf_op jit(solution)/shard_map/all_to_all | solution.py:207
  69.9 6.1 %all-to-all-done.values = f32[4,64,256]{2,1,0:T(8,128)} async-done(((f32[4,64,256]{2,1,0:T(8,128)}), f32[4,64,256]{2,1,0:T(8,128)}, u32[]{:S(2)}, u32[]{:S(2)}) %all-to-all-start) | async-done | bytes 262176 | tf_op jit(solution)/shard_map/all_to_all | solution.py:207
  79.8 2.4 %collective-permute-start.10 = (bf16[64,1920]{1,0:T(8,128)(2,1)S(1)}, bf16[64,1920]{1,0:T(8,128)(2,1)S(1)}, u32[]{:S(2)}, u32[]{:S(2)}) collective-permute-start(bf16[64,1920]{1,0:T(8,128)(2,1)S(1)} %shard_map.32), channel_id=1, source_target_pairs={{0,8},{1,9},{2,10},{3,11},{4,12},{5,13},{6,14},{7,15},{8,0},{9,1},... | collective-permute-start | bytes 737288 | tf_op jit(solution)/shard_map/ppermute | solution.py:201
  82.7 11.4 %collective-permute-done.10.received = bf16[64,1920]{1,0:T(8,128)(2,1)S(1)} collective-permute-done((bf16[64,1920]{1,0:T(8,128)(2,1)S(1)}, bf16[64,1920]{1,0:T(8,128)(2,1)S(1)}, u32[]{:S(2)}, u32[]{:S(2)}) %collective-permute-start.10) | collective-permute-done | bytes 245792 | tf_op jit(solution)/shard_map/ppermute | solution.py:201
  97.0 8.9 %all_to_all.30 = f32[4,1,4096]{2,1,0:T(1,128)} all-to-all(f32[4,1,4096]{2,1,0:T(1,128)S(1)} %reshape.31), channel_id=1, replica_groups={{0,4,8,12},{1,5,9,13},{2,6,10,14},{3,7,11,15},{16,20,24,28},{17,21,25,2..., dimensions={0} | all-to-all | bytes 131072 | tf_op jit(solution)/shard_map/all_to_all | solution.py:207
  106.5 1.6 reduce
  110.4 1.6 reshape.33
  112.0 3.9 %all-to-all-start.2 = ((f32[4,1,4096]{2,1,0:T(1,128)}), f32[4,1,4096]{2,1,0:T(1,128)}, u32[]{:S(2)}, u32[]{:S(2)}) async-start(f32[4,1,4096]{2,1,0:T(1,128)} %reshape.33), calls=%async_computation.2 | async-start | bytes 131072 | tf_op jit(solution)/shard_map/all_to_all | solution.py:207
  120.1 2.3 %reduce.1 = f32[4,4096]{1,0:T(4,128)} reduce(f32[4,1,4096]{2,1,0:T(1,128)} %all-to-all-done.2, f32[]{:T(128)} %broadcast.23), dimensions={1}, to_apply=%all_to_all.20.reduce_sub_computation | reduce | bytes 131076 | tf_op jit(solution)/shard_map/all_to_all | solution.py:207
  122.4 1.6 reshape.34
  124.0 1.4 fusion.5.gram
  125.4 5.3 %collective-permute-done.11.basis = bf16[64,1920]{1,0:T(8,128)(2,1)} collective-permute-done((bf16[64,1920]{1,0:T(8,128)(2,1)}, bf16[64,1920]{1,0:T(8,128)(2,1)}, u32[]{:S(2)}, u32[]{:S(2)}) %collective-permute-start.11) | collective-permute-done | bytes 245792 | tf_op jit(solution)/shard_map/ppermute | solution.py:201
  132.6 1.7 shard_map.36
  136.4 4.1 %all-to-all-start.3 = ((f32[4,64,256]{2,1,0:T(8,128)}), f32[4,64,256]{2,1,0:T(8,128)}, u32[]{:S(2)}, u32[]{:S(2)}) async-start(f32[4,64,256]{2,1,0:T(8,128)} %broadcast_in_dim.21), calls=%async_computation.3 | async-start | bytes 524288 | tf_op jit(solution)/shard_map/all_to_all | solution.py:207
  140.4 3.2 %shard_map.37.refs_0_ = f32[64,64]{1,0:T(8,128)} custom-call(f32[64,64]{1,0:T(8,128)} %fusion.5.gram), custom_call_target="tpu_custom_call" | custom-call | flops 100000 | bytes 32768 | tf_op jit(solution)/shard_map/pallas_call | solution.py:182
  143.6 2.8 %all-to-all-done.3.values = f32[4,64,256]{2,1,0:T(8,128)} async-done(((f32[4,64,256]{2,1,0:T(8,128)}), f32[4,64,256]{2,1,0:T(8,128)}, u32[]{:S(2)}, u32[]{:S(2)}) %all-to-all-start.3) | async-done | bytes 262176 | tf_op jit(solution)/shard_map/all_to_all | solution.py:207
  147.2 1.3 shard_map.38.refs_8_
  151.8 13.7 %collective-permute-done.14.received = bf16[64,1920]{1,0:T(8,128)(2,1)S(1)} collective-permute-done((bf16[64,1920]{1,0:T(8,128)(2,1)S(1)}, bf16[64,1920]{1,0:T(8,128)(2,1)S(1)}, u32[]{:S(2)}, u32[]{:S(2)}) %collective-permute-start.14) | collective-permute-done | bytes 245792 | tf_op jit(solution)/shard_map/ppermute | solution.py:201
  166.2 8.1 %all_to_all.31 = f32[4,1,4096]{2,1,0:T(1,128)S(1)} all-to-all(f32[4,1,4096]{2,1,0:T(1,128)S(1)} %reshape.35), channel_id=1, replica_groups={{0,4,8,12},{1,5,9,13},{2,6,10,14},{3,7,11,15},{16,20,24,28},{17,21,25,2..., dimensions={0} | all-to-all | bytes 131072 | tf_op jit(solution)/shard_map/all_to_all | solution.py:207
  175.4 6.5 %all_to_all.32 = f32[4,1,4096]{2,1,0:T(1,128)S(1)} all-to-all(f32[4,1,4096]{2,1,0:T(1,128)S(1)} %reshape.37), channel_id=1, replica_groups={{0,1,2,3},{4,5,6,7},{8,9,10,11},{12,13,14,15},{16,17,18,19},{20,21,22,2..., dimensions={0} | all-to-all | bytes 131072 | tf_op jit(solution)/shard_map/all_to_all | solution.py:207
  182.8 3.2 %shard_map.42 = f32[64,1920]{1,0:T(8,128)} custom-call(f32[64,64]{1,0:T(8,128)S(1)} %fusion.1.gram, f32[64,1920]{1,0:T(8,128)S(1)} %get-tuple-element.48.loading), custom_call_target="tpu_custom_call" | custom-call | tf_op jit(solution)/shard_map/pallas_call | solution.py:193
  (75 shorter events, 30.2 us)
Async XLA Ops:
  5.7 5.0 %collective-permute-start = (bf16[64,3840]{1,0:T(8,128)(2,1)}, bf16[64,3840]{1,0:T(8,128)(2,1)S(1)}, u32[]{:S(2)}, u32[]{:S(2)}) collective-permute-start(bf16[64,3840]{1,0:T(8,128)(2,1)} %get-tuple-element.28), channel_id=1, source_target_pairs={{0,1},{1,0},{2,3},{3,2},{4,5},{5,4},{6,7},{7,6},{8,9},{9,8},{10,11... | collective-permute-start | bytes 1474568 | tf_op jit(solution)/shard_map/ppermute | solution.py:201
  6.2 14.9 %collective-permute-start.1 = (bf16[64,3840]{1,0:T(8,128)(2,1)}, bf16[64,3840]{1,0:T(8,128)(2,1)S(1)}, u32[]{:S(2)}, u32[]{:S(2)}) collective-permute-start(bf16[64,3840]{1,0:T(8,128)(2,1)} %get-tuple-element.29), channel_id=1, source_target_pairs={{0,2},{1,3},{2,0},{3,1},{4,6},{5,7},{6,4},{7,5},{8,10},{9,11},{10,... | collective-permute-start | bytes 1474568 | tf_op jit(solution)/shard_map/ppermute | solution.py:201
  8.8 22.3 %collective-permute-start.2 = (bf16[64,3840]{1,0:T(8,128)(2,1)}, bf16[64,3840]{1,0:T(8,128)(2,1)S(1)}, u32[]{:S(2)}, u32[]{:S(2)}) collective-permute-start(bf16[64,3840]{1,0:T(8,128)(2,1)} %get-tuple-element.30), channel_id=1, source_target_pairs={{0,3},{1,2},{2,1},{3,0},{4,7},{5,6},{6,5},{7,4},{8,11},{9,10},{10,... | collective-permute-start | bytes 1474568 | tf_op jit(solution)/shard_map/ppermute | solution.py:201
  8.9 24.9 %collective-permute-start.3 = (bf16[64,3840]{1,0:T(8,128)(2,1)}, bf16[64,3840]{1,0:T(8,128)(2,1)S(1)}, u32[]{:S(2)}, u32[]{:S(2)}) collective-permute-start(bf16[64,3840]{1,0:T(8,128)(2,1)} %get-tuple-element.31), channel_id=1, source_target_pairs={{0,4},{1,5},{2,6},{3,7},{4,0},{5,1},{6,2},{7,3},{8,12},{9,13},{10,... | collective-permute-start | bytes 1474568 | tf_op jit(solution)/shard_map/ppermute | solution.py:201
  10.7 23.1 %collective-permute-start.4 = (bf16[64,3840]{1,0:T(8,128)(2,1)}, bf16[64,3840]{1,0:T(8,128)(2,1)S(1)}, u32[]{:S(2)}, u32[]{:S(2)}) collective-permute-start(bf16[64,3840]{1,0:T(8,128)(2,1)} %get-tuple-element.32), channel_id=1, source_target_pairs={{0,5},{1,4},{2,7},{3,6},{4,1},{5,0},{6,3},{7,2},{8,13},{9,12},{10,... | collective-permute-start | bytes 1474568 | tf_op jit(solution)/shard_map/ppermute | solution.py:201
  10.7 39.9 %collective-permute-start.5 = (bf16[64,3840]{1,0:T(8,128)(2,1)}, bf16[64,3840]{1,0:T(8,128)(2,1)S(1)}, u32[]{:S(2)}, u32[]{:S(2)}) collective-permute-start(bf16[64,3840]{1,0:T(8,128)(2,1)} %get-tuple-element.33), channel_id=1, source_target_pairs={{0,6},{1,7},{2,4},{3,5},{4,2},{5,3},{6,0},{7,1},{8,14},{9,15},{10,... | collective-permute-start | bytes 1474568 | tf_op jit(solution)/shard_map/ppermute | solution.py:201
  21.1 38.9 %collective-permute-start.6 = (bf16[64,3840]{1,0:T(8,128)(2,1)}, bf16[64,3840]{1,0:T(8,128)(2,1)S(1)}, u32[]{:S(2)}, u32[]{:S(2)}) collective-permute-start(bf16[64,3840]{1,0:T(8,128)(2,1)} %get-tuple-element.34), channel_id=1, source_target_pairs={{0,7},{1,6},{2,5},{3,4},{4,3},{5,2},{6,1},{7,0},{8,15},{9,14},{10,... | collective-permute-start | bytes 1474568 | tf_op jit(solution)/shard_map/ppermute | solution.py:201
  31.1 31.8 %collective-permute-start.7 = (bf16[64,1920]{1,0:T(8,128)(2,1)}, bf16[64,1920]{1,0:T(8,128)(2,1)S(1)}, u32[]{:S(2)}, u32[]{:S(2)}) collective-permute-start(bf16[64,1920]{1,0:T(8,128)(2,1)} %bitcast.1.basis), channel_id=1, source_target_pairs={{0,8},{1,9},{2,10},{3,11},{4,12},{5,13},{6,14},{7,15},{8,0},{9,1},... | collective-permute-start | bytes 737288 | tf_op jit(solution)/shard_map/ppermute | solution.py:201
  60.0 3.7 %copy-start.2 = (bf16[64,3840]{1,0:T(8,128)(2,1)}, bf16[64,3840]{1,0:T(8,128)(2,1)S(1)}, u32[]{:S(2)}) copy-start(bf16[64,3840]{1,0:T(8,128)(2,1)S(1)} %collective-permute-done.6.refs_7_) | copy-start | bytes 1474564
  60.0 1.2 copy-start
  61.2 17.1 %copy-start.1 = (bf16[64,3840]{1,0:T(8,128)(2,1)S(1)}, bf16[64,3840]{1,0:T(8,128)(2,1)}, u32[]{:S(2)}) copy-start(bf16[64,3840]{1,0:T(8,128)(2,1)} %get-tuple-element.27.refs_0_) | copy-start | bytes 1474564
  63.7 1.4 collective-permute-start.8
  65.8 10.1 %all-to-all-start = ((f32[4,64,256]{2,1,0:T(8,128)}), f32[4,64,256]{2,1,0:T(8,128)}, u32[]{:S(2)}, u32[]{:S(2)}) async-start(f32[4,64,256]{2,1,0:T(8,128)} %broadcast_in_dim.18), calls=%async_computation | async-start | bytes 524288 | tf_op jit(solution)/shard_map/all_to_all | solution.py:207
  77.0 1.3 collective-permute-start.9
  78.3 1.0 copy-start.3
  79.8 14.3 %collective-permute-start.10 = (bf16[64,1920]{1,0:T(8,128)(2,1)S(1)}, bf16[64,1920]{1,0:T(8,128)(2,1)S(1)}, u32[]{:S(2)}, u32[]{:S(2)}) collective-permute-start(bf16[64,1920]{1,0:T(8,128)(2,1)S(1)} %shard_map.32), channel_id=1, source_target_pairs={{0,8},{1,9},{2,10},{3,11},{4,12},{5,13},{6,14},{7,15},{8,0},{9,1},... | collective-permute-start | bytes 737288 | tf_op jit(solution)/shard_map/ppermute | solution.py:201
  94.6 0.7 copy-start.7
  112.0 8.1 %all-to-all-start.2 = ((f32[4,1,4096]{2,1,0:T(1,128)}), f32[4,1,4096]{2,1,0:T(1,128)}, u32[]{:S(2)}, u32[]{:S(2)}) async-start(f32[4,1,4096]{2,1,0:T(1,128)} %reshape.33), calls=%async_computation.2 | async-start | bytes 131072 | tf_op jit(solution)/shard_map/all_to_all | solution.py:207
  116.0 14.8 %collective-permute-start.11 = (bf16[64,1920]{1,0:T(8,128)(2,1)}, bf16[64,1920]{1,0:T(8,128)(2,1)}, u32[]{:S(2)}, u32[]{:S(2)}) collective-permute-start(bf16[64,1920]{1,0:T(8,128)(2,1)} %copy-done.7), channel_id=1, source_target_pairs={{0,8},{1,9},{2,10},{3,11},{4,12},{5,13},{6,14},{7,15},{8,0},{9,1},... | collective-permute-start | bytes 737288 | tf_op jit(solution)/shard_map/ppermute | solution.py:201
  116.8 1.0 copy-start.4
  117.8 0.9 copy-start.8
  119.5 0.6 copy-start.10
  130.8 1.0 copy-start.5
  131.8 0.8 copy-start.11
  134.3 1.3 collective-permute-start.12
  136.4 10.1 %all-to-all-start.3 = ((f32[4,64,256]{2,1,0:T(8,128)}), f32[4,64,256]{2,1,0:T(8,128)}, u32[]{:S(2)}, u32[]{:S(2)}) async-start(f32[4,64,256]{2,1,0:T(8,128)} %broadcast_in_dim.21), calls=%async_computation.3 | async-start | bytes 524288 | tf_op jit(solution)/shard_map/all_to_all | solution.py:207
  146.4 0.8 copy-start.9
  148.5 1.3 collective-permute-start.13
  149.8 1.0 copy-start.6
  151.2 14.3 %collective-permute-start.14 = (bf16[64,1920]{1,0:T(8,128)(2,1)S(1)}, bf16[64,1920]{1,0:T(8,128)(2,1)S(1)}, u32[]{:S(2)}, u32[]{:S(2)}) collective-permute-start(bf16[64,1920]{1,0:T(8,128)(2,1)S(1)} %shard_map.39), channel_id=1, source_target_pairs={{0,8},{1,9},{2,10},{3,11},{4,12},{5,13},{6,14},{7,15},{8,0},{9,1},... | collective-permute-start | bytes 737288 | tf_op jit(solution)/shard_map/ppermute | solution.py:201

commit v5 on v3

v5 whole, which is shorter than its diff:
```python
import functools
import math

import jax
import jax.numpy as jnp
from jax import lax
from jax.experimental import pallas as pl
from jax.experimental.pallas import tpu as pltpu
from jax.sharding import PartitionSpec as P

GENES = 30720
ITERS = 2
GROUP = 8
BIG = pltpu.CompilerParams(vmem_limit_bytes=16 * 2**20)
VMEM = pl.BlockSpec(memory_space=pltpu.VMEM)
HIGHEST = lax.Precision.HIGHEST
f32, bf16 = jnp.float32, jnp.bfloat16


def nn(a, b, precision=None):
    return lax.dot_general(a, b, (((1,), (0,)), ((), ())), precision=precision, preferred_element_type=f32)


def nt(a, b, precision=None):
    return lax.dot_general(a, b, (((1,), (1,)), ((), ())), precision=precision, preferred_element_type=f32)


def three(x):
    high = x.astype(bf16)
    rest = x - high.astype(f32)
    middle = rest.astype(bf16)
    return high, middle, (rest - middle.astype(f32)).astype(bf16)


def exact_nn(a, b):
    a1, a2, a3 = three(a)
    b1, b2, b3 = three(b)
    return nn(jnp.concatenate([a3, a2, a1, a2, a1, a1], axis=1), jnp.concatenate([b1, b2, b3, b1, b2, b1], axis=0))


def exact_gram(a):
    size = a.shape[0]
    parts = jnp.concatenate(three(a), axis=0)
    every = nt(parts, parts)

    def part(i, j):
        return every[i * size:(i + 1) * size, j * size:(j + 1) * size]

    small = (part(0, 2) + part(2, 0)) + part(1, 1)
    return part(0, 0) + ((part(0, 1) + part(1, 0)) + small)


def struct(shape, dtype):
    return jax.ShapeDtypeStruct(shape, dtype)


def cost(flops, bytes_accessed):
    return pl.CostEstimate(flops=flops, bytes_accessed=bytes_accessed, transcendentals=0)


def pack_kernel(ids, matrix, *refs):
    outs, sem = refs[:-1], refs[-1]
    width = outs[0].shape[1] // 2
    copies = []
    for k, out in enumerate(outs):
        for j in range(2):
            start = pl.multiple_of(ids[2 * k + j] * width, 128)
            copies.append(pltpu.make_async_copy(
                matrix.at[:, pl.ds(start, width)], out.at[:, pl.ds(j * width, width)], sem.at[2 * k + j]))
    for copy in copies:
        copy.start()
    for copy in copies:
        copy.wait()


def pack(matrix, ids, width, direct):
    rows, count = matrix.shape[0], ids.shape[0] // 2
    return pl.pallas_call(
        pack_kernel,
        in_specs=[pl.BlockSpec(memory_space=pltpu.SMEM), pl.BlockSpec(memory_space=pltpu.HBM)],
        out_specs=[VMEM] * count,
        out_shape=[struct((rows, 2 * width), matrix.dtype)] * count,
        scratch_shapes=[pltpu.SemaphoreType.DMA((2 * count,))],
        compiler_params=pltpu.CompilerParams(vmem_limit_bytes=(60 if direct else 16) * 2**20),
        cost_estimate=cost(0, 8 * rows * count * width),
    )(ids, matrix)


def call(kernel, args, outs, estimate):
    return pl.pallas_call(
        kernel, in_specs=[VMEM] * len(args), out_specs=[VMEM] * len(outs), out_shape=outs,
        compiler_params=BIG, cost_estimate=estimate,
    )(*args)


def scores_kernel(pairs, blocks, counts, picked, joined, with_gram, width, *refs):
    refs = list(refs)
    bases = [[refs.pop(0) for _ in range(count)] for count in counts]
    slots = {k: refs.pop(0) for k in picked}
    gram = refs.pop(0)[...] if with_gram else None
    before, outs = refs[:-2], refs[-2:]
    rank = gram.shape[0] if with_gram else 0
    for odd in range(2):
        left = 0
        if joined:
            left = before[odd].shape[1]
            outs[odd][:, :left] = before[odd][...]
        for pair in pairs:
            value = 0.0
            for block, parts in zip(blocks, bases):
                start = block * width
                for part in parts:
                    stop = min(start + part.shape[1], (block + 1) * width)
                    big = [slots[4 * pair + odd][:, start:stop], slots[4 * pair + 2 + odd][:, start:stop]]
                    value = value + nt(jnp.concatenate(big, axis=0), part[:, :stop - start])
                    start = stop
            value = value.T
            lanes = slice(left, left + value.shape[1])
            left += value.shape[1]
            outs[odd][:, lanes] = value + before[odd][:, lanes] if before and not joined else value
        if with_gram:
            tail = bases[-1][-1]
            first = tail.shape[1] - 3 * rank
            theirs = [tail[:, first + i * rank:first + (i + 1) * rank].astype(f32) for i in range(3)]
            outs[odd][:, left:] = gram + ((theirs[0] + theirs[1]) + theirs[2])


def scores(slots, pairs, blocks, bases, before=(), joined=False, gram=None):
    rank = bases[0][0].shape[0]
    width = slots[pairs[0] * 4].shape[1] // 2
    picked = [4 * pair + k for pair in pairs for k in range(4)]
    rows = slots[picked[0]].shape[0]
    cells = 2 * rows * len(pairs) + (before[0].shape[1] if joined else 0) + (0 if gram is None else rank)
    counts = [len(parts) for parts in bases]
    args = [x for parts in bases for x in parts] + [slots[k] for k in picked]
    args += ([] if gram is None else [gram]) + list(before)
    work = rows * len(picked) * width * len(blocks)
    kernel = functools.partial(scores_kernel, pairs, blocks, counts, picked, joined, gram is not None, width)
    return call(kernel, args, [struct((rank, cells), f32)] * 2, cost(2 * rank * work, 2 * work))


def image_kernel(normalised, *refs):
    values, out = [ref[...] for ref in refs[:-1]], refs[-1]
    cells = out.shape[1]
    size = cells // (GROUP // 2)

    def turned(x, mask):
        return jnp.concatenate([x[:, (j ^ mask) * size:((j ^ mask) + 1) * size] for j in range(GROUP // 2)], axis=1)

    value = (values[0][:, :cells] + turned(values[1], 1)) + (turned(values[2], 2) + turned(values[3], 3))
    if normalised:
        gram = [x[:, cells:] for x in values]
        value = exact_nn(inverse_factor((gram[0] + gram[1]) + (gram[2] + gram[3])), value)
    out[...] = value.astype(bf16)


def image_of(value, mates, rows, normalised):
    rank, cells = value.shape[0], rows * GROUP // 2
    return call(functools.partial(image_kernel, normalised), [value, *mates], [struct((rank, cells), bf16)],
                cost(12 * value.size * rank, 16 * value.size))[0]


def terms_kernel(block, width, *refs):
    slots, images, outs = refs[:GROUP], refs[GROUP:GROUP + 2], refs[GROUP + 2:]
    start = block * width
    for out in outs:
        step = out.shape[1] // 2 if out.shape[1] % 256 == 0 else out.shape[1]
        for left in range(0, out.shape[1], step):
            total = 0.0
            for odd in range(2):
                big = jnp.concatenate([ref[:, start:start + step] for ref in slots[odd::2]], axis=0)
                total = total + nn(images[odd][...], big)
            out[:, left:left + step] = total.astype(out.dtype)
            start += step


def terms(slots, block, images, cuts, dtype):
    rank, width = images[0].shape[0], slots[0].shape[1] // 2
    cells = slots[0].shape[0] * GROUP
    return call(functools.partial(terms_kernel, block, width), [*slots, *images], [struct((rank, w), dtype) for w in cuts],
                cost(2 * rank * cells * width, 2 * cells * width))


def fold_kernel(final, received, own, *refs):
    before, outs = refs[:-2], refs[-2:]
    width = own.shape[1]
    value = own[...] + received[...].astype(f32)
    outs[0][:, :width] = value.astype(outs[0].dtype)
    gram = exact_gram(value)
    for ref in before:
        gram = gram + ref[...]
    outs[1][...] = gram
    if final:
        for i, part in enumerate(three(gram)):
            outs[0][:, width + i * part.shape[1]:width + (i + 1) * part.shape[1]] = part


def fold(received, own, before, dtype, final):
    rank, width = own.shape
    return call(functools.partial(fold_kernel, final), [received, own, *before],
                [struct((rank, width + (3 * rank if final else 0)), dtype), struct((rank, rank), f32)],
                cost(12 * rank * own.size, 12 * own.size))


def inverse_factor(gram):
    size = gram.shape[0]
    row = lax.broadcasted_iota(jnp.int32, (size, size), 0)
    column = lax.broadcasted_iota(jnp.int32, (size, size), 1)
    both = jnp.concatenate([gram, jnp.where(row == column, 1.0, 0.0).astype(f32)], axis=1)
    panels = size // 8
    shape = (8, 2 * size)
    blocks = [both[8 * b:8 * b + 8] for b in range(panels)]
    inner = lax.broadcasted_iota(jnp.int32, shape, 0)
    done = []
    for b in range(panels):
        columns = [
            {k: jnp.broadcast_to(blocks[k][:, 8 * b + t:8 * b + t + 1], shape) for k in range(b, panels)}
            for t in range(8)
        ]
        for t in range(8):
            root = lax.rsqrt(jnp.broadcast_to(columns[t][b][t:t + 1], shape))
            scaled = {k: x * root for k, x in columns[t].items()}
            for s in range(t + 1, 8):
                along = jnp.broadcast_to(scaled[b][s:s + 1], shape)
                for k in range(b, panels):
                    columns[s][k] = columns[s][k] - scaled[k] * along
            pivot = jnp.broadcast_to(blocks[b][t:t + 1], shape) * root
            done.append(pivot[:1])
            for k in range(b, panels):
                factor = jnp.where(inner > t, scaled[k], 0.0) if k == b else scaled[k]
                blocks[k] = blocks[k] - factor * pivot
    return jnp.concatenate(done, axis=0)[:, size:]


def output_kernel(scale, gram, loading, out):
    out[...] = exact_nn(inverse_factor(gram[...]), loading[...]) * scale


def output_call(gram, loading):
    return pl.pallas_call(
        functools.partial(output_kernel, math.sqrt(GENES)),
        in_specs=[VMEM, VMEM], out_specs=VMEM, out_shape=struct(loading.shape, f32),
        compiler_params=pltpu.CompilerParams(vmem_limit_bytes=16 * 2**20),
    )(gram, loading)


def mate(value, cells, mask):
    return lax.ppermute(value, "cell", [(i, i ^ mask) for i in range(cells)])


def total_over_cells(value, cells):
    for one, two in ((GROUP, 1), (2, 4)):
        value = (value + mate(value, cells, one)) + (mate(value, cells, one | two) + mate(value, cells, two))
    return value


def square_program(cells, expression, start_basis):
    width, rows = start_basis.shape[0], expression.shape[0]
    index = lax.axis_index("cell").astype(jnp.int32)
    slots = [None] * GROUP
    for masks, direct in (((2, 4), True), ((1, 6, 3, 5, 7, 0), False)):
        members = index ^ jnp.array(masks, jnp.int32)
        ids = jnp.stack([members, members ^ GROUP], axis=1).reshape(-1)
        for k, packed in zip(masks, pack(expression, ids, width, direct)):
            slots[k] = mate(packed, cells, k) if k else packed

    def image_from(totals, normalised):
        even, odd = totals
        even = even + mate(odd, cells, 1)
        image = image_of(even, [mate(even, cells, mask) for mask in (2, 4, 6)], rows, normalised)
        return image, mate(image, cells, 1)

    def terms_and_received(images, cuts):
        sent = terms(slots, 1, images, cuts, bf16)
        own = terms(slots, 0, images, cuts, f32)
        return zip([mate(x, cells, GROUP) for x in sent], own)

    half = -(-6 * width // 1280) * 128
    basis = start_basis.T
    bases = [[basis], [mate(basis, cells, GROUP)]]
    images = image_from(scores(slots, (1,), (0, 1), bases, scores(slots, (0,), (0, 1), bases), True), False)
    for _ in range(1, ITERS):
        parts, copies, gram = [], [], []
        for received, own in terms_and_received(images, (half, width - half)):
            part, total = fold(received, own, gram, bf16, bool(parts))
            gram = [total]
            parts.append(part)
            copies.append(mate(part, cells, GROUP))
        early = scores(slots, (0, 1), (0,), [parts])
        images = image_from(scores(slots, (0, 1), (1,), [copies], early, gram=gram[0]), True)
    ((received, own),) = terms_and_received(images, (width,))
    loading, gram = fold(received, own, [], f32, False)
    return output_call(total_over_cells(gram, cells), loading).T


def plain_program(expression, start_basis):
    basis = start_basis
    for _ in range(ITERS):
        whole = lax.all_gather(basis, "cell", axis=0, tiled=True)
        partial = jnp.dot(expression, whole, preferred_element_type=f32)
        image = lax.psum(partial, "gene").astype(bf16)
        partial = lax.dot_general(expression, image, (((0,), (0,)), ((), ())), preferred_element_type=f32)
        loading = lax.psum_scatter(partial, "cell", scatter_dimension=0, tiled=True)
        gram = lax.dot_general(loading, loading, (((0,), (0,)), ((), ())), precision=HIGHEST, preferred_element_type=f32)
        lower = jnp.linalg.cholesky(lax.psum(gram, ("cell", "gene")))
        ortho = jax.scipy.linalg.solve_triangular(lower, loading.T, lower=True).T
        basis = ortho.astype(bf16)
    return ortho * math.sqrt(GENES)


def solution(mesh):
    cells, genes = mesh.shape["cell"], mesh.shape["gene"]

    def on_device(expression, start_basis):
        width, rank = start_basis.shape
        fits = genes == 1 and cells == 2 * GROUP and width % 128 == 0 and rank == 64
        if fits and expression.shape[0] % 16 == 0:
            return square_program(cells, expression, start_basis)
        return plain_program(expression, start_basis)

    return jax.shard_map(
        on_device,
        mesh=mesh,
        in_specs=(P(("groups", "cell"), "gene"), P(("groups", "gene", "cell"), None)),
        out_specs=P(("groups", "gene", "cell"), None),
        check_vma=False,
    )
```

time: 147 us -> 145 us (0.986)
  starting transfers between devices: 34.6 us -> 30.2 us
  waiting for transfers between devices: 91.9 us -> 95.3 us
    pallas_call x3 -> x0, Pallas kernels: 4.52 us -> none  [the longest x1 3.24 us: factor_call(): pl.pallas_call(factor_kernel, in_specs=[VMEM], out_specs=VMEM, out_shape=...]
    ppermute x33 -> x29, starting transfers between devices: 34.6 us -> 30.2 us  [mate(): return lax.ppermute(value, 'cell', [(i, i ^ mask) for i in range(cells)])]
    ppermute x33 -> x29, waiting for transfers between devices: 91.9 us -> 95.3 us  [mate(): return lax.ppermute(value, 'cell', [(i, i ^ mask) for i in range(cells)])]
    pallas_call x1 -> x2, Pallas kernels: 1.52 us -> 4.34 us  [pack(): pl.pallas_call(pack_kernel, in_specs=[pl.BlockSpec(memory_space=pltpu.SME...]
    pallas_call x10 -> x13, Pallas kernels: 5.71 us -> 8.31 us  [call(): pl.pallas_call(kernel, in_specs=[VMEM] * len(args), out_specs=[VMEM] * le...]
    unnamed x10 -> x8, local copies, waits for them, and re-layouts: 3.91 us -> 2.13 us
  transfers between devices with their start and end apart: 33 -> 29, of which waited for: 21 -> 22; matrix products, arithmetic and copies ran while one was open for 0% -> 0% of each run, Pallas kernels for 4% -> 3%
where the time goes in v5:
time: 145 us
  waiting for transfers between devices  95.3 us (66%)
  starting transfers between devices  30.2 us (21%)
  Pallas kernels  15.6 us (11%)
  local copies, waits for them, and re-layouts  2.98 us (2%)
    ppermute x29, waiting for transfers between devices, mate(): return lax.ppermute(value, 'cell', [(i, i ^ mask) for i in range(cells)])  95.3 us
    ppermute x29, starting transfers between devices, mate(): return lax.ppermute(value, 'cell', [(i, i ^ mask) for i in range(cells)])  30.2 us
    pallas_call x13, Pallas kernels, call(): pl.pallas_call(kernel, in_specs=[VMEM] * len(args), out_specs=[VMEM] * le...  8.31 us
    pallas_call x2, Pallas kernels, pack(): pl.pallas_call(pack_kernel, in_specs=[pl.BlockSpec(memory_space=pltpu.SME...  4.34 us
    pallas_call x1, Pallas kernels, output_call(): pl.pallas_call(functools.partial(output_kernel, math.sqrt(GENES)), in_spe...  2.98 us
  transfers between devices with their start and end apart: 29, of which 22 were waited for; matrix products, arithmetic and copies ran while one was open for 0% of the time, Pallas kernels for 3%

profile of v5, /device:TPU:0, one launch (start us, length us, event | category | flops | bytes accessed | tf_op | source)
XLA Modules:
  0.0 145.0 jit_solution(10775821190521206186)
XLA Ops:
  1.4 3.1 %shard_map.47 = (bf16[64,3840]{1,0:T(8,128)(2,1)}, bf16[64,3840]{1,0:T(8,128)(2,1)}) custom-call(s32[4]{0:T(128)} %reshape.7.ids, bf16[64,30720]{1,0:T(8,128)(2,1)} %matrix.3), custom_call_target="tpu_custom_call" | custom-call | bytes 1966080 | tf_op jit(solution)/shard_map/pallas_call | solution.py:78
  4.5 3.0 %collective-permute-start.1 = (bf16[64,3840]{1,0:T(8,128)(2,1)}, bf16[64,3840]{1,0:T(8,128)(2,1)S(1)}, u32[]{:S(2)}, u32[]{:S(2)}) collective-permute-start(bf16[64,3840]{1,0:T(8,128)(2,1)} %get-tuple-element.33), channel_id=1, source_target_pairs={{0,2},{1,3},{2,0},{3,1},{4,6},{5,7},{6,4},{7,5},{8,10},{9,11},{10,... | collective-permute-start | bytes 1474568 | tf_op jit(solution)/shard_map/ppermute | solution.py:248
  7.7 2.1 %copy-done = bf16[64,30720]{1,0:T(8,128)(2,1)S(1)} copy-done((bf16[64,30720]{1,0:T(8,128)(2,1)S(1)}, bf16[64,30720]{1,0:T(8,128)(2,1)}, u32[]{:S(2)}) %copy-start) | copy-done | bytes 3932184
  9.8 1.3 shard_map.46
  11.2 2.7 %collective-permute-start.7 = (bf16[64,1920]{1,0:T(8,128)(2,1)S(1)}, bf16[64,1920]{1,0:T(8,128)(2,1)S(1)}, u32[]{:S(2)}, u32[]{:S(2)}) collective-permute-start(bf16[64,1920]{1,0:T(8,128)(2,1)S(1)} %bitcast.10), channel_id=1, source_target_pairs={{0,8},{1,9},{2,10},{3,11},{4,12},{5,13},{6,14},{7,15},{8,0},{9,1},... | collective-permute-start | bytes 737288 | tf_op jit(solution)/shard_map/ppermute | solution.py:248
  14.1 1.6 %collective-permute-start.3 = (bf16[64,3840]{1,0:T(8,128)(2,1)S(1)}, bf16[64,3840]{1,0:T(8,128)(2,1)S(1)}, u32[]{:S(2)}, u32[]{:S(2)}) collective-permute-start(bf16[64,3840]{1,0:T(8,128)(2,1)S(1)} %copy-done.3), channel_id=1, source_target_pairs={{0,4},{1,5},{2,6},{3,7},{4,0},{5,1},{6,2},{7,3},{8,12},{9,13},{10,... | collective-permute-start | bytes 1474568 | tf_op jit(solution)/shard_map/ppermute | solution.py:248
  15.7 10.1 %collective-permute-done.7.refs_1_ = bf16[64,1920]{1,0:T(8,128)(2,1)S(1)} collective-permute-done((bf16[64,1920]{1,0:T(8,128)(2,1)S(1)}, bf16[64,1920]{1,0:T(8,128)(2,1)S(1)}, u32[]{:S(2)}, u32[]{:S(2)}) %collective-permute-start.7) | collective-permute-done | bytes 245792 | tf_op jit(solution)/shard_map/ppermute | solution.py:248
  27.1 1.7 %collective-permute-start.6 = (bf16[64,3840]{1,0:T(8,128)(2,1)S(1)}, bf16[64,3840]{1,0:T(8,128)(2,1)S(1)}, u32[]{:S(2)}, u32[]{:S(2)}) collective-permute-start(bf16[64,3840]{1,0:T(8,128)(2,1)S(1)} %get-tuple-element.38), channel_id=1, source_target_pairs={{0,7},{1,6},{2,5},{3,4},{4,3},{5,2},{6,1},{7,0},{8,15},{9,14},{10,... | collective-permute-start | bytes 1474568 | tf_op jit(solution)/shard_map/ppermute | solution.py:248
  29.5 2.8 %collective-permute-done.3.refs_2_.refs_4_.refs_6_ = bf16[64,3840]{1,0:T(8,128)(2,1)S(1)} collective-permute-done((bf16[64,3840]{1,0:T(8,128)(2,1)S(1)}, bf16[64,3840]{1,0:T(8,128)(2,1)S(1)}, u32[]{:S(2)}, u32[]{:S(2)}) %collective-permute-start.3) | collective-permute-done | bytes 491552 | tf_op jit(solution)/shard_map/ppermute | solution.py:248
  32.3 9.4 %collective-permute-done.4.refs_3_.refs_5_.refs_7_ = bf16[64,3840]{1,0:T(8,128)(2,1)S(1)} collective-permute-done((bf16[64,3840]{1,0:T(8,128)(2,1)S(1)}, bf16[64,3840]{1,0:T(8,128)(2,1)S(1)}, u32[]{:S(2)}, u32[]{:S(2)}) %collective-permute-start.4) | collective-permute-done | bytes 491552 | tf_op jit(solution)/shard_map/ppermute | solution.py:248
  41.7 12.5 %collective-permute-done.5.refs_4_.refs_6_.refs_8_ = bf16[64,3840]{1,0:T(8,128)(2,1)S(1)} collective-permute-done((bf16[64,3840]{1,0:T(8,128)(2,1)S(1)}, bf16[64,3840]{1,0:T(8,128)(2,1)S(1)}, u32[]{:S(2)}, u32[]{:S(2)}) %collective-permute-start.5) | collective-permute-done | bytes 491552 | tf_op jit(solution)/shard_map/ppermute | solution.py:248
  54.2 9.4 %collective-permute-done.6.refs_5_.refs_7_.refs_9_ = bf16[64,3840]{1,0:T(8,128)(2,1)S(1)} collective-permute-done((bf16[64,3840]{1,0:T(8,128)(2,1)S(1)}, bf16[64,3840]{1,0:T(8,128)(2,1)S(1)}, u32[]{:S(2)}, u32[]{:S(2)}) %collective-permute-start.6) | collective-permute-done | bytes 491552 | tf_op jit(solution)/shard_map/ppermute | solution.py:248
  67.8 1.5 %collective-permute-start.9 = (f32[64,256]{1,0:T(8,128)S(1)}, f32[64,256]{1,0:T(8,128)S(1)}, u32[]{:S(2)}, u32[]{:S(2)}) collective-permute-start(f32[64,256]{1,0:T(8,128)S(1)} %add.24.refs_0_), channel_id=1, source_target_pairs={{0,2},{1,3},{2,0},{3,1},{4,6},{5,7},{6,4},{7,5},{8,10},{9,11},{10,... | collective-permute-start | bytes 196616 | tf_op jit(solution)/shard_map/ppermute | solution.py:248
  69.3 2.3 %collective-permute-done.11.refs_3_ = f32[64,256]{1,0:T(8,128)S(1)} collective-permute-done((f32[64,256]{1,0:T(8,128)S(1)}, f32[64,256]{1,0:T(8,128)S(1)}, u32[]{:S(2)}, u32[]{:S(2)}) %collective-permute-start.11) | collective-permute-done | bytes 65568 | tf_op jit(solution)/shard_map/ppermute | solution.py:248
  72.6 1.2 collective-permute-done.12.refs_9_
  75.1 2.2 %collective-permute-start.15 = (bf16[64,768]{1,0:T(8,128)(2,1)S(1)}, bf16[64,768]{1,0:T(8,128)(2,1)S(1)}, u32[]{:S(2)}, u32[]{:S(2)}) collective-permute-start(bf16[64,768]{1,0:T(8,128)(2,1)S(1)} %get-tuple-element.46), channel_id=1, source_target_pairs={{0,8},{1,9},{2,10},{3,11},{4,12},{5,13},{6,14},{7,15},{8,0},{9,1},... | collective-permute-start | bytes 294920 | tf_op jit(solution)/shard_map/ppermute | solution.py:248
  77.7 8.9 %collective-permute-done.13.received = bf16[64,1152]{1,0:T(8,128)(2,1)S(1)} collective-permute-done((bf16[64,1152]{1,0:T(8,128)(2,1)S(1)}, bf16[64,1152]{1,0:T(8,128)(2,1)S(1)}, u32[]{:S(2)}, u32[]{:S(2)}) %collective-permute-start.13) | collective-permute-done | bytes 147488 | tf_op jit(solution)/shard_map/ppermute | solution.py:248
  87.2 1.3 collective-permute-done.15.received
  89.0 1.6 %collective-permute-start.16 = (bf16[64,960]{1,0:T(8,128)(2,1)S(1)}, bf16[64,960]{1,0:T(8,128)(2,1)S(1)}, u32[]{:S(2)}, u32[]{:S(2)}) collective-permute-start(bf16[64,960]{1,0:T(8,128)(2,1)S(1)} %get-tuple-element.49.refs_1_), channel_id=1, source_target_pairs={{0,8},{1,9},{2,10},{3,11},{4,12},{5,13},{6,14},{7,15},{8,0},{9,1},... | collective-permute-start | bytes 368648 | tf_op jit(solution)/shard_map/ppermute | solution.py:248
  91.4 10.0 %collective-permute-done.16.refs_1_ = bf16[64,960]{1,0:T(8,128)(2,1)S(1)} collective-permute-done((bf16[64,960]{1,0:T(8,128)(2,1)S(1)}, bf16[64,960]{1,0:T(8,128)(2,1)S(1)}, u32[]{:S(2)}, u32[]{:S(2)}) %collective-permute-start.16) | collective-permute-done | bytes 122912 | tf_op jit(solution)/shard_map/ppermute | solution.py:248
  102.3 1.3 collective-permute-done.17
  103.6 2.8 %collective-permute-start.19 = (f32[64,320]{1,0:T(8,128)S(1)}, f32[64,320]{1,0:T(8,128)S(1)}, u32[]{:S(2)}, u32[]{:S(2)}) collective-permute-start(f32[64,320]{1,0:T(8,128)S(1)} %add.25.refs_0_), channel_id=1, source_target_pairs={{0,4},{1,5},{2,6},{3,7},{4,0},{5,1},{6,2},{7,3},{8,12},{9,13},{10,... | collective-permute-start | bytes 245768 | tf_op jit(solution)/shard_map/ppermute | solution.py:248
  107.1 3.0 %collective-permute-done.20.refs_3_ = f32[64,320]{1,0:T(8,128)S(1)} collective-permute-done((f32[64,320]{1,0:T(8,128)S(1)}, f32[64,320]{1,0:T(8,128)S(1)}, u32[]{:S(2)}, u32[]{:S(2)}) %collective-permute-start.20) | collective-permute-done | bytes 81952 | tf_op jit(solution)/shard_map/ppermute | solution.py:248
  110.2 1.2 collective-permute-done.19.refs_2_
  111.5 2.0 %shard_map.57.refs_8_ = bf16[64,256]{1,0:T(8,128)(2,1)S(1)} custom-call(f32[64,320]{1,0:T(8,128)S(1)} %add.25.refs_0_, f32[64,320]{1,0:T(8,128)S(1)} %collective-permute-done.18.refs_1_, f32[64,320]{1,0:T(8,128)S(1)} %collective-permute-done.19.refs_2_, f32[64,320]{1,0:T(8,128)S(1)} %collective-permute-done.20.refs_3_), custom_call_target="tpu_custom_call" | custom-call | flops 15728640 | bytes 327680 | tf_op jit(solution)/shard_map/pallas_call | solution.py:90
  113.5 1.2 collective-permute-done.21.refs_9_
  116.2 12.9 %collective-permute-done.22.received = bf16[64,1920]{1,0:T(8,128)(2,1)S(1)} collective-permute-done((bf16[64,1920]{1,0:T(8,128)(2,1)S(1)}, bf16[64,1920]{1,0:T(8,128)(2,1)S(1)}, u32[]{:S(2)}, u32[]{:S(2)}) %collective-permute-start.22) | collective-permute-done | bytes 245792 | tf_op jit(solution)/shard_map/ppermute | solution.py:248
  129.8 3.0 %collective-permute-start.23 = (f32[64,64]{1,0:T(8,128)S(1)}, f32[64,64]{1,0:T(8,128)S(1)}, u32[]{:S(2)}, u32[]{:S(2)}) collective-permute-start(f32[64,64]{1,0:T(8,128)S(1)} %get-tuple-element.55), channel_id=1, source_target_pairs={{0,8},{1,9},{2,10},{3,11},{4,12},{5,13},{6,14},{7,15},{8,0},{9,1},... | collective-permute-start | bytes 49160 | tf_op jit(solution)/shard_map/ppermute | solution.py:248
  132.7 1.3 collective-permute-done.24
  135.1 2.0 %collective-permute-start.28 = (f32[64,64]{1,0:T(8,128)S(1)}, f32[64,64]{1,0:T(8,128)S(1)}, u32[]{:S(2)}, u32[]{:S(2)}) collective-permute-start(f32[64,64]{1,0:T(8,128)S(1)} %add_add_fusion.1), channel_id=1, source_target_pairs={{0,4},{1,5},{2,6},{3,7},{4,0},{5,1},{6,2},{7,3},{8,12},{9,13},{10,... | collective-permute-start | bytes 49160 | tf_op jit(solution)/shard_map/ppermute | solution.py:248
  139.2 2.7 %collective-permute-done.27 = f32[64,64]{1,0:T(8,128)S(1)} collective-permute-done((f32[64,64]{1,0:T(8,128)S(1)}, f32[64,64]{1,0:T(8,128)S(1)}, u32[]{:S(2)}, u32[]{:S(2)}) %collective-permute-start.27) | collective-permute-done | bytes 16416 | tf_op jit(solution)/shard_map/ppermute | solution.py:248
  142.0 3.0 %shard_map.61 = f32[64,1920]{1,0:T(8,128)} custom-call(f32[64,64]{1,0:T(8,128)S(1)} %add_add_fusion.gram, f32[64,1920]{1,0:T(8,128)S(1)} %get-tuple-element.56.loading), custom_call_target="tpu_custom_call" | custom-call | tf_op jit(solution)/shard_map/pallas_call | solution.py:240
  (62 shorter events, 19.7 us)
Async XLA Ops:
  0.0 7.5 %copy-start.2 = (s32[6]{0:T(128)S(1)}, s32[6]{0:T(128)}, u32[]{:S(2)}) copy-start(s32[6]{0:T(128)} %constant.12.clone) | copy-start | bytes 76
  1.4 9.8 %copy-start.1 = (bf16[1920,64]{0,1:T(8,128)(2,1)S(1)}, bf16[1920,64]{0,1:T(8,128)(2,1)}, u32[]{:S(2)}) copy-start(bf16[1920,64]{0,1:T(8,128)(2,1)} %param.5) | copy-start | bytes 737284
  4.5 21.6 %collective-permute-start.1 = (bf16[64,3840]{1,0:T(8,128)(2,1)}, bf16[64,3840]{1,0:T(8,128)(2,1)S(1)}, u32[]{:S(2)}, u32[]{:S(2)}) collective-permute-start(bf16[64,3840]{1,0:T(8,128)(2,1)} %get-tuple-element.33), channel_id=1, source_target_pairs={{0,2},{1,3},{2,0},{3,1},{4,6},{5,7},{6,4},{7,5},{8,10},{9,11},{10,... | collective-permute-start | bytes 1474568 | tf_op jit(solution)/shard_map/ppermute | solution.py:248
  9.8 4.3 %copy-start.3 = (bf16[64,3840]{1,0:T(8,128)(2,1)S(1)}, bf16[64,3840]{1,0:T(8,128)(2,1)}, u32[]{:S(2)}) copy-start(bf16[64,3840]{1,0:T(8,128)(2,1)} %get-tuple-element.35) | copy-start | bytes 1474564
  11.1 16.0 %collective-permute-start = (bf16[64,3840]{1,0:T(8,128)(2,1)S(1)}, bf16[64,3840]{1,0:T(8,128)(2,1)S(1)}, u32[]{:S(2)}, u32[]{:S(2)}) collective-permute-start(bf16[64,3840]{1,0:T(8,128)(2,1)S(1)} %get-tuple-element.32), channel_id=1, source_target_pairs={{0,1},{1,0},{2,3},{3,2},{4,5},{5,4},{6,7},{7,6},{8,9},{9,8},{10,11... | collective-permute-start | bytes 1474568 | tf_op jit(solution)/shard_map/ppermute | solution.py:248
  11.2 14.6 %collective-permute-start.7 = (bf16[64,1920]{1,0:T(8,128)(2,1)S(1)}, bf16[64,1920]{1,0:T(8,128)(2,1)S(1)}, u32[]{:S(2)}, u32[]{:S(2)}) collective-permute-start(bf16[64,1920]{1,0:T(8,128)(2,1)S(1)} %bitcast.10), channel_id=1, source_target_pairs={{0,8},{1,9},{2,10},{3,11},{4,12},{5,13},{6,14},{7,15},{8,0},{9,1},... | collective-permute-start | bytes 737288 | tf_op jit(solution)/shard_map/ppermute | solution.py:248
  13.8 15.0 %collective-permute-start.2 = (bf16[64,3840]{1,0:T(8,128)(2,1)S(1)}, bf16[64,3840]{1,0:T(8,128)(2,1)S(1)}, u32[]{:S(2)}, u32[]{:S(2)}) collective-permute-start(bf16[64,3840]{1,0:T(8,128)(2,1)S(1)} %get-tuple-element.34), channel_id=1, source_target_pairs={{0,3},{1,2},{2,1},{3,0},{4,7},{5,6},{6,5},{7,4},{8,11},{9,10},{10,... | collective-permute-start | bytes 1474568 | tf_op jit(solution)/shard_map/ppermute | solution.py:248
  14.1 18.2 %collective-permute-start.3 = (bf16[64,3840]{1,0:T(8,128)(2,1)S(1)}, bf16[64,3840]{1,0:T(8,128)(2,1)S(1)}, u32[]{:S(2)}, u32[]{:S(2)}) collective-permute-start(bf16[64,3840]{1,0:T(8,128)(2,1)S(1)} %copy-done.3), channel_id=1, source_target_pairs={{0,4},{1,5},{2,6},{3,7},{4,0},{5,1},{6,2},{7,3},{8,12},{9,13},{10,... | collective-permute-start | bytes 1474568 | tf_op jit(solution)/shard_map/ppermute | solution.py:248
  25.8 15.9 %collective-permute-start.4 = (bf16[64,3840]{1,0:T(8,128)(2,1)S(1)}, bf16[64,3840]{1,0:T(8,128)(2,1)S(1)}, u32[]{:S(2)}, u32[]{:S(2)}) collective-permute-start(bf16[64,3840]{1,0:T(8,128)(2,1)S(1)} %get-tuple-element.36), channel_id=1, source_target_pairs={{0,5},{1,4},{2,7},{3,6},{4,1},{5,0},{6,3},{7,2},{8,13},{9,12},{10,... | collective-permute-start | bytes 1474568 | tf_op jit(solution)/shard_map/ppermute | solution.py:248
  26.1 28.2 %collective-permute-start.5 = (bf16[64,3840]{1,0:T(8,128)(2,1)S(1)}, bf16[64,3840]{1,0:T(8,128)(2,1)S(1)}, u32[]{:S(2)}, u32[]{:S(2)}) collective-permute-start(bf16[64,3840]{1,0:T(8,128)(2,1)S(1)} %get-tuple-element.37), channel_id=1, source_target_pairs={{0,6},{1,7},{2,4},{3,5},{4,2},{5,3},{6,0},{7,1},{8,14},{9,15},{10,... | collective-permute-start | bytes 1474568 | tf_op jit(solution)/shard_map/ppermute | solution.py:248
  27.1 36.5 %collective-permute-start.6 = (bf16[64,3840]{1,0:T(8,128)(2,1)S(1)}, bf16[64,3840]{1,0:T(8,128)(2,1)S(1)}, u32[]{:S(2)}, u32[]{:S(2)}) collective-permute-start(bf16[64,3840]{1,0:T(8,128)(2,1)S(1)} %get-tuple-element.38), channel_id=1, source_target_pairs={{0,7},{1,6},{2,5},{3,4},{4,3},{5,2},{6,1},{7,0},{8,15},{9,14},{10,... | collective-permute-start | bytes 1474568 | tf_op jit(solution)/shard_map/ppermute | solution.py:248
  64.4 1.4 collective-permute-start.8
  65.7 5.9 %collective-permute-start.11 = (f32[64,256]{1,0:T(8,128)S(1)}, f32[64,256]{1,0:T(8,128)S(1)}, u32[]{:S(2)}, u32[]{:S(2)}) collective-permute-start(f32[64,256]{1,0:T(8,128)S(1)} %add.24.refs_0_), channel_id=1, source_target_pairs={{0,6},{1,7},{2,4},{3,5},{4,2},{5,3},{6,0},{7,1},{8,14},{9,15},{10,... | collective-permute-start | bytes 196616 | tf_op jit(solution)/shard_map/ppermute | solution.py:248
  66.8 4.8 %collective-permute-start.10 = (f32[64,256]{1,0:T(8,128)S(1)}, f32[64,256]{1,0:T(8,128)S(1)}, u32[]{:S(2)}, u32[]{:S(2)}) collective-permute-start(f32[64,256]{1,0:T(8,128)S(1)} %add.24.refs_0_), channel_id=1, source_target_pairs={{0,4},{1,5},{2,6},{3,7},{4,0},{5,1},{6,2},{7,3},{8,12},{9,13},{10,... | collective-permute-start | bytes 196616 | tf_op jit(solution)/shard_map/ppermute | solution.py:248
  67.8 4.6 %collective-permute-start.9 = (f32[64,256]{1,0:T(8,128)S(1)}, f32[64,256]{1,0:T(8,128)S(1)}, u32[]{:S(2)}, u32[]{:S(2)}) collective-permute-start(f32[64,256]{1,0:T(8,128)S(1)} %add.24.refs_0_), channel_id=1, source_target_pairs={{0,2},{1,3},{2,0},{3,1},{4,6},{5,7},{6,4},{7,5},{8,10},{9,11},{10,... | collective-permute-start | bytes 196616 | tf_op jit(solution)/shard_map/ppermute | solution.py:248
  72.5 1.3 collective-permute-start.12
  74.3 12.4 %collective-permute-start.13 = (bf16[64,1152]{1,0:T(8,128)(2,1)S(1)}, bf16[64,1152]{1,0:T(8,128)(2,1)S(1)}, u32[]{:S(2)}, u32[]{:S(2)}) collective-permute-start(bf16[64,1152]{1,0:T(8,128)(2,1)S(1)} %get-tuple-element.43), channel_id=1, source_target_pairs={{0,8},{1,9},{2,10},{3,11},{4,12},{5,13},{6,14},{7,15},{8,0},{9,1},... | collective-permute-start | bytes 442376 | tf_op jit(solution)/shard_map/ppermute | solution.py:248
  75.1 13.5 %collective-permute-start.15 = (bf16[64,768]{1,0:T(8,128)(2,1)S(1)}, bf16[64,768]{1,0:T(8,128)(2,1)S(1)}, u32[]{:S(2)}, u32[]{:S(2)}) collective-permute-start(bf16[64,768]{1,0:T(8,128)(2,1)S(1)} %get-tuple-element.46), channel_id=1, source_target_pairs={{0,8},{1,9},{2,10},{3,11},{4,12},{5,13},{6,14},{7,15},{8,0},{9,1},... | collective-permute-start | bytes 294920 | tf_op jit(solution)/shard_map/ppermute | solution.py:248
  87.1 14.3 %collective-permute-start.14 = (bf16[64,1152]{1,0:T(8,128)(2,1)S(1)}, bf16[64,1152]{1,0:T(8,128)(2,1)S(1)}, u32[]{:S(2)}, u32[]{:S(2)}) collective-permute-start(bf16[64,1152]{1,0:T(8,128)(2,1)S(1)} %get-tuple-element.45.refs_0_), channel_id=1, source_target_pairs={{0,8},{1,9},{2,10},{3,11},{4,12},{5,13},{6,14},{7,15},{8,0},{9,1},... | collective-permute-start | bytes 442376 | tf_op jit(solution)/shard_map/ppermute | solution.py:248
  89.0 12.4 %collective-permute-start.16 = (bf16[64,960]{1,0:T(8,128)(2,1)S(1)}, bf16[64,960]{1,0:T(8,128)(2,1)S(1)}, u32[]{:S(2)}, u32[]{:S(2)}) collective-permute-start(bf16[64,960]{1,0:T(8,128)(2,1)S(1)} %get-tuple-element.49.refs_1_), channel_id=1, source_target_pairs={{0,8},{1,9},{2,10},{3,11},{4,12},{5,13},{6,14},{7,15},{8,0},{9,1},... | collective-permute-start | bytes 368648 | tf_op jit(solution)/shard_map/ppermute | solution.py:248
  102.2 1.4 collective-permute-start.17
  103.6 6.6 %collective-permute-start.20 = (f32[64,320]{1,0:T(8,128)S(1)}, f32[64,320]{1,0:T(8,128)S(1)}, u32[]{:S(2)}, u32[]{:S(2)}) collective-permute-start(f32[64,320]{1,0:T(8,128)S(1)} %add.25.refs_0_), channel_id=1, source_target_pairs={{0,6},{1,7},{2,4},{3,5},{4,2},{5,3},{6,0},{7,1},{8,14},{9,15},{10,... | collective-permute-start | bytes 245768 | tf_op jit(solution)/shard_map/ppermute | solution.py:248
  103.6 7.8 %collective-permute-start.19 = (f32[64,320]{1,0:T(8,128)S(1)}, f32[64,320]{1,0:T(8,128)S(1)}, u32[]{:S(2)}, u32[]{:S(2)}) collective-permute-start(f32[64,320]{1,0:T(8,128)S(1)} %add.25.refs_0_), channel_id=1, source_target_pairs={{0,4},{1,5},{2,6},{3,7},{4,0},{5,1},{6,2},{7,3},{8,12},{9,13},{10,... | collective-permute-start | bytes 245768 | tf_op jit(solution)/shard_map/ppermute | solution.py:248
  106.5 5.0 %collective-permute-start.18 = (f32[64,320]{1,0:T(8,128)S(1)}, f32[64,320]{1,0:T(8,128)S(1)}, u32[]{:S(2)}, u32[]{:S(2)}) collective-permute-start(f32[64,320]{1,0:T(8,128)S(1)} %add.25.refs_0_), channel_id=1, source_target_pairs={{0,2},{1,3},{2,0},{3,1},{4,6},{5,7},{6,4},{7,5},{8,10},{9,11},{10,... | collective-permute-start | bytes 245768 | tf_op jit(solution)/shard_map/ppermute | solution.py:248
  113.5 1.2 collective-permute-start.21
  115.2 13.9 %collective-permute-start.22 = (bf16[64,1920]{1,0:T(8,128)(2,1)S(1)}, bf16[64,1920]{1,0:T(8,128)(2,1)S(1)}, u32[]{:S(2)}, u32[]{:S(2)}) collective-permute-start(bf16[64,1920]{1,0:T(8,128)(2,1)S(1)} %shard_map.58), channel_id=1, source_target_pairs={{0,8},{1,9},{2,10},{3,11},{4,12},{5,13},{6,14},{7,15},{8,0},{9,1},... | collective-permute-start | bytes 737288 | tf_op jit(solution)/shard_map/ppermute | solution.py:248
  129.6 3.1 %collective-permute-start.25 = (f32[64,64]{1,0:T(8,128)S(1)}, f32[64,64]{1,0:T(8,128)S(1)}, u32[]{:S(2)}, u32[]{:S(2)}) collective-permute-start(f32[64,64]{1,0:T(8,128)S(1)} %get-tuple-element.55), channel_id=1, source_target_pairs={{0,1},{1,0},{2,3},{3,2},{4,5},{5,4},{6,7},{7,6},{8,9},{9,8},{10,11... | collective-permute-start | bytes 49160 | tf_op jit(solution)/shard_map/ppermute | solution.py:248
  129.7 4.3 %collective-permute-start.24 = (f32[64,64]{1,0:T(8,128)S(1)}, f32[64,64]{1,0:T(8,128)S(1)}, u32[]{:S(2)}, u32[]{:S(2)}) collective-permute-start(f32[64,64]{1,0:T(8,128)S(1)} %get-tuple-element.55), channel_id=1, source_target_pairs={{0,9},{1,8},{2,11},{3,10},{4,13},{5,12},{6,15},{7,14},{8,1},{9,0},... | collective-permute-start | bytes 49160 | tf_op jit(solution)/shard_map/ppermute | solution.py:248
  129.8 5.3 %collective-permute-start.23 = (f32[64,64]{1,0:T(8,128)S(1)}, f32[64,64]{1,0:T(8,128)S(1)}, u32[]{:S(2)}, u32[]{:S(2)}) collective-permute-start(f32[64,64]{1,0:T(8,128)S(1)} %get-tuple-element.55), channel_id=1, source_target_pairs={{0,8},{1,9},{2,10},{3,11},{4,12},{5,13},{6,14},{7,15},{8,0},{9,1},... | collective-permute-start | bytes 49160 | tf_op jit(solution)/shard_map/ppermute | solution.py:248
  135.1 4.2 %collective-permute-start.28 = (f32[64,64]{1,0:T(8,128)S(1)}, f32[64,64]{1,0:T(8,128)S(1)}, u32[]{:S(2)}, u32[]{:S(2)}) collective-permute-start(f32[64,64]{1,0:T(8,128)S(1)} %add_add_fusion.1), channel_id=1, source_target_pairs={{0,4},{1,5},{2,6},{3,7},{4,0},{5,1},{6,2},{7,3},{8,12},{9,13},{10,... | collective-permute-start | bytes 49160 | tf_op jit(solution)/shard_map/ppermute | solution.py:248
  137.0 4.9 %collective-permute-start.27 = (f32[64,64]{1,0:T(8,128)S(1)}, f32[64,64]{1,0:T(8,128)S(1)}, u32[]{:S(2)}, u32[]{:S(2)}) collective-permute-start(f32[64,64]{1,0:T(8,128)S(1)} %add_add_fusion.1), channel_id=1, source_target_pairs={{0,6},{1,7},{2,4},{3,5},{4,2},{5,3},{6,0},{7,1},{8,14},{9,15},{10,... | collective-permute-start | bytes 49160 | tf_op jit(solution)/shard_map/ppermute | solution.py:248
  137.7 4.3 %collective-permute-start.26 = (f32[64,64]{1,0:T(8,128)S(1)}, f32[64,64]{1,0:T(8,128)S(1)}, u32[]{:S(2)}, u32[]{:S(2)}) collective-permute-start(f32[64,64]{1,0:T(8,128)S(1)} %add_add_fusion.1), channel_id=1, source_target_pairs={{0,2},{1,3},{2,0},{3,1},{4,6},{5,7},{6,4},{7,5},{8,10},{9,11},{10,... | collective-permute-start | bytes 49160 | tf_op jit(solution)/shard_map/ppermute | solution.py:248
  (1 other events, 2.1 us)

commit v6 on v5

--- a/solution.py
+++ b/solution.py
@@ -73,7 +73,7 @@
         copy.wait()
 
 
-def pack(matrix, ids, width, direct):
+def pack(matrix, ids, width):
     rows, count = matrix.shape[0], ids.shape[0] // 2
     return pl.pallas_call(
         pack_kernel,
@@ -81,7 +81,7 @@
         out_specs=[VMEM] * count,
         out_shape=[struct((rows, 2 * width), matrix.dtype)] * count,
         scratch_shapes=[pltpu.SemaphoreType.DMA((2 * count,))],
-        compiler_params=pltpu.CompilerParams(vmem_limit_bytes=(60 if direct else 16) * 2**20),
+        compiler_params=BIG,
         cost_estimate=cost(0, 8 * rows * count * width),
     )(ids, matrix)
 
@@ -93,50 +93,47 @@
     )(*args)
 
 
-def scores_kernel(pairs, blocks, counts, picked, joined, with_gram, width, *refs):
+def scores_kernel(work, counts, picked, with_gram, width, *refs):
     refs = list(refs)
-    bases = [[refs.pop(0) for _ in range(count)] for count in counts]
+    bases = {block: [refs.pop(0) for _ in range(count)] for block, count in counts}
     slots = {k: refs.pop(0) for k in picked}
     gram = refs.pop(0)[...] if with_gram else None
     before, outs = refs[:-2], refs[-2:]
     rank = gram.shape[0] if with_gram else 0
     for odd in range(2):
         left = 0
-        if joined:
-            left = before[odd].shape[1]
-            outs[odd][:, :left] = before[odd][...]
-        for pair in pairs:
+        for pair, blocks in work:
             value = 0.0
-            for block, parts in zip(blocks, bases):
+            for block in blocks:
                 start = block * width
-                for part in parts:
+                for part in bases[block]:
                     stop = min(start + part.shape[1], (block + 1) * width)
                     big = [slots[4 * pair + odd][:, start:stop], slots[4 * pair + 2 + odd][:, start:stop]]
                     value = value + nt(jnp.concatenate(big, axis=0), part[:, :stop - start])
                     start = stop
             value = value.T
             lanes = slice(left, left + value.shape[1])
-            left += value.shape[1]
-            outs[odd][:, lanes] = value + before[odd][:, lanes] if before and not joined else value
+            left = lanes.stop
+            known = before and lanes.stop <= before[odd].shape[1]
+            outs[odd][:, lanes] = value + before[odd][:, lanes] if known else value
         if with_gram:
-            tail = bases[-1][-1]
+            tail = bases[counts[-1][0]][-1]
             first = tail.shape[1] - 3 * rank
             theirs = [tail[:, first + i * rank:first + (i + 1) * rank].astype(f32) for i in range(3)]
             outs[odd][:, left:] = gram + ((theirs[0] + theirs[1]) + theirs[2])
 
 
-def scores(slots, pairs, blocks, bases, before=(), joined=False, gram=None):
-    rank = bases[0][0].shape[0]
-    width = slots[pairs[0] * 4].shape[1] // 2
-    picked = [4 * pair + k for pair in pairs for k in range(4)]
-    rows = slots[picked[0]].shape[0]
-    cells = 2 * rows * len(pairs) + (before[0].shape[1] if joined else 0) + (0 if gram is None else rank)
-    counts = [len(parts) for parts in bases]
-    args = [x for parts in bases for x in parts] + [slots[k] for k in picked]
+def scores(slots, work, bases, before=(), gram=None):
+    rank = next(iter(bases.values()))[0].shape[0]
+    picked = [4 * pair + k for pair, _ in work for k in range(4)]
+    rows, width = slots[picked[0]].shape[0], slots[picked[0]].shape[1] // 2
+    cells = 2 * rows * len(work) + (0 if gram is None else rank)
+    counts = [(block, len(parts)) for block, parts in bases.items()]
+    args = [x for parts in bases.values() for x in parts] + [slots[k] for k in picked]
     args += ([] if gram is None else [gram]) + list(before)
-    work = rows * len(picked) * width * len(blocks)
-    kernel = functools.partial(scores_kernel, pairs, blocks, counts, picked, joined, gram is not None, width)
-    return call(kernel, args, [struct((rank, cells), f32)] * 2, cost(2 * rank * work, 2 * work))
+    size = 4 * rows * width * sum(len(blocks) for _, blocks in work)
+    kernel = functools.partial(scores_kernel, work, counts, picked, gram is not None, width)
+    return call(kernel, args, [struct((rank, cells), f32)] * 2, cost(2 * rank * size, 2 * size))
 
 
 def image_kernel(normalised, *refs):
@@ -147,10 +144,10 @@
     def turned(x, mask):
         return jnp.concatenate([x[:, (j ^ mask) * size:((j ^ mask) + 1) * size] for j in range(GROUP // 2)], axis=1)
 
-    value = (values[0][:, :cells] + turned(values[1], 1)) + (turned(values[2], 2) + turned(values[3], 3))
+    value = (values[0][:, :cells] + turned(values[3], 3)) + (turned(values[1], 1) + turned(values[2], 2))
     if normalised:
         gram = [x[:, cells:] for x in values]
-        value = exact_nn(inverse_factor((gram[0] + gram[1]) + (gram[2] + gram[3])), value)
+        value = exact_nn(inverse_factor((gram[0] + gram[3]) + (gram[1] + gram[2])), value)
     out[...] = value.astype(bf16)
 
 
@@ -244,30 +241,33 @@
     )(gram, loading)
 
 
-def mate(value, cells, mask):
-    return lax.ppermute(value, "cell", [(i, i ^ mask) for i in range(cells)])
+def mate(value, cells, mask, other=None):
+    masks = (mask, mask if other is None else other)
+    return lax.ppermute(value, "cell", [(i, i ^ masks[i % 2]) for i in range(cells)])
+
+
+def legs(value, cells):
+    return [mate(value, cells, 2, 4), mate(value, cells, 4, 2), mate(value, cells, 6)]
 
 
 def total_over_cells(value, cells):
-    for one, two in ((GROUP, 1), (2, 4)):
-        value = (value + mate(value, cells, one)) + (mate(value, cells, one | two) + mate(value, cells, two))
-    return value
+    value = (value + mate(value, cells, GROUP | 1)) + (mate(value, cells, GROUP) + mate(value, cells, 1))
+    one, two, both = legs(value, cells)
+    return (value + both) + (one + two)
 
 
 def square_program(cells, expression, start_basis):
     width, rows = start_basis.shape[0], expression.shape[0]
     index = lax.axis_index("cell").astype(jnp.int32)
-    slots = [None] * GROUP
-    for masks, direct in (((2, 4), True), ((1, 6, 3, 5, 7, 0), False)):
-        members = index ^ jnp.array(masks, jnp.int32)
-        ids = jnp.stack([members, members ^ GROUP], axis=1).reshape(-1)
-        for k, packed in zip(masks, pack(expression, ids, width, direct)):
-            slots[k] = mate(packed, cells, k) if k else packed
+    masks = ((0, 0), (1, 1), (2, 4), (3, 5), (4, 2), (5, 3), (6, 6), (7, 7))
+    members = index ^ jnp.where(index % 2 == 0, *jnp.array(masks, jnp.int32).T)
+    packs = pack(expression, jnp.stack([members, members ^ GROUP], axis=1).reshape(-1), width)
+    slots = [mate(x, cells, *pair) if k else x for k, (x, pair) in enumerate(zip(packs, masks))]
 
     def image_from(totals, normalised):
         even, odd = totals
         even = even + mate(odd, cells, 1)
-        image = image_of(even, [mate(even, cells, mask) for mask in (2, 4, 6)], rows, normalised)
+        image = image_of(even, legs(even, cells), rows, normalised)
         return image, mate(image, cells, 1)
 
     def terms_and_received(images, cuts):
@@ -275,19 +275,20 @@
         own = terms(slots, 0, images, cuts, f32)
         return zip([mate(x, cells, GROUP) for x in sent], own)
 
-    half = -(-6 * width // 1280) * 128
+    first = -(-6 * width // 1280) * 128
     basis = start_basis.T
-    bases = [[basis], [mate(basis, cells, GROUP)]]
-    images = image_from(scores(slots, (1,), (0, 1), bases, scores(slots, (0,), (0, 1), bases), True), False)
+    bases = {0: [basis], 1: [mate(basis, cells, GROUP)]}
+    early = scores(slots, [(0, (0,))], {0: [basis]})
+    images = image_from(scores(slots, [(0, (1,)), (1, (0, 1))], bases, early), False)
     for _ in range(1, ITERS):
         parts, copies, gram = [], [], []
-        for received, own in terms_and_received(images, (half, width - half)):
+        for received, own in terms_and_received(images, (first, width - first)):
             part, total = fold(received, own, gram, bf16, bool(parts))
             gram = [total]
             parts.append(part)
             copies.append(mate(part, cells, GROUP))
-        early = scores(slots, (0, 1), (0,), [parts])
-        images = image_from(scores(slots, (0, 1), (1,), [copies], early, gram=gram[0]), True)
+        early = scores(slots, [(0, (0,)), (1, (0,))], {0: parts})
+        images = image_from(scores(slots, [(0, (1,)), (1, (1,))], {1: copies}, early, gram[0]), True)
     ((received, own),) = terms_and_received(images, (width,))
     loading, gram = fold(received, own, [], f32, False)
     return output_call(total_over_cells(gram, cells), loading).T

time: 145 us -> 141 us (0.972)
  waiting for transfers between devices: 95.3 us -> 89.2 us
  starting transfers between devices: 30.2 us -> 35.8 us
  Pallas kernels: 15.6 us -> 12.8 us
    ppermute x29, waiting for transfers between devices: 95.3 us -> 89.2 us  [mate(): lax.ppermute(value, 'cell', [(i, i ^ masks[i % 2]) for i in range(cells)])]
    ppermute x29, starting transfers between devices: 30.2 us -> 35.8 us  [mate(): lax.ppermute(value, 'cell', [(i, i ^ masks[i % 2]) for i in range(cells)])]
    pallas_call x2 -> x1, Pallas kernels: 4.34 us -> 1.52 us  [pack(): pl.pallas_call(pack_kernel, in_specs=[pl.BlockSpec(memory_space=pltpu.SME...]
  transfers between devices with their start and end apart: 29 -> 29, of which waited for: 22 -> 19; matrix products, arithmetic and copies ran while one was open for 0% -> 0% of each run, Pallas kernels for 3% -> 2%
where the time goes in v6:
time: 141 us
  waiting for transfers between devices  89.2 us (63%)
  starting transfers between devices  35.8 us (25%)
  Pallas kernels  12.8 us (9%)
  local copies, waits for them, and re-layouts  2.29 us (2%)
    ppermute x29, waiting for transfers between devices, mate(): lax.ppermute(value, 'cell', [(i, i ^ masks[i % 2]) for i in range(cells)])  89.2 us
    ppermute x29, starting transfers between devices, mate(): lax.ppermute(value, 'cell', [(i, i ^ masks[i % 2]) for i in range(cells)])  35.8 us
    pallas_call x13, Pallas kernels, call(): pl.pallas_call(kernel, in_specs=[VMEM] * len(args), out_specs=[VMEM] * le...  8.32 us
    pallas_call x1, Pallas kernels, output_call(): pl.pallas_call(functools.partial(output_kernel, math.sqrt(GENES)), in_spe...  2.98 us
  transfers between devices with their start and end apart: 29, of which 19 were waited for; matrix products, arithmetic and copies ran while one was open for 0% of the time, Pallas kernels for 2%

profile of v6, /device:TPU:0, one launch (start us, length us, event | category | flops | bytes accessed | tf_op | source)
XLA Modules:
  0.0 141.0 jit_solution(17850643442027754059)
XLA Ops:
  0.8 2.1 %copy-done = bf16[64,30720]{1,0:T(8,128)(2,1)S(1)} copy-done((bf16[64,30720]{1,0:T(8,128)(2,1)S(1)}, bf16[64,30720]{1,0:T(8,128)(2,1)}, u32[]{:S(2)}) %copy-start) | copy-done | bytes 3932184
  3.0 1.5 %shard_map.37 = (bf16[64,3840]{1,0:T(8,128)(2,1)S(1)}, bf16[64,3840]{1,0:T(8,128)(2,1)S(1)}, bf16[64,3840]{1,0:T(8,128)(2,1)S(1)}, bf16[64,3840]{1,0:T(8,128)(2,...) custom-call(s32[16]{0:T(128)S(1)} %reshape.38.ids, ...), custom_call_target="tpu_custom_call" | custom-call | bytes 7864320 | tf_op jit(solution)/shard_map/pallas_call | solution.py:78
  5.0 2.6 %collective-permute-start.1 = (bf16[64,3840]{1,0:T(8,128)(2,1)S(1)}, bf16[64,3840]{1,0:T(8,128)(2,1)S(1)}, u32[]{:S(2)}, u32[]{:S(2)}) collective-permute-start(bf16[64,3840]{1,0:T(8,128)(2,1)S(1)} %get-tuple-element.33), channel_id=1, source_target_pairs={{0,2},{1,5},{2,0},{3,7},{4,6},{5,1},{6,4},{7,3},{8,10},{9,13},{10,... | collective-permute-start | bytes 1474568 | tf_op jit(solution)/shard_map/ppermute | solution.py:246
  7.6 1.3 collective-permute-start.2
  9.4 2.7 %collective-permute-start.5 = (bf16[64,3840]{1,0:T(8,128)(2,1)S(1)}, bf16[64,3840]{1,0:T(8,128)(2,1)S(1)}, u32[]{:S(2)}, u32[]{:S(2)}) collective-permute-start(bf16[64,3840]{1,0:T(8,128)(2,1)S(1)} %get-tuple-element.37), channel_id=1, source_target_pairs={{0,6},{1,7},{2,4},{3,5},{4,2},{5,3},{6,0},{7,1},{8,14},{9,15},{10,... | collective-permute-start | bytes 1474568 | tf_op jit(solution)/shard_map/ppermute | solution.py:246
  12.1 5.8 %collective-permute-done.1.refs_3_.refs_4_.refs_2_ = bf16[64,3840]{1,0:T(8,128)(2,1)S(1)} collective-permute-done((bf16[64,3840]{1,0:T(8,128)(2,1)S(1)}, bf16[64,3840]{1,0:T(8,128)(2,1)S(1)}, u32[]{:S(2)}, u32[]{:S(2)}) %collective-permute-start.1) | collective-permute-done | bytes 491552 | tf_op jit(solution)/shard_map/ppermute | solution.py:246
  18.0 2.8 %collective-permute-start.6 = (bf16[64,3840]{1,0:T(8,128)(2,1)S(1)}, bf16[64,3840]{1,0:T(8,128)(2,1)S(1)}, u32[]{:S(2)}, u32[]{:S(2)}) collective-permute-start(bf16[64,3840]{1,0:T(8,128)(2,1)S(1)} %get-tuple-element.38), channel_id=1, source_target_pairs={{0,7},{1,6},{2,5},{3,4},{4,3},{5,2},{6,1},{7,0},{8,15},{9,14},{10,... | collective-permute-start | bytes 1474568 | tf_op jit(solution)/shard_map/ppermute | solution.py:246
  20.8 10.3 %collective-permute-done.2.refs_4_.refs_5_.refs_3_ = bf16[64,3840]{1,0:T(8,128)(2,1)S(1)} collective-permute-done((bf16[64,3840]{1,0:T(8,128)(2,1)S(1)}, bf16[64,3840]{1,0:T(8,128)(2,1)S(1)}, u32[]{:S(2)}, u32[]{:S(2)}) %collective-permute-start.2) | collective-permute-done | bytes 491552 | tf_op jit(solution)/shard_map/ppermute | solution.py:246
  31.1 2.3 %collective-permute-start.7 = (bf16[64,1920]{1,0:T(8,128)(2,1)S(1)}, bf16[64,1920]{1,0:T(8,128)(2,1)S(1)}, u32[]{:S(2)}, u32[]{:S(2)}) collective-permute-start(bf16[64,1920]{1,0:T(8,128)(2,1)S(1)} %bitcast.5), channel_id=1, source_target_pairs={{0,8},{1,9},{2,10},{3,11},{4,12},{5,13},{6,14},{7,15},{8,0},{9,1},... | collective-permute-start | bytes 737288 | tf_op jit(solution)/shard_map/ppermute | solution.py:246
  33.8 21.9 %collective-permute-done.7.refs_1_ = bf16[64,1920]{1,0:T(8,128)(2,1)S(1)} collective-permute-done((bf16[64,1920]{1,0:T(8,128)(2,1)S(1)}, bf16[64,1920]{1,0:T(8,128)(2,1)S(1)}, u32[]{:S(2)}, u32[]{:S(2)}) %collective-permute-start.7) | collective-permute-done | bytes 245792 | tf_op jit(solution)/shard_map/ppermute | solution.py:246
  56.7 1.6 %collective-permute-start.8 = (f32[64,256]{1,0:T(8,128)S(1)}, f32[64,256]{1,0:T(8,128)S(1)}, u32[]{:S(2)}, u32[]{:S(2)}) collective-permute-start(f32[64,256]{1,0:T(8,128)S(1)} %get-tuple-element.42), channel_id=1, source_target_pairs={{0,1},{1,0},{2,3},{3,2},{4,5},{5,4},{6,7},{7,6},{8,9},{9,8},{10,11... | collective-permute-start | bytes 196616 | tf_op jit(solution)/shard_map/ppermute | solution.py:246
  59.2 2.9 %collective-permute-start.11 = (f32[64,256]{1,0:T(8,128)S(1)}, f32[64,256]{1,0:T(8,128)S(1)}, u32[]{:S(2)}, u32[]{:S(2)}) collective-permute-start(f32[64,256]{1,0:T(8,128)S(1)} %add.29.refs_0_), channel_id=1, source_target_pairs={{0,6},{1,7},{2,4},{3,5},{4,2},{5,3},{6,0},{7,1},{8,14},{9,15},{10,... | collective-permute-start | bytes 196616 | tf_op jit(solution)/shard_map/ppermute | solution.py:246
  63.0 1.8 %collective-permute-done.11.refs_3_ = f32[64,256]{1,0:T(8,128)S(1)} collective-permute-done((f32[64,256]{1,0:T(8,128)S(1)}, f32[64,256]{1,0:T(8,128)S(1)}, u32[]{:S(2)}, u32[]{:S(2)}) %collective-permute-start.11) | collective-permute-done | bytes 65568 | tf_op jit(solution)/shard_map/ppermute | solution.py:246
  64.8 1.8 %collective-permute-done.10.refs_2_ = f32[64,256]{1,0:T(8,128)S(1)} collective-permute-done((f32[64,256]{1,0:T(8,128)S(1)}, f32[64,256]{1,0:T(8,128)S(1)}, u32[]{:S(2)}, u32[]{:S(2)}) %collective-permute-start.10) | collective-permute-done | bytes 65568 | tf_op jit(solution)/shard_map/ppermute | solution.py:246
  68.4 3.0 %collective-permute-start.13 = (bf16[64,1152]{1,0:T(8,128)(2,1)S(1)}, bf16[64,1152]{1,0:T(8,128)(2,1)S(1)}, u32[]{:S(2)}, u32[]{:S(2)}) collective-permute-start(bf16[64,1152]{1,0:T(8,128)(2,1)S(1)} %get-tuple-element.43), channel_id=1, source_target_pairs={{0,8},{1,9},{2,10},{3,11},{4,12},{5,13},{6,14},{7,15},{8,0},{9,1},... | collective-permute-start | bytes 442376 | tf_op jit(solution)/shard_map/ppermute | solution.py:246
  71.9 9.4 %collective-permute-done.13.received = bf16[64,1152]{1,0:T(8,128)(2,1)S(1)} collective-permute-done((bf16[64,1152]{1,0:T(8,128)(2,1)S(1)}, bf16[64,1152]{1,0:T(8,128)(2,1)S(1)}, u32[]{:S(2)}, u32[]{:S(2)}) %collective-permute-start.13) | collective-permute-done | bytes 147488 | tf_op jit(solution)/shard_map/ppermute | solution.py:246
  83.5 1.9 %collective-permute-start.16 = (bf16[64,960]{1,0:T(8,128)(2,1)S(1)}, bf16[64,960]{1,0:T(8,128)(2,1)S(1)}, u32[]{:S(2)}, u32[]{:S(2)}) collective-permute-start(bf16[64,960]{1,0:T(8,128)(2,1)S(1)} %get-tuple-element.49.refs_1_), channel_id=1, source_target_pairs={{0,8},{1,9},{2,10},{3,11},{4,12},{5,13},{6,14},{7,15},{8,0},{9,1},... | collective-permute-start | bytes 368648 | tf_op jit(solution)/shard_map/ppermute | solution.py:246
  86.1 7.6 %collective-permute-done.16.refs_1_ = bf16[64,960]{1,0:T(8,128)(2,1)S(1)} collective-permute-done((bf16[64,960]{1,0:T(8,128)(2,1)S(1)}, bf16[64,960]{1,0:T(8,128)(2,1)S(1)}, u32[]{:S(2)}, u32[]{:S(2)}) %collective-permute-start.16) | collective-permute-done | bytes 122912 | tf_op jit(solution)/shard_map/ppermute | solution.py:246
  94.5 1.3 collective-permute-done.17
  95.8 2.1 %collective-permute-start.20 = (f32[64,320]{1,0:T(8,128)S(1)}, f32[64,320]{1,0:T(8,128)S(1)}, u32[]{:S(2)}, u32[]{:S(2)}) collective-permute-start(f32[64,320]{1,0:T(8,128)S(1)} %add.30.refs_0_), channel_id=1, source_target_pairs={{0,6},{1,7},{2,4},{3,5},{4,2},{5,3},{6,0},{7,1},{8,14},{9,15},{10,... | collective-permute-start | bytes 245768 | tf_op jit(solution)/shard_map/ppermute | solution.py:246
  97.9 3.0 %collective-permute-start.19 = (f32[64,320]{1,0:T(8,128)S(1)}, f32[64,320]{1,0:T(8,128)S(1)}, u32[]{:S(2)}, u32[]{:S(2)}) collective-permute-start(f32[64,320]{1,0:T(8,128)S(1)} %add.30.refs_0_), channel_id=1, source_target_pairs={{0,4},{1,3},{2,6},{3,1},{4,0},{5,7},{6,2},{7,5},{8,12},{9,11},{10,... | collective-permute-start | bytes 245768 | tf_op jit(solution)/shard_map/ppermute | solution.py:246
  101.6 4.2 %collective-permute-done.19.refs_2_ = f32[64,320]{1,0:T(8,128)S(1)} collective-permute-done((f32[64,320]{1,0:T(8,128)S(1)}, f32[64,320]{1,0:T(8,128)S(1)}, u32[]{:S(2)}, u32[]{:S(2)}) %collective-permute-start.19) | collective-permute-done | bytes 81952 | tf_op jit(solution)/shard_map/ppermute | solution.py:246
  105.8 2.0 %shard_map.47.refs_8_ = bf16[64,256]{1,0:T(8,128)(2,1)S(1)} custom-call(f32[64,320]{1,0:T(8,128)S(1)} %add.30.refs_0_, f32[64,320]{1,0:T(8,128)S(1)} %collective-permute-done.18.refs_1_, f32[64,320]{1,0:T(8,128)S(1)} %collective-permute-done.19.refs_2_, f32[64,320]{1,0:T(8,128)S(1)} %collective-permute-done.20.refs_3_), custom_call_target="tpu_custom_call" | custom-call | flops 15728640 | bytes 327680 | tf_op jit(solution)/shard_map/pallas_call | solution.py:90
  107.8 1.2 collective-permute-done.21.refs_9_
  110.9 12.8 %collective-permute-done.22.received = bf16[64,1920]{1,0:T(8,128)(2,1)S(1)} collective-permute-done((bf16[64,1920]{1,0:T(8,128)(2,1)S(1)}, bf16[64,1920]{1,0:T(8,128)(2,1)S(1)}, u32[]{:S(2)}, u32[]{:S(2)}) %collective-permute-start.22) | collective-permute-done | bytes 245792 | tf_op jit(solution)/shard_map/ppermute | solution.py:246
  124.5 2.7 %collective-permute-start.23 = (f32[64,64]{1,0:T(8,128)S(1)}, f32[64,64]{1,0:T(8,128)S(1)}, u32[]{:S(2)}, u32[]{:S(2)}) collective-permute-start(f32[64,64]{1,0:T(8,128)S(1)} %get-tuple-element.55), channel_id=1, source_target_pairs={{0,9},{1,8},{2,11},{3,10},{4,13},{5,12},{6,15},{7,14},{8,1},{9,0},... | collective-permute-start | bytes 49160 | tf_op jit(solution)/shard_map/ppermute | solution.py:246
  127.2 2.3 %collective-permute-done.24 = f32[64,64]{1,0:T(8,128)S(1)} collective-permute-done((f32[64,64]{1,0:T(8,128)S(1)}, f32[64,64]{1,0:T(8,128)S(1)}, u32[]{:S(2)}, u32[]{:S(2)}) %collective-permute-start.24) | collective-permute-done | bytes 16416 | tf_op jit(solution)/shard_map/ppermute | solution.py:246
  129.5 1.8 %collective-permute-start.28 = (f32[64,64]{1,0:T(8,128)S(1)}, f32[64,64]{1,0:T(8,128)S(1)}, u32[]{:S(2)}, u32[]{:S(2)}) collective-permute-start(f32[64,64]{1,0:T(8,128)S(1)} %add_add_fusion.1), channel_id=1, source_target_pairs={{0,4},{1,3},{2,6},{3,1},{4,0},{5,7},{6,2},{7,5},{8,12},{9,11},{10,... | collective-permute-start | bytes 49160 | tf_op jit(solution)/shard_map/ppermute | solution.py:246
  131.4 1.8 %collective-permute-start.27 = (f32[64,64]{1,0:T(8,128)S(1)}, f32[64,64]{1,0:T(8,128)S(1)}, u32[]{:S(2)}, u32[]{:S(2)}) collective-permute-start(f32[64,64]{1,0:T(8,128)S(1)} %add_add_fusion.1), channel_id=1, source_target_pairs={{0,2},{1,5},{2,0},{3,7},{4,6},{5,1},{6,4},{7,3},{8,10},{9,13},{10,... | collective-permute-start | bytes 49160 | tf_op jit(solution)/shard_map/ppermute | solution.py:246
  133.5 1.8 %collective-permute-done.27 = f32[64,64]{1,0:T(8,128)S(1)} collective-permute-done((f32[64,64]{1,0:T(8,128)S(1)}, f32[64,64]{1,0:T(8,128)S(1)}, u32[]{:S(2)}, u32[]{:S(2)}) %collective-permute-start.27) | collective-permute-done | bytes 16416 | tf_op jit(solution)/shard_map/ppermute | solution.py:246
  135.3 2.7 %collective-permute-done.26 = f32[64,64]{1,0:T(8,128)S(1)} collective-permute-done((f32[64,64]{1,0:T(8,128)S(1)}, f32[64,64]{1,0:T(8,128)S(1)}, u32[]{:S(2)}, u32[]{:S(2)}) %collective-permute-start.26) | collective-permute-done | bytes 16416 | tf_op jit(solution)/shard_map/ppermute | solution.py:246
  138.0 3.0 %shard_map.51 = f32[64,1920]{1,0:T(8,128)} custom-call(f32[64,64]{1,0:T(8,128)S(1)} %add_add_fusion.gram, f32[64,1920]{1,0:T(8,128)S(1)} %get-tuple-element.56.loading), custom_call_target="tpu_custom_call" | custom-call | tf_op jit(solution)/shard_map/pallas_call | solution.py:237
  (53 shorter events, 14.7 us)
Async XLA Ops:
  0.8 2.1 %copy-start = (bf16[64,30720]{1,0:T(8,128)(2,1)S(1)}, bf16[64,30720]{1,0:T(8,128)(2,1)}, u32[]{:S(2)}) copy-start(bf16[64,30720]{1,0:T(8,128)(2,1)} %matrix.1) | copy-start | bytes 11796484
  3.0 28.2 %copy-start.1 = (bf16[1920,64]{0,1:T(8,128)(2,1)S(1)}, bf16[1920,64]{0,1:T(8,128)(2,1)}, u32[]{:S(2)}) copy-start(bf16[1920,64]{0,1:T(8,128)(2,1)} %param.4) | copy-start | bytes 737284
  4.5 4.9 %collective-permute-start = (bf16[64,3840]{1,0:T(8,128)(2,1)S(1)}, bf16[64,3840]{1,0:T(8,128)(2,1)S(1)}, u32[]{:S(2)}, u32[]{:S(2)}) collective-permute-start(bf16[64,3840]{1,0:T(8,128)(2,1)S(1)} %get-tuple-element.32), channel_id=1, source_target_pairs={{0,1},{1,0},{2,3},{3,2},{4,5},{5,4},{6,7},{7,6},{8,9},{9,8},{10,11... | collective-permute-start | bytes 1474568 | tf_op jit(solution)/shard_map/ppermute | solution.py:246
  5.0 12.9 %collective-permute-start.1 = (bf16[64,3840]{1,0:T(8,128)(2,1)S(1)}, bf16[64,3840]{1,0:T(8,128)(2,1)S(1)}, u32[]{:S(2)}, u32[]{:S(2)}) collective-permute-start(bf16[64,3840]{1,0:T(8,128)(2,1)S(1)} %get-tuple-element.33), channel_id=1, source_target_pairs={{0,2},{1,5},{2,0},{3,7},{4,6},{5,1},{6,4},{7,3},{8,10},{9,13},{10,... | collective-permute-start | bytes 1474568 | tf_op jit(solution)/shard_map/ppermute | solution.py:246
  7.6 23.5 %collective-permute-start.2 = (bf16[64,3840]{1,0:T(8,128)(2,1)S(1)}, bf16[64,3840]{1,0:T(8,128)(2,1)S(1)}, u32[]{:S(2)}, u32[]{:S(2)}) collective-permute-start(bf16[64,3840]{1,0:T(8,128)(2,1)S(1)} %get-tuple-element.34), channel_id=1, source_target_pairs={{0,3},{1,4},{2,1},{3,6},{4,7},{5,0},{6,5},{7,2},{8,11},{9,12},{10,... | collective-permute-start | bytes 1474568 | tf_op jit(solution)/shard_map/ppermute | solution.py:246
  8.9 46.8 %collective-permute-start.3 = (bf16[64,3840]{1,0:T(8,128)(2,1)S(1)}, bf16[64,3840]{1,0:T(8,128)(2,1)S(1)}, u32[]{:S(2)}, u32[]{:S(2)}) collective-permute-start(bf16[64,3840]{1,0:T(8,128)(2,1)S(1)} %get-tuple-element.35), channel_id=1, source_target_pairs={{0,4},{1,3},{2,6},{3,1},{4,0},{5,7},{6,2},{7,5},{8,12},{9,11},{10,... | collective-permute-start | bytes 1474568 | tf_op jit(solution)/shard_map/ppermute | solution.py:246
  9.4 46.3 %collective-permute-start.4 = (bf16[64,3840]{1,0:T(8,128)(2,1)S(1)}, bf16[64,3840]{1,0:T(8,128)(2,1)S(1)}, u32[]{:S(2)}, u32[]{:S(2)}) collective-permute-start(bf16[64,3840]{1,0:T(8,128)(2,1)S(1)} %get-tuple-element.36), channel_id=1, source_target_pairs={{0,5},{1,2},{2,7},{3,0},{4,1},{5,6},{6,3},{7,4},{8,13},{9,10},{10,... | collective-permute-start | bytes 1474568 | tf_op jit(solution)/shard_map/ppermute | solution.py:246
  9.4 46.3 %collective-permute-start.5 = (bf16[64,3840]{1,0:T(8,128)(2,1)S(1)}, bf16[64,3840]{1,0:T(8,128)(2,1)S(1)}, u32[]{:S(2)}, u32[]{:S(2)}) collective-permute-start(bf16[64,3840]{1,0:T(8,128)(2,1)S(1)} %get-tuple-element.37), channel_id=1, source_target_pairs={{0,6},{1,7},{2,4},{3,5},{4,2},{5,3},{6,0},{7,1},{8,14},{9,15},{10,... | collective-permute-start | bytes 1474568 | tf_op jit(solution)/shard_map/ppermute | solution.py:246
  18.0 37.8 %collective-permute-start.6 = (bf16[64,3840]{1,0:T(8,128)(2,1)S(1)}, bf16[64,3840]{1,0:T(8,128)(2,1)S(1)}, u32[]{:S(2)}, u32[]{:S(2)}) collective-permute-start(bf16[64,3840]{1,0:T(8,128)(2,1)S(1)} %get-tuple-element.38), channel_id=1, source_target_pairs={{0,7},{1,6},{2,5},{3,4},{4,3},{5,2},{6,1},{7,0},{8,15},{9,14},{10,... | collective-permute-start | bytes 1474568 | tf_op jit(solution)/shard_map/ppermute | solution.py:246
  31.1 24.6 %collective-permute-start.7 = (bf16[64,1920]{1,0:T(8,128)(2,1)S(1)}, bf16[64,1920]{1,0:T(8,128)(2,1)S(1)}, u32[]{:S(2)}, u32[]{:S(2)}) collective-permute-start(bf16[64,1920]{1,0:T(8,128)(2,1)S(1)} %bitcast.5), channel_id=1, source_target_pairs={{0,8},{1,9},{2,10},{3,11},{4,12},{5,13},{6,14},{7,15},{8,0},{9,1},... | collective-permute-start | bytes 737288 | tf_op jit(solution)/shard_map/ppermute | solution.py:246
  56.7 2.5 %collective-permute-start.8 = (f32[64,256]{1,0:T(8,128)S(1)}, f32[64,256]{1,0:T(8,128)S(1)}, u32[]{:S(2)}, u32[]{:S(2)}) collective-permute-start(f32[64,256]{1,0:T(8,128)S(1)} %get-tuple-element.42), channel_id=1, source_target_pairs={{0,1},{1,0},{2,3},{3,2},{4,5},{5,4},{6,7},{7,6},{8,9},{9,8},{10,11... | collective-permute-start | bytes 196616 | tf_op jit(solution)/shard_map/ppermute | solution.py:246
  59.2 5.5 %collective-permute-start.11 = (f32[64,256]{1,0:T(8,128)S(1)}, f32[64,256]{1,0:T(8,128)S(1)}, u32[]{:S(2)}, u32[]{:S(2)}) collective-permute-start(f32[64,256]{1,0:T(8,128)S(1)} %add.29.refs_0_), channel_id=1, source_target_pairs={{0,6},{1,7},{2,4},{3,5},{4,2},{5,3},{6,0},{7,1},{8,14},{9,15},{10,... | collective-permute-start | bytes 196616 | tf_op jit(solution)/shard_map/ppermute | solution.py:246
  62.1 4.4 %collective-permute-start.10 = (f32[64,256]{1,0:T(8,128)S(1)}, f32[64,256]{1,0:T(8,128)S(1)}, u32[]{:S(2)}, u32[]{:S(2)}) collective-permute-start(f32[64,256]{1,0:T(8,128)S(1)} %add.29.refs_0_), channel_id=1, source_target_pairs={{0,4},{1,3},{2,6},{3,1},{4,0},{5,7},{6,2},{7,5},{8,12},{9,11},{10,... | collective-permute-start | bytes 196616 | tf_op jit(solution)/shard_map/ppermute | solution.py:246
  62.1 4.4 %collective-permute-start.9 = (f32[64,256]{1,0:T(8,128)S(1)}, f32[64,256]{1,0:T(8,128)S(1)}, u32[]{:S(2)}, u32[]{:S(2)}) collective-permute-start(f32[64,256]{1,0:T(8,128)S(1)} %add.29.refs_0_), channel_id=1, source_target_pairs={{0,2},{1,5},{2,0},{3,7},{4,6},{5,1},{6,4},{7,3},{8,10},{9,13},{10,... | collective-permute-start | bytes 196616 | tf_op jit(solution)/shard_map/ppermute | solution.py:246
  66.7 1.3 collective-permute-start.12
  68.4 12.9 %collective-permute-start.13 = (bf16[64,1152]{1,0:T(8,128)(2,1)S(1)}, bf16[64,1152]{1,0:T(8,128)(2,1)S(1)}, u32[]{:S(2)}, u32[]{:S(2)}) collective-permute-start(bf16[64,1152]{1,0:T(8,128)(2,1)S(1)} %get-tuple-element.43), channel_id=1, source_target_pairs={{0,8},{1,9},{2,10},{3,11},{4,12},{5,13},{6,14},{7,15},{8,0},{9,1},... | collective-permute-start | bytes 442376 | tf_op jit(solution)/shard_map/ppermute | solution.py:246
  71.4 11.5 %collective-permute-start.15 = (bf16[64,768]{1,0:T(8,128)(2,1)S(1)}, bf16[64,768]{1,0:T(8,128)(2,1)S(1)}, u32[]{:S(2)}, u32[]{:S(2)}) collective-permute-start(bf16[64,768]{1,0:T(8,128)(2,1)S(1)} %get-tuple-element.46), channel_id=1, source_target_pairs={{0,8},{1,9},{2,10},{3,11},{4,12},{5,13},{6,14},{7,15},{8,0},{9,1},... | collective-permute-start | bytes 294920 | tf_op jit(solution)/shard_map/ppermute | solution.py:246
  81.8 11.9 %collective-permute-start.14 = (bf16[64,1152]{1,0:T(8,128)(2,1)S(1)}, bf16[64,1152]{1,0:T(8,128)(2,1)S(1)}, u32[]{:S(2)}, u32[]{:S(2)}) collective-permute-start(bf16[64,1152]{1,0:T(8,128)(2,1)S(1)} %get-tuple-element.45.refs_0_), channel_id=1, source_target_pairs={{0,8},{1,9},{2,10},{3,11},{4,12},{5,13},{6,14},{7,15},{8,0},{9,1},... | collective-permute-start | bytes 442376 | tf_op jit(solution)/shard_map/ppermute | solution.py:246
  83.5 10.2 %collective-permute-start.16 = (bf16[64,960]{1,0:T(8,128)(2,1)S(1)}, bf16[64,960]{1,0:T(8,128)(2,1)S(1)}, u32[]{:S(2)}, u32[]{:S(2)}) collective-permute-start(bf16[64,960]{1,0:T(8,128)(2,1)S(1)} %get-tuple-element.49.refs_1_), channel_id=1, source_target_pairs={{0,8},{1,9},{2,10},{3,11},{4,12},{5,13},{6,14},{7,15},{8,0},{9,1},... | collective-permute-start | bytes 368648 | tf_op jit(solution)/shard_map/ppermute | solution.py:246
  94.4 1.4 collective-permute-start.17
  95.8 5.8 %collective-permute-start.20 = (f32[64,320]{1,0:T(8,128)S(1)}, f32[64,320]{1,0:T(8,128)S(1)}, u32[]{:S(2)}, u32[]{:S(2)}) collective-permute-start(f32[64,320]{1,0:T(8,128)S(1)} %add.30.refs_0_), channel_id=1, source_target_pairs={{0,6},{1,7},{2,4},{3,5},{4,2},{5,3},{6,0},{7,1},{8,14},{9,15},{10,... | collective-permute-start | bytes 245768 | tf_op jit(solution)/shard_map/ppermute | solution.py:246
  97.9 8.0 %collective-permute-start.19 = (f32[64,320]{1,0:T(8,128)S(1)}, f32[64,320]{1,0:T(8,128)S(1)}, u32[]{:S(2)}, u32[]{:S(2)}) collective-permute-start(f32[64,320]{1,0:T(8,128)S(1)} %add.30.refs_0_), channel_id=1, source_target_pairs={{0,4},{1,3},{2,6},{3,1},{4,0},{5,7},{6,2},{7,5},{8,12},{9,11},{10,... | collective-permute-start | bytes 245768 | tf_op jit(solution)/shard_map/ppermute | solution.py:246
  100.9 4.9 %collective-permute-start.18 = (f32[64,320]{1,0:T(8,128)S(1)}, f32[64,320]{1,0:T(8,128)S(1)}, u32[]{:S(2)}, u32[]{:S(2)}) collective-permute-start(f32[64,320]{1,0:T(8,128)S(1)} %add.30.refs_0_), channel_id=1, source_target_pairs={{0,2},{1,5},{2,0},{3,7},{4,6},{5,1},{6,4},{7,3},{8,10},{9,13},{10,... | collective-permute-start | bytes 245768 | tf_op jit(solution)/shard_map/ppermute | solution.py:246
  107.8 1.2 collective-permute-start.21
  109.5 14.3 %collective-permute-start.22 = (bf16[64,1920]{1,0:T(8,128)(2,1)S(1)}, bf16[64,1920]{1,0:T(8,128)(2,1)S(1)}, u32[]{:S(2)}, u32[]{:S(2)}) collective-permute-start(bf16[64,1920]{1,0:T(8,128)(2,1)S(1)} %shard_map.48), channel_id=1, source_target_pairs={{0,8},{1,9},{2,10},{3,11},{4,12},{5,13},{6,14},{7,15},{8,0},{9,1},... | collective-permute-start | bytes 737288 | tf_op jit(solution)/shard_map/ppermute | solution.py:246
  124.3 2.8 %collective-permute-start.25 = (f32[64,64]{1,0:T(8,128)S(1)}, f32[64,64]{1,0:T(8,128)S(1)}, u32[]{:S(2)}, u32[]{:S(2)}) collective-permute-start(f32[64,64]{1,0:T(8,128)S(1)} %get-tuple-element.55), channel_id=1, source_target_pairs={{0,1},{1,0},{2,3},{3,2},{4,5},{5,4},{6,7},{7,6},{8,9},{9,8},{10,11... | collective-permute-start | bytes 49160 | tf_op jit(solution)/shard_map/ppermute | solution.py:246
  124.4 5.1 %collective-permute-start.24 = (f32[64,64]{1,0:T(8,128)S(1)}, f32[64,64]{1,0:T(8,128)S(1)}, u32[]{:S(2)}, u32[]{:S(2)}) collective-permute-start(f32[64,64]{1,0:T(8,128)S(1)} %get-tuple-element.55), channel_id=1, source_target_pairs={{0,8},{1,9},{2,10},{3,11},{4,12},{5,13},{6,14},{7,15},{8,0},{9,1},... | collective-permute-start | bytes 49160 | tf_op jit(solution)/shard_map/ppermute | solution.py:246
  124.5 5.0 %collective-permute-start.23 = (f32[64,64]{1,0:T(8,128)S(1)}, f32[64,64]{1,0:T(8,128)S(1)}, u32[]{:S(2)}, u32[]{:S(2)}) collective-permute-start(f32[64,64]{1,0:T(8,128)S(1)} %get-tuple-element.55), channel_id=1, source_target_pairs={{0,9},{1,8},{2,11},{3,10},{4,13},{5,12},{6,15},{7,14},{8,1},{9,0},... | collective-permute-start | bytes 49160 | tf_op jit(solution)/shard_map/ppermute | solution.py:246
  129.5 4.0 %collective-permute-start.28 = (f32[64,64]{1,0:T(8,128)S(1)}, f32[64,64]{1,0:T(8,128)S(1)}, u32[]{:S(2)}, u32[]{:S(2)}) collective-permute-start(f32[64,64]{1,0:T(8,128)S(1)} %add_add_fusion.1), channel_id=1, source_target_pairs={{0,4},{1,3},{2,6},{3,1},{4,0},{5,7},{6,2},{7,5},{8,12},{9,11},{10,... | collective-permute-start | bytes 49160 | tf_op jit(solution)/shard_map/ppermute | solution.py:246
  131.4 3.9 %collective-permute-start.27 = (f32[64,64]{1,0:T(8,128)S(1)}, f32[64,64]{1,0:T(8,128)S(1)}, u32[]{:S(2)}, u32[]{:S(2)}) collective-permute-start(f32[64,64]{1,0:T(8,128)S(1)} %add_add_fusion.1), channel_id=1, source_target_pairs={{0,2},{1,5},{2,0},{3,7},{4,6},{5,1},{6,4},{7,3},{8,10},{9,13},{10,... | collective-permute-start | bytes 49160 | tf_op jit(solution)/shard_map/ppermute | solution.py:246
  133.2 4.8 %collective-permute-start.26 = (f32[64,64]{1,0:T(8,128)S(1)}, f32[64,64]{1,0:T(8,128)S(1)}, u32[]{:S(2)}, u32[]{:S(2)}) collective-permute-start(f32[64,64]{1,0:T(8,128)S(1)} %add_add_fusion.1), channel_id=1, source_target_pairs={{0,6},{1,7},{2,4},{3,5},{4,2},{5,3},{6,0},{7,1},{8,14},{9,15},{10,... | collective-permute-start | bytes 49160 | tf_op jit(solution)/shard_map/ppermute | solution.py:246

commit v7 on v6

--- a/solution.py
+++ b/solution.py
@@ -58,13 +58,15 @@
     return pl.CostEstimate(flops=flops, bytes_accessed=bytes_accessed, transcendentals=0)
 
 
-def pack_kernel(ids, matrix, *refs):
+def pack_kernel(masks, matrix, *refs):
     outs, sem = refs[:-1], refs[-1]
     width = outs[0].shape[1] // 2
+    index = lax.axis_index("cell")
     copies = []
-    for k, out in enumerate(outs):
-        for j in range(2):
-            start = pl.multiple_of(ids[2 * k + j] * width, 128)
+    for k, (out, pair) in enumerate(zip(outs, masks)):
+        member = index ^ jnp.where(index % 2 == 0, *pair)
+        for j, block in enumerate((member, member ^ GROUP)):
+            start = pl.multiple_of(block * width, 128)
             copies.append(pltpu.make_async_copy(
                 matrix.at[:, pl.ds(start, width)], out.at[:, pl.ds(j * width, width)], sem.at[2 * k + j]))
     for copy in copies:
@@ -73,17 +75,17 @@
         copy.wait()
 
 
-def pack(matrix, ids, width):
-    rows, count = matrix.shape[0], ids.shape[0] // 2
+def pack(matrix, masks, width):
+    rows, count = matrix.shape[0], len(masks)
     return pl.pallas_call(
-        pack_kernel,
-        in_specs=[pl.BlockSpec(memory_space=pltpu.SMEM), pl.BlockSpec(memory_space=pltpu.HBM)],
+        functools.partial(pack_kernel, masks),
+        in_specs=[pl.BlockSpec(memory_space=pltpu.HBM)],
         out_specs=[VMEM] * count,
         out_shape=[struct((rows, 2 * width), matrix.dtype)] * count,
         scratch_shapes=[pltpu.SemaphoreType.DMA((2 * count,))],
         compiler_params=BIG,
         cost_estimate=cost(0, 8 * rows * count * width),
-    )(ids, matrix)
+    )(matrix)
 
 
 def call(kernel, args, outs, estimate):
@@ -111,11 +113,13 @@
                     big = [slots[4 * pair + odd][:, start:stop], slots[4 * pair + 2 + odd][:, start:stop]]
                     value = value + nt(jnp.concatenate(big, axis=0), part[:, :stop - start])
                     start = stop
-            value = value.T
-            lanes = slice(left, left + value.shape[1])
+            lanes = slice(left, left + 2 * next(iter(slots.values())).shape[0])
             left = lanes.stop
-            known = before and lanes.stop <= before[odd].shape[1]
-            outs[odd][:, lanes] = value + before[odd][:, lanes] if known else value
+            if blocks:
+                value = value.T
+            if before and lanes.stop <= before[odd].shape[1]:
+                value = value + before[odd][:, lanes]
+            outs[odd][:, lanes] = value
         if with_gram:
             tail = bases[counts[-1][0]][-1]
             first = tail.shape[1] - 3 * rank
@@ -125,7 +129,7 @@
 
 def scores(slots, work, bases, before=(), gram=None):
     rank = next(iter(bases.values()))[0].shape[0]
-    picked = [4 * pair + k for pair, _ in work for k in range(4)]
+    picked = [4 * pair + k for pair, blocks in work if blocks for k in range(4)]
     rows, width = slots[picked[0]].shape[0], slots[picked[0]].shape[1] // 2
     cells = 2 * rows * len(work) + (0 if gram is None else rank)
     counts = [(block, len(parts)) for block, parts in bases.items()]
@@ -251,17 +255,16 @@
 
 
 def total_over_cells(value, cells):
-    value = (value + mate(value, cells, GROUP | 1)) + (mate(value, cells, GROUP) + mate(value, cells, 1))
+    value = value + mate(value, cells, GROUP)
+    value = value + mate(value, cells, 1)
     one, two, both = legs(value, cells)
     return (value + both) + (one + two)
 
 
 def square_program(cells, expression, start_basis):
     width, rows = start_basis.shape[0], expression.shape[0]
-    index = lax.axis_index("cell").astype(jnp.int32)
     masks = ((0, 0), (1, 1), (2, 4), (3, 5), (4, 2), (5, 3), (6, 6), (7, 7))
-    members = index ^ jnp.where(index % 2 == 0, *jnp.array(masks, jnp.int32).T)
-    packs = pack(expression, jnp.stack([members, members ^ GROUP], axis=1).reshape(-1), width)
+    packs = pack(expression, masks, width)
     slots = [mate(x, cells, *pair) if k else x for k, (x, pair) in enumerate(zip(packs, masks))]
 
     def image_from(totals, normalised):
@@ -278,8 +281,8 @@
     first = -(-6 * width // 1280) * 128
     basis = start_basis.T
     bases = {0: [basis], 1: [mate(basis, cells, GROUP)]}
-    early = scores(slots, [(0, (0,))], {0: [basis]})
-    images = image_from(scores(slots, [(0, (1,)), (1, (0, 1))], bases, early), False)
+    early = scores(slots, [(0, (0, 1))], bases)
+    images = image_from(scores(slots, [(0, ()), (1, (0, 1))], bases, early), False)
     for _ in range(1, ITERS):
         parts, copies, gram = [], [], []
         for received, own in terms_and_received(images, (first, width - first)):

time: 141 us -> 137 us (0.972)
  starting transfers between devices: 35.8 us -> 34.2 us
    ppermute x29 -> x28, starting transfers between devices: 35.8 us -> 34.2 us  [mate(): lax.ppermute(value, 'cell', [(i, i ^ masks[i % 2]) for i in range(cells)])]
    ppermute x29 -> x28, waiting for transfers between devices: 89.2 us -> 88 us  [mate(): lax.ppermute(value, 'cell', [(i, i ^ masks[i % 2]) for i in range(cells)])]
  transfers between devices with their start and end apart: 29 -> 28, of which waited for: 19 -> 23; matrix products, arithmetic and copies ran while one was open for 0% -> 0% of each run, Pallas kernels for 2% -> 2%
where the time goes in v7:
time: 137 us
  waiting for transfers between devices  88 us (64%)
  starting transfers between devices  34.2 us (25%)
  Pallas kernels  12.1 us (9%)
  local copies, waits for them, and re-layouts  2.12 us (2%)
    ppermute x28, waiting for transfers between devices, mate(): lax.ppermute(value, 'cell', [(i, i ^ masks[i % 2]) for i in range(cells)])  88 us
    ppermute x28, starting transfers between devices, mate(): lax.ppermute(value, 'cell', [(i, i ^ masks[i % 2]) for i in range(cells)])  34.2 us
    pallas_call x13, Pallas kernels, call(): pl.pallas_call(kernel, in_specs=[VMEM] * len(args), out_specs=[VMEM] * le...  8.29 us
    pallas_call x1, Pallas kernels, output_call(): pl.pallas_call(functools.partial(output_kernel, math.sqrt(GENES)), in_spe...  2.98 us
  transfers between devices with their start and end apart: 28, of which 23 were waited for; matrix products, arithmetic and copies ran while one was open for 0% of the time, Pallas kernels for 2%

profile of v7, /device:TPU:0, one launch (start us, length us, event | category | flops | bytes accessed | tf_op | source)
XLA Modules:
  0.0 136.6 jit_solution(12756650860268583780)
XLA Ops:
  0.0 2.1 %copy-done = bf16[64,30720]{1,0:T(8,128)(2,1)S(1)} copy-done((bf16[64,30720]{1,0:T(8,128)(2,1)S(1)}, bf16[64,30720]{1,0:T(8,128)(2,1)}, u32[]{:S(2)}) %copy-start) | copy-done | bytes 3932184
  3.5 2.6 %collective-permute-start.1 = (bf16[64,3840]{1,0:T(8,128)(2,1)S(1)}, bf16[64,3840]{1,0:T(8,128)(2,1)S(1)}, u32[]{:S(2)}, u32[]{:S(2)}) collective-permute-start(bf16[64,3840]{1,0:T(8,128)(2,1)S(1)} %get-tuple-element.33), channel_id=1, source_target_pairs={{0,2},{1,5},{2,0},{3,7},{4,6},{5,1},{6,4},{7,3},{8,10},{9,13},{10,... | collective-permute-start | bytes 1474568 | tf_op jit(solution)/shard_map/ppermute | solution.py:250
  6.1 2.6 %collective-permute-start.7 = (bf16[64,1920]{1,0:T(8,128)(2,1)S(1)}, bf16[64,1920]{1,0:T(8,128)(2,1)S(1)}, u32[]{:S(2)}, u32[]{:S(2)}) collective-permute-start(bf16[64,1920]{1,0:T(8,128)(2,1)S(1)} %bitcast.2), channel_id=1, source_target_pairs={{0,8},{1,9},{2,10},{3,11},{4,12},{5,13},{6,14},{7,15},{8,0},{9,1},... | collective-permute-start | bytes 737288 | tf_op jit(solution)/shard_map/ppermute | solution.py:250
  10.3 7.5 %collective-permute-done.7.refs_1_ = bf16[64,1920]{1,0:T(8,128)(2,1)S(1)} collective-permute-done((bf16[64,1920]{1,0:T(8,128)(2,1)S(1)}, bf16[64,1920]{1,0:T(8,128)(2,1)S(1)}, u32[]{:S(2)}, u32[]{:S(2)}) %collective-permute-start.7) | collective-permute-done | bytes 245792 | tf_op jit(solution)/shard_map/ppermute | solution.py:250
  17.8 5.6 %collective-permute-start.4 = (bf16[64,3840]{1,0:T(8,128)(2,1)S(1)}, bf16[64,3840]{1,0:T(8,128)(2,1)S(1)}, u32[]{:S(2)}, u32[]{:S(2)}) collective-permute-start(bf16[64,3840]{1,0:T(8,128)(2,1)S(1)} %get-tuple-element.36), channel_id=1, source_target_pairs={{0,5},{1,2},{2,7},{3,0},{4,1},{5,6},{6,3},{7,4},{8,13},{9,10},{10,... | collective-permute-start | bytes 1474568 | tf_op jit(solution)/shard_map/ppermute | solution.py:250
  23.4 2.1 %collective-permute-start.6 = (bf16[64,3840]{1,0:T(8,128)(2,1)S(1)}, bf16[64,3840]{1,0:T(8,128)(2,1)S(1)}, u32[]{:S(2)}, u32[]{:S(2)}) collective-permute-start(bf16[64,3840]{1,0:T(8,128)(2,1)S(1)} %get-tuple-element.38), channel_id=1, source_target_pairs={{0,7},{1,6},{2,5},{3,4},{4,3},{5,2},{6,1},{7,0},{8,15},{9,14},{10,... | collective-permute-start | bytes 1474568 | tf_op jit(solution)/shard_map/ppermute | solution.py:250
  25.5 4.9 %collective-permute-done.2.refs_5_.refs_3_ = bf16[64,3840]{1,0:T(8,128)(2,1)S(1)} collective-permute-done((bf16[64,3840]{1,0:T(8,128)(2,1)S(1)}, bf16[64,3840]{1,0:T(8,128)(2,1)S(1)}, u32[]{:S(2)}, u32[]{:S(2)}) %collective-permute-start.2) | collective-permute-done | bytes 491552 | tf_op jit(solution)/shard_map/ppermute | solution.py:250
  31.2 5.0 %collective-permute-done.4.refs_3_.refs_5_.refs_7_ = bf16[64,3840]{1,0:T(8,128)(2,1)S(1)} collective-permute-done((bf16[64,3840]{1,0:T(8,128)(2,1)S(1)}, bf16[64,3840]{1,0:T(8,128)(2,1)S(1)}, u32[]{:S(2)}, u32[]{:S(2)}) %collective-permute-start.4) | collective-permute-done | bytes 491552 | tf_op jit(solution)/shard_map/ppermute | solution.py:250
  36.2 11.8 %collective-permute-done.5.refs_4_.refs_6_.refs_8_ = bf16[64,3840]{1,0:T(8,128)(2,1)S(1)} collective-permute-done((bf16[64,3840]{1,0:T(8,128)(2,1)S(1)}, bf16[64,3840]{1,0:T(8,128)(2,1)S(1)}, u32[]{:S(2)}, u32[]{:S(2)}) %collective-permute-start.5) | collective-permute-done | bytes 491552 | tf_op jit(solution)/shard_map/ppermute | solution.py:250
  48.0 6.1 %collective-permute-done.6.refs_5_.refs_7_.refs_9_ = bf16[64,3840]{1,0:T(8,128)(2,1)S(1)} collective-permute-done((bf16[64,3840]{1,0:T(8,128)(2,1)S(1)}, bf16[64,3840]{1,0:T(8,128)(2,1)S(1)}, u32[]{:S(2)}, u32[]{:S(2)}) %collective-permute-start.6) | collective-permute-done | bytes 491552 | tf_op jit(solution)/shard_map/ppermute | solution.py:250
  54.9 1.7 %collective-permute-start.8 = (f32[64,256]{1,0:T(8,128)S(1)}, f32[64,256]{1,0:T(8,128)S(1)}, u32[]{:S(2)}, u32[]{:S(2)}) collective-permute-start(f32[64,256]{1,0:T(8,128)S(1)} %get-tuple-element.42), channel_id=1, source_target_pairs={{0,1},{1,0},{2,3},{3,2},{4,5},{5,4},{6,7},{7,6},{8,9},{9,8},{10,11... | collective-permute-start | bytes 196616 | tf_op jit(solution)/shard_map/ppermute | solution.py:250
  57.5 1.6 %collective-permute-start.11 = (f32[64,256]{1,0:T(8,128)S(1)}, f32[64,256]{1,0:T(8,128)S(1)}, u32[]{:S(2)}, u32[]{:S(2)}) collective-permute-start(f32[64,256]{1,0:T(8,128)S(1)} %add.21.refs_0_), channel_id=1, source_target_pairs={{0,6},{1,7},{2,4},{3,5},{4,2},{5,3},{6,0},{7,1},{8,14},{9,15},{10,... | collective-permute-start | bytes 196616 | tf_op jit(solution)/shard_map/ppermute | solution.py:250
  59.3 1.7 %collective-permute-start.9 = (f32[64,256]{1,0:T(8,128)S(1)}, f32[64,256]{1,0:T(8,128)S(1)}, u32[]{:S(2)}, u32[]{:S(2)}) collective-permute-start(f32[64,256]{1,0:T(8,128)S(1)} %add.21.refs_0_), channel_id=1, source_target_pairs={{0,2},{1,5},{2,0},{3,7},{4,6},{5,1},{6,4},{7,3},{8,10},{9,13},{10,... | collective-permute-start | bytes 196616 | tf_op jit(solution)/shard_map/ppermute | solution.py:250
  61.0 1.9 %collective-permute-done.11.refs_3_ = f32[64,256]{1,0:T(8,128)S(1)} collective-permute-done((f32[64,256]{1,0:T(8,128)S(1)}, f32[64,256]{1,0:T(8,128)S(1)}, u32[]{:S(2)}, u32[]{:S(2)}) %collective-permute-start.11) | collective-permute-done | bytes 65568 | tf_op jit(solution)/shard_map/ppermute | solution.py:250
  64.4 1.2 collective-permute-done.12.refs_9_
  66.0 2.7 %collective-permute-start.13 = (bf16[64,1152]{1,0:T(8,128)(2,1)S(1)}, bf16[64,1152]{1,0:T(8,128)(2,1)S(1)}, u32[]{:S(2)}, u32[]{:S(2)}) collective-permute-start(bf16[64,1152]{1,0:T(8,128)(2,1)S(1)} %get-tuple-element.43), channel_id=1, source_target_pairs={{0,8},{1,9},{2,10},{3,11},{4,12},{5,13},{6,14},{7,15},{8,0},{9,1},... | collective-permute-start | bytes 442376 | tf_op jit(solution)/shard_map/ppermute | solution.py:250
  69.4 9.5 %collective-permute-done.13.received = bf16[64,1152]{1,0:T(8,128)(2,1)S(1)} collective-permute-done((bf16[64,1152]{1,0:T(8,128)(2,1)S(1)}, bf16[64,1152]{1,0:T(8,128)(2,1)S(1)}, u32[]{:S(2)}, u32[]{:S(2)}) %collective-permute-start.13) | collective-permute-done | bytes 147488 | tf_op jit(solution)/shard_map/ppermute | solution.py:250
  80.8 2.2 %collective-permute-start.16 = (bf16[64,960]{1,0:T(8,128)(2,1)S(1)}, bf16[64,960]{1,0:T(8,128)(2,1)S(1)}, u32[]{:S(2)}, u32[]{:S(2)}) collective-permute-start(bf16[64,960]{1,0:T(8,128)(2,1)S(1)} %get-tuple-element.49.refs_1_), channel_id=1, source_target_pairs={{0,8},{1,9},{2,10},{3,11},{4,12},{5,13},{6,14},{7,15},{8,0},{9,1},... | collective-permute-start | bytes 368648 | tf_op jit(solution)/shard_map/ppermute | solution.py:250
  83.7 9.8 %collective-permute-done.16.refs_1_ = bf16[64,960]{1,0:T(8,128)(2,1)S(1)} collective-permute-done((bf16[64,960]{1,0:T(8,128)(2,1)S(1)}, bf16[64,960]{1,0:T(8,128)(2,1)S(1)}, u32[]{:S(2)}, u32[]{:S(2)}) %collective-permute-start.16) | collective-permute-done | bytes 122912 | tf_op jit(solution)/shard_map/ppermute | solution.py:250
  94.3 1.3 collective-permute-done.17
  95.6 1.1 collective-permute-start.20
  96.7 1.6 %collective-permute-start.19 = (f32[64,320]{1,0:T(8,128)S(1)}, f32[64,320]{1,0:T(8,128)S(1)}, u32[]{:S(2)}, u32[]{:S(2)}) collective-permute-start(f32[64,320]{1,0:T(8,128)S(1)} %add.22.refs_0_), channel_id=1, source_target_pairs={{0,4},{1,3},{2,6},{3,1},{4,0},{5,7},{6,2},{7,5},{8,12},{9,11},{10,... | collective-permute-start | bytes 245768 | tf_op jit(solution)/shard_map/ppermute | solution.py:250
  99.2 3.1 %collective-permute-done.20.refs_3_ = f32[64,320]{1,0:T(8,128)S(1)} collective-permute-done((f32[64,320]{1,0:T(8,128)S(1)}, f32[64,320]{1,0:T(8,128)S(1)}, u32[]{:S(2)}, u32[]{:S(2)}) %collective-permute-start.20) | collective-permute-done | bytes 81952 | tf_op jit(solution)/shard_map/ppermute | solution.py:250
  103.3 2.0 %shard_map.38.refs_8_ = bf16[64,256]{1,0:T(8,128)(2,1)S(1)} custom-call(f32[64,320]{1,0:T(8,128)S(1)} %add.22.refs_0_, f32[64,320]{1,0:T(8,128)S(1)} %collective-permute-done.18.refs_1_, f32[64,320]{1,0:T(8,128)S(1)} %collective-permute-done.19.refs_2_, f32[64,320]{1,0:T(8,128)S(1)} %collective-permute-done.20.refs_3_), custom_call_target="tpu_custom_call" | custom-call | flops 15728640 | bytes 327680 | tf_op jit(solution)/shard_map/pallas_call | solution.py:92
  105.3 1.2 collective-permute-done.21.refs_9_
  107.0 1.4 %collective-permute-start.22 = (bf16[64,1920]{1,0:T(8,128)(2,1)S(1)}, bf16[64,1920]{1,0:T(8,128)(2,1)S(1)}, u32[]{:S(2)}, u32[]{:S(2)}) collective-permute-start(bf16[64,1920]{1,0:T(8,128)(2,1)S(1)} %shard_map.39), channel_id=1, source_target_pairs={{0,8},{1,9},{2,10},{3,11},{4,12},{5,13},{6,14},{7,15},{8,0},{9,1},... | collective-permute-start | bytes 737288 | tf_op jit(solution)/shard_map/ppermute | solution.py:250
  108.9 12.3 %collective-permute-done.22.received = bf16[64,1920]{1,0:T(8,128)(2,1)S(1)} collective-permute-done((bf16[64,1920]{1,0:T(8,128)(2,1)S(1)}, bf16[64,1920]{1,0:T(8,128)(2,1)S(1)}, u32[]{:S(2)}, u32[]{:S(2)}) %collective-permute-start.22) | collective-permute-done | bytes 245792 | tf_op jit(solution)/shard_map/ppermute | solution.py:250
  121.9 4.8 %collective-permute-done.23 = f32[64,64]{1,0:T(8,128)S(1)} collective-permute-done((f32[64,64]{1,0:T(8,128)S(1)}, f32[64,64]{1,0:T(8,128)S(1)}, u32[]{:S(2)}, u32[]{:S(2)}) %collective-permute-start.23) | collective-permute-done | bytes 16416 | tf_op jit(solution)/shard_map/ppermute | solution.py:250
  126.7 1.2 collective-permute-done.24
  128.8 2.6 %collective-permute-start.25 = (f32[64,64]{1,0:T(8,128)S(1)}, f32[64,64]{1,0:T(8,128)S(1)}, u32[]{:S(2)}, u32[]{:S(2)}) collective-permute-start(f32[64,64]{1,0:T(8,128)S(1)} %add.24), channel_id=1, source_target_pairs={{0,6},{1,7},{2,4},{3,5},{4,2},{5,3},{6,0},{7,1},{8,14},{9,15},{10,... | collective-permute-start | bytes 49160 | tf_op jit(solution)/shard_map/ppermute | solution.py:250
  132.0 1.6 %collective-permute-done.25 = f32[64,64]{1,0:T(8,128)S(1)} collective-permute-done((f32[64,64]{1,0:T(8,128)S(1)}, f32[64,64]{1,0:T(8,128)S(1)}, u32[]{:S(2)}, u32[]{:S(2)}) %collective-permute-start.25) | collective-permute-done | bytes 16416 | tf_op jit(solution)/shard_map/ppermute | solution.py:250
  133.6 3.0 %shard_map.42 = f32[64,1920]{1,0:T(8,128)} custom-call(f32[64,64]{1,0:T(8,128)S(1)} %add_add_fusion.gram, f32[64,1920]{1,0:T(8,128)S(1)} %get-tuple-element.56.loading), custom_call_target="tpu_custom_call" | custom-call | tf_op jit(solution)/shard_map/pallas_call | solution.py:241
  (48 shorter events, 16.8 us)
Async XLA Ops:
  0.0 2.1 %copy-start = (bf16[64,30720]{1,0:T(8,128)(2,1)S(1)}, bf16[64,30720]{1,0:T(8,128)(2,1)}, u32[]{:S(2)}) copy-start(bf16[64,30720]{1,0:T(8,128)(2,1)} %matrix.1) | copy-start | bytes 11796484
  2.1 4.0 %copy-start.1 = (bf16[1920,64]{0,1:T(8,128)(2,1)S(1)}, bf16[1920,64]{0,1:T(8,128)(2,1)}, u32[]{:S(2)}) copy-start(bf16[1920,64]{0,1:T(8,128)(2,1)} %param.3) | copy-start | bytes 737284
  3.0 20.4 %collective-permute-start = (bf16[64,3840]{1,0:T(8,128)(2,1)S(1)}, bf16[64,3840]{1,0:T(8,128)(2,1)S(1)}, u32[]{:S(2)}, u32[]{:S(2)}) collective-permute-start(bf16[64,3840]{1,0:T(8,128)(2,1)S(1)} %get-tuple-element.32), channel_id=1, source_target_pairs={{0,1},{1,0},{2,3},{3,2},{4,5},{5,4},{6,7},{7,6},{8,9},{9,8},{10,11... | collective-permute-start | bytes 1474568 | tf_op jit(solution)/shard_map/ppermute | solution.py:250
  3.5 19.9 %collective-permute-start.1 = (bf16[64,3840]{1,0:T(8,128)(2,1)S(1)}, bf16[64,3840]{1,0:T(8,128)(2,1)S(1)}, u32[]{:S(2)}, u32[]{:S(2)}) collective-permute-start(bf16[64,3840]{1,0:T(8,128)(2,1)S(1)} %get-tuple-element.33), channel_id=1, source_target_pairs={{0,2},{1,5},{2,0},{3,7},{4,6},{5,1},{6,4},{7,3},{8,10},{9,13},{10,... | collective-permute-start | bytes 1474568 | tf_op jit(solution)/shard_map/ppermute | solution.py:250
  6.1 11.7 %collective-permute-start.7 = (bf16[64,1920]{1,0:T(8,128)(2,1)S(1)}, bf16[64,1920]{1,0:T(8,128)(2,1)S(1)}, u32[]{:S(2)}, u32[]{:S(2)}) collective-permute-start(bf16[64,1920]{1,0:T(8,128)(2,1)S(1)} %bitcast.2), channel_id=1, source_target_pairs={{0,8},{1,9},{2,10},{3,11},{4,12},{5,13},{6,14},{7,15},{8,0},{9,1},... | collective-permute-start | bytes 737288 | tf_op jit(solution)/shard_map/ppermute | solution.py:250
  8.7 21.8 %collective-permute-start.2 = (bf16[64,3840]{1,0:T(8,128)(2,1)S(1)}, bf16[64,3840]{1,0:T(8,128)(2,1)S(1)}, u32[]{:S(2)}, u32[]{:S(2)}) collective-permute-start(bf16[64,3840]{1,0:T(8,128)(2,1)S(1)} %get-tuple-element.34), channel_id=1, source_target_pairs={{0,3},{1,4},{2,1},{3,6},{4,7},{5,0},{6,5},{7,2},{8,11},{9,12},{10,... | collective-permute-start | bytes 1474568 | tf_op jit(solution)/shard_map/ppermute | solution.py:250
  9.7 21.4 %collective-permute-start.3 = (bf16[64,3840]{1,0:T(8,128)(2,1)S(1)}, bf16[64,3840]{1,0:T(8,128)(2,1)S(1)}, u32[]{:S(2)}, u32[]{:S(2)}) collective-permute-start(bf16[64,3840]{1,0:T(8,128)(2,1)S(1)} %get-tuple-element.35), channel_id=1, source_target_pairs={{0,4},{1,3},{2,6},{3,1},{4,0},{5,7},{6,2},{7,5},{8,12},{9,11},{10,... | collective-permute-start | bytes 1474568 | tf_op jit(solution)/shard_map/ppermute | solution.py:250
  17.8 18.4 %collective-permute-start.4 = (bf16[64,3840]{1,0:T(8,128)(2,1)S(1)}, bf16[64,3840]{1,0:T(8,128)(2,1)S(1)}, u32[]{:S(2)}, u32[]{:S(2)}) collective-permute-start(bf16[64,3840]{1,0:T(8,128)(2,1)S(1)} %get-tuple-element.36), channel_id=1, source_target_pairs={{0,5},{1,2},{2,7},{3,0},{4,1},{5,6},{6,3},{7,4},{8,13},{9,10},{10,... | collective-permute-start | bytes 1474568 | tf_op jit(solution)/shard_map/ppermute | solution.py:250
  23.4 24.6 %collective-permute-start.5 = (bf16[64,3840]{1,0:T(8,128)(2,1)S(1)}, bf16[64,3840]{1,0:T(8,128)(2,1)S(1)}, u32[]{:S(2)}, u32[]{:S(2)}) collective-permute-start(bf16[64,3840]{1,0:T(8,128)(2,1)S(1)} %get-tuple-element.37), channel_id=1, source_target_pairs={{0,6},{1,7},{2,4},{3,5},{4,2},{5,3},{6,0},{7,1},{8,14},{9,15},{10,... | collective-permute-start | bytes 1474568 | tf_op jit(solution)/shard_map/ppermute | solution.py:250
  23.4 30.7 %collective-permute-start.6 = (bf16[64,3840]{1,0:T(8,128)(2,1)S(1)}, bf16[64,3840]{1,0:T(8,128)(2,1)S(1)}, u32[]{:S(2)}, u32[]{:S(2)}) collective-permute-start(bf16[64,3840]{1,0:T(8,128)(2,1)S(1)} %get-tuple-element.38), channel_id=1, source_target_pairs={{0,7},{1,6},{2,5},{3,4},{4,3},{5,2},{6,1},{7,0},{8,15},{9,14},{10,... | collective-permute-start | bytes 1474568 | tf_op jit(solution)/shard_map/ppermute | solution.py:250
  54.9 2.6 %collective-permute-start.8 = (f32[64,256]{1,0:T(8,128)S(1)}, f32[64,256]{1,0:T(8,128)S(1)}, u32[]{:S(2)}, u32[]{:S(2)}) collective-permute-start(f32[64,256]{1,0:T(8,128)S(1)} %get-tuple-element.42), channel_id=1, source_target_pairs={{0,1},{1,0},{2,3},{3,2},{4,5},{5,4},{6,7},{7,6},{8,9},{9,8},{10,11... | collective-permute-start | bytes 196616 | tf_op jit(solution)/shard_map/ppermute | solution.py:250
  57.5 5.4 %collective-permute-start.11 = (f32[64,256]{1,0:T(8,128)S(1)}, f32[64,256]{1,0:T(8,128)S(1)}, u32[]{:S(2)}, u32[]{:S(2)}) collective-permute-start(f32[64,256]{1,0:T(8,128)S(1)} %add.21.refs_0_), channel_id=1, source_target_pairs={{0,6},{1,7},{2,4},{3,5},{4,2},{5,3},{6,0},{7,1},{8,14},{9,15},{10,... | collective-permute-start | bytes 196616 | tf_op jit(solution)/shard_map/ppermute | solution.py:250
  59.1 4.7 %collective-permute-start.10 = (f32[64,256]{1,0:T(8,128)S(1)}, f32[64,256]{1,0:T(8,128)S(1)}, u32[]{:S(2)}, u32[]{:S(2)}) collective-permute-start(f32[64,256]{1,0:T(8,128)S(1)} %add.21.refs_0_), channel_id=1, source_target_pairs={{0,4},{1,3},{2,6},{3,1},{4,0},{5,7},{6,2},{7,5},{8,12},{9,11},{10,... | collective-permute-start | bytes 196616 | tf_op jit(solution)/shard_map/ppermute | solution.py:250
  59.3 4.9 %collective-permute-start.9 = (f32[64,256]{1,0:T(8,128)S(1)}, f32[64,256]{1,0:T(8,128)S(1)}, u32[]{:S(2)}, u32[]{:S(2)}) collective-permute-start(f32[64,256]{1,0:T(8,128)S(1)} %add.21.refs_0_), channel_id=1, source_target_pairs={{0,2},{1,5},{2,0},{3,7},{4,6},{5,1},{6,4},{7,3},{8,10},{9,13},{10,... | collective-permute-start | bytes 196616 | tf_op jit(solution)/shard_map/ppermute | solution.py:250
  64.3 1.3 collective-permute-start.12
  66.0 12.9 %collective-permute-start.13 = (bf16[64,1152]{1,0:T(8,128)(2,1)S(1)}, bf16[64,1152]{1,0:T(8,128)(2,1)S(1)}, u32[]{:S(2)}, u32[]{:S(2)}) collective-permute-start(bf16[64,1152]{1,0:T(8,128)(2,1)S(1)} %get-tuple-element.43), channel_id=1, source_target_pairs={{0,8},{1,9},{2,10},{3,11},{4,12},{5,13},{6,14},{7,15},{8,0},{9,1},... | collective-permute-start | bytes 442376 | tf_op jit(solution)/shard_map/ppermute | solution.py:250
  68.7 11.6 %collective-permute-start.15 = (bf16[64,768]{1,0:T(8,128)(2,1)S(1)}, bf16[64,768]{1,0:T(8,128)(2,1)S(1)}, u32[]{:S(2)}, u32[]{:S(2)}) collective-permute-start(bf16[64,768]{1,0:T(8,128)(2,1)S(1)} %get-tuple-element.46), channel_id=1, source_target_pairs={{0,8},{1,9},{2,10},{3,11},{4,12},{5,13},{6,14},{7,15},{8,0},{9,1},... | collective-permute-start | bytes 294920 | tf_op jit(solution)/shard_map/ppermute | solution.py:250
  79.4 14.1 %collective-permute-start.14 = (bf16[64,1152]{1,0:T(8,128)(2,1)S(1)}, bf16[64,1152]{1,0:T(8,128)(2,1)S(1)}, u32[]{:S(2)}, u32[]{:S(2)}) collective-permute-start(bf16[64,1152]{1,0:T(8,128)(2,1)S(1)} %get-tuple-element.45.refs_0_), channel_id=1, source_target_pairs={{0,8},{1,9},{2,10},{3,11},{4,12},{5,13},{6,14},{7,15},{8,0},{9,1},... | collective-permute-start | bytes 442376 | tf_op jit(solution)/shard_map/ppermute | solution.py:250
  80.8 12.7 %collective-permute-start.16 = (bf16[64,960]{1,0:T(8,128)(2,1)S(1)}, bf16[64,960]{1,0:T(8,128)(2,1)S(1)}, u32[]{:S(2)}, u32[]{:S(2)}) collective-permute-start(bf16[64,960]{1,0:T(8,128)(2,1)S(1)} %get-tuple-element.49.refs_1_), channel_id=1, source_target_pairs={{0,8},{1,9},{2,10},{3,11},{4,12},{5,13},{6,14},{7,15},{8,0},{9,1},... | collective-permute-start | bytes 368648 | tf_op jit(solution)/shard_map/ppermute | solution.py:250
  94.2 1.4 %collective-permute-start.17 = (f32[64,320]{1,0:T(8,128)S(1)}, f32[64,320]{1,0:T(8,128)S(1)}, u32[]{:S(2)}, u32[]{:S(2)}) collective-permute-start(f32[64,320]{1,0:T(8,128)S(1)} %get-tuple-element.54), channel_id=1, source_target_pairs={{0,1},{1,0},{2,3},{3,2},{4,5},{5,4},{6,7},{7,6},{8,9},{9,8},{10,11... | collective-permute-start | bytes 245768 | tf_op jit(solution)/shard_map/ppermute | solution.py:250
  95.6 6.7 %collective-permute-start.20 = (f32[64,320]{1,0:T(8,128)S(1)}, f32[64,320]{1,0:T(8,128)S(1)}, u32[]{:S(2)}, u32[]{:S(2)}) collective-permute-start(f32[64,320]{1,0:T(8,128)S(1)} %add.22.refs_0_), channel_id=1, source_target_pairs={{0,6},{1,7},{2,4},{3,5},{4,2},{5,3},{6,0},{7,1},{8,14},{9,15},{10,... | collective-permute-start | bytes 245768 | tf_op jit(solution)/shard_map/ppermute | solution.py:250
  96.7 6.5 %collective-permute-start.19 = (f32[64,320]{1,0:T(8,128)S(1)}, f32[64,320]{1,0:T(8,128)S(1)}, u32[]{:S(2)}, u32[]{:S(2)}) collective-permute-start(f32[64,320]{1,0:T(8,128)S(1)} %add.22.refs_0_), channel_id=1, source_target_pairs={{0,4},{1,3},{2,6},{3,1},{4,0},{5,7},{6,2},{7,5},{8,12},{9,11},{10,... | collective-permute-start | bytes 245768 | tf_op jit(solution)/shard_map/ppermute | solution.py:250
  98.2 5.1 %collective-permute-start.18 = (f32[64,320]{1,0:T(8,128)S(1)}, f32[64,320]{1,0:T(8,128)S(1)}, u32[]{:S(2)}, u32[]{:S(2)}) collective-permute-start(f32[64,320]{1,0:T(8,128)S(1)} %add.22.refs_0_), channel_id=1, source_target_pairs={{0,2},{1,5},{2,0},{3,7},{4,6},{5,1},{6,4},{7,3},{8,10},{9,13},{10,... | collective-permute-start | bytes 245768 | tf_op jit(solution)/shard_map/ppermute | solution.py:250
  105.3 1.2 collective-permute-start.21
  107.0 14.2 %collective-permute-start.22 = (bf16[64,1920]{1,0:T(8,128)(2,1)S(1)}, bf16[64,1920]{1,0:T(8,128)(2,1)S(1)}, u32[]{:S(2)}, u32[]{:S(2)}) collective-permute-start(bf16[64,1920]{1,0:T(8,128)(2,1)S(1)} %shard_map.39), channel_id=1, source_target_pairs={{0,8},{1,9},{2,10},{3,11},{4,12},{5,13},{6,14},{7,15},{8,0},{9,1},... | collective-permute-start | bytes 737288 | tf_op jit(solution)/shard_map/ppermute | solution.py:250
  121.8 4.9 %collective-permute-start.23 = (f32[64,64]{1,0:T(8,128)S(1)}, f32[64,64]{1,0:T(8,128)S(1)}, u32[]{:S(2)}, u32[]{:S(2)}) collective-permute-start(f32[64,64]{1,0:T(8,128)S(1)} %get-tuple-element.55), channel_id=1, source_target_pairs={{0,8},{1,9},{2,10},{3,11},{4,12},{5,13},{6,14},{7,15},{8,0},{9,1},... | collective-permute-start | bytes 49160 | tf_op jit(solution)/shard_map/ppermute | solution.py:250
  126.7 1.2 collective-permute-start.24
  127.9 4.1 %collective-permute-start.27 = (f32[64,64]{1,0:T(8,128)S(1)}, f32[64,64]{1,0:T(8,128)S(1)}, u32[]{:S(2)}, u32[]{:S(2)}) collective-permute-start(f32[64,64]{1,0:T(8,128)S(1)} %add.24), channel_id=1, source_target_pairs={{0,4},{1,3},{2,6},{3,1},{4,0},{5,7},{6,2},{7,5},{8,12},{9,11},{10,... | collective-permute-start | bytes 49160 | tf_op jit(solution)/shard_map/ppermute | solution.py:250
  127.9 4.1 %collective-permute-start.26 = (f32[64,64]{1,0:T(8,128)S(1)}, f32[64,64]{1,0:T(8,128)S(1)}, u32[]{:S(2)}, u32[]{:S(2)}) collective-permute-start(f32[64,64]{1,0:T(8,128)S(1)} %add.24), channel_id=1, source_target_pairs={{0,2},{1,5},{2,0},{3,7},{4,6},{5,1},{6,4},{7,3},{8,10},{9,13},{10,... | collective-permute-start | bytes 49160 | tf_op jit(solution)/shard_map/ppermute | solution.py:250
  128.8 4.8 %collective-permute-start.25 = (f32[64,64]{1,0:T(8,128)S(1)}, f32[64,64]{1,0:T(8,128)S(1)}, u32[]{:S(2)}, u32[]{:S(2)}) collective-permute-start(f32[64,64]{1,0:T(8,128)S(1)} %add.24), channel_id=1, source_target_pairs={{0,6},{1,7},{2,4},{3,5},{4,2},{5,3},{6,0},{7,1},{8,14},{9,15},{10,... | collective-permute-start | bytes 49160 | tf_op jit(solution)/shard_map/ppermute | solution.py:250

commit v8 on v7

--- a/solution.py
+++ b/solution.py
@@ -234,7 +234,10 @@
 
 
 def output_kernel(scale, gram, loading, out):
-    out[...] = exact_nn(inverse_factor(gram[...]), loading[...]) * scale
+    total = gram[0]
+    for device in range(1, gram.shape[0]):
+        total = total + gram[device]
+    out[...] = exact_nn(inverse_factor(total), loading[...]) * scale
 
 
 def output_call(gram, loading):
@@ -254,18 +257,14 @@
     return [mate(value, cells, 2, 4), mate(value, cells, 4, 2), mate(value, cells, 6)]
 
 
-def total_over_cells(value, cells):
-    value = value + mate(value, cells, GROUP)
-    value = value + mate(value, cells, 1)
-    one, two, both = legs(value, cells)
-    return (value + both) + (one + two)
-
-
 def square_program(cells, expression, start_basis):
     width, rows = start_basis.shape[0], expression.shape[0]
     masks = ((0, 0), (1, 1), (2, 4), (3, 5), (4, 2), (5, 3), (6, 6), (7, 7))
     packs = pack(expression, masks, width)
-    slots = [mate(x, cells, *pair) if k else x for k, (x, pair) in enumerate(zip(packs, masks))]
+    slots = [mate(x, cells, *pair) if k else x for k, (x, pair) in enumerate(zip(packs[:7], masks))]
+    leaving, slots[1] = lax.optimization_barrier((start_basis.T, slots[1]))
+    basis_mate, *late = lax.optimization_barrier((mate(leaving, cells, GROUP), *packs[7:]))
+    slots += [mate(x, cells, *pair) for x, pair in zip(late, masks[7:])]
 
     def image_from(totals, normalised):
         even, odd = totals
@@ -280,7 +279,7 @@
 
     first = -(-6 * width // 1280) * 128
     basis = start_basis.T
-    bases = {0: [basis], 1: [mate(basis, cells, GROUP)]}
+    bases = {0: [basis], 1: [basis_mate]}
     early = scores(slots, [(0, (0, 1))], bases)
     images = image_from(scores(slots, [(0, ()), (1, (0, 1))], bases, early), False)
     for _ in range(1, ITERS):
@@ -294,7 +293,7 @@
         images = image_from(scores(slots, [(0, (1,)), (1, (1,))], {1: copies}, early, gram[0]), True)
     ((received, own),) = terms_and_received(images, (width,))
     loading, gram = fold(received, own, [], f32, False)
-    return output_call(total_over_cells(gram, cells), loading).T
+    return output_call(lax.all_gather(gram, "cell"), loading).T
 
 
 def plain_program(expression, start_basis):

time: 137 us -> 146 us (1.066)
  blocking collectives: 0 us -> 20.6 us
  waiting for transfers between devices: 88 us -> 79.6 us
  starting transfers between devices: 34.2 us -> 30.7 us
    all_gather x0 -> x1, blocking collectives: none -> 20.6 us  [square_program(): return output_call(lax.all_gather(gram, 'cell'), loading).T]
    ppermute x28 -> x23, waiting for transfers between devices: 88 us -> 79.6 us  [mate(): lax.ppermute(value, 'cell', [(i, i ^ masks[i % 2]) for i in range(cells)])]
    ppermute x28 -> x23, starting transfers between devices: 34.2 us -> 30.7 us  [mate(): lax.ppermute(value, 'cell', [(i, i ^ masks[i % 2]) for i in range(cells)])]
  transfers between devices with their start and end apart: 28 -> 23, of which waited for: 23 -> 19; matrix products, arithmetic and copies ran while one was open for 0% -> 0% of each run, Pallas kernels for 2% -> 2%
where the time goes in v8:
time: 146 us; the launch traced here: 145 us
  waiting for transfers between devices  79.6 us (55%)
  starting transfers between devices  30.7 us (21%)
  blocking collectives  20.6 us (14%)
  Pallas kernels  12.1 us (8%)
  local copies, waits for them, and re-layouts  2.12 us (1%)
    ppermute x23, waiting for transfers between devices, mate(): lax.ppermute(value, 'cell', [(i, i ^ masks[i % 2]) for i in range(cells)])  79.6 us
    ppermute x23, starting transfers between devices, mate(): lax.ppermute(value, 'cell', [(i, i ^ masks[i % 2]) for i in range(cells)])  30.7 us
    all_gather x1, blocking collectives, square_program(): return output_call(lax.all_gather(gram, 'cell'), loading).T  20.6 us
    pallas_call x13, Pallas kernels, call(): pl.pallas_call(kernel, in_specs=[VMEM] * len(args), out_specs=[VMEM] * le...  8.29 us
    pallas_call x1, Pallas kernels, output_call(): pl.pallas_call(functools.partial(output_kernel, math.sqrt(GENES)), in_spe...  2.98 us
  transfers between devices with their start and end apart: 23, of which 19 were waited for; matrix products, arithmetic and copies ran while one was open for 0% of the time, Pallas kernels for 2%

profile of v8, /device:TPU:0, one launch (start us, length us, event | category | flops | bytes accessed | tf_op | source)
XLA Modules:
  0.0 145.4 jit_solution(17346637937230314593)
XLA Ops:
  0.0 2.1 %copy-done = bf16[64,30720]{1,0:T(8,128)(2,1)S(1)} copy-done((bf16[64,30720]{1,0:T(8,128)(2,1)S(1)}, bf16[64,30720]{1,0:T(8,128)(2,1)}, u32[]{:S(2)}) %copy-start) | copy-done | bytes 3932184
  3.5 2.6 %collective-permute-start.1 = (bf16[64,3840]{1,0:T(8,128)(2,1)S(1)}, bf16[64,3840]{1,0:T(8,128)(2,1)S(1)}, u32[]{:S(2)}, u32[]{:S(2)}) collective-permute-start(bf16[64,3840]{1,0:T(8,128)(2,1)S(1)} %get-tuple-element.38), channel_id=1, source_target_pairs={{0,2},{1,5},{2,0},{3,7},{4,6},{5,1},{6,4},{7,3},{8,10},{9,13},{10,... | collective-permute-start | bytes 1474568 | tf_op jit(solution)/shard_map/ppermute | solution.py:253
  6.1 2.9 %collective-permute-start.6 = (bf16[64,1920]{1,0:T(8,128)(2,1)S(1)}, bf16[64,1920]{1,0:T(8,128)(2,1)S(1)}, u32[]{:S(2)}, u32[]{:S(2)}) collective-permute-start(bf16[64,1920]{1,0:T(8,128)(2,1)S(1)} %bitcast.4), channel_id=1, source_target_pairs={{0,8},{1,9},{2,10},{3,11},{4,12},{5,13},{6,14},{7,15},{8,0},{9,1},... | collective-permute-start | bytes 737288 | tf_op jit(solution)/shard_map/ppermute | solution.py:253
  9.0 1.0 collective-permute-start.2
  9.9 1.6 %collective-permute-start.3 = (bf16[64,3840]{1,0:T(8,128)(2,1)S(1)}, bf16[64,3840]{1,0:T(8,128)(2,1)S(1)}, u32[]{:S(2)}, u32[]{:S(2)}) collective-permute-start(bf16[64,3840]{1,0:T(8,128)(2,1)S(1)} %get-tuple-element.40), channel_id=1, source_target_pairs={{0,4},{1,3},{2,6},{3,1},{4,0},{5,7},{6,2},{7,5},{8,12},{9,11},{10,... | collective-permute-start | bytes 1474568 | tf_op jit(solution)/shard_map/ppermute | solution.py:253
  11.9 6.0 %collective-permute-done.6.refs_1_ = bf16[64,1920]{1,0:T(8,128)(2,1)S(1)} collective-permute-done((bf16[64,1920]{1,0:T(8,128)(2,1)S(1)}, bf16[64,1920]{1,0:T(8,128)(2,1)S(1)}, u32[]{:S(2)}, u32[]{:S(2)}) %collective-permute-start.6) | collective-permute-done | bytes 245792 | tf_op jit(solution)/shard_map/ppermute | solution.py:253
  17.9 4.3 %collective-permute-start.5 = (bf16[64,3840]{1,0:T(8,128)(2,1)S(1)}, bf16[64,3840]{1,0:T(8,128)(2,1)S(1)}, u32[]{:S(2)}, u32[]{:S(2)}) collective-permute-start(bf16[64,3840]{1,0:T(8,128)(2,1)S(1)} %get-tuple-element.42), channel_id=1, source_target_pairs={{0,6},{1,7},{2,4},{3,5},{4,2},{5,3},{6,0},{7,1},{8,14},{9,15},{10,... | collective-permute-start | bytes 1474568 | tf_op jit(solution)/shard_map/ppermute | solution.py:253
  22.3 1.9 %collective-permute-start.7 = (bf16[64,3840]{1,0:T(8,128)(2,1)S(1)}, bf16[64,3840]{1,0:T(8,128)(2,1)S(1)}, u32[]{:S(2)}, u32[]{:S(2)}) collective-permute-start(bf16[64,3840]{1,0:T(8,128)(2,1)S(1)} %get-tuple-element.45), channel_id=1, source_target_pairs={{0,7},{1,6},{2,5},{3,4},{4,3},{5,2},{6,1},{7,0},{8,15},{9,14},{10,... | collective-permute-start | bytes 1474568 | tf_op jit(solution)/shard_map/ppermute | solution.py:253
  24.1 6.2 %collective-permute-done.2.refs_5_.refs_3_ = bf16[64,3840]{1,0:T(8,128)(2,1)S(1)} collective-permute-done((bf16[64,3840]{1,0:T(8,128)(2,1)S(1)}, bf16[64,3840]{1,0:T(8,128)(2,1)S(1)}, u32[]{:S(2)}, u32[]{:S(2)}) %collective-permute-start.2) | collective-permute-done | bytes 491552 | tf_op jit(solution)/shard_map/ppermute | solution.py:253
  31.1 5.4 %collective-permute-done.4.refs_3_.refs_5_.refs_7_ = bf16[64,3840]{1,0:T(8,128)(2,1)S(1)} collective-permute-done((bf16[64,3840]{1,0:T(8,128)(2,1)S(1)}, bf16[64,3840]{1,0:T(8,128)(2,1)S(1)}, u32[]{:S(2)}, u32[]{:S(2)}) %collective-permute-start.4) | collective-permute-done | bytes 491552 | tf_op jit(solution)/shard_map/ppermute | solution.py:253
  36.5 11.8 %collective-permute-done.5.refs_4_.refs_6_.refs_8_ = bf16[64,3840]{1,0:T(8,128)(2,1)S(1)} collective-permute-done((bf16[64,3840]{1,0:T(8,128)(2,1)S(1)}, bf16[64,3840]{1,0:T(8,128)(2,1)S(1)}, u32[]{:S(2)}, u32[]{:S(2)}) %collective-permute-start.5) | collective-permute-done | bytes 491552 | tf_op jit(solution)/shard_map/ppermute | solution.py:253
  48.3 5.9 %collective-permute-done.7.refs_5_.refs_7_.refs_9_ = bf16[64,3840]{1,0:T(8,128)(2,1)S(1)} collective-permute-done((bf16[64,3840]{1,0:T(8,128)(2,1)S(1)}, bf16[64,3840]{1,0:T(8,128)(2,1)S(1)}, u32[]{:S(2)}, u32[]{:S(2)}) %collective-permute-start.7) | collective-permute-done | bytes 491552 | tf_op jit(solution)/shard_map/ppermute | solution.py:253
  54.9 1.7 %collective-permute-start.8 = (f32[64,256]{1,0:T(8,128)S(1)}, f32[64,256]{1,0:T(8,128)S(1)}, u32[]{:S(2)}, u32[]{:S(2)}) collective-permute-start(f32[64,256]{1,0:T(8,128)S(1)} %get-tuple-element.50), channel_id=1, source_target_pairs={{0,1},{1,0},{2,3},{3,2},{4,5},{5,4},{6,7},{7,6},{8,9},{9,8},{10,11... | collective-permute-start | bytes 196616 | tf_op jit(solution)/shard_map/ppermute | solution.py:253
  57.5 1.6 %collective-permute-start.11 = (f32[64,256]{1,0:T(8,128)S(1)}, f32[64,256]{1,0:T(8,128)S(1)}, u32[]{:S(2)}, u32[]{:S(2)}) collective-permute-start(f32[64,256]{1,0:T(8,128)S(1)} %add.6.refs_0_), channel_id=1, source_target_pairs={{0,6},{1,7},{2,4},{3,5},{4,2},{5,3},{6,0},{7,1},{8,14},{9,15},{10,... | collective-permute-start | bytes 196616 | tf_op jit(solution)/shard_map/ppermute | solution.py:253
  59.3 1.7 %collective-permute-start.9 = (f32[64,256]{1,0:T(8,128)S(1)}, f32[64,256]{1,0:T(8,128)S(1)}, u32[]{:S(2)}, u32[]{:S(2)}) collective-permute-start(f32[64,256]{1,0:T(8,128)S(1)} %add.6.refs_0_), channel_id=1, source_target_pairs={{0,2},{1,5},{2,0},{3,7},{4,6},{5,1},{6,4},{7,3},{8,10},{9,13},{10,... | collective-permute-start | bytes 196616 | tf_op jit(solution)/shard_map/ppermute | solution.py:253
  61.0 1.9 %collective-permute-done.11.refs_3_ = f32[64,256]{1,0:T(8,128)S(1)} collective-permute-done((f32[64,256]{1,0:T(8,128)S(1)}, f32[64,256]{1,0:T(8,128)S(1)}, u32[]{:S(2)}, u32[]{:S(2)}) %collective-permute-start.11) | collective-permute-done | bytes 65568 | tf_op jit(solution)/shard_map/ppermute | solution.py:253
  64.4 1.2 collective-permute-done.12.refs_9_
  66.0 2.7 %collective-permute-start.13 = (bf16[64,1152]{1,0:T(8,128)(2,1)S(1)}, bf16[64,1152]{1,0:T(8,128)(2,1)S(1)}, u32[]{:S(2)}, u32[]{:S(2)}) collective-permute-start(bf16[64,1152]{1,0:T(8,128)(2,1)S(1)} %get-tuple-element.51), channel_id=1, source_target_pairs={{0,8},{1,9},{2,10},{3,11},{4,12},{5,13},{6,14},{7,15},{8,0},{9,1},... | collective-permute-start | bytes 442376 | tf_op jit(solution)/shard_map/ppermute | solution.py:253
  69.4 9.5 %collective-permute-done.13.received = bf16[64,1152]{1,0:T(8,128)(2,1)S(1)} collective-permute-done((bf16[64,1152]{1,0:T(8,128)(2,1)S(1)}, bf16[64,1152]{1,0:T(8,128)(2,1)S(1)}, u32[]{:S(2)}, u32[]{:S(2)}) %collective-permute-start.13) | collective-permute-done | bytes 147488 | tf_op jit(solution)/shard_map/ppermute | solution.py:253
  80.8 2.2 %collective-permute-start.16 = (bf16[64,960]{1,0:T(8,128)(2,1)S(1)}, bf16[64,960]{1,0:T(8,128)(2,1)S(1)}, u32[]{:S(2)}, u32[]{:S(2)}) collective-permute-start(bf16[64,960]{1,0:T(8,128)(2,1)S(1)} %get-tuple-element.57.refs_1_), channel_id=1, source_target_pairs={{0,8},{1,9},{2,10},{3,11},{4,12},{5,13},{6,14},{7,15},{8,0},{9,1},... | collective-permute-start | bytes 368648 | tf_op jit(solution)/shard_map/ppermute | solution.py:253
  83.7 9.8 %collective-permute-done.16.refs_1_ = bf16[64,960]{1,0:T(8,128)(2,1)S(1)} collective-permute-done((bf16[64,960]{1,0:T(8,128)(2,1)S(1)}, bf16[64,960]{1,0:T(8,128)(2,1)S(1)}, u32[]{:S(2)}, u32[]{:S(2)}) %collective-permute-start.16) | collective-permute-done | bytes 122912 | tf_op jit(solution)/shard_map/ppermute | solution.py:253
  94.3 1.3 collective-permute-done.17
  95.6 1.1 collective-permute-start.20
  96.7 1.6 %collective-permute-start.19 = (f32[64,320]{1,0:T(8,128)S(1)}, f32[64,320]{1,0:T(8,128)S(1)}, u32[]{:S(2)}, u32[]{:S(2)}) collective-permute-start(f32[64,320]{1,0:T(8,128)S(1)} %add.7.refs_0_), channel_id=1, source_target_pairs={{0,4},{1,3},{2,6},{3,1},{4,0},{5,7},{6,2},{7,5},{8,12},{9,11},{10,... | collective-permute-start | bytes 245768 | tf_op jit(solution)/shard_map/ppermute | solution.py:253
  99.2 3.1 %collective-permute-done.20.refs_3_ = f32[64,320]{1,0:T(8,128)S(1)} collective-permute-done((f32[64,320]{1,0:T(8,128)S(1)}, f32[64,320]{1,0:T(8,128)S(1)}, u32[]{:S(2)}, u32[]{:S(2)}) %collective-permute-start.20) | collective-permute-done | bytes 81952 | tf_op jit(solution)/shard_map/ppermute | solution.py:253
  102.3 0.9 collective-permute-done.19.refs_2_
  103.3 2.0 %shard_map.38.refs_8_ = bf16[64,256]{1,0:T(8,128)(2,1)S(1)} custom-call(f32[64,320]{1,0:T(8,128)S(1)} %add.7.refs_0_, f32[64,320]{1,0:T(8,128)S(1)} %collective-permute-done.18.refs_1_, f32[64,320]{1,0:T(8,128)S(1)} %collective-permute-done.19.refs_2_, f32[64,320]{1,0:T(8,128)S(1)} %collective-permute-done.20.refs_3_), custom_call_target="tpu_custom_call" | custom-call | flops 15728640 | bytes 327680 | tf_op jit(solution)/shard_map/pallas_call | solution.py:92
  105.3 1.2 collective-permute-done.21.refs_9_
  107.0 1.4 collective-permute-start.22
  108.9 12.3 %collective-permute-done.22.received = bf16[64,1920]{1,0:T(8,128)(2,1)S(1)} collective-permute-done((bf16[64,1920]{1,0:T(8,128)(2,1)S(1)}, bf16[64,1920]{1,0:T(8,128)(2,1)S(1)}, u32[]{:S(2)}, u32[]{:S(2)}) %collective-permute-start.22) | collective-permute-done | bytes 245792 | tf_op jit(solution)/shard_map/ppermute | solution.py:253
  121.8 20.6 %all-gather = f32[1024,64]{1,0:T(8,128)S(1)} all-gather(f32[64,64]{1,0:T(8,128)S(1)} %get-tuple-element.63), channel_id=2, replica_groups=mesh['groups'=2,'cell'=16,'gene'=1] {'cell'}, dimensions={0}, use_global_device_ids=true | all-gather | bytes 278528 | tf_op jit(solution)/shard_map/all_gather | solution.py:296
  142.4 3.0 %shard_map.42 = f32[64,1920]{1,0:T(8,128)} custom-call(f32[16,64,64]{2,1,0:T(8,128)S(1)} %bitcast.3, f32[64,1920]{1,0:T(8,128)S(1)} %get-tuple-element.64.loading), custom_call_target="tpu_custom_call" | custom-call | tf_op jit(solution)/shard_map/pallas_call | solution.py:244
  (36 shorter events, 13.0 us)
Async XLA Ops:
  0.0 2.1 %copy-start = (bf16[64,30720]{1,0:T(8,128)(2,1)S(1)}, bf16[64,30720]{1,0:T(8,128)(2,1)}, u32[]{:S(2)}) copy-start(bf16[64,30720]{1,0:T(8,128)(2,1)} %matrix.1) | copy-start | bytes 11796484
  2.1 4.0 %copy-start.1 = (bf16[1920,64]{0,1:T(8,128)(2,1)S(1)}, bf16[1920,64]{0,1:T(8,128)(2,1)}, u32[]{:S(2)}) copy-start(bf16[1920,64]{0,1:T(8,128)(2,1)} %param.3) | copy-start | bytes 737284
  3.0 3.1 %collective-permute-start = (bf16[64,3840]{1,0:T(8,128)(2,1)S(1)}, bf16[64,3840]{1,0:T(8,128)(2,1)S(1)}, u32[]{:S(2)}, u32[]{:S(2)}) collective-permute-start(bf16[64,3840]{1,0:T(8,128)(2,1)S(1)} %get-tuple-element.36), channel_id=1, source_target_pairs={{0,1},{1,0},{2,3},{3,2},{4,5},{5,4},{6,7},{7,6},{8,9},{9,8},{10,11... | collective-permute-start | bytes 1474568 | tf_op jit(solution)/shard_map/ppermute | solution.py:253
  3.5 18.8 %collective-permute-start.1 = (bf16[64,3840]{1,0:T(8,128)(2,1)S(1)}, bf16[64,3840]{1,0:T(8,128)(2,1)S(1)}, u32[]{:S(2)}, u32[]{:S(2)}) collective-permute-start(bf16[64,3840]{1,0:T(8,128)(2,1)S(1)} %get-tuple-element.38), channel_id=1, source_target_pairs={{0,2},{1,5},{2,0},{3,7},{4,6},{5,1},{6,4},{7,3},{8,10},{9,13},{10,... | collective-permute-start | bytes 1474568 | tf_op jit(solution)/shard_map/ppermute | solution.py:253
  6.1 11.8 %collective-permute-start.6 = (bf16[64,1920]{1,0:T(8,128)(2,1)S(1)}, bf16[64,1920]{1,0:T(8,128)(2,1)S(1)}, u32[]{:S(2)}, u32[]{:S(2)}) collective-permute-start(bf16[64,1920]{1,0:T(8,128)(2,1)S(1)} %bitcast.4), channel_id=1, source_target_pairs={{0,8},{1,9},{2,10},{3,11},{4,12},{5,13},{6,14},{7,15},{8,0},{9,1},... | collective-permute-start | bytes 737288 | tf_op jit(solution)/shard_map/ppermute | solution.py:253
  9.0 21.4 %collective-permute-start.2 = (bf16[64,3840]{1,0:T(8,128)(2,1)S(1)}, bf16[64,3840]{1,0:T(8,128)(2,1)S(1)}, u32[]{:S(2)}, u32[]{:S(2)}) collective-permute-start(bf16[64,3840]{1,0:T(8,128)(2,1)S(1)} %get-tuple-element.39), channel_id=1, source_target_pairs={{0,3},{1,4},{2,1},{3,6},{4,7},{5,0},{6,5},{7,2},{8,11},{9,12},{10,... | collective-permute-start | bytes 1474568 | tf_op jit(solution)/shard_map/ppermute | solution.py:253
  9.9 21.1 %collective-permute-start.3 = (bf16[64,3840]{1,0:T(8,128)(2,1)S(1)}, bf16[64,3840]{1,0:T(8,128)(2,1)S(1)}, u32[]{:S(2)}, u32[]{:S(2)}) collective-permute-start(bf16[64,3840]{1,0:T(8,128)(2,1)S(1)} %get-tuple-element.40), channel_id=1, source_target_pairs={{0,4},{1,3},{2,6},{3,1},{4,0},{5,7},{6,2},{7,5},{8,12},{9,11},{10,... | collective-permute-start | bytes 1474568 | tf_op jit(solution)/shard_map/ppermute | solution.py:253
  11.5 25.0 %collective-permute-start.4 = (bf16[64,3840]{1,0:T(8,128)(2,1)S(1)}, bf16[64,3840]{1,0:T(8,128)(2,1)S(1)}, u32[]{:S(2)}, u32[]{:S(2)}) collective-permute-start(bf16[64,3840]{1,0:T(8,128)(2,1)S(1)} %get-tuple-element.41), channel_id=1, source_target_pairs={{0,5},{1,2},{2,7},{3,0},{4,1},{5,6},{6,3},{7,4},{8,13},{9,10},{10,... | collective-permute-start | bytes 1474568 | tf_op jit(solution)/shard_map/ppermute | solution.py:253
  17.9 30.3 %collective-permute-start.5 = (bf16[64,3840]{1,0:T(8,128)(2,1)S(1)}, bf16[64,3840]{1,0:T(8,128)(2,1)S(1)}, u32[]{:S(2)}, u32[]{:S(2)}) collective-permute-start(bf16[64,3840]{1,0:T(8,128)(2,1)S(1)} %get-tuple-element.42), channel_id=1, source_target_pairs={{0,6},{1,7},{2,4},{3,5},{4,2},{5,3},{6,0},{7,1},{8,14},{9,15},{10,... | collective-permute-start | bytes 1474568 | tf_op jit(solution)/shard_map/ppermute | solution.py:253
  22.3 31.9 %collective-permute-start.7 = (bf16[64,3840]{1,0:T(8,128)(2,1)S(1)}, bf16[64,3840]{1,0:T(8,128)(2,1)S(1)}, u32[]{:S(2)}, u32[]{:S(2)}) collective-permute-start(bf16[64,3840]{1,0:T(8,128)(2,1)S(1)} %get-tuple-element.45), channel_id=1, source_target_pairs={{0,7},{1,6},{2,5},{3,4},{4,3},{5,2},{6,1},{7,0},{8,15},{9,14},{10,... | collective-permute-start | bytes 1474568 | tf_op jit(solution)/shard_map/ppermute | solution.py:253
  54.9 2.6 %collective-permute-start.8 = (f32[64,256]{1,0:T(8,128)S(1)}, f32[64,256]{1,0:T(8,128)S(1)}, u32[]{:S(2)}, u32[]{:S(2)}) collective-permute-start(f32[64,256]{1,0:T(8,128)S(1)} %get-tuple-element.50), channel_id=1, source_target_pairs={{0,1},{1,0},{2,3},{3,2},{4,5},{5,4},{6,7},{7,6},{8,9},{9,8},{10,11... | collective-permute-start | bytes 196616 | tf_op jit(solution)/shard_map/ppermute | solution.py:253
  57.5 5.4 %collective-permute-start.11 = (f32[64,256]{1,0:T(8,128)S(1)}, f32[64,256]{1,0:T(8,128)S(1)}, u32[]{:S(2)}, u32[]{:S(2)}) collective-permute-start(f32[64,256]{1,0:T(8,128)S(1)} %add.6.refs_0_), channel_id=1, source_target_pairs={{0,6},{1,7},{2,4},{3,5},{4,2},{5,3},{6,0},{7,1},{8,14},{9,15},{10,... | collective-permute-start | bytes 196616 | tf_op jit(solution)/shard_map/ppermute | solution.py:253
  59.1 4.6 %collective-permute-start.10 = (f32[64,256]{1,0:T(8,128)S(1)}, f32[64,256]{1,0:T(8,128)S(1)}, u32[]{:S(2)}, u32[]{:S(2)}) collective-permute-start(f32[64,256]{1,0:T(8,128)S(1)} %add.6.refs_0_), channel_id=1, source_target_pairs={{0,4},{1,3},{2,6},{3,1},{4,0},{5,7},{6,2},{7,5},{8,12},{9,11},{10,... | collective-permute-start | bytes 196616 | tf_op jit(solution)/shard_map/ppermute | solution.py:253
  59.3 4.9 %collective-permute-start.9 = (f32[64,256]{1,0:T(8,128)S(1)}, f32[64,256]{1,0:T(8,128)S(1)}, u32[]{:S(2)}, u32[]{:S(2)}) collective-permute-start(f32[64,256]{1,0:T(8,128)S(1)} %add.6.refs_0_), channel_id=1, source_target_pairs={{0,2},{1,5},{2,0},{3,7},{4,6},{5,1},{6,4},{7,3},{8,10},{9,13},{10,... | collective-permute-start | bytes 196616 | tf_op jit(solution)/shard_map/ppermute | solution.py:253
  64.3 1.3 collective-permute-start.12
  66.0 12.9 %collective-permute-start.13 = (bf16[64,1152]{1,0:T(8,128)(2,1)S(1)}, bf16[64,1152]{1,0:T(8,128)(2,1)S(1)}, u32[]{:S(2)}, u32[]{:S(2)}) collective-permute-start(bf16[64,1152]{1,0:T(8,128)(2,1)S(1)} %get-tuple-element.51), channel_id=1, source_target_pairs={{0,8},{1,9},{2,10},{3,11},{4,12},{5,13},{6,14},{7,15},{8,0},{9,1},... | collective-permute-start | bytes 442376 | tf_op jit(solution)/shard_map/ppermute | solution.py:253
  68.7 11.6 %collective-permute-start.15 = (bf16[64,768]{1,0:T(8,128)(2,1)S(1)}, bf16[64,768]{1,0:T(8,128)(2,1)S(1)}, u32[]{:S(2)}, u32[]{:S(2)}) collective-permute-start(bf16[64,768]{1,0:T(8,128)(2,1)S(1)} %get-tuple-element.54), channel_id=1, source_target_pairs={{0,8},{1,9},{2,10},{3,11},{4,12},{5,13},{6,14},{7,15},{8,0},{9,1},... | collective-permute-start | bytes 294920 | tf_op jit(solution)/shard_map/ppermute | solution.py:253
  79.4 14.1 %collective-permute-start.14 = (bf16[64,1152]{1,0:T(8,128)(2,1)S(1)}, bf16[64,1152]{1,0:T(8,128)(2,1)S(1)}, u32[]{:S(2)}, u32[]{:S(2)}) collective-permute-start(bf16[64,1152]{1,0:T(8,128)(2,1)S(1)} %get-tuple-element.53.refs_0_), channel_id=1, source_target_pairs={{0,8},{1,9},{2,10},{3,11},{4,12},{5,13},{6,14},{7,15},{8,0},{9,1},... | collective-permute-start | bytes 442376 | tf_op jit(solution)/shard_map/ppermute | solution.py:253
  80.8 12.7 %collective-permute-start.16 = (bf16[64,960]{1,0:T(8,128)(2,1)S(1)}, bf16[64,960]{1,0:T(8,128)(2,1)S(1)}, u32[]{:S(2)}, u32[]{:S(2)}) collective-permute-start(bf16[64,960]{1,0:T(8,128)(2,1)S(1)} %get-tuple-element.57.refs_1_), channel_id=1, source_target_pairs={{0,8},{1,9},{2,10},{3,11},{4,12},{5,13},{6,14},{7,15},{8,0},{9,1},... | collective-permute-start | bytes 368648 | tf_op jit(solution)/shard_map/ppermute | solution.py:253
  94.2 1.4 collective-permute-start.17
  95.6 6.7 %collective-permute-start.20 = (f32[64,320]{1,0:T(8,128)S(1)}, f32[64,320]{1,0:T(8,128)S(1)}, u32[]{:S(2)}, u32[]{:S(2)}) collective-permute-start(f32[64,320]{1,0:T(8,128)S(1)} %add.7.refs_0_), channel_id=1, source_target_pairs={{0,6},{1,7},{2,4},{3,5},{4,2},{5,3},{6,0},{7,1},{8,14},{9,15},{10,... | collective-permute-start | bytes 245768 | tf_op jit(solution)/shard_map/ppermute | solution.py:253
  96.7 6.5 %collective-permute-start.19 = (f32[64,320]{1,0:T(8,128)S(1)}, f32[64,320]{1,0:T(8,128)S(1)}, u32[]{:S(2)}, u32[]{:S(2)}) collective-permute-start(f32[64,320]{1,0:T(8,128)S(1)} %add.7.refs_0_), channel_id=1, source_target_pairs={{0,4},{1,3},{2,6},{3,1},{4,0},{5,7},{6,2},{7,5},{8,12},{9,11},{10,... | collective-permute-start | bytes 245768 | tf_op jit(solution)/shard_map/ppermute | solution.py:253
  98.2 5.1 %collective-permute-start.18 = (f32[64,320]{1,0:T(8,128)S(1)}, f32[64,320]{1,0:T(8,128)S(1)}, u32[]{:S(2)}, u32[]{:S(2)}) collective-permute-start(f32[64,320]{1,0:T(8,128)S(1)} %add.7.refs_0_), channel_id=1, source_target_pairs={{0,2},{1,5},{2,0},{3,7},{4,6},{5,1},{6,4},{7,3},{8,10},{9,13},{10,... | collective-permute-start | bytes 245768 | tf_op jit(solution)/shard_map/ppermute | solution.py:253
  105.3 1.2 collective-permute-start.21
  107.0 14.2 %collective-permute-start.22 = (bf16[64,1920]{1,0:T(8,128)(2,1)S(1)}, bf16[64,1920]{1,0:T(8,128)(2,1)S(1)}, u32[]{:S(2)}, u32[]{:S(2)}) collective-permute-start(bf16[64,1920]{1,0:T(8,128)(2,1)S(1)} %shard_map.39), channel_id=1, source_target_pairs={{0,8},{1,9},{2,10},{3,11},{4,12},{5,13},{6,14},{7,15},{8,0},{9,1},... | collective-permute-start | bytes 737288 | tf_op jit(solution)/shard_map/ppermute | solution.py:253

commit v9 on v7

--- a/solution.py
+++ b/solution.py
@@ -233,8 +233,20 @@
     return jnp.concatenate(done, axis=0)[:, size:]
 
 
+def sum_of(stack):
+    return (stack[0] + stack[1]) + (stack[2] + stack[3])
+
+
+def sum_kernel(stack, out):
+    out[...] = sum_of(stack)
+
+
+def sum_call(stack):
+    return call(sum_kernel, [stack], [struct(stack.shape[1:], f32)], cost(stack.size, 4 * stack.size))[0]
+
+
 def output_kernel(scale, gram, loading, out):
-    out[...] = exact_nn(inverse_factor(gram[...]), loading[...]) * scale
+    out[...] = exact_nn(inverse_factor(sum_of(gram)), loading[...]) * scale
 
 
 def output_call(gram, loading):
@@ -254,11 +266,9 @@
     return [mate(value, cells, 2, 4), mate(value, cells, 4, 2), mate(value, cells, 6)]
 
 
-def total_over_cells(value, cells):
-    value = value + mate(value, cells, GROUP)
-    value = value + mate(value, cells, 1)
-    one, two, both = legs(value, cells)
-    return (value + both) + (one + two)
+def gathered(value, cells, low, high):
+    groups = [[base, base ^ low, base ^ high, base ^ low ^ high] for base in range(cells) if not base & (low | high)]
+    return lax.all_gather(value, "cell", axis_index_groups=groups)
 
 
 def square_program(cells, expression, start_basis):
@@ -294,7 +304,8 @@
         images = image_from(scores(slots, [(0, (1,)), (1, (1,))], {1: copies}, early, gram[0]), True)
     ((received, own),) = terms_and_received(images, (width,))
     loading, gram = fold(received, own, [], f32, False)
-    return output_call(total_over_cells(gram, cells), loading).T
+    gram = sum_call(gathered(gram, cells, GROUP, 1))
+    return output_call(gathered(gram, cells, 2, 4), loading).T
 
 
 def plain_program(expression, start_basis):

time: 137 us -> 148 us (1.080)
  blocking collectives: 0 us -> 23.1 us
  waiting for transfers between devices: 88 us -> 79.7 us
  starting transfers between devices: 34.2 us -> 30.6 us
    all_gather x0 -> x2, blocking collectives: none -> 23.1 us  [gathered(): return lax.all_gather(value, 'cell', axis_index_groups=groups)]
    ppermute x28 -> x23, waiting for transfers between devices: 88 us -> 79.7 us  [mate(): lax.ppermute(value, 'cell', [(i, i ^ masks[i % 2]) for i in range(cells)])]
    ppermute x28 -> x23, starting transfers between devices: 34.2 us -> 30.6 us  [mate(): lax.ppermute(value, 'cell', [(i, i ^ masks[i % 2]) for i in range(cells)])]
    pallas_call x13 -> x14, Pallas kernels: 8.29 us -> 8.3 us  [call(): pl.pallas_call(kernel, in_specs=[VMEM] * len(args), out_specs=[VMEM] * le...]
  transfers between devices with their start and end apart: 28 -> 23, of which waited for: 23 -> 19; matrix products, arithmetic and copies ran while one was open for 0% -> 0% of each run, Pallas kernels for 2% -> 2%
where the time goes in v9:
time: 148 us
  waiting for transfers between devices  79.7 us (54%)
  starting transfers between devices  30.6 us (21%)
  blocking collectives  23.1 us (16%)
  Pallas kernels  12.1 us (8%)
  local copies, waits for them, and re-layouts  2.12 us (1%)
    ppermute x23, waiting for transfers between devices, mate(): lax.ppermute(value, 'cell', [(i, i ^ masks[i % 2]) for i in range(cells)])  79.7 us
    ppermute x23, starting transfers between devices, mate(): lax.ppermute(value, 'cell', [(i, i ^ masks[i % 2]) for i in range(cells)])  30.6 us
    all_gather x2, blocking collectives, gathered(): return lax.all_gather(value, 'cell', axis_index_groups=groups)  23.1 us
    pallas_call x14, Pallas kernels, call(): pl.pallas_call(kernel, in_specs=[VMEM] * len(args), out_specs=[VMEM] * le...  8.3 us
    pallas_call x1, Pallas kernels, output_call(): pl.pallas_call(functools.partial(output_kernel, math.sqrt(GENES)), in_spe...  2.98 us
  transfers between devices with their start and end apart: 23, of which 19 were waited for; matrix products, arithmetic and copies ran while one was open for 0% of the time, Pallas kernels for 2%

profile of v9, /device:TPU:0, one launch (start us, length us, event | category | flops | bytes accessed | tf_op | source)
XLA Modules:
  0.0 147.9 jit_solution(5186121838610797395)
XLA Ops:
  0.0 2.1 %copy-done = bf16[64,30720]{1,0:T(8,128)(2,1)S(1)} copy-done((bf16[64,30720]{1,0:T(8,128)(2,1)S(1)}, bf16[64,30720]{1,0:T(8,128)(2,1)}, u32[]{:S(2)}) %copy-start) | copy-done | bytes 3932184
  3.5 2.6 %collective-permute-start.1 = (bf16[64,3840]{1,0:T(8,128)(2,1)S(1)}, bf16[64,3840]{1,0:T(8,128)(2,1)S(1)}, u32[]{:S(2)}, u32[]{:S(2)}) collective-permute-start(bf16[64,3840]{1,0:T(8,128)(2,1)S(1)} %get-tuple-element.33), channel_id=1, source_target_pairs={{0,2},{1,5},{2,0},{3,7},{4,6},{5,1},{6,4},{7,3},{8,10},{9,13},{10,... | collective-permute-start | bytes 1474568 | tf_op jit(solution)/shard_map/ppermute | solution.py:262
  6.1 2.6 %collective-permute-start.7 = (bf16[64,1920]{1,0:T(8,128)(2,1)S(1)}, bf16[64,1920]{1,0:T(8,128)(2,1)S(1)}, u32[]{:S(2)}, u32[]{:S(2)}) collective-permute-start(bf16[64,1920]{1,0:T(8,128)(2,1)S(1)} %bitcast.4), channel_id=1, source_target_pairs={{0,8},{1,9},{2,10},{3,11},{4,12},{5,13},{6,14},{7,15},{8,0},{9,1},... | collective-permute-start | bytes 737288 | tf_op jit(solution)/shard_map/ppermute | solution.py:262
  8.7 1.1 collective-permute-start.2
  10.3 7.5 %collective-permute-done.7.refs_1_ = bf16[64,1920]{1,0:T(8,128)(2,1)S(1)} collective-permute-done((bf16[64,1920]{1,0:T(8,128)(2,1)S(1)}, bf16[64,1920]{1,0:T(8,128)(2,1)S(1)}, u32[]{:S(2)}, u32[]{:S(2)}) %collective-permute-start.7) | collective-permute-done | bytes 245792 | tf_op jit(solution)/shard_map/ppermute | solution.py:262
  17.8 5.6 %collective-permute-start.4 = (bf16[64,3840]{1,0:T(8,128)(2,1)S(1)}, bf16[64,3840]{1,0:T(8,128)(2,1)S(1)}, u32[]{:S(2)}, u32[]{:S(2)}) collective-permute-start(bf16[64,3840]{1,0:T(8,128)(2,1)S(1)} %get-tuple-element.36), channel_id=1, source_target_pairs={{0,5},{1,2},{2,7},{3,0},{4,1},{5,6},{6,3},{7,4},{8,13},{9,10},{10,... | collective-permute-start | bytes 1474568 | tf_op jit(solution)/shard_map/ppermute | solution.py:262
  23.4 2.1 %collective-permute-start.6 = (bf16[64,3840]{1,0:T(8,128)(2,1)S(1)}, bf16[64,3840]{1,0:T(8,128)(2,1)S(1)}, u32[]{:S(2)}, u32[]{:S(2)}) collective-permute-start(bf16[64,3840]{1,0:T(8,128)(2,1)S(1)} %get-tuple-element.38), channel_id=1, source_target_pairs={{0,7},{1,6},{2,5},{3,4},{4,3},{5,2},{6,1},{7,0},{8,15},{9,14},{10,... | collective-permute-start | bytes 1474568 | tf_op jit(solution)/shard_map/ppermute | solution.py:262
  25.5 4.9 %collective-permute-done.2.refs_5_.refs_3_ = bf16[64,3840]{1,0:T(8,128)(2,1)S(1)} collective-permute-done((bf16[64,3840]{1,0:T(8,128)(2,1)S(1)}, bf16[64,3840]{1,0:T(8,128)(2,1)S(1)}, u32[]{:S(2)}, u32[]{:S(2)}) %collective-permute-start.2) | collective-permute-done | bytes 491552 | tf_op jit(solution)/shard_map/ppermute | solution.py:262
  31.2 5.0 %collective-permute-done.4.refs_3_.refs_5_.refs_7_ = bf16[64,3840]{1,0:T(8,128)(2,1)S(1)} collective-permute-done((bf16[64,3840]{1,0:T(8,128)(2,1)S(1)}, bf16[64,3840]{1,0:T(8,128)(2,1)S(1)}, u32[]{:S(2)}, u32[]{:S(2)}) %collective-permute-start.4) | collective-permute-done | bytes 491552 | tf_op jit(solution)/shard_map/ppermute | solution.py:262
  36.2 11.8 %collective-permute-done.5.refs_4_.refs_6_.refs_8_ = bf16[64,3840]{1,0:T(8,128)(2,1)S(1)} collective-permute-done((bf16[64,3840]{1,0:T(8,128)(2,1)S(1)}, bf16[64,3840]{1,0:T(8,128)(2,1)S(1)}, u32[]{:S(2)}, u32[]{:S(2)}) %collective-permute-start.5) | collective-permute-done | bytes 491552 | tf_op jit(solution)/shard_map/ppermute | solution.py:262
  48.0 6.1 %collective-permute-done.6.refs_5_.refs_7_.refs_9_ = bf16[64,3840]{1,0:T(8,128)(2,1)S(1)} collective-permute-done((bf16[64,3840]{1,0:T(8,128)(2,1)S(1)}, bf16[64,3840]{1,0:T(8,128)(2,1)S(1)}, u32[]{:S(2)}, u32[]{:S(2)}) %collective-permute-start.6) | collective-permute-done | bytes 491552 | tf_op jit(solution)/shard_map/ppermute | solution.py:262
  54.9 1.7 %collective-permute-start.8 = (f32[64,256]{1,0:T(8,128)S(1)}, f32[64,256]{1,0:T(8,128)S(1)}, u32[]{:S(2)}, u32[]{:S(2)}) collective-permute-start(f32[64,256]{1,0:T(8,128)S(1)} %get-tuple-element.42), channel_id=1, source_target_pairs={{0,1},{1,0},{2,3},{3,2},{4,5},{5,4},{6,7},{7,6},{8,9},{9,8},{10,11... | collective-permute-start | bytes 196616 | tf_op jit(solution)/shard_map/ppermute | solution.py:262
  57.5 1.6 %collective-permute-start.11 = (f32[64,256]{1,0:T(8,128)S(1)}, f32[64,256]{1,0:T(8,128)S(1)}, u32[]{:S(2)}, u32[]{:S(2)}) collective-permute-start(f32[64,256]{1,0:T(8,128)S(1)} %add.6.refs_0_), channel_id=1, source_target_pairs={{0,6},{1,7},{2,4},{3,5},{4,2},{5,3},{6,0},{7,1},{8,14},{9,15},{10,... | collective-permute-start | bytes 196616 | tf_op jit(solution)/shard_map/ppermute | solution.py:262
  59.3 1.7 %collective-permute-start.9 = (f32[64,256]{1,0:T(8,128)S(1)}, f32[64,256]{1,0:T(8,128)S(1)}, u32[]{:S(2)}, u32[]{:S(2)}) collective-permute-start(f32[64,256]{1,0:T(8,128)S(1)} %add.6.refs_0_), channel_id=1, source_target_pairs={{0,2},{1,5},{2,0},{3,7},{4,6},{5,1},{6,4},{7,3},{8,10},{9,13},{10,... | collective-permute-start | bytes 196616 | tf_op jit(solution)/shard_map/ppermute | solution.py:262
  61.0 1.9 %collective-permute-done.11.refs_3_ = f32[64,256]{1,0:T(8,128)S(1)} collective-permute-done((f32[64,256]{1,0:T(8,128)S(1)}, f32[64,256]{1,0:T(8,128)S(1)}, u32[]{:S(2)}, u32[]{:S(2)}) %collective-permute-start.11) | collective-permute-done | bytes 65568 | tf_op jit(solution)/shard_map/ppermute | solution.py:262
  64.4 1.2 collective-permute-done.12.refs_9_
  66.0 2.7 %collective-permute-start.13 = (bf16[64,1152]{1,0:T(8,128)(2,1)S(1)}, bf16[64,1152]{1,0:T(8,128)(2,1)S(1)}, u32[]{:S(2)}, u32[]{:S(2)}) collective-permute-start(bf16[64,1152]{1,0:T(8,128)(2,1)S(1)} %get-tuple-element.43), channel_id=1, source_target_pairs={{0,8},{1,9},{2,10},{3,11},{4,12},{5,13},{6,14},{7,15},{8,0},{9,1},... | collective-permute-start | bytes 442376 | tf_op jit(solution)/shard_map/ppermute | solution.py:262
  69.4 9.5 %collective-permute-done.13.received = bf16[64,1152]{1,0:T(8,128)(2,1)S(1)} collective-permute-done((bf16[64,1152]{1,0:T(8,128)(2,1)S(1)}, bf16[64,1152]{1,0:T(8,128)(2,1)S(1)}, u32[]{:S(2)}, u32[]{:S(2)}) %collective-permute-start.13) | collective-permute-done | bytes 147488 | tf_op jit(solution)/shard_map/ppermute | solution.py:262
  80.8 2.2 %collective-permute-start.16 = (bf16[64,960]{1,0:T(8,128)(2,1)S(1)}, bf16[64,960]{1,0:T(8,128)(2,1)S(1)}, u32[]{:S(2)}, u32[]{:S(2)}) collective-permute-start(bf16[64,960]{1,0:T(8,128)(2,1)S(1)} %get-tuple-element.49.refs_1_), channel_id=1, source_target_pairs={{0,8},{1,9},{2,10},{3,11},{4,12},{5,13},{6,14},{7,15},{8,0},{9,1},... | collective-permute-start | bytes 368648 | tf_op jit(solution)/shard_map/ppermute | solution.py:262
  83.7 9.8 %collective-permute-done.16.refs_1_ = bf16[64,960]{1,0:T(8,128)(2,1)S(1)} collective-permute-done((bf16[64,960]{1,0:T(8,128)(2,1)S(1)}, bf16[64,960]{1,0:T(8,128)(2,1)S(1)}, u32[]{:S(2)}, u32[]{:S(2)}) %collective-permute-start.16) | collective-permute-done | bytes 122912 | tf_op jit(solution)/shard_map/ppermute | solution.py:262
  94.3 1.3 collective-permute-done.17
  95.6 1.1 collective-permute-start.20
  96.7 1.6 %collective-permute-start.19 = (f32[64,320]{1,0:T(8,128)S(1)}, f32[64,320]{1,0:T(8,128)S(1)}, u32[]{:S(2)}, u32[]{:S(2)}) collective-permute-start(f32[64,320]{1,0:T(8,128)S(1)} %add.7.refs_0_), channel_id=1, source_target_pairs={{0,4},{1,3},{2,6},{3,1},{4,0},{5,7},{6,2},{7,5},{8,12},{9,11},{10,... | collective-permute-start | bytes 245768 | tf_op jit(solution)/shard_map/ppermute | solution.py:262
  99.2 3.1 %collective-permute-done.20.refs_3_ = f32[64,320]{1,0:T(8,128)S(1)} collective-permute-done((f32[64,320]{1,0:T(8,128)S(1)}, f32[64,320]{1,0:T(8,128)S(1)}, u32[]{:S(2)}, u32[]{:S(2)}) %collective-permute-start.20) | collective-permute-done | bytes 81952 | tf_op jit(solution)/shard_map/ppermute | solution.py:262
  102.3 0.9 collective-permute-done.19.refs_2_
  103.3 2.0 %shard_map.38.refs_8_ = bf16[64,256]{1,0:T(8,128)(2,1)S(1)} custom-call(f32[64,320]{1,0:T(8,128)S(1)} %add.7.refs_0_, f32[64,320]{1,0:T(8,128)S(1)} %collective-permute-done.18.refs_1_, f32[64,320]{1,0:T(8,128)S(1)} %collective-permute-done.19.refs_2_, f32[64,320]{1,0:T(8,128)S(1)} %collective-permute-done.20.refs_3_), custom_call_target="tpu_custom_call" | custom-call | flops 15728640 | bytes 327680 | tf_op jit(solution)/shard_map/pallas_call | solution.py:92
  105.3 1.2 collective-permute-done.21.refs_9_
  107.0 1.4 collective-permute-start.22
  108.9 12.3 %collective-permute-done.22.received = bf16[64,1920]{1,0:T(8,128)(2,1)S(1)} collective-permute-done((bf16[64,1920]{1,0:T(8,128)(2,1)S(1)}, bf16[64,1920]{1,0:T(8,128)(2,1)S(1)}, u32[]{:S(2)}, u32[]{:S(2)}) %collective-permute-start.22) | collective-permute-done | bytes 245792 | tf_op jit(solution)/shard_map/ppermute | solution.py:262
  121.8 11.7 %all-gather = f32[256,64]{1,0:T(8,128)S(1)} all-gather(f32[64,64]{1,0:T(8,128)S(1)} %get-tuple-element.55), channel_id=2, replica_groups={{0,8,1,9},{2,10,3,11},{4,12,5,13},{6,14,7,15},{16,24,17,25},{18,26,19,2..., dimensions={0}, use_global_device_ids=true | all-gather | bytes 81920 | tf_op jit(solution)/shard_map/all_gather | solution.py:271
  133.5 11.4 %all-gather.1 = f32[256,64]{1,0:T(8,128)S(1)} all-gather(f32[64,64]{1,0:T(8,128)S(1)} %shard_map.42), channel_id=3, replica_groups={{0,2,4,6},{1,3,5,7},{8,10,12,14},{9,11,13,15},{16,18,20,22},{17,19,21,2..., dimensions={0}, use_global_device_ids=true | all-gather | bytes 81920 | tf_op jit(solution)/shard_map/all_gather | solution.py:271
  144.9 3.0 %shard_map.43 = f32[64,1920]{1,0:T(8,128)} custom-call(f32[4,64,64]{2,1,0:T(8,128)S(1)} %bitcast.7, f32[64,1920]{1,0:T(8,128)S(1)} %get-tuple-element.56.loading), custom_call_target="tpu_custom_call" | custom-call | tf_op jit(solution)/shard_map/pallas_call | solution.py:253
  (38 shorter events, 13.1 us)
Async XLA Ops:
  0.0 2.1 %copy-start = (bf16[64,30720]{1,0:T(8,128)(2,1)S(1)}, bf16[64,30720]{1,0:T(8,128)(2,1)}, u32[]{:S(2)}) copy-start(bf16[64,30720]{1,0:T(8,128)(2,1)} %matrix.1) | copy-start | bytes 11796484
  2.1 4.0 %copy-start.1 = (bf16[1920,64]{0,1:T(8,128)(2,1)S(1)}, bf16[1920,64]{0,1:T(8,128)(2,1)}, u32[]{:S(2)}) copy-start(bf16[1920,64]{0,1:T(8,128)(2,1)} %param.3) | copy-start | bytes 737284
  3.0 20.4 %collective-permute-start = (bf16[64,3840]{1,0:T(8,128)(2,1)S(1)}, bf16[64,3840]{1,0:T(8,128)(2,1)S(1)}, u32[]{:S(2)}, u32[]{:S(2)}) collective-permute-start(bf16[64,3840]{1,0:T(8,128)(2,1)S(1)} %get-tuple-element.32), channel_id=1, source_target_pairs={{0,1},{1,0},{2,3},{3,2},{4,5},{5,4},{6,7},{7,6},{8,9},{9,8},{10,11... | collective-permute-start | bytes 1474568 | tf_op jit(solution)/shard_map/ppermute | solution.py:262
  3.5 19.9 %collective-permute-start.1 = (bf16[64,3840]{1,0:T(8,128)(2,1)S(1)}, bf16[64,3840]{1,0:T(8,128)(2,1)S(1)}, u32[]{:S(2)}, u32[]{:S(2)}) collective-permute-start(bf16[64,3840]{1,0:T(8,128)(2,1)S(1)} %get-tuple-element.33), channel_id=1, source_target_pairs={{0,2},{1,5},{2,0},{3,7},{4,6},{5,1},{6,4},{7,3},{8,10},{9,13},{10,... | collective-permute-start | bytes 1474568 | tf_op jit(solution)/shard_map/ppermute | solution.py:262
  6.1 11.7 %collective-permute-start.7 = (bf16[64,1920]{1,0:T(8,128)(2,1)S(1)}, bf16[64,1920]{1,0:T(8,128)(2,1)S(1)}, u32[]{:S(2)}, u32[]{:S(2)}) collective-permute-start(bf16[64,1920]{1,0:T(8,128)(2,1)S(1)} %bitcast.4), channel_id=1, source_target_pairs={{0,8},{1,9},{2,10},{3,11},{4,12},{5,13},{6,14},{7,15},{8,0},{9,1},... | collective-permute-start | bytes 737288 | tf_op jit(solution)/shard_map/ppermute | solution.py:262
  8.7 21.8 %collective-permute-start.2 = (bf16[64,3840]{1,0:T(8,128)(2,1)S(1)}, bf16[64,3840]{1,0:T(8,128)(2,1)S(1)}, u32[]{:S(2)}, u32[]{:S(2)}) collective-permute-start(bf16[64,3840]{1,0:T(8,128)(2,1)S(1)} %get-tuple-element.34), channel_id=1, source_target_pairs={{0,3},{1,4},{2,1},{3,6},{4,7},{5,0},{6,5},{7,2},{8,11},{9,12},{10,... | collective-permute-start | bytes 1474568 | tf_op jit(solution)/shard_map/ppermute | solution.py:262
  9.7 21.4 %collective-permute-start.3 = (bf16[64,3840]{1,0:T(8,128)(2,1)S(1)}, bf16[64,3840]{1,0:T(8,128)(2,1)S(1)}, u32[]{:S(2)}, u32[]{:S(2)}) collective-permute-start(bf16[64,3840]{1,0:T(8,128)(2,1)S(1)} %get-tuple-element.35), channel_id=1, source_target_pairs={{0,4},{1,3},{2,6},{3,1},{4,0},{5,7},{6,2},{7,5},{8,12},{9,11},{10,... | collective-permute-start | bytes 1474568 | tf_op jit(solution)/shard_map/ppermute | solution.py:262
  17.8 18.4 %collective-permute-start.4 = (bf16[64,3840]{1,0:T(8,128)(2,1)S(1)}, bf16[64,3840]{1,0:T(8,128)(2,1)S(1)}, u32[]{:S(2)}, u32[]{:S(2)}) collective-permute-start(bf16[64,3840]{1,0:T(8,128)(2,1)S(1)} %get-tuple-element.36), channel_id=1, source_target_pairs={{0,5},{1,2},{2,7},{3,0},{4,1},{5,6},{6,3},{7,4},{8,13},{9,10},{10,... | collective-permute-start | bytes 1474568 | tf_op jit(solution)/shard_map/ppermute | solution.py:262
  23.4 24.6 %collective-permute-start.5 = (bf16[64,3840]{1,0:T(8,128)(2,1)S(1)}, bf16[64,3840]{1,0:T(8,128)(2,1)S(1)}, u32[]{:S(2)}, u32[]{:S(2)}) collective-permute-start(bf16[64,3840]{1,0:T(8,128)(2,1)S(1)} %get-tuple-element.37), channel_id=1, source_target_pairs={{0,6},{1,7},{2,4},{3,5},{4,2},{5,3},{6,0},{7,1},{8,14},{9,15},{10,... | collective-permute-start | bytes 1474568 | tf_op jit(solution)/shard_map/ppermute | solution.py:262
  23.4 30.7 %collective-permute-start.6 = (bf16[64,3840]{1,0:T(8,128)(2,1)S(1)}, bf16[64,3840]{1,0:T(8,128)(2,1)S(1)}, u32[]{:S(2)}, u32[]{:S(2)}) collective-permute-start(bf16[64,3840]{1,0:T(8,128)(2,1)S(1)} %get-tuple-element.38), channel_id=1, source_target_pairs={{0,7},{1,6},{2,5},{3,4},{4,3},{5,2},{6,1},{7,0},{8,15},{9,14},{10,... | collective-permute-start | bytes 1474568 | tf_op jit(solution)/shard_map/ppermute | solution.py:262
  54.9 2.6 %collective-permute-start.8 = (f32[64,256]{1,0:T(8,128)S(1)}, f32[64,256]{1,0:T(8,128)S(1)}, u32[]{:S(2)}, u32[]{:S(2)}) collective-permute-start(f32[64,256]{1,0:T(8,128)S(1)} %get-tuple-element.42), channel_id=1, source_target_pairs={{0,1},{1,0},{2,3},{3,2},{4,5},{5,4},{6,7},{7,6},{8,9},{9,8},{10,11... | collective-permute-start | bytes 196616 | tf_op jit(solution)/shard_map/ppermute | solution.py:262
  57.5 5.4 %collective-permute-start.11 = (f32[64,256]{1,0:T(8,128)S(1)}, f32[64,256]{1,0:T(8,128)S(1)}, u32[]{:S(2)}, u32[]{:S(2)}) collective-permute-start(f32[64,256]{1,0:T(8,128)S(1)} %add.6.refs_0_), channel_id=1, source_target_pairs={{0,6},{1,7},{2,4},{3,5},{4,2},{5,3},{6,0},{7,1},{8,14},{9,15},{10,... | collective-permute-start | bytes 196616 | tf_op jit(solution)/shard_map/ppermute | solution.py:262
  59.1 4.7 %collective-permute-start.10 = (f32[64,256]{1,0:T(8,128)S(1)}, f32[64,256]{1,0:T(8,128)S(1)}, u32[]{:S(2)}, u32[]{:S(2)}) collective-permute-start(f32[64,256]{1,0:T(8,128)S(1)} %add.6.refs_0_), channel_id=1, source_target_pairs={{0,4},{1,3},{2,6},{3,1},{4,0},{5,7},{6,2},{7,5},{8,12},{9,11},{10,... | collective-permute-start | bytes 196616 | tf_op jit(solution)/shard_map/ppermute | solution.py:262
  59.3 4.9 %collective-permute-start.9 = (f32[64,256]{1,0:T(8,128)S(1)}, f32[64,256]{1,0:T(8,128)S(1)}, u32[]{:S(2)}, u32[]{:S(2)}) collective-permute-start(f32[64,256]{1,0:T(8,128)S(1)} %add.6.refs_0_), channel_id=1, source_target_pairs={{0,2},{1,5},{2,0},{3,7},{4,6},{5,1},{6,4},{7,3},{8,10},{9,13},{10,... | collective-permute-start | bytes 196616 | tf_op jit(solution)/shard_map/ppermute | solution.py:262
  64.3 1.3 collective-permute-start.12
  66.0 12.9 %collective-permute-start.13 = (bf16[64,1152]{1,0:T(8,128)(2,1)S(1)}, bf16[64,1152]{1,0:T(8,128)(2,1)S(1)}, u32[]{:S(2)}, u32[]{:S(2)}) collective-permute-start(bf16[64,1152]{1,0:T(8,128)(2,1)S(1)} %get-tuple-element.43), channel_id=1, source_target_pairs={{0,8},{1,9},{2,10},{3,11},{4,12},{5,13},{6,14},{7,15},{8,0},{9,1},... | collective-permute-start | bytes 442376 | tf_op jit(solution)/shard_map/ppermute | solution.py:262
  68.7 11.6 %collective-permute-start.15 = (bf16[64,768]{1,0:T(8,128)(2,1)S(1)}, bf16[64,768]{1,0:T(8,128)(2,1)S(1)}, u32[]{:S(2)}, u32[]{:S(2)}) collective-permute-start(bf16[64,768]{1,0:T(8,128)(2,1)S(1)} %get-tuple-element.46), channel_id=1, source_target_pairs={{0,8},{1,9},{2,10},{3,11},{4,12},{5,13},{6,14},{7,15},{8,0},{9,1},... | collective-permute-start | bytes 294920 | tf_op jit(solution)/shard_map/ppermute | solution.py:262
  79.4 14.1 %collective-permute-start.14 = (bf16[64,1152]{1,0:T(8,128)(2,1)S(1)}, bf16[64,1152]{1,0:T(8,128)(2,1)S(1)}, u32[]{:S(2)}, u32[]{:S(2)}) collective-permute-start(bf16[64,1152]{1,0:T(8,128)(2,1)S(1)} %get-tuple-element.45.refs_0_), channel_id=1, source_target_pairs={{0,8},{1,9},{2,10},{3,11},{4,12},{5,13},{6,14},{7,15},{8,0},{9,1},... | collective-permute-start | bytes 442376 | tf_op jit(solution)/shard_map/ppermute | solution.py:262
  80.8 12.7 %collective-permute-start.16 = (bf16[64,960]{1,0:T(8,128)(2,1)S(1)}, bf16[64,960]{1,0:T(8,128)(2,1)S(1)}, u32[]{:S(2)}, u32[]{:S(2)}) collective-permute-start(bf16[64,960]{1,0:T(8,128)(2,1)S(1)} %get-tuple-element.49.refs_1_), channel_id=1, source_target_pairs={{0,8},{1,9},{2,10},{3,11},{4,12},{5,13},{6,14},{7,15},{8,0},{9,1},... | collective-permute-start | bytes 368648 | tf_op jit(solution)/shard_map/ppermute | solution.py:262
  94.2 1.4 collective-permute-start.17
  95.6 6.7 %collective-permute-start.20 = (f32[64,320]{1,0:T(8,128)S(1)}, f32[64,320]{1,0:T(8,128)S(1)}, u32[]{:S(2)}, u32[]{:S(2)}) collective-permute-start(f32[64,320]{1,0:T(8,128)S(1)} %add.7.refs_0_), channel_id=1, source_target_pairs={{0,6},{1,7},{2,4},{3,5},{4,2},{5,3},{6,0},{7,1},{8,14},{9,15},{10,... | collective-permute-start | bytes 245768 | tf_op jit(solution)/shard_map/ppermute | solution.py:262
  96.7 6.5 %collective-permute-start.19 = (f32[64,320]{1,0:T(8,128)S(1)}, f32[64,320]{1,0:T(8,128)S(1)}, u32[]{:S(2)}, u32[]{:S(2)}) collective-permute-start(f32[64,320]{1,0:T(8,128)S(1)} %add.7.refs_0_), channel_id=1, source_target_pairs={{0,4},{1,3},{2,6},{3,1},{4,0},{5,7},{6,2},{7,5},{8,12},{9,11},{10,... | collective-permute-start | bytes 245768 | tf_op jit(solution)/shard_map/ppermute | solution.py:262
  98.2 5.1 %collective-permute-start.18 = (f32[64,320]{1,0:T(8,128)S(1)}, f32[64,320]{1,0:T(8,128)S(1)}, u32[]{:S(2)}, u32[]{:S(2)}) collective-permute-start(f32[64,320]{1,0:T(8,128)S(1)} %add.7.refs_0_), channel_id=1, source_target_pairs={{0,2},{1,5},{2,0},{3,7},{4,6},{5,1},{6,4},{7,3},{8,10},{9,13},{10,... | collective-permute-start | bytes 245768 | tf_op jit(solution)/shard_map/ppermute | solution.py:262
  105.3 1.2 collective-permute-start.21
  107.0 14.2 %collective-permute-start.22 = (bf16[64,1920]{1,0:T(8,128)(2,1)S(1)}, bf16[64,1920]{1,0:T(8,128)(2,1)S(1)}, u32[]{:S(2)}, u32[]{:S(2)}) collective-permute-start(bf16[64,1920]{1,0:T(8,128)(2,1)S(1)} %shard_map.39), channel_id=1, source_target_pairs={{0,8},{1,9},{2,10},{3,11},{4,12},{5,13},{6,14},{7,15},{8,0},{9,1},... | collective-permute-start | bytes 737288 | tf_op jit(solution)/shard_map/ppermute | solution.py:262

commit v10 on v7

--- a/solution.py
+++ b/solution.py
@@ -95,23 +95,22 @@
     )(*args)
 
 
-def scores_kernel(work, counts, picked, with_gram, width, *refs):
+def scores_kernel(work, counts, picked, with_gram, width, offset, *refs):
     refs = list(refs)
     bases = {block: [refs.pop(0) for _ in range(count)] for block, count in counts}
     slots = {k: refs.pop(0) for k in picked}
     gram = refs.pop(0)[...] if with_gram else None
     before, outs = refs[:-2], refs[-2:]
-    rank = gram.shape[0] if with_gram else 0
     for odd in range(2):
         left = 0
         for pair, blocks in work:
             value = 0.0
             for block in blocks:
-                start = block * width
+                start = block * width + offset
                 for part in bases[block]:
-                    stop = min(start + part.shape[1], (block + 1) * width)
+                    stop = start + part.shape[1]
                     big = [slots[4 * pair + odd][:, start:stop], slots[4 * pair + 2 + odd][:, start:stop]]
-                    value = value + nt(jnp.concatenate(big, axis=0), part[:, :stop - start])
+                    value = value + nt(jnp.concatenate(big, axis=0), part[...])
                     start = stop
             lanes = slice(left, left + 2 * next(iter(slots.values())).shape[0])
             left = lanes.stop
@@ -121,13 +120,10 @@
                 value = value + before[odd][:, lanes]
             outs[odd][:, lanes] = value
         if with_gram:
-            tail = bases[counts[-1][0]][-1]
-            first = tail.shape[1] - 3 * rank
-            theirs = [tail[:, first + i * rank:first + (i + 1) * rank].astype(f32) for i in range(3)]
-            outs[odd][:, left:] = gram + ((theirs[0] + theirs[1]) + theirs[2])
-
-
-def scores(slots, work, bases, before=(), gram=None):
+            outs[odd][:, left:] = gram
+
+
+def scores(slots, work, bases, before=(), gram=None, offset=0):
     rank = next(iter(bases.values()))[0].shape[0]
     picked = [4 * pair + k for pair, blocks in work if blocks for k in range(4)]
     rows, width = slots[picked[0]].shape[0], slots[picked[0]].shape[1] // 2
@@ -136,7 +132,7 @@
     args = [x for parts in bases.values() for x in parts] + [slots[k] for k in picked]
     args += ([] if gram is None else [gram]) + list(before)
     size = 4 * rows * width * sum(len(blocks) for _, blocks in work)
-    kernel = functools.partial(scores_kernel, work, counts, picked, gram is not None, width)
+    kernel = functools.partial(scores_kernel, work, counts, picked, gram is not None, width, offset)
     return call(kernel, args, [struct((rank, cells), f32)] * 2, cost(2 * rank * size, 2 * size))
 
 
@@ -161,46 +157,58 @@
                 cost(12 * value.size * rank, 16 * value.size))[0]
 
 
-def terms_kernel(block, width, *refs):
-    slots, images, outs = refs[:GROUP], refs[GROUP:GROUP + 2], refs[GROUP + 2:]
-    start = block * width
-    for out in outs:
-        step = out.shape[1] // 2 if out.shape[1] % 256 == 0 else out.shape[1]
-        for left in range(0, out.shape[1], step):
+def terms_kernel(starts, *refs):
+    slots, images, out = refs[:GROUP], refs[GROUP:GROUP + 2], refs[-1]
+    width = out.shape[1]
+    rank = out.shape[0] // len(starts)
+    step = width // 2 if width % 256 == 0 else width
+    for part, start in enumerate(starts):
+        for left in range(0, width, step):
             total = 0.0
             for odd in range(2):
-                big = jnp.concatenate([ref[:, start:start + step] for ref in slots[odd::2]], axis=0)
+                big = jnp.concatenate([ref[:, start + left:start + left + step] for ref in slots[odd::2]], axis=0)
                 total = total + nn(images[odd][...], big)
-            out[:, left:left + step] = total.astype(out.dtype)
-            start += step
-
-
-def terms(slots, block, images, cuts, dtype):
-    rank, width = images[0].shape[0], slots[0].shape[1] // 2
-    cells = slots[0].shape[0] * GROUP
-    return call(functools.partial(terms_kernel, block, width), [*slots, *images], [struct((rank, w), dtype) for w in cuts],
-                cost(2 * rank * cells * width, 2 * cells * width))
-
-
-def fold_kernel(final, received, own, *refs):
-    before, outs = refs[:-2], refs[-2:]
-    width = own.shape[1]
+            out[part * rank:(part + 1) * rank, left:left + step] = total.astype(out.dtype)
+
+
+def terms(slots, starts, width, images, dtype):
+    rank, cells = images[0].shape[0], slots[0].shape[0] * GROUP
+    size = cells * width * len(starts)
+    return call(functools.partial(terms_kernel, starts), [*slots, *images],
+                [struct((rank * len(starts), width), dtype)], cost(2 * rank * size, 2 * size))[0]
+
+
+def both_kernel(sent, received, *refs):
+    before, rows, gram = refs[:-3], refs[-3:-1], refs[-1]
+    rank = rows[0].shape[0]
+    grams = []
+    for block in range(2):
+        mine, theirs = slice(block * rank, (block + 1) * rank), slice((1 - block) * rank, (2 - block) * rank)
+        value = sent[mine].astype(f32) + received[theirs].astype(f32)
+        rows[block][...] = value.astype(bf16)
+        grams.append(exact_gram(value))
+    total = grams[0] + grams[1]
+    for ref in before:
+        total = total + ref[...]
+    gram[...] = total
+
+
+def both(sent, received, before):
+    rank, width = sent.shape[0] // 2, sent.shape[1]
+    return call(both_kernel, [sent, received, *before], [struct((rank, width), bf16)] * 2 + [struct((rank, rank), f32)],
+                cost(24 * rank * rank * width, 24 * rank * width))
+
+
+def loading_kernel(received, own, loading, gram):
     value = own[...] + received[...].astype(f32)
-    outs[0][:, :width] = value.astype(outs[0].dtype)
-    gram = exact_gram(value)
-    for ref in before:
-        gram = gram + ref[...]
-    outs[1][...] = gram
-    if final:
-        for i, part in enumerate(three(gram)):
-            outs[0][:, width + i * part.shape[1]:width + (i + 1) * part.shape[1]] = part
-
-
-def fold(received, own, before, dtype, final):
+    loading[...] = value
+    gram[...] = exact_gram(value)
+
+
+def loading_and_gram(received, own):
     rank, width = own.shape
-    return call(functools.partial(fold_kernel, final), [received, own, *before],
-                [struct((rank, width + (3 * rank if final else 0)), dtype), struct((rank, rank), f32)],
-                cost(12 * rank * own.size, 12 * own.size))
+    return call(loading_kernel, [received, own], [struct((rank, width), f32), struct((rank, rank), f32)],
+                cost(12 * rank * rank * width, 12 * rank * width))
 
 
 def inverse_factor(gram):
@@ -255,10 +263,9 @@
 
 
 def total_over_cells(value, cells):
-    value = value + mate(value, cells, GROUP)
-    value = value + mate(value, cells, 1)
-    one, two, both = legs(value, cells)
-    return (value + both) + (one + two)
+    value = (value + mate(value, cells, GROUP | 1)) + (mate(value, cells, GROUP) + mate(value, cells, 1))
+    one, two, both_ways = legs(value, cells)
+    return (value + both_ways) + (one + two)
 
 
 def square_program(cells, expression, start_basis):
@@ -272,11 +279,6 @@
         even = even + mate(odd, cells, 1)
         image = image_of(even, legs(even, cells), rows, normalised)
         return image, mate(image, cells, 1)
-
-    def terms_and_received(images, cuts):
-        sent = terms(slots, 1, images, cuts, bf16)
-        own = terms(slots, 0, images, cuts, f32)
-        return zip([mate(x, cells, GROUP) for x in sent], own)
 
     first = -(-6 * width // 1280) * 128
     basis = start_basis.T
@@ -284,16 +286,16 @@
     early = scores(slots, [(0, (0, 1))], bases)
     images = image_from(scores(slots, [(0, ()), (1, (0, 1))], bases, early), False)
     for _ in range(1, ITERS):
-        parts, copies, gram = [], [], []
-        for received, own in terms_and_received(images, (first, width - first)):
-            part, total = fold(received, own, gram, bf16, bool(parts))
+        totals, gram = (), []
+        for start, stop in ((0, first), (first, width)):
+            sent = terms(slots, (start, width + start), stop - start, images, bf16)
+            own, other, total = both(sent, mate(sent, cells, GROUP), gram)
             gram = [total]
-            parts.append(part)
-            copies.append(mate(part, cells, GROUP))
-        early = scores(slots, [(0, (0,)), (1, (0,))], {0: parts})
-        images = image_from(scores(slots, [(0, (1,)), (1, (1,))], {1: copies}, early, gram[0]), True)
-    ((received, own),) = terms_and_received(images, (width,))
-    loading, gram = fold(received, own, [], f32, False)
+            totals = scores(slots, [(0, (0, 1)), (1, (0, 1))], {0: [own], 1: [other]}, totals,
+                            total if stop == width else None, start)
+        images = image_from(totals, True)
+    received = mate(terms(slots, (width,), width, images, bf16), cells, GROUP)
+    loading, gram = loading_and_gram(received, terms(slots, (0,), width, images, f32))
     return output_call(total_over_cells(gram, cells), loading).T
 
 

time: 137 us -> 137 us (level)
  starting transfers between devices: 34.2 us -> 36.6 us
  waiting for transfers between devices: 88 us -> 85.7 us
    ppermute x28 -> x27, starting transfers between devices: 34.2 us -> 36.6 us  [mate(): lax.ppermute(value, 'cell', [(i, i ^ masks[i % 2]) for i in range(cells)])]
    ppermute x28 -> x27, waiting for transfers between devices: 88 us -> 85.7 us  [mate(): lax.ppermute(value, 'cell', [(i, i ^ masks[i % 2]) for i in range(cells)])]
  transfers between devices with their start and end apart: 28 -> 27, of which waited for: 23 -> 22; matrix products, arithmetic and copies ran while one was open for 0% -> 0% of each run, Pallas kernels for 2% -> 2%
where the time goes in v10:
time: 137 us
  waiting for transfers between devices  85.7 us (63%)
  starting transfers between devices  36.6 us (27%)
  Pallas kernels  12.3 us (9%)
  local copies, waits for them, and re-layouts  2.12 us (2%)
    ppermute x27, waiting for transfers between devices, mate(): lax.ppermute(value, 'cell', [(i, i ^ masks[i % 2]) for i in range(cells)])  85.7 us
    ppermute x27, starting transfers between devices, mate(): lax.ppermute(value, 'cell', [(i, i ^ masks[i % 2]) for i in range(cells)])  36.6 us
    pallas_call x13, Pallas kernels, call(): pl.pallas_call(kernel, in_specs=[VMEM] * len(args), out_specs=[VMEM] * le...  8.41 us
    pallas_call x1, Pallas kernels, output_call(): pl.pallas_call(functools.partial(output_kernel, math.sqrt(GENES)), in_spe...  2.98 us
  transfers between devices with their start and end apart: 27, of which 22 were waited for; matrix products, arithmetic and copies ran while one was open for 0% of the time, Pallas kernels for 2%

profile of v10, /device:TPU:0, one launch (start us, length us, event | category | flops | bytes accessed | tf_op | source)
XLA Modules:
  0.0 136.8 jit_solution(8493386275791256994)
XLA Ops:
  0.0 2.1 %copy-done = bf16[64,30720]{1,0:T(8,128)(2,1)S(1)} copy-done((bf16[64,30720]{1,0:T(8,128)(2,1)S(1)}, bf16[64,30720]{1,0:T(8,128)(2,1)}, u32[]{:S(2)}) %copy-start) | copy-done | bytes 3932184
  3.5 2.6 %collective-permute-start.1 = (bf16[64,3840]{1,0:T(8,128)(2,1)S(1)}, bf16[64,3840]{1,0:T(8,128)(2,1)S(1)}, u32[]{:S(2)}, u32[]{:S(2)}) collective-permute-start(bf16[64,3840]{1,0:T(8,128)(2,1)S(1)} %get-tuple-element.31), channel_id=1, source_target_pairs={{0,2},{1,5},{2,0},{3,7},{4,6},{5,1},{6,4},{7,3},{8,10},{9,13},{10,... | collective-permute-start | bytes 1474568 | tf_op jit(solution)/shard_map/ppermute | solution.py:258
  6.1 2.6 %collective-permute-start.7 = (bf16[64,1920]{1,0:T(8,128)(2,1)S(1)}, bf16[64,1920]{1,0:T(8,128)(2,1)S(1)}, u32[]{:S(2)}, u32[]{:S(2)}) collective-permute-start(bf16[64,1920]{1,0:T(8,128)(2,1)S(1)} %bitcast.2), channel_id=1, source_target_pairs={{0,8},{1,9},{2,10},{3,11},{4,12},{5,13},{6,14},{7,15},{8,0},{9,1},... | collective-permute-start | bytes 737288 | tf_op jit(solution)/shard_map/ppermute | solution.py:258
  10.3 7.5 %collective-permute-done.7.refs_1_ = bf16[64,1920]{1,0:T(8,128)(2,1)S(1)} collective-permute-done((bf16[64,1920]{1,0:T(8,128)(2,1)S(1)}, bf16[64,1920]{1,0:T(8,128)(2,1)S(1)}, u32[]{:S(2)}, u32[]{:S(2)}) %collective-permute-start.7) | collective-permute-done | bytes 245792 | tf_op jit(solution)/shard_map/ppermute | solution.py:258
  17.8 5.6 %collective-permute-start.4 = (bf16[64,3840]{1,0:T(8,128)(2,1)S(1)}, bf16[64,3840]{1,0:T(8,128)(2,1)S(1)}, u32[]{:S(2)}, u32[]{:S(2)}) collective-permute-start(bf16[64,3840]{1,0:T(8,128)(2,1)S(1)} %get-tuple-element.34), channel_id=1, source_target_pairs={{0,5},{1,2},{2,7},{3,0},{4,1},{5,6},{6,3},{7,4},{8,13},{9,10},{10,... | collective-permute-start | bytes 1474568 | tf_op jit(solution)/shard_map/ppermute | solution.py:258
  23.4 2.1 %collective-permute-start.6 = (bf16[64,3840]{1,0:T(8,128)(2,1)S(1)}, bf16[64,3840]{1,0:T(8,128)(2,1)S(1)}, u32[]{:S(2)}, u32[]{:S(2)}) collective-permute-start(bf16[64,3840]{1,0:T(8,128)(2,1)S(1)} %get-tuple-element.36), channel_id=1, source_target_pairs={{0,7},{1,6},{2,5},{3,4},{4,3},{5,2},{6,1},{7,0},{8,15},{9,14},{10,... | collective-permute-start | bytes 1474568 | tf_op jit(solution)/shard_map/ppermute | solution.py:258
  25.5 4.9 %collective-permute-done.2.refs_5_.refs_3_ = bf16[64,3840]{1,0:T(8,128)(2,1)S(1)} collective-permute-done((bf16[64,3840]{1,0:T(8,128)(2,1)S(1)}, bf16[64,3840]{1,0:T(8,128)(2,1)S(1)}, u32[]{:S(2)}, u32[]{:S(2)}) %collective-permute-start.2) | collective-permute-done | bytes 491552 | tf_op jit(solution)/shard_map/ppermute | solution.py:258
  31.2 5.0 %collective-permute-done.4.refs_3_.refs_5_.refs_7_ = bf16[64,3840]{1,0:T(8,128)(2,1)S(1)} collective-permute-done((bf16[64,3840]{1,0:T(8,128)(2,1)S(1)}, bf16[64,3840]{1,0:T(8,128)(2,1)S(1)}, u32[]{:S(2)}, u32[]{:S(2)}) %collective-permute-start.4) | collective-permute-done | bytes 491552 | tf_op jit(solution)/shard_map/ppermute | solution.py:258
  36.2 11.8 %collective-permute-done.5.refs_4_.refs_6_.refs_8_ = bf16[64,3840]{1,0:T(8,128)(2,1)S(1)} collective-permute-done((bf16[64,3840]{1,0:T(8,128)(2,1)S(1)}, bf16[64,3840]{1,0:T(8,128)(2,1)S(1)}, u32[]{:S(2)}, u32[]{:S(2)}) %collective-permute-start.5) | collective-permute-done | bytes 491552 | tf_op jit(solution)/shard_map/ppermute | solution.py:258
  48.0 6.1 %collective-permute-done.6.refs_5_.refs_7_.refs_9_ = bf16[64,3840]{1,0:T(8,128)(2,1)S(1)} collective-permute-done((bf16[64,3840]{1,0:T(8,128)(2,1)S(1)}, bf16[64,3840]{1,0:T(8,128)(2,1)S(1)}, u32[]{:S(2)}, u32[]{:S(2)}) %collective-permute-start.6) | collective-permute-done | bytes 491552 | tf_op jit(solution)/shard_map/ppermute | solution.py:258
  54.9 1.7 %collective-permute-start.8 = (f32[64,256]{1,0:T(8,128)S(1)}, f32[64,256]{1,0:T(8,128)S(1)}, u32[]{:S(2)}, u32[]{:S(2)}) collective-permute-start(f32[64,256]{1,0:T(8,128)S(1)} %get-tuple-element.40), channel_id=1, source_target_pairs={{0,1},{1,0},{2,3},{3,2},{4,5},{5,4},{6,7},{7,6},{8,9},{9,8},{10,11... | collective-permute-start | bytes 196616 | tf_op jit(solution)/shard_map/ppermute | solution.py:258
  57.5 1.6 %collective-permute-start.10 = (f32[64,256]{1,0:T(8,128)S(1)}, f32[64,256]{1,0:T(8,128)S(1)}, u32[]{:S(2)}, u32[]{:S(2)}) collective-permute-start(f32[64,256]{1,0:T(8,128)S(1)} %add.24.refs_0_), channel_id=1, source_target_pairs={{0,4},{1,3},{2,6},{3,1},{4,0},{5,7},{6,2},{7,5},{8,12},{9,11},{10,... | collective-permute-start | bytes 196616 | tf_op jit(solution)/shard_map/ppermute | solution.py:258
  59.3 1.7 %collective-permute-start.9 = (f32[64,256]{1,0:T(8,128)S(1)}, f32[64,256]{1,0:T(8,128)S(1)}, u32[]{:S(2)}, u32[]{:S(2)}) collective-permute-start(f32[64,256]{1,0:T(8,128)S(1)} %add.24.refs_0_), channel_id=1, source_target_pairs={{0,2},{1,5},{2,0},{3,7},{4,6},{5,1},{6,4},{7,3},{8,10},{9,13},{10,... | collective-permute-start | bytes 196616 | tf_op jit(solution)/shard_map/ppermute | solution.py:258
  62.0 2.4 %collective-permute-done.11.refs_3_ = f32[64,256]{1,0:T(8,128)S(1)} collective-permute-done((f32[64,256]{1,0:T(8,128)S(1)}, f32[64,256]{1,0:T(8,128)S(1)}, u32[]{:S(2)}, u32[]{:S(2)}) %collective-permute-start.11) | collective-permute-done | bytes 65568 | tf_op jit(solution)/shard_map/ppermute | solution.py:258
  66.2 2.8 %collective-permute-start.14 = (bf16[128,1152]{1,0:T(8,128)(2,1)S(1)}, bf16[128,1152]{1,0:T(8,128)(2,1)S(1)}, u32[]{:S(2)}, u32[]{:S(2)}) collective-permute-start(bf16[128,1152]{1,0:T(8,128)(2,1)S(1)} %shard_map.33.sent), channel_id=1, source_target_pairs={{0,8},{1,9},{2,10},{3,11},{4,12},{5,13},{6,14},{7,15},{8,0},{9,1},... | collective-permute-start | bytes 884744 | tf_op jit(solution)/shard_map/ppermute | solution.py:258
  69.7 17.9 %collective-permute-done.14.received = bf16[128,1152]{1,0:T(8,128)(2,1)S(1)} collective-permute-done((bf16[128,1152]{1,0:T(8,128)(2,1)S(1)}, bf16[128,1152]{1,0:T(8,128)(2,1)S(1)}, u32[]{:S(2)}, u32[]{:S(2)}) %collective-permute-start.14) | collective-permute-done | bytes 294944 | tf_op jit(solution)/shard_map/ppermute | solution.py:258
  89.0 2.0 %collective-permute-done.13.received = bf16[128,768]{1,0:T(8,128)(2,1)S(1)} collective-permute-done((bf16[128,768]{1,0:T(8,128)(2,1)S(1)}, bf16[128,768]{1,0:T(8,128)(2,1)S(1)}, u32[]{:S(2)}, u32[]{:S(2)}) %collective-permute-start.13) | collective-permute-done | bytes 196640 | tf_op jit(solution)/shard_map/ppermute | solution.py:258
  92.3 1.3 collective-permute-done.15
  93.6 1.2 collective-permute-start.16
  95.5 1.7 %collective-permute-start.18 = (f32[64,320]{1,0:T(8,128)S(1)}, f32[64,320]{1,0:T(8,128)S(1)}, u32[]{:S(2)}, u32[]{:S(2)}) collective-permute-start(f32[64,320]{1,0:T(8,128)S(1)} %add.25.refs_0_), channel_id=1, source_target_pairs={{0,6},{1,7},{2,4},{3,5},{4,2},{5,3},{6,0},{7,1},{8,14},{9,15},{10,... | collective-permute-start | bytes 245768 | tf_op jit(solution)/shard_map/ppermute | solution.py:258
  97.2 1.9 %collective-permute-done.16.refs_1_ = f32[64,320]{1,0:T(8,128)S(1)} collective-permute-done((f32[64,320]{1,0:T(8,128)S(1)}, f32[64,320]{1,0:T(8,128)S(1)}, u32[]{:S(2)}, u32[]{:S(2)}) %collective-permute-start.16) | collective-permute-done | bytes 81952 | tf_op jit(solution)/shard_map/ppermute | solution.py:258
  99.9 1.8 %collective-permute-done.18.refs_3_ = f32[64,320]{1,0:T(8,128)S(1)} collective-permute-done((f32[64,320]{1,0:T(8,128)S(1)}, f32[64,320]{1,0:T(8,128)S(1)}, u32[]{:S(2)}, u32[]{:S(2)}) %collective-permute-start.18) | collective-permute-done | bytes 81952 | tf_op jit(solution)/shard_map/ppermute | solution.py:258
  101.7 2.0 %shard_map.38.refs_8_ = bf16[64,256]{1,0:T(8,128)(2,1)S(1)} custom-call(f32[64,320]{1,0:T(8,128)S(1)} %add.25.refs_0_, f32[64,320]{1,0:T(8,128)S(1)} %collective-permute-done.16.refs_1_, f32[64,320]{1,0:T(8,128)S(1)} %collective-permute-done.17.refs_2_, f32[64,320]{1,0:T(8,128)S(1)} %collective-permute-done.18.refs_3_), custom_call_target="tpu_custom_call" | custom-call | flops 15728640 | bytes 327680 | tf_op jit(solution)/shard_map/pallas_call | solution.py:92
  105.4 2.7 %collective-permute-start.20 = (bf16[64,1920]{1,0:T(8,128)(2,1)S(1)}, bf16[64,1920]{1,0:T(8,128)(2,1)S(1)}, u32[]{:S(2)}, u32[]{:S(2)}) collective-permute-start(bf16[64,1920]{1,0:T(8,128)(2,1)S(1)} %shard_map.39), channel_id=1, source_target_pairs={{0,8},{1,9},{2,10},{3,11},{4,12},{5,13},{6,14},{7,15},{8,0},{9,1},... | collective-permute-start | bytes 737288 | tf_op jit(solution)/shard_map/ppermute | solution.py:258
  108.5 11.1 %collective-permute-done.20.received = bf16[64,1920]{1,0:T(8,128)(2,1)S(1)} collective-permute-done((bf16[64,1920]{1,0:T(8,128)(2,1)S(1)}, bf16[64,1920]{1,0:T(8,128)(2,1)S(1)}, u32[]{:S(2)}, u32[]{:S(2)}) %collective-permute-start.20) | collective-permute-done | bytes 245792 | tf_op jit(solution)/shard_map/ppermute | solution.py:258
  120.3 2.0 %collective-permute-start.22 = (f32[64,64]{1,0:T(8,128)S(1)}, f32[64,64]{1,0:T(8,128)S(1)}, u32[]{:S(2)}, u32[]{:S(2)}) collective-permute-start(f32[64,64]{1,0:T(8,128)S(1)} %get-tuple-element.51), channel_id=1, source_target_pairs={{0,8},{1,9},{2,10},{3,11},{4,12},{5,13},{6,14},{7,15},{8,0},{9,1},... | collective-permute-start | bytes 49160 | tf_op jit(solution)/shard_map/ppermute | solution.py:258
  123.0 2.0 %collective-permute-done.21 = f32[64,64]{1,0:T(8,128)S(1)} collective-permute-done((f32[64,64]{1,0:T(8,128)S(1)}, f32[64,64]{1,0:T(8,128)S(1)}, u32[]{:S(2)}, u32[]{:S(2)}) %collective-permute-start.21) | collective-permute-done | bytes 16416 | tf_op jit(solution)/shard_map/ppermute | solution.py:258
  125.9 2.7 %collective-permute-start.24 = (f32[64,64]{1,0:T(8,128)S(1)}, f32[64,64]{1,0:T(8,128)S(1)}, u32[]{:S(2)}, u32[]{:S(2)}) collective-permute-start(f32[64,64]{1,0:T(8,128)S(1)} %add_add_fusion.1), channel_id=1, source_target_pairs={{0,6},{1,7},{2,4},{3,5},{4,2},{5,3},{6,0},{7,1},{8,14},{9,15},{10,... | collective-permute-start | bytes 49160 | tf_op jit(solution)/shard_map/ppermute | solution.py:258
  128.6 1.3 collective-permute-start.25
  130.8 1.7 %collective-permute-done.25 = f32[64,64]{1,0:T(8,128)S(1)} collective-permute-done((f32[64,64]{1,0:T(8,128)S(1)}, f32[64,64]{1,0:T(8,128)S(1)}, u32[]{:S(2)}, u32[]{:S(2)}) %collective-permute-start.25) | collective-permute-done | bytes 16416 | tf_op jit(solution)/shard_map/ppermute | solution.py:258
  132.5 1.3 collective-permute-done.26
  133.8 3.0 %shard_map.42 = f32[64,1920]{1,0:T(8,128)} custom-call(f32[64,64]{1,0:T(8,128)S(1)} %add_add_fusion.gram, f32[64,1920]{1,0:T(8,128)S(1)} %get-tuple-element.52.loading), custom_call_target="tpu_custom_call" | custom-call | tf_op jit(solution)/shard_map/pallas_call | solution.py:249
  (45 shorter events, 18.4 us)
Async XLA Ops:
  0.0 2.1 %copy-start = (bf16[64,30720]{1,0:T(8,128)(2,1)S(1)}, bf16[64,30720]{1,0:T(8,128)(2,1)}, u32[]{:S(2)}) copy-start(bf16[64,30720]{1,0:T(8,128)(2,1)} %matrix.1) | copy-start | bytes 11796484
  2.1 4.0 %copy-start.1 = (bf16[1920,64]{0,1:T(8,128)(2,1)S(1)}, bf16[1920,64]{0,1:T(8,128)(2,1)}, u32[]{:S(2)}) copy-start(bf16[1920,64]{0,1:T(8,128)(2,1)} %param.3) | copy-start | bytes 737284
  3.0 20.4 %collective-permute-start = (bf16[64,3840]{1,0:T(8,128)(2,1)S(1)}, bf16[64,3840]{1,0:T(8,128)(2,1)S(1)}, u32[]{:S(2)}, u32[]{:S(2)}) collective-permute-start(bf16[64,3840]{1,0:T(8,128)(2,1)S(1)} %get-tuple-element.30), channel_id=1, source_target_pairs={{0,1},{1,0},{2,3},{3,2},{4,5},{5,4},{6,7},{7,6},{8,9},{9,8},{10,11... | collective-permute-start | bytes 1474568 | tf_op jit(solution)/shard_map/ppermute | solution.py:258
  3.5 19.9 %collective-permute-start.1 = (bf16[64,3840]{1,0:T(8,128)(2,1)S(1)}, bf16[64,3840]{1,0:T(8,128)(2,1)S(1)}, u32[]{:S(2)}, u32[]{:S(2)}) collective-permute-start(bf16[64,3840]{1,0:T(8,128)(2,1)S(1)} %get-tuple-element.31), channel_id=1, source_target_pairs={{0,2},{1,5},{2,0},{3,7},{4,6},{5,1},{6,4},{7,3},{8,10},{9,13},{10,... | collective-permute-start | bytes 1474568 | tf_op jit(solution)/shard_map/ppermute | solution.py:258
  6.1 11.7 %collective-permute-start.7 = (bf16[64,1920]{1,0:T(8,128)(2,1)S(1)}, bf16[64,1920]{1,0:T(8,128)(2,1)S(1)}, u32[]{:S(2)}, u32[]{:S(2)}) collective-permute-start(bf16[64,1920]{1,0:T(8,128)(2,1)S(1)} %bitcast.2), channel_id=1, source_target_pairs={{0,8},{1,9},{2,10},{3,11},{4,12},{5,13},{6,14},{7,15},{8,0},{9,1},... | collective-permute-start | bytes 737288 | tf_op jit(solution)/shard_map/ppermute | solution.py:258
  8.7 21.8 %collective-permute-start.2 = (bf16[64,3840]{1,0:T(8,128)(2,1)S(1)}, bf16[64,3840]{1,0:T(8,128)(2,1)S(1)}, u32[]{:S(2)}, u32[]{:S(2)}) collective-permute-start(bf16[64,3840]{1,0:T(8,128)(2,1)S(1)} %get-tuple-element.32), channel_id=1, source_target_pairs={{0,3},{1,4},{2,1},{3,6},{4,7},{5,0},{6,5},{7,2},{8,11},{9,12},{10,... | collective-permute-start | bytes 1474568 | tf_op jit(solution)/shard_map/ppermute | solution.py:258
  9.7 21.4 %collective-permute-start.3 = (bf16[64,3840]{1,0:T(8,128)(2,1)S(1)}, bf16[64,3840]{1,0:T(8,128)(2,1)S(1)}, u32[]{:S(2)}, u32[]{:S(2)}) collective-permute-start(bf16[64,3840]{1,0:T(8,128)(2,1)S(1)} %get-tuple-element.33), channel_id=1, source_target_pairs={{0,4},{1,3},{2,6},{3,1},{4,0},{5,7},{6,2},{7,5},{8,12},{9,11},{10,... | collective-permute-start | bytes 1474568 | tf_op jit(solution)/shard_map/ppermute | solution.py:258
  17.8 18.4 %collective-permute-start.4 = (bf16[64,3840]{1,0:T(8,128)(2,1)S(1)}, bf16[64,3840]{1,0:T(8,128)(2,1)S(1)}, u32[]{:S(2)}, u32[]{:S(2)}) collective-permute-start(bf16[64,3840]{1,0:T(8,128)(2,1)S(1)} %get-tuple-element.34), channel_id=1, source_target_pairs={{0,5},{1,2},{2,7},{3,0},{4,1},{5,6},{6,3},{7,4},{8,13},{9,10},{10,... | collective-permute-start | bytes 1474568 | tf_op jit(solution)/shard_map/ppermute | solution.py:258
  23.4 24.6 %collective-permute-start.5 = (bf16[64,3840]{1,0:T(8,128)(2,1)S(1)}, bf16[64,3840]{1,0:T(8,128)(2,1)S(1)}, u32[]{:S(2)}, u32[]{:S(2)}) collective-permute-start(bf16[64,3840]{1,0:T(8,128)(2,1)S(1)} %get-tuple-element.35), channel_id=1, source_target_pairs={{0,6},{1,7},{2,4},{3,5},{4,2},{5,3},{6,0},{7,1},{8,14},{9,15},{10,... | collective-permute-start | bytes 1474568 | tf_op jit(solution)/shard_map/ppermute | solution.py:258
  23.4 30.7 %collective-permute-start.6 = (bf16[64,3840]{1,0:T(8,128)(2,1)S(1)}, bf16[64,3840]{1,0:T(8,128)(2,1)S(1)}, u32[]{:S(2)}, u32[]{:S(2)}) collective-permute-start(bf16[64,3840]{1,0:T(8,128)(2,1)S(1)} %get-tuple-element.36), channel_id=1, source_target_pairs={{0,7},{1,6},{2,5},{3,4},{4,3},{5,2},{6,1},{7,0},{8,15},{9,14},{10,... | collective-permute-start | bytes 1474568 | tf_op jit(solution)/shard_map/ppermute | solution.py:258
  54.9 2.6 %collective-permute-start.8 = (f32[64,256]{1,0:T(8,128)S(1)}, f32[64,256]{1,0:T(8,128)S(1)}, u32[]{:S(2)}, u32[]{:S(2)}) collective-permute-start(f32[64,256]{1,0:T(8,128)S(1)} %get-tuple-element.40), channel_id=1, source_target_pairs={{0,1},{1,0},{2,3},{3,2},{4,5},{5,4},{6,7},{7,6},{8,9},{9,8},{10,11... | collective-permute-start | bytes 196616 | tf_op jit(solution)/shard_map/ppermute | solution.py:258
  57.5 4.5 %collective-permute-start.10 = (f32[64,256]{1,0:T(8,128)S(1)}, f32[64,256]{1,0:T(8,128)S(1)}, u32[]{:S(2)}, u32[]{:S(2)}) collective-permute-start(f32[64,256]{1,0:T(8,128)S(1)} %add.24.refs_0_), channel_id=1, source_target_pairs={{0,4},{1,3},{2,6},{3,1},{4,0},{5,7},{6,2},{7,5},{8,12},{9,11},{10,... | collective-permute-start | bytes 196616 | tf_op jit(solution)/shard_map/ppermute | solution.py:258
  59.1 5.2 %collective-permute-start.11 = (f32[64,256]{1,0:T(8,128)S(1)}, f32[64,256]{1,0:T(8,128)S(1)}, u32[]{:S(2)}, u32[]{:S(2)}) collective-permute-start(f32[64,256]{1,0:T(8,128)S(1)} %add.24.refs_0_), channel_id=1, source_target_pairs={{0,6},{1,7},{2,4},{3,5},{4,2},{5,3},{6,0},{7,1},{8,14},{9,15},{10,... | collective-permute-start | bytes 196616 | tf_op jit(solution)/shard_map/ppermute | solution.py:258
  59.3 5.0 %collective-permute-start.9 = (f32[64,256]{1,0:T(8,128)S(1)}, f32[64,256]{1,0:T(8,128)S(1)}, u32[]{:S(2)}, u32[]{:S(2)}) collective-permute-start(f32[64,256]{1,0:T(8,128)S(1)} %add.24.refs_0_), channel_id=1, source_target_pairs={{0,2},{1,5},{2,0},{3,7},{4,6},{5,1},{6,4},{7,3},{8,10},{9,13},{10,... | collective-permute-start | bytes 196616 | tf_op jit(solution)/shard_map/ppermute | solution.py:258
  64.5 1.3 collective-permute-start.12
  66.2 21.3 %collective-permute-start.14 = (bf16[128,1152]{1,0:T(8,128)(2,1)S(1)}, bf16[128,1152]{1,0:T(8,128)(2,1)S(1)}, u32[]{:S(2)}, u32[]{:S(2)}) collective-permute-start(bf16[128,1152]{1,0:T(8,128)(2,1)S(1)} %shard_map.33.sent), channel_id=1, source_target_pairs={{0,8},{1,9},{2,10},{3,11},{4,12},{5,13},{6,14},{7,15},{8,0},{9,1},... | collective-permute-start | bytes 884744 | tf_op jit(solution)/shard_map/ppermute | solution.py:258
  69.4 21.7 %collective-permute-start.13 = (bf16[128,768]{1,0:T(8,128)(2,1)S(1)}, bf16[128,768]{1,0:T(8,128)(2,1)S(1)}, u32[]{:S(2)}, u32[]{:S(2)}) collective-permute-start(bf16[128,768]{1,0:T(8,128)(2,1)S(1)} %shard_map.32.sent), channel_id=1, source_target_pairs={{0,8},{1,9},{2,10},{3,11},{4,12},{5,13},{6,14},{7,15},{8,0},{9,1},... | collective-permute-start | bytes 589832 | tf_op jit(solution)/shard_map/ppermute | solution.py:258
  92.2 1.4 collective-permute-start.15
  93.6 5.5 %collective-permute-start.16 = (f32[64,320]{1,0:T(8,128)S(1)}, f32[64,320]{1,0:T(8,128)S(1)}, u32[]{:S(2)}, u32[]{:S(2)}) collective-permute-start(f32[64,320]{1,0:T(8,128)S(1)} %add.25.refs_0_), channel_id=1, source_target_pairs={{0,2},{1,5},{2,0},{3,7},{4,6},{5,1},{6,4},{7,3},{8,10},{9,13},{10,... | collective-permute-start | bytes 245768 | tf_op jit(solution)/shard_map/ppermute | solution.py:258
  94.9 5.1 %collective-permute-start.17 = (f32[64,320]{1,0:T(8,128)S(1)}, f32[64,320]{1,0:T(8,128)S(1)}, u32[]{:S(2)}, u32[]{:S(2)}) collective-permute-start(f32[64,320]{1,0:T(8,128)S(1)} %add.25.refs_0_), channel_id=1, source_target_pairs={{0,4},{1,3},{2,6},{3,1},{4,0},{5,7},{6,2},{7,5},{8,12},{9,11},{10,... | collective-permute-start | bytes 245768 | tf_op jit(solution)/shard_map/ppermute | solution.py:258
  95.5 6.2 %collective-permute-start.18 = (f32[64,320]{1,0:T(8,128)S(1)}, f32[64,320]{1,0:T(8,128)S(1)}, u32[]{:S(2)}, u32[]{:S(2)}) collective-permute-start(f32[64,320]{1,0:T(8,128)S(1)} %add.25.refs_0_), channel_id=1, source_target_pairs={{0,6},{1,7},{2,4},{3,5},{4,2},{5,3},{6,0},{7,1},{8,14},{9,15},{10,... | collective-permute-start | bytes 245768 | tf_op jit(solution)/shard_map/ppermute | solution.py:258
  103.7 1.2 collective-permute-start.19
  105.4 14.3 %collective-permute-start.20 = (bf16[64,1920]{1,0:T(8,128)(2,1)S(1)}, bf16[64,1920]{1,0:T(8,128)(2,1)S(1)}, u32[]{:S(2)}, u32[]{:S(2)}) collective-permute-start(bf16[64,1920]{1,0:T(8,128)(2,1)S(1)} %shard_map.39), channel_id=1, source_target_pairs={{0,8},{1,9},{2,10},{3,11},{4,12},{5,13},{6,14},{7,15},{8,0},{9,1},... | collective-permute-start | bytes 737288 | tf_op jit(solution)/shard_map/ppermute | solution.py:258
  120.2 4.8 %collective-permute-start.21 = (f32[64,64]{1,0:T(8,128)S(1)}, f32[64,64]{1,0:T(8,128)S(1)}, u32[]{:S(2)}, u32[]{:S(2)}) collective-permute-start(f32[64,64]{1,0:T(8,128)S(1)} %get-tuple-element.51), channel_id=1, source_target_pairs={{0,9},{1,8},{2,11},{3,10},{4,13},{5,12},{6,15},{7,14},{8,1},{9,0},... | collective-permute-start | bytes 49160 | tf_op jit(solution)/shard_map/ppermute | solution.py:258
  120.3 5.6 %collective-permute-start.22 = (f32[64,64]{1,0:T(8,128)S(1)}, f32[64,64]{1,0:T(8,128)S(1)}, u32[]{:S(2)}, u32[]{:S(2)}) collective-permute-start(f32[64,64]{1,0:T(8,128)S(1)} %get-tuple-element.51), channel_id=1, source_target_pairs={{0,8},{1,9},{2,10},{3,11},{4,12},{5,13},{6,14},{7,15},{8,0},{9,1},... | collective-permute-start | bytes 49160 | tf_op jit(solution)/shard_map/ppermute | solution.py:258
  122.3 3.5 %collective-permute-start.23 = (f32[64,64]{1,0:T(8,128)S(1)}, f32[64,64]{1,0:T(8,128)S(1)}, u32[]{:S(2)}, u32[]{:S(2)}) collective-permute-start(f32[64,64]{1,0:T(8,128)S(1)} %get-tuple-element.51), channel_id=1, source_target_pairs={{0,1},{1,0},{2,3},{3,2},{4,5},{5,4},{6,7},{7,6},{8,9},{9,8},{10,11... | collective-permute-start | bytes 49160 | tf_op jit(solution)/shard_map/ppermute | solution.py:258
  125.9 4.9 %collective-permute-start.24 = (f32[64,64]{1,0:T(8,128)S(1)}, f32[64,64]{1,0:T(8,128)S(1)}, u32[]{:S(2)}, u32[]{:S(2)}) collective-permute-start(f32[64,64]{1,0:T(8,128)S(1)} %add_add_fusion.1), channel_id=1, source_target_pairs={{0,6},{1,7},{2,4},{3,5},{4,2},{5,3},{6,0},{7,1},{8,14},{9,15},{10,... | collective-permute-start | bytes 49160 | tf_op jit(solution)/shard_map/ppermute | solution.py:258
  128.6 3.9 %collective-permute-start.25 = (f32[64,64]{1,0:T(8,128)S(1)}, f32[64,64]{1,0:T(8,128)S(1)}, u32[]{:S(2)}, u32[]{:S(2)}) collective-permute-start(f32[64,64]{1,0:T(8,128)S(1)} %add_add_fusion.1), channel_id=1, source_target_pairs={{0,2},{1,5},{2,0},{3,7},{4,6},{5,1},{6,4},{7,3},{8,10},{9,13},{10,... | collective-permute-start | bytes 49160 | tf_op jit(solution)/shard_map/ppermute | solution.py:258
  129.9 3.9 %collective-permute-start.26 = (f32[64,64]{1,0:T(8,128)S(1)}, f32[64,64]{1,0:T(8,128)S(1)}, u32[]{:S(2)}, u32[]{:S(2)}) collective-permute-start(f32[64,64]{1,0:T(8,128)S(1)} %add_add_fusion.1), channel_id=1, source_target_pairs={{0,4},{1,3},{2,6},{3,1},{4,0},{5,7},{6,2},{7,5},{8,12},{9,11},{10,... | collective-permute-start | bytes 49160 | tf_op jit(solution)/shard_map/ppermute | solution.py:258

commit v11 on v10

--- a/solution.py
+++ b/solution.py
@@ -59,20 +59,22 @@
 
 
 def pack_kernel(masks, matrix, *refs):
-    outs, sem = refs[:-1], refs[-1]
-    width = outs[0].shape[1] // 2
+    outs, held, sem = refs[:-2], refs[-2], refs[-1]
+    rows, width = matrix.shape[0], outs[0].shape[1] // 2
+    step = 16 if rows % 16 == 0 else rows
     index = lax.axis_index("cell")
-    copies = []
-    for k, (out, pair) in enumerate(zip(outs, masks)):
-        member = index ^ jnp.where(index % 2 == 0, *pair)
-        for j, block in enumerate((member, member ^ GROUP)):
-            start = pl.multiple_of(block * width, 128)
-            copies.append(pltpu.make_async_copy(
-                matrix.at[:, pl.ds(start, width)], out.at[:, pl.ds(j * width, width)], sem.at[2 * k + j]))
+    copies = [pltpu.make_async_copy(matrix.at[pl.ds(low, step)], held.at[pl.ds(low, step)], sem.at[i])
+              for i, low in enumerate(range(0, rows, step))]
     for copy in copies:
         copy.start()
-    for copy in copies:
+    for i, copy in enumerate(copies):
         copy.wait()
+        some = pl.ds(i * step, step)
+        for out, pair in zip(outs, masks):
+            member = index ^ jnp.where(index % 2 == 0, *pair)
+            for j, block in enumerate((member, member ^ GROUP)):
+                start = pl.multiple_of(block * width, 128)
+                out[some, pl.ds(j * width, width)] = held[some, pl.ds(start, width)]
 
 
 def pack(matrix, masks, width):
@@ -82,8 +84,8 @@
         in_specs=[pl.BlockSpec(memory_space=pltpu.HBM)],
         out_specs=[VMEM] * count,
         out_shape=[struct((rows, 2 * width), matrix.dtype)] * count,
-        scratch_shapes=[pltpu.SemaphoreType.DMA((2 * count,))],
-        compiler_params=BIG,
+        scratch_shapes=[pltpu.VMEM(matrix.shape, matrix.dtype), pltpu.SemaphoreType.DMA((rows // 16 if rows % 16 == 0 else 1,))],
+        compiler_params=pltpu.CompilerParams(vmem_limit_bytes=48 * 2**20),
         cost_estimate=cost(0, 8 * rows * count * width),
     )(matrix)
 
@@ -95,13 +97,13 @@
     )(*args)
 
 
-def scores_kernel(work, counts, picked, with_gram, width, offset, *refs):
+def scores_kernel(work, odds, counts, picked, with_gram, width, offset, *refs):
     refs = list(refs)
     bases = {block: [refs.pop(0) for _ in range(count)] for block, count in counts}
     slots = {k: refs.pop(0) for k in picked}
     gram = refs.pop(0)[...] if with_gram else None
-    before, outs = refs[:-2], refs[-2:]
-    for odd in range(2):
+    before, outs = refs[:-len(odds)], refs[-len(odds):]
+    for i, odd in enumerate(odds):
         left = 0
         for pair, blocks in work:
             value = 0.0
@@ -116,24 +118,24 @@
             left = lanes.stop
             if blocks:
                 value = value.T
-            if before and lanes.stop <= before[odd].shape[1]:
-                value = value + before[odd][:, lanes]
-            outs[odd][:, lanes] = value
+            if before and lanes.stop <= before[i].shape[1]:
+                value = value + before[i][:, lanes]
+            outs[i][:, lanes] = value
         if with_gram:
-            outs[odd][:, left:] = gram
-
-
-def scores(slots, work, bases, before=(), gram=None, offset=0):
+            outs[i][:, left:] = gram
+
+
+def scores(slots, work, bases, before=(), gram=None, offset=0, odds=(0, 1)):
     rank = next(iter(bases.values()))[0].shape[0]
-    picked = [4 * pair + k for pair, blocks in work if blocks for k in range(4)]
+    picked = [4 * pair + 2 * k + odd for pair, blocks in work if blocks for k in range(2) for odd in odds]
     rows, width = slots[picked[0]].shape[0], slots[picked[0]].shape[1] // 2
     cells = 2 * rows * len(work) + (0 if gram is None else rank)
     counts = [(block, len(parts)) for block, parts in bases.items()]
     args = [x for parts in bases.values() for x in parts] + [slots[k] for k in picked]
     args += ([] if gram is None else [gram]) + list(before)
-    size = 4 * rows * width * sum(len(blocks) for _, blocks in work)
-    kernel = functools.partial(scores_kernel, work, counts, picked, gram is not None, width, offset)
-    return call(kernel, args, [struct((rank, cells), f32)] * 2, cost(2 * rank * size, 2 * size))
+    size = 2 * len(odds) * rows * width * sum(len(blocks) for _, blocks in work)
+    kernel = functools.partial(scores_kernel, work, odds, counts, picked, gram is not None, width, offset)
+    return call(kernel, args, [struct((rank, cells), f32)] * len(odds), cost(2 * rank * size, 2 * size))
 
 
 def image_kernel(normalised, *refs):
@@ -226,13 +228,17 @@
             {k: jnp.broadcast_to(blocks[k][:, 8 * b + t:8 * b + t + 1], shape) for k in range(b, panels)}
             for t in range(8)
         ]
+        corner = {(s, t): jnp.broadcast_to(columns[t][b][s:s + 1], shape) for t in range(8) for s in range(t, 8)}
         for t in range(8):
-            root = lax.rsqrt(jnp.broadcast_to(columns[t][b][t:t + 1], shape))
+            root = lax.rsqrt(corner[t, t])
+            along = {s: corner[s, t] * root for s in range(t + 1, 8)}
+            for u in range(t + 1, 8):
+                for s in range(u, 8):
+                    corner[s, u] = corner[s, u] - along[s] * along[u]
             scaled = {k: x * root for k, x in columns[t].items()}
             for s in range(t + 1, 8):
-                along = jnp.broadcast_to(scaled[b][s:s + 1], shape)
                 for k in range(b, panels):
-                    columns[s][k] = columns[s][k] - scaled[k] * along
+                    columns[s][k] = columns[s][k] - scaled[k] * along[s]
             pivot = jnp.broadcast_to(blocks[b][t:t + 1], shape) * root
             done.append(pivot[:1])
             for k in range(b, panels):
@@ -274,8 +280,9 @@
     packs = pack(expression, masks, width)
     slots = [mate(x, cells, *pair) if k else x for k, (x, pair) in enumerate(zip(packs, masks))]
 
-    def image_from(totals, normalised):
-        even, odd = totals
+    def image_from(work, bases, before, normalised, *rest):
+        (odd,) = scores(slots, work, bases, before[1:], *rest, odds=(1,))
+        (even,) = scores(slots, work, bases, before[:1], *rest, odds=(0,))
         even = even + mate(odd, cells, 1)
         image = image_of(even, legs(even, cells), rows, normalised)
         return image, mate(image, cells, 1)
@@ -284,16 +291,17 @@
     basis = start_basis.T
     bases = {0: [basis], 1: [mate(basis, cells, GROUP)]}
     early = scores(slots, [(0, (0, 1))], bases)
-    images = image_from(scores(slots, [(0, ()), (1, (0, 1))], bases, early), False)
+    images = image_from([(0, ()), (1, (0, 1))], bases, early, False)
+    everything = [(0, (0, 1)), (1, (0, 1))]
     for _ in range(1, ITERS):
-        totals, gram = (), []
+        rows_of, total = [], []
         for start, stop in ((0, first), (first, width)):
             sent = terms(slots, (start, width + start), stop - start, images, bf16)
-            own, other, total = both(sent, mate(sent, cells, GROUP), gram)
-            gram = [total]
-            totals = scores(slots, [(0, (0, 1)), (1, (0, 1))], {0: [own], 1: [other]}, totals,
-                            total if stop == width else None, start)
-        images = image_from(totals, True)
+            own, other, gram = both(sent, mate(sent, cells, GROUP), total)
+            rows_of.append({0: [own], 1: [other]})
+            total = [gram]
+        early = scores(slots, everything, rows_of[0])
+        images = image_from(everything, rows_of[1], early, True, gram, first)
     received = mate(terms(slots, (width,), width, images, bf16), cells, GROUP)
     loading, gram = loading_and_gram(received, terms(slots, (0,), width, images, f32))
     return output_call(total_over_cells(gram, cells), loading).T

time: 137 us -> 135 us (0.985)
  local copies, waits for them, and re-layouts: 2.12 us -> 0.01 us
  Pallas kernels: 12.3 us -> 14.3 us
    unnamed x4 -> x2, local copies, waits for them, and re-layouts: 2.12 us -> 0.01 us
    pallas_call x13 -> x15, Pallas kernels: 8.41 us -> 8.92 us  [call(): pl.pallas_call(kernel, in_specs=[VMEM] * len(args), out_specs=[VMEM] * le...]
  transfers between devices with their start and end apart: 27 -> 27, of which waited for: 22 -> 21; matrix products, arithmetic and copies ran while one was open for 0% -> 0% of each run, Pallas kernels for 2% -> 3%
where the time goes in v11:
time: 135 us
  waiting for transfers between devices  84.6 us (63%)
  starting transfers between devices  35.9 us (27%)
  Pallas kernels  14.3 us (11%)
    ppermute x27, waiting for transfers between devices, mate(): lax.ppermute(value, 'cell', [(i, i ^ masks[i % 2]) for i in range(cells)])  84.6 us
    ppermute x27, starting transfers between devices, mate(): lax.ppermute(value, 'cell', [(i, i ^ masks[i % 2]) for i in range(cells)])  35.9 us
    pallas_call x15, Pallas kernels, call(): pl.pallas_call(kernel, in_specs=[VMEM] * len(args), out_specs=[VMEM] * le...  8.92 us
    pallas_call x1, Pallas kernels, output_call(): pl.pallas_call(functools.partial(output_kernel, math.sqrt(GENES)), in_spe...  3.12 us
  transfers between devices with their start and end apart: 27, of which 21 were waited for; matrix products, arithmetic and copies ran while one was open for 0% of the time, Pallas kernels for 3%

profile of v11, /device:TPU:0, one launch (start us, length us, event | category | flops | bytes accessed | tf_op | source)
XLA Modules:
  0.0 134.9 jit_solution(7172462274145483419)
XLA Ops:
  0.0 2.2 %shard_map.28 = (bf16[64,3840]{1,0:T(8,128)(2,1)S(1)}, bf16[64,3840]{1,0:T(8,128)(2,1)S(1)}, bf16[64,3840]{1,0:T(8,128)(2,1)S(1)}, bf16[64,3840]{1,0:T(8,128)(2,...) custom-call(bf16[64,30720]{1,0:T(8,128)(2,1)} %matrix.1), custom_call_target="tpu_custom_call" | custom-call | bytes 7864320 | tf_op jit(solution)/shard_map/pallas_call | solution.py:82
  2.8 2.6 %collective-permute-start.1 = (bf16[64,3840]{1,0:T(8,128)(2,1)S(1)}, bf16[64,3840]{1,0:T(8,128)(2,1)S(1)}, u32[]{:S(2)}, u32[]{:S(2)}) collective-permute-start(bf16[64,3840]{1,0:T(8,128)(2,1)S(1)} %get-tuple-element.27), channel_id=1, source_target_pairs={{0,2},{1,5},{2,0},{3,7},{4,6},{5,1},{6,4},{7,3},{8,10},{9,13},{10,... | collective-permute-start | bytes 1474568 | tf_op jit(solution)/shard_map/ppermute | solution.py:264
  5.4 2.6 %collective-permute-start.7 = (bf16[64,1920]{1,0:T(8,128)(2,1)S(1)}, bf16[64,1920]{1,0:T(8,128)(2,1)S(1)}, u32[]{:S(2)}, u32[]{:S(2)}) collective-permute-start(bf16[64,1920]{1,0:T(8,128)(2,1)S(1)} %bitcast.2), channel_id=1, source_target_pairs={{0,8},{1,9},{2,10},{3,11},{4,12},{5,13},{6,14},{7,15},{8,0},{9,1},... | collective-permute-start | bytes 737288 | tf_op jit(solution)/shard_map/ppermute | solution.py:264
  7.9 1.1 collective-permute-start.2
  9.7 7.4 %collective-permute-done.7.refs_1_ = bf16[64,1920]{1,0:T(8,128)(2,1)S(1)} collective-permute-done((bf16[64,1920]{1,0:T(8,128)(2,1)S(1)}, bf16[64,1920]{1,0:T(8,128)(2,1)S(1)}, u32[]{:S(2)}, u32[]{:S(2)}) %collective-permute-start.7) | collective-permute-done | bytes 245792 | tf_op jit(solution)/shard_map/ppermute | solution.py:264
  17.1 7.6 %collective-permute-start.6 = (bf16[64,3840]{1,0:T(8,128)(2,1)S(1)}, bf16[64,3840]{1,0:T(8,128)(2,1)S(1)}, u32[]{:S(2)}, u32[]{:S(2)}) collective-permute-start(bf16[64,3840]{1,0:T(8,128)(2,1)S(1)} %get-tuple-element.32), channel_id=1, source_target_pairs={{0,7},{1,6},{2,5},{3,4},{4,3},{5,2},{6,1},{7,0},{8,15},{9,14},{10,... | collective-permute-start | bytes 1474568 | tf_op jit(solution)/shard_map/ppermute | solution.py:264
  25.6 4.0 %collective-permute-done.2.refs_5_.refs_3_ = bf16[64,3840]{1,0:T(8,128)(2,1)S(1)} collective-permute-done((bf16[64,3840]{1,0:T(8,128)(2,1)S(1)}, bf16[64,3840]{1,0:T(8,128)(2,1)S(1)}, u32[]{:S(2)}, u32[]{:S(2)}) %collective-permute-start.2) | collective-permute-done | bytes 491552 | tf_op jit(solution)/shard_map/ppermute | solution.py:264
  30.3 11.6 %collective-permute-done.6.refs_3_.refs_7_.refs_9_.refs_5_ = bf16[64,3840]{1,0:T(8,128)(2,1)S(1)} collective-permute-done((bf16[64,3840]{1,0:T(8,128)(2,1)S(1)}, bf16[64,3840]{1,0:T(8,128)(2,1)S(1)}, u32[]{:S(2)}, u32[]{:S(2)}) %collective-permute-start.6) | collective-permute-done | bytes 491552 | tf_op jit(solution)/shard_map/ppermute | solution.py:264
  42.5 4.5 %collective-permute-done.3.refs_2_.refs_4_.refs_6_ = bf16[64,3840]{1,0:T(8,128)(2,1)S(1)} collective-permute-done((bf16[64,3840]{1,0:T(8,128)(2,1)S(1)}, bf16[64,3840]{1,0:T(8,128)(2,1)S(1)}, u32[]{:S(2)}, u32[]{:S(2)}) %collective-permute-start.3) | collective-permute-done | bytes 491552 | tf_op jit(solution)/shard_map/ppermute | solution.py:264
  47.0 8.2 %collective-permute-done.5.refs_3_.refs_6_.refs_8_.refs_5_ = bf16[64,3840]{1,0:T(8,128)(2,1)S(1)} collective-permute-done((bf16[64,3840]{1,0:T(8,128)(2,1)S(1)}, bf16[64,3840]{1,0:T(8,128)(2,1)S(1)}, u32[]{:S(2)}, u32[]{:S(2)}) %collective-permute-start.5) | collective-permute-done | bytes 491552 | tf_op jit(solution)/shard_map/ppermute | solution.py:264
  55.7 1.7 %collective-permute-start.10 = (f32[64,256]{1,0:T(8,128)S(1)}, f32[64,256]{1,0:T(8,128)S(1)}, u32[]{:S(2)}, u32[]{:S(2)}) collective-permute-start(f32[64,256]{1,0:T(8,128)S(1)} %add.24.refs_0_), channel_id=1, source_target_pairs={{0,4},{1,3},{2,6},{3,1},{4,0},{5,7},{6,2},{7,5},{8,12},{9,11},{10,... | collective-permute-start | bytes 196616 | tf_op jit(solution)/shard_map/ppermute | solution.py:264
  57.6 1.6 %collective-permute-start.9 = (f32[64,256]{1,0:T(8,128)S(1)}, f32[64,256]{1,0:T(8,128)S(1)}, u32[]{:S(2)}, u32[]{:S(2)}) collective-permute-start(f32[64,256]{1,0:T(8,128)S(1)} %add.24.refs_0_), channel_id=1, source_target_pairs={{0,2},{1,5},{2,0},{3,7},{4,6},{5,1},{6,4},{7,3},{8,10},{9,13},{10,... | collective-permute-start | bytes 196616 | tf_op jit(solution)/shard_map/ppermute | solution.py:264
  60.3 2.3 %collective-permute-done.11.refs_3_ = f32[64,256]{1,0:T(8,128)S(1)} collective-permute-done((f32[64,256]{1,0:T(8,128)S(1)}, f32[64,256]{1,0:T(8,128)S(1)}, u32[]{:S(2)}, u32[]{:S(2)}) %collective-permute-start.11) | collective-permute-done | bytes 65568 | tf_op jit(solution)/shard_map/ppermute | solution.py:264
  62.8 1.2 collective-permute-done.12.refs_9_
  64.5 2.8 %collective-permute-start.14 = (bf16[128,1152]{1,0:T(8,128)(2,1)S(1)}, bf16[128,1152]{1,0:T(8,128)(2,1)S(1)}, u32[]{:S(2)}, u32[]{:S(2)}) collective-permute-start(bf16[128,1152]{1,0:T(8,128)(2,1)S(1)} %shard_map.34.sent), channel_id=1, source_target_pairs={{0,8},{1,9},{2,10},{3,11},{4,12},{5,13},{6,14},{7,15},{8,0},{9,1},... | collective-permute-start | bytes 884744 | tf_op jit(solution)/shard_map/ppermute | solution.py:264
  67.9 17.7 %collective-permute-done.14.received = bf16[128,1152]{1,0:T(8,128)(2,1)S(1)} collective-permute-done((bf16[128,1152]{1,0:T(8,128)(2,1)S(1)}, bf16[128,1152]{1,0:T(8,128)(2,1)S(1)}, u32[]{:S(2)}, u32[]{:S(2)}) %collective-permute-start.14) | collective-permute-done | bytes 294944 | tf_op jit(solution)/shard_map/ppermute | solution.py:264
  87.1 2.3 %collective-permute-done.13.received = bf16[128,768]{1,0:T(8,128)(2,1)S(1)} collective-permute-done((bf16[128,768]{1,0:T(8,128)(2,1)S(1)}, bf16[128,768]{1,0:T(8,128)(2,1)S(1)}, u32[]{:S(2)}, u32[]{:S(2)}) %collective-permute-start.13) | collective-permute-done | bytes 196640 | tf_op jit(solution)/shard_map/ppermute | solution.py:264
  91.7 1.2 collective-permute-start.16
  93.4 1.9 %collective-permute-start.18 = (f32[64,320]{1,0:T(8,128)S(1)}, f32[64,320]{1,0:T(8,128)S(1)}, u32[]{:S(2)}, u32[]{:S(2)}) collective-permute-start(f32[64,320]{1,0:T(8,128)S(1)} %add.25.refs_0_), channel_id=1, source_target_pairs={{0,6},{1,7},{2,4},{3,5},{4,2},{5,3},{6,0},{7,1},{8,14},{9,15},{10,... | collective-permute-start | bytes 245768 | tf_op jit(solution)/shard_map/ppermute | solution.py:264
  95.2 2.0 %collective-permute-done.16.refs_1_ = f32[64,320]{1,0:T(8,128)S(1)} collective-permute-done((f32[64,320]{1,0:T(8,128)S(1)}, f32[64,320]{1,0:T(8,128)S(1)}, u32[]{:S(2)}, u32[]{:S(2)}) %collective-permute-start.16) | collective-permute-done | bytes 81952 | tf_op jit(solution)/shard_map/ppermute | solution.py:264
  97.9 1.7 %collective-permute-done.18.refs_3_ = f32[64,320]{1,0:T(8,128)S(1)} collective-permute-done((f32[64,320]{1,0:T(8,128)S(1)}, f32[64,320]{1,0:T(8,128)S(1)}, u32[]{:S(2)}, u32[]{:S(2)}) %collective-permute-start.18) | collective-permute-done | bytes 81952 | tf_op jit(solution)/shard_map/ppermute | solution.py:264
  99.6 2.1 %shard_map.40.refs_8_ = bf16[64,256]{1,0:T(8,128)(2,1)S(1)} custom-call(f32[64,320]{1,0:T(8,128)S(1)} %add.25.refs_0_, f32[64,320]{1,0:T(8,128)S(1)} %collective-permute-done.16.refs_1_, f32[64,320]{1,0:T(8,128)S(1)} %collective-permute-done.17.refs_2_, f32[64,320]{1,0:T(8,128)S(1)} %collective-permute-done.18.refs_3_), custom_call_target="tpu_custom_call" | custom-call | flops 15728640 | bytes 327680 | tf_op jit(solution)/shard_map/pallas_call | solution.py:94
  101.8 1.2 collective-permute-done.19.refs_9_
  103.4 2.7 %collective-permute-start.20 = (bf16[64,1920]{1,0:T(8,128)(2,1)S(1)}, bf16[64,1920]{1,0:T(8,128)(2,1)S(1)}, u32[]{:S(2)}, u32[]{:S(2)}) collective-permute-start(bf16[64,1920]{1,0:T(8,128)(2,1)S(1)} %shard_map.41), channel_id=1, source_target_pairs={{0,8},{1,9},{2,10},{3,11},{4,12},{5,13},{6,14},{7,15},{8,0},{9,1},... | collective-permute-start | bytes 737288 | tf_op jit(solution)/shard_map/ppermute | solution.py:264
  106.6 11.1 %collective-permute-done.20.received = bf16[64,1920]{1,0:T(8,128)(2,1)S(1)} collective-permute-done((bf16[64,1920]{1,0:T(8,128)(2,1)S(1)}, bf16[64,1920]{1,0:T(8,128)(2,1)S(1)}, u32[]{:S(2)}, u32[]{:S(2)}) %collective-permute-start.20) | collective-permute-done | bytes 245792 | tf_op jit(solution)/shard_map/ppermute | solution.py:264
  118.3 2.0 %collective-permute-start.22 = (f32[64,64]{1,0:T(8,128)S(1)}, f32[64,64]{1,0:T(8,128)S(1)}, u32[]{:S(2)}, u32[]{:S(2)}) collective-permute-start(f32[64,64]{1,0:T(8,128)S(1)} %get-tuple-element.43), channel_id=1, source_target_pairs={{0,8},{1,9},{2,10},{3,11},{4,12},{5,13},{6,14},{7,15},{8,0},{9,1},... | collective-permute-start | bytes 49160 | tf_op jit(solution)/shard_map/ppermute | solution.py:264
  121.1 2.0 %collective-permute-done.21 = f32[64,64]{1,0:T(8,128)S(1)} collective-permute-done((f32[64,64]{1,0:T(8,128)S(1)}, f32[64,64]{1,0:T(8,128)S(1)}, u32[]{:S(2)}, u32[]{:S(2)}) %collective-permute-start.21) | collective-permute-done | bytes 16416 | tf_op jit(solution)/shard_map/ppermute | solution.py:264
  123.9 2.6 %collective-permute-start.24 = (f32[64,64]{1,0:T(8,128)S(1)}, f32[64,64]{1,0:T(8,128)S(1)}, u32[]{:S(2)}, u32[]{:S(2)}) collective-permute-start(f32[64,64]{1,0:T(8,128)S(1)} %add_add_fusion.1), channel_id=1, source_target_pairs={{0,6},{1,7},{2,4},{3,5},{4,2},{5,3},{6,0},{7,1},{8,14},{9,15},{10,... | collective-permute-start | bytes 49160 | tf_op jit(solution)/shard_map/ppermute | solution.py:264
  126.5 1.4 %collective-permute-start.25 = (f32[64,64]{1,0:T(8,128)S(1)}, f32[64,64]{1,0:T(8,128)S(1)}, u32[]{:S(2)}, u32[]{:S(2)}) collective-permute-start(f32[64,64]{1,0:T(8,128)S(1)} %add_add_fusion.1), channel_id=1, source_target_pairs={{0,2},{1,5},{2,0},{3,7},{4,6},{5,1},{6,4},{7,3},{8,10},{9,13},{10,... | collective-permute-start | bytes 49160 | tf_op jit(solution)/shard_map/ppermute | solution.py:264
  128.8 1.6 %collective-permute-done.25 = f32[64,64]{1,0:T(8,128)S(1)} collective-permute-done((f32[64,64]{1,0:T(8,128)S(1)}, f32[64,64]{1,0:T(8,128)S(1)}, u32[]{:S(2)}, u32[]{:S(2)}) %collective-permute-start.25) | collective-permute-done | bytes 16416 | tf_op jit(solution)/shard_map/ppermute | solution.py:264
  130.4 1.4 %collective-permute-done.26 = f32[64,64]{1,0:T(8,128)S(1)} collective-permute-done((f32[64,64]{1,0:T(8,128)S(1)}, f32[64,64]{1,0:T(8,128)S(1)}, u32[]{:S(2)}, u32[]{:S(2)}) %collective-permute-start.26) | collective-permute-done | bytes 16416 | tf_op jit(solution)/shard_map/ppermute | solution.py:264
  131.8 3.1 %shard_map.44 = f32[64,1920]{1,0:T(8,128)} custom-call(f32[64,64]{1,0:T(8,128)S(1)} %add_add_fusion.gram, f32[64,1920]{1,0:T(8,128)S(1)} %get-tuple-element.44.loading), custom_call_target="tpu_custom_call" | custom-call | tf_op jit(solution)/shard_map/pallas_call | solution.py:255
  (45 shorter events, 15.3 us)
Async XLA Ops:
  0.0 5.4 %copy-start = (bf16[1920,64]{0,1:T(8,128)(2,1)S(1)}, bf16[1920,64]{0,1:T(8,128)(2,1)}, u32[]{:S(2)}) copy-start(bf16[1920,64]{0,1:T(8,128)(2,1)} %param.3) | copy-start | bytes 737284
  2.2 22.5 %collective-permute-start = (bf16[64,3840]{1,0:T(8,128)(2,1)S(1)}, bf16[64,3840]{1,0:T(8,128)(2,1)S(1)}, u32[]{:S(2)}, u32[]{:S(2)}) collective-permute-start(bf16[64,3840]{1,0:T(8,128)(2,1)S(1)} %get-tuple-element.26), channel_id=1, source_target_pairs={{0,1},{1,0},{2,3},{3,2},{4,5},{5,4},{6,7},{7,6},{8,9},{9,8},{10,11... | collective-permute-start | bytes 1474568 | tf_op jit(solution)/shard_map/ppermute | solution.py:264
  2.8 22.0 %collective-permute-start.1 = (bf16[64,3840]{1,0:T(8,128)(2,1)S(1)}, bf16[64,3840]{1,0:T(8,128)(2,1)S(1)}, u32[]{:S(2)}, u32[]{:S(2)}) collective-permute-start(bf16[64,3840]{1,0:T(8,128)(2,1)S(1)} %get-tuple-element.27), channel_id=1, source_target_pairs={{0,2},{1,5},{2,0},{3,7},{4,6},{5,1},{6,4},{7,3},{8,10},{9,13},{10,... | collective-permute-start | bytes 1474568 | tf_op jit(solution)/shard_map/ppermute | solution.py:264
  5.4 11.7 %collective-permute-start.7 = (bf16[64,1920]{1,0:T(8,128)(2,1)S(1)}, bf16[64,1920]{1,0:T(8,128)(2,1)S(1)}, u32[]{:S(2)}, u32[]{:S(2)}) collective-permute-start(bf16[64,1920]{1,0:T(8,128)(2,1)S(1)} %bitcast.2), channel_id=1, source_target_pairs={{0,8},{1,9},{2,10},{3,11},{4,12},{5,13},{6,14},{7,15},{8,0},{9,1},... | collective-permute-start | bytes 737288 | tf_op jit(solution)/shard_map/ppermute | solution.py:264
  7.9 21.6 %collective-permute-start.2 = (bf16[64,3840]{1,0:T(8,128)(2,1)S(1)}, bf16[64,3840]{1,0:T(8,128)(2,1)S(1)}, u32[]{:S(2)}, u32[]{:S(2)}) collective-permute-start(bf16[64,3840]{1,0:T(8,128)(2,1)S(1)} %get-tuple-element.28), channel_id=1, source_target_pairs={{0,3},{1,4},{2,1},{3,6},{4,7},{5,0},{6,5},{7,2},{8,11},{9,12},{10,... | collective-permute-start | bytes 1474568 | tf_op jit(solution)/shard_map/ppermute | solution.py:264
  9.0 21.3 %collective-permute-start.4 = (bf16[64,3840]{1,0:T(8,128)(2,1)S(1)}, bf16[64,3840]{1,0:T(8,128)(2,1)S(1)}, u32[]{:S(2)}, u32[]{:S(2)}) collective-permute-start(bf16[64,3840]{1,0:T(8,128)(2,1)S(1)} %get-tuple-element.30), channel_id=1, source_target_pairs={{0,5},{1,2},{2,7},{3,0},{4,1},{5,6},{6,3},{7,4},{8,13},{9,10},{10,... | collective-permute-start | bytes 1474568 | tf_op jit(solution)/shard_map/ppermute | solution.py:264
  17.1 24.9 %collective-permute-start.6 = (bf16[64,3840]{1,0:T(8,128)(2,1)S(1)}, bf16[64,3840]{1,0:T(8,128)(2,1)S(1)}, u32[]{:S(2)}, u32[]{:S(2)}) collective-permute-start(bf16[64,3840]{1,0:T(8,128)(2,1)S(1)} %get-tuple-element.32), channel_id=1, source_target_pairs={{0,7},{1,6},{2,5},{3,4},{4,3},{5,2},{6,1},{7,0},{8,15},{9,14},{10,... | collective-permute-start | bytes 1474568 | tf_op jit(solution)/shard_map/ppermute | solution.py:264
  24.7 22.3 %collective-permute-start.3 = (bf16[64,3840]{1,0:T(8,128)(2,1)S(1)}, bf16[64,3840]{1,0:T(8,128)(2,1)S(1)}, u32[]{:S(2)}, u32[]{:S(2)}) collective-permute-start(bf16[64,3840]{1,0:T(8,128)(2,1)S(1)} %get-tuple-element.29), channel_id=1, source_target_pairs={{0,4},{1,3},{2,6},{3,1},{4,0},{5,7},{6,2},{7,5},{8,12},{9,11},{10,... | collective-permute-start | bytes 1474568 | tf_op jit(solution)/shard_map/ppermute | solution.py:264
  24.7 30.5 %collective-permute-start.5 = (bf16[64,3840]{1,0:T(8,128)(2,1)S(1)}, bf16[64,3840]{1,0:T(8,128)(2,1)S(1)}, u32[]{:S(2)}, u32[]{:S(2)}) collective-permute-start(bf16[64,3840]{1,0:T(8,128)(2,1)S(1)} %get-tuple-element.31), channel_id=1, source_target_pairs={{0,6},{1,7},{2,4},{3,5},{4,2},{5,3},{6,0},{7,1},{8,14},{9,15},{10,... | collective-permute-start | bytes 1474568 | tf_op jit(solution)/shard_map/ppermute | solution.py:264
  42.4 13.3 %collective-permute-start.8 = (f32[64,256]{1,0:T(8,128)S(1)}, f32[64,256]{1,0:T(8,128)S(1)}, u32[]{:S(2)}, u32[]{:S(2)}) collective-permute-start(f32[64,256]{1,0:T(8,128)S(1)} %shard_map.31), channel_id=1, source_target_pairs={{0,1},{1,0},{2,3},{3,2},{4,5},{5,4},{6,7},{7,6},{8,9},{9,8},{10,11... | collective-permute-start | bytes 196616 | tf_op jit(solution)/shard_map/ppermute | solution.py:264
  55.7 4.6 %collective-permute-start.10 = (f32[64,256]{1,0:T(8,128)S(1)}, f32[64,256]{1,0:T(8,128)S(1)}, u32[]{:S(2)}, u32[]{:S(2)}) collective-permute-start(f32[64,256]{1,0:T(8,128)S(1)} %add.24.refs_0_), channel_id=1, source_target_pairs={{0,4},{1,3},{2,6},{3,1},{4,0},{5,7},{6,2},{7,5},{8,12},{9,11},{10,... | collective-permute-start | bytes 196616 | tf_op jit(solution)/shard_map/ppermute | solution.py:264
  57.4 5.2 %collective-permute-start.11 = (f32[64,256]{1,0:T(8,128)S(1)}, f32[64,256]{1,0:T(8,128)S(1)}, u32[]{:S(2)}, u32[]{:S(2)}) collective-permute-start(f32[64,256]{1,0:T(8,128)S(1)} %add.24.refs_0_), channel_id=1, source_target_pairs={{0,6},{1,7},{2,4},{3,5},{4,2},{5,3},{6,0},{7,1},{8,14},{9,15},{10,... | collective-permute-start | bytes 196616 | tf_op jit(solution)/shard_map/ppermute | solution.py:264
  57.6 5.0 %collective-permute-start.9 = (f32[64,256]{1,0:T(8,128)S(1)}, f32[64,256]{1,0:T(8,128)S(1)}, u32[]{:S(2)}, u32[]{:S(2)}) collective-permute-start(f32[64,256]{1,0:T(8,128)S(1)} %add.24.refs_0_), channel_id=1, source_target_pairs={{0,2},{1,5},{2,0},{3,7},{4,6},{5,1},{6,4},{7,3},{8,10},{9,13},{10,... | collective-permute-start | bytes 196616 | tf_op jit(solution)/shard_map/ppermute | solution.py:264
  62.7 1.3 collective-permute-start.12
  64.5 21.2 %collective-permute-start.14 = (bf16[128,1152]{1,0:T(8,128)(2,1)S(1)}, bf16[128,1152]{1,0:T(8,128)(2,1)S(1)}, u32[]{:S(2)}, u32[]{:S(2)}) collective-permute-start(bf16[128,1152]{1,0:T(8,128)(2,1)S(1)} %shard_map.34.sent), channel_id=1, source_target_pairs={{0,8},{1,9},{2,10},{3,11},{4,12},{5,13},{6,14},{7,15},{8,0},{9,1},... | collective-permute-start | bytes 884744 | tf_op jit(solution)/shard_map/ppermute | solution.py:264
  67.7 21.7 %collective-permute-start.13 = (bf16[128,768]{1,0:T(8,128)(2,1)S(1)}, bf16[128,768]{1,0:T(8,128)(2,1)S(1)}, u32[]{:S(2)}, u32[]{:S(2)}) collective-permute-start(bf16[128,768]{1,0:T(8,128)(2,1)S(1)} %shard_map.33.sent), channel_id=1, source_target_pairs={{0,8},{1,9},{2,10},{3,11},{4,12},{5,13},{6,14},{7,15},{8,0},{9,1},... | collective-permute-start | bytes 589832 | tf_op jit(solution)/shard_map/ppermute | solution.py:264
  90.3 1.4 %collective-permute-start.15 = (f32[64,320]{1,0:T(8,128)S(1)}, f32[64,320]{1,0:T(8,128)S(1)}, u32[]{:S(2)}, u32[]{:S(2)}) collective-permute-start(f32[64,320]{1,0:T(8,128)S(1)} %shard_map.39), channel_id=1, source_target_pairs={{0,1},{1,0},{2,3},{3,2},{4,5},{5,4},{6,7},{7,6},{8,9},{9,8},{10,11... | collective-permute-start | bytes 245768 | tf_op jit(solution)/shard_map/ppermute | solution.py:264
  91.7 5.5 %collective-permute-start.16 = (f32[64,320]{1,0:T(8,128)S(1)}, f32[64,320]{1,0:T(8,128)S(1)}, u32[]{:S(2)}, u32[]{:S(2)}) collective-permute-start(f32[64,320]{1,0:T(8,128)S(1)} %add.25.refs_0_), channel_id=1, source_target_pairs={{0,2},{1,5},{2,0},{3,7},{4,6},{5,1},{6,4},{7,3},{8,10},{9,13},{10,... | collective-permute-start | bytes 245768 | tf_op jit(solution)/shard_map/ppermute | solution.py:264
  92.9 5.0 %collective-permute-start.17 = (f32[64,320]{1,0:T(8,128)S(1)}, f32[64,320]{1,0:T(8,128)S(1)}, u32[]{:S(2)}, u32[]{:S(2)}) collective-permute-start(f32[64,320]{1,0:T(8,128)S(1)} %add.25.refs_0_), channel_id=1, source_target_pairs={{0,4},{1,3},{2,6},{3,1},{4,0},{5,7},{6,2},{7,5},{8,12},{9,11},{10,... | collective-permute-start | bytes 245768 | tf_op jit(solution)/shard_map/ppermute | solution.py:264
  93.4 6.2 %collective-permute-start.18 = (f32[64,320]{1,0:T(8,128)S(1)}, f32[64,320]{1,0:T(8,128)S(1)}, u32[]{:S(2)}, u32[]{:S(2)}) collective-permute-start(f32[64,320]{1,0:T(8,128)S(1)} %add.25.refs_0_), channel_id=1, source_target_pairs={{0,6},{1,7},{2,4},{3,5},{4,2},{5,3},{6,0},{7,1},{8,14},{9,15},{10,... | collective-permute-start | bytes 245768 | tf_op jit(solution)/shard_map/ppermute | solution.py:264
  101.7 1.2 collective-permute-start.19
  103.4 14.3 %collective-permute-start.20 = (bf16[64,1920]{1,0:T(8,128)(2,1)S(1)}, bf16[64,1920]{1,0:T(8,128)(2,1)S(1)}, u32[]{:S(2)}, u32[]{:S(2)}) collective-permute-start(bf16[64,1920]{1,0:T(8,128)(2,1)S(1)} %shard_map.41), channel_id=1, source_target_pairs={{0,8},{1,9},{2,10},{3,11},{4,12},{5,13},{6,14},{7,15},{8,0},{9,1},... | collective-permute-start | bytes 737288 | tf_op jit(solution)/shard_map/ppermute | solution.py:264
  118.3 4.8 %collective-permute-start.21 = (f32[64,64]{1,0:T(8,128)S(1)}, f32[64,64]{1,0:T(8,128)S(1)}, u32[]{:S(2)}, u32[]{:S(2)}) collective-permute-start(f32[64,64]{1,0:T(8,128)S(1)} %get-tuple-element.43), channel_id=1, source_target_pairs={{0,9},{1,8},{2,11},{3,10},{4,13},{5,12},{6,15},{7,14},{8,1},{9,0},... | collective-permute-start | bytes 49160 | tf_op jit(solution)/shard_map/ppermute | solution.py:264
  118.3 5.6 %collective-permute-start.22 = (f32[64,64]{1,0:T(8,128)S(1)}, f32[64,64]{1,0:T(8,128)S(1)}, u32[]{:S(2)}, u32[]{:S(2)}) collective-permute-start(f32[64,64]{1,0:T(8,128)S(1)} %get-tuple-element.43), channel_id=1, source_target_pairs={{0,8},{1,9},{2,10},{3,11},{4,12},{5,13},{6,14},{7,15},{8,0},{9,1},... | collective-permute-start | bytes 49160 | tf_op jit(solution)/shard_map/ppermute | solution.py:264
  120.4 3.5 %collective-permute-start.23 = (f32[64,64]{1,0:T(8,128)S(1)}, f32[64,64]{1,0:T(8,128)S(1)}, u32[]{:S(2)}, u32[]{:S(2)}) collective-permute-start(f32[64,64]{1,0:T(8,128)S(1)} %get-tuple-element.43), channel_id=1, source_target_pairs={{0,1},{1,0},{2,3},{3,2},{4,5},{5,4},{6,7},{7,6},{8,9},{9,8},{10,11... | collective-permute-start | bytes 49160 | tf_op jit(solution)/shard_map/ppermute | solution.py:264
  123.9 4.9 %collective-permute-start.24 = (f32[64,64]{1,0:T(8,128)S(1)}, f32[64,64]{1,0:T(8,128)S(1)}, u32[]{:S(2)}, u32[]{:S(2)}) collective-permute-start(f32[64,64]{1,0:T(8,128)S(1)} %add_add_fusion.1), channel_id=1, source_target_pairs={{0,6},{1,7},{2,4},{3,5},{4,2},{5,3},{6,0},{7,1},{8,14},{9,15},{10,... | collective-permute-start | bytes 49160 | tf_op jit(solution)/shard_map/ppermute | solution.py:264
  126.5 3.9 %collective-permute-start.25 = (f32[64,64]{1,0:T(8,128)S(1)}, f32[64,64]{1,0:T(8,128)S(1)}, u32[]{:S(2)}, u32[]{:S(2)}) collective-permute-start(f32[64,64]{1,0:T(8,128)S(1)} %add_add_fusion.1), channel_id=1, source_target_pairs={{0,2},{1,5},{2,0},{3,7},{4,6},{5,1},{6,4},{7,3},{8,10},{9,13},{10,... | collective-permute-start | bytes 49160 | tf_op jit(solution)/shard_map/ppermute | solution.py:264
  127.9 3.9 %collective-permute-start.26 = (f32[64,64]{1,0:T(8,128)S(1)}, f32[64,64]{1,0:T(8,128)S(1)}, u32[]{:S(2)}, u32[]{:S(2)}) collective-permute-start(f32[64,64]{1,0:T(8,128)S(1)} %add_add_fusion.1), channel_id=1, source_target_pairs={{0,4},{1,3},{2,6},{3,1},{4,0},{5,7},{6,2},{7,5},{8,12},{9,11},{10,... | collective-permute-start | bytes 49160 | tf_op jit(solution)/shard_map/ppermute | solution.py:264

commit v12 on v11

--- a/solution.py
+++ b/solution.py
@@ -33,9 +33,14 @@
 
 
 def exact_nn(a, b):
-    a1, a2, a3 = three(a)
-    b1, b2, b3 = three(b)
-    return nn(jnp.concatenate([a3, a2, a1, a2, a1, a1], axis=1), jnp.concatenate([b1, b2, b3, b1, b2, b1], axis=0))
+    size = a.shape[0]
+    parts = three(a)
+    total = 0.0
+    for count, part in zip((1, 2, 3), reversed(three(b))):
+        product = nn(jnp.concatenate(parts[:count], axis=0), part)
+        for i in reversed(range(count)):
+            total = total + product[i * size:(i + 1) * size]
+    return total
 
 
 def exact_gram(a):
@@ -104,7 +109,7 @@
     gram = refs.pop(0)[...] if with_gram else None
     before, outs = refs[:-len(odds)], refs[-len(odds):]
     for i, odd in enumerate(odds):
-        left = 0
+        left, values = 0, []
         for pair, blocks in work:
             value = 0.0
             for block in blocks:
@@ -120,22 +125,29 @@
                 value = value.T
             if before and lanes.stop <= before[i].shape[1]:
                 value = value + before[i][:, lanes]
-            outs[i][:, lanes] = value
+            values.append(value)
         if with_gram:
-            outs[i][:, left:] = gram
+            rank = gram.shape[0]
+            rows = rank * rank // left
+            for j in range(rank // rows):
+                outs[i][rank:, j * rank:(j + 1) * rank] = gram[j * rows:(j + 1) * rows]
+            outs[i][:rank] = jnp.concatenate(values, axis=1)
+        else:
+            outs[i][...] = jnp.concatenate(values, axis=1) if len(values) > 1 else values[0]
 
 
 def scores(slots, work, bases, before=(), gram=None, offset=0, odds=(0, 1)):
     rank = next(iter(bases.values()))[0].shape[0]
     picked = [4 * pair + 2 * k + odd for pair, blocks in work if blocks for k in range(2) for odd in odds]
     rows, width = slots[picked[0]].shape[0], slots[picked[0]].shape[1] // 2
-    cells = 2 * rows * len(work) + (0 if gram is None else rank)
+    cells = 2 * rows * len(work)
+    height = rank + (0 if gram is None else rank * rank // cells)
     counts = [(block, len(parts)) for block, parts in bases.items()]
     args = [x for parts in bases.values() for x in parts] + [slots[k] for k in picked]
     args += ([] if gram is None else [gram]) + list(before)
     size = 2 * len(odds) * rows * width * sum(len(blocks) for _, blocks in work)
     kernel = functools.partial(scores_kernel, work, odds, counts, picked, gram is not None, width, offset)
-    return call(kernel, args, [struct((rank, cells), f32)] * len(odds), cost(2 * rank * size, 2 * size))
+    return call(kernel, args, [struct((height, cells), f32)] * len(odds), cost(2 * rank * size, 2 * size))
 
 
 def image_kernel(normalised, *refs):
@@ -146,15 +158,19 @@
     def turned(x, mask):
         return jnp.concatenate([x[:, (j ^ mask) * size:((j ^ mask) + 1) * size] for j in range(GROUP // 2)], axis=1)
 
-    value = (values[0][:, :cells] + turned(values[3], 3)) + (turned(values[1], 1) + turned(values[2], 2))
+    rank = out.shape[0]
+    top = [x[:rank] for x in values]
+    value = (top[0] + turned(top[3], 3)) + (turned(top[1], 1) + turned(top[2], 2))
     if normalised:
-        gram = [x[:, cells:] for x in values]
-        value = exact_nn(inverse_factor((gram[0] + gram[3]) + (gram[1] + gram[2])), value)
+        below = [x[rank:] for x in values]
+        below = (below[0] + below[3]) + (below[1] + below[2])
+        gram = jnp.concatenate([below[:, j * rank:(j + 1) * rank] for j in range(cells // rank)], axis=0)
+        value = exact_nn(inverse_factor(gram), value)
     out[...] = value.astype(bf16)
 
 
-def image_of(value, mates, rows, normalised):
-    rank, cells = value.shape[0], rows * GROUP // 2
+def image_of(value, mates, rank, normalised):
+    cells = value.shape[1]
     return call(functools.partial(image_kernel, normalised), [value, *mates], [struct((rank, cells), bf16)],
                 cost(12 * value.size * rank, 16 * value.size))[0]
 
@@ -201,15 +217,19 @@
                 cost(24 * rank * rank * width, 24 * rank * width))
 
 
-def loading_kernel(received, own, loading, gram):
+def loading_kernel(received, own, *refs):
+    before, loading, gram = refs[:-2], refs[-2], refs[-1]
     value = own[...] + received[...].astype(f32)
     loading[...] = value
-    gram[...] = exact_gram(value)
-
-
-def loading_and_gram(received, own):
+    total = exact_gram(value)
+    for ref in before:
+        total = total + ref[...]
+    gram[...] = total
+
+
+def loading_and_gram(received, own, before):
     rank, width = own.shape
-    return call(loading_kernel, [received, own], [struct((rank, width), f32), struct((rank, rank), f32)],
+    return call(loading_kernel, [received, own, *before], [struct((rank, width), f32), struct((rank, rank), f32)],
                 cost(12 * rank * rank * width, 12 * rank * width))
 
 
@@ -228,17 +248,13 @@
             {k: jnp.broadcast_to(blocks[k][:, 8 * b + t:8 * b + t + 1], shape) for k in range(b, panels)}
             for t in range(8)
         ]
-        corner = {(s, t): jnp.broadcast_to(columns[t][b][s:s + 1], shape) for t in range(8) for s in range(t, 8)}
         for t in range(8):
-            root = lax.rsqrt(corner[t, t])
-            along = {s: corner[s, t] * root for s in range(t + 1, 8)}
-            for u in range(t + 1, 8):
-                for s in range(u, 8):
-                    corner[s, u] = corner[s, u] - along[s] * along[u]
+            root = lax.rsqrt(jnp.broadcast_to(columns[t][b][t:t + 1], shape))
             scaled = {k: x * root for k, x in columns[t].items()}
             for s in range(t + 1, 8):
+                along = jnp.broadcast_to(scaled[b][s:s + 1], shape)
                 for k in range(b, panels):
-                    columns[s][k] = columns[s][k] - scaled[k] * along[s]
+                    columns[s][k] = columns[s][k] - scaled[k] * along
             pivot = jnp.broadcast_to(blocks[b][t:t + 1], shape) * root
             done.append(pivot[:1])
             for k in range(b, panels):
@@ -247,16 +263,19 @@
     return jnp.concatenate(done, axis=0)[:, size:]
 
 
-def output_kernel(scale, gram, loading, out):
-    out[...] = exact_nn(inverse_factor(gram[...]), loading[...]) * scale
-
-
-def output_call(gram, loading):
-    return pl.pallas_call(
-        functools.partial(output_kernel, math.sqrt(GENES)),
-        in_specs=[VMEM, VMEM], out_specs=VMEM, out_shape=struct(loading.shape, f32),
-        compiler_params=pltpu.CompilerParams(vmem_limit_bytes=16 * 2**20),
-    )(gram, loading)
+def output_kernel(scale, gram, *refs):
+    parts, out = refs[:-1], refs[-1]
+    inverse = inverse_factor(gram[...]) * scale
+    start = 0
+    for part in parts:
+        out[:, start:start + part.shape[1]] = exact_nn(inverse, part[...])
+        start += part.shape[1]
+
+
+def output_call(gram, parts):
+    rank, width = gram.shape[0], sum(x.shape[1] for x in parts)
+    return call(functools.partial(output_kernel, math.sqrt(GENES)), [gram, *parts], [struct((rank, width), f32)],
+                cost(12 * rank * rank * width, 8 * rank * width))[0]
 
 
 def mate(value, cells, mask, other=None):
@@ -274,8 +293,16 @@
     return (value + both_ways) + (one + two)
 
 
+def cuts(width, *percents):
+    edges = [0]
+    for percent in percents:
+        edges.append(edges[-1] + -(-percent * width // 12800) * 128)
+    edges = [edge for edge in edges if edge < width] + [width]
+    return list(zip(edges, edges[1:]))
+
+
 def square_program(cells, expression, start_basis):
-    width, rows = start_basis.shape[0], expression.shape[0]
+    width, rank = start_basis.shape
     masks = ((0, 0), (1, 1), (2, 4), (3, 5), (4, 2), (5, 3), (6, 6), (7, 7))
     packs = pack(expression, masks, width)
     slots = [mate(x, cells, *pair) if k else x for k, (x, pair) in enumerate(zip(packs, masks))]
@@ -284,27 +311,35 @@
         (odd,) = scores(slots, work, bases, before[1:], *rest, odds=(1,))
         (even,) = scores(slots, work, bases, before[:1], *rest, odds=(0,))
         even = even + mate(odd, cells, 1)
-        image = image_of(even, legs(even, cells), rows, normalised)
+        image = image_of(even, legs(even, cells), rank, normalised)
         return image, mate(image, cells, 1)
 
-    first = -(-6 * width // 1280) * 128
     basis = start_basis.T
     bases = {0: [basis], 1: [mate(basis, cells, GROUP)]}
     early = scores(slots, [(0, (0, 1))], bases)
     images = image_from([(0, ()), (1, (0, 1))], bases, early, False)
     everything = [(0, (0, 1)), (1, (0, 1))]
     for _ in range(1, ITERS):
-        rows_of, total = [], []
-        for start, stop in ((0, first), (first, width)):
+        total, before = [], ()
+        arrived = []
+        for start, stop in cuts(width, 45, 33):
             sent = terms(slots, (start, width + start), stop - start, images, bf16)
-            own, other, gram = both(sent, mate(sent, cells, GROUP), total)
-            rows_of.append({0: [own], 1: [other]})
-            total = [gram]
-        early = scores(slots, everything, rows_of[0])
-        images = image_from(everything, rows_of[1], early, True, gram, first)
-    received = mate(terms(slots, (width,), width, images, bf16), cells, GROUP)
-    loading, gram = loading_and_gram(received, terms(slots, (0,), width, images, f32))
-    return output_call(total_over_cells(gram, cells), loading).T
+            arrived.append((start, stop, sent, mate(sent, cells, GROUP)))
+        for start, stop, sent, received in arrived:
+            if before:
+                received, *before = lax.optimization_barrier((received, *before))
+            own, other, gram = both(sent, received, total)
+            total, rows = [gram], {0: [own], 1: [other]}
+            if stop < width:
+                before = scores(slots, everything, rows, before, offset=start)
+        images = image_from(everything, rows, before, True, gram, start)
+    parts, total = [], []
+    for start, stop in cuts(width, 60):
+        received = mate(terms(slots, (width + start,), stop - start, images, bf16), cells, GROUP)
+        rows, gram = loading_and_gram(received, terms(slots, (start,), stop - start, images, f32), total)
+        parts.append(rows)
+        total = [gram]
+    return output_call(total_over_cells(gram, cells), parts).T
 
 
 def plain_program(expression, start_basis):

time: 135 us -> 134 us (level)
  waiting for transfers between devices: 84.6 us -> 78.9 us
  starting transfers between devices: 35.9 us -> 38.7 us
  Pallas kernels: 14.3 us -> 15.7 us
    ppermute x27 -> x29, waiting for transfers between devices: 84.6 us -> 78.9 us  [mate(): lax.ppermute(value, 'cell', [(i, i ^ masks[i % 2]) for i in range(cells)])]
    pallas_call x15 -> x22, Pallas kernels: 8.92 us -> 13.4 us  [call(): pl.pallas_call(kernel, in_specs=[VMEM] * len(args), out_specs=[VMEM] * le...]
    pallas_call x1 -> x0, Pallas kernels: 3.12 us -> none  [output_call(): pl.pallas_call(functools.partial(output_kernel, math.sqrt(GENES)), in_spe...]
    ppermute x27 -> x29, starting transfers between devices: 35.9 us -> 38.7 us  [mate(): lax.ppermute(value, 'cell', [(i, i ^ masks[i % 2]) for i in range(cells)])]
  transfers between devices with their start and end apart: 27 -> 29, of which waited for: 21 -> 23; matrix products, arithmetic and copies ran while one was open for 0% -> 0% of each run, Pallas kernels for 3% -> 5%
where the time goes in v12:
time: 134 us
  waiting for transfers between devices  78.9 us (59%)
  starting transfers between devices  38.7 us (29%)
  Pallas kernels  15.7 us (12%)
    ppermute x29, waiting for transfers between devices, mate(): lax.ppermute(value, 'cell', [(i, i ^ masks[i % 2]) for i in range(cells)])  78.9 us
    ppermute x29, starting transfers between devices, mate(): lax.ppermute(value, 'cell', [(i, i ^ masks[i % 2]) for i in range(cells)])  38.7 us
    pallas_call x22, Pallas kernels, call(): pl.pallas_call(kernel, in_specs=[VMEM] * len(args), out_specs=[VMEM] * le...  13.4 us
  transfers between devices with their start and end apart: 29, of which 23 were waited for; matrix products, arithmetic and copies ran while one was open for 0% of the time, Pallas kernels for 5%

profile of v12, /device:TPU:0, one launch (start us, length us, event | category | flops | bytes accessed | tf_op | source)
XLA Modules:
  0.0 133.5 jit_solution(15859783278893205673)
XLA Ops:
  0.0 2.2 %shard_map.28 = (bf16[64,3840]{1,0:T(8,128)(2,1)S(1)}, bf16[64,3840]{1,0:T(8,128)(2,1)S(1)}, bf16[64,3840]{1,0:T(8,128)(2,1)S(1)}, bf16[64,3840]{1,0:T(8,128)(2,...) custom-call(bf16[64,30720]{1,0:T(8,128)(2,1)} %matrix.1), custom_call_target="tpu_custom_call" | custom-call | bytes 7864320 | tf_op jit(solution)/shard_map/pallas_call | solution.py:87
  2.8 2.6 %collective-permute-start.1 = (bf16[64,3840]{1,0:T(8,128)(2,1)S(1)}, bf16[64,3840]{1,0:T(8,128)(2,1)S(1)}, u32[]{:S(2)}, u32[]{:S(2)}) collective-permute-start(bf16[64,3840]{1,0:T(8,128)(2,1)S(1)} %get-tuple-element.40), channel_id=1, source_target_pairs={{0,2},{1,5},{2,0},{3,7},{4,6},{5,1},{6,4},{7,3},{8,10},{9,13},{10,... | collective-permute-start | bytes 1474568 | tf_op jit(solution)/shard_map/ppermute | solution.py:283
  5.4 2.6 %collective-permute-start.7 = (bf16[64,1920]{1,0:T(8,128)(2,1)S(1)}, bf16[64,1920]{1,0:T(8,128)(2,1)S(1)}, u32[]{:S(2)}, u32[]{:S(2)}) collective-permute-start(bf16[64,1920]{1,0:T(8,128)(2,1)S(1)} %bitcast.2), channel_id=1, source_target_pairs={{0,8},{1,9},{2,10},{3,11},{4,12},{5,13},{6,14},{7,15},{8,0},{9,1},... | collective-permute-start | bytes 737288 | tf_op jit(solution)/shard_map/ppermute | solution.py:283
  9.7 7.4 %collective-permute-done.7.refs_1_ = bf16[64,1920]{1,0:T(8,128)(2,1)S(1)} collective-permute-done((bf16[64,1920]{1,0:T(8,128)(2,1)S(1)}, bf16[64,1920]{1,0:T(8,128)(2,1)S(1)}, u32[]{:S(2)}, u32[]{:S(2)}) %collective-permute-start.7) | collective-permute-done | bytes 245792 | tf_op jit(solution)/shard_map/ppermute | solution.py:283
  17.1 7.6 %collective-permute-start.6 = (bf16[64,3840]{1,0:T(8,128)(2,1)S(1)}, bf16[64,3840]{1,0:T(8,128)(2,1)S(1)}, u32[]{:S(2)}, u32[]{:S(2)}) collective-permute-start(bf16[64,3840]{1,0:T(8,128)(2,1)S(1)} %get-tuple-element.45), channel_id=1, source_target_pairs={{0,7},{1,6},{2,5},{3,4},{4,3},{5,2},{6,1},{7,0},{8,15},{9,14},{10,... | collective-permute-start | bytes 1474568 | tf_op jit(solution)/shard_map/ppermute | solution.py:283
  25.6 4.0 %collective-permute-done.2.refs_5_.refs_3_ = bf16[64,3840]{1,0:T(8,128)(2,1)S(1)} collective-permute-done((bf16[64,3840]{1,0:T(8,128)(2,1)S(1)}, bf16[64,3840]{1,0:T(8,128)(2,1)S(1)}, u32[]{:S(2)}, u32[]{:S(2)}) %collective-permute-start.2) | collective-permute-done | bytes 491552 | tf_op jit(solution)/shard_map/ppermute | solution.py:283
  30.3 11.6 %collective-permute-done.6.refs_3_.refs_7_.refs_9_.refs_5_ = bf16[64,3840]{1,0:T(8,128)(2,1)S(1)} collective-permute-done((bf16[64,3840]{1,0:T(8,128)(2,1)S(1)}, bf16[64,3840]{1,0:T(8,128)(2,1)S(1)}, u32[]{:S(2)}, u32[]{:S(2)}) %collective-permute-start.6) | collective-permute-done | bytes 491552 | tf_op jit(solution)/shard_map/ppermute | solution.py:283
  42.5 4.5 %collective-permute-done.3.refs_2_.refs_4_.refs_6_ = bf16[64,3840]{1,0:T(8,128)(2,1)S(1)} collective-permute-done((bf16[64,3840]{1,0:T(8,128)(2,1)S(1)}, bf16[64,3840]{1,0:T(8,128)(2,1)S(1)}, u32[]{:S(2)}, u32[]{:S(2)}) %collective-permute-start.3) | collective-permute-done | bytes 491552 | tf_op jit(solution)/shard_map/ppermute | solution.py:283
  47.0 8.2 %collective-permute-done.5.refs_3_.refs_6_.refs_8_.refs_5_ = bf16[64,3840]{1,0:T(8,128)(2,1)S(1)} collective-permute-done((bf16[64,3840]{1,0:T(8,128)(2,1)S(1)}, bf16[64,3840]{1,0:T(8,128)(2,1)S(1)}, u32[]{:S(2)}, u32[]{:S(2)}) %collective-permute-start.5) | collective-permute-done | bytes 491552 | tf_op jit(solution)/shard_map/ppermute | solution.py:283
  55.7 1.7 %collective-permute-start.10 = (f32[64,256]{1,0:T(8,128)S(1)}, f32[64,256]{1,0:T(8,128)S(1)}, u32[]{:S(2)}, u32[]{:S(2)}) collective-permute-start(f32[64,256]{1,0:T(8,128)S(1)} %add.24.refs_0_), channel_id=1, source_target_pairs={{0,4},{1,3},{2,6},{3,1},{4,0},{5,7},{6,2},{7,5},{8,12},{9,11},{10,... | collective-permute-start | bytes 196616 | tf_op jit(solution)/shard_map/ppermute | solution.py:283
  57.6 1.6 %collective-permute-start.9 = (f32[64,256]{1,0:T(8,128)S(1)}, f32[64,256]{1,0:T(8,128)S(1)}, u32[]{:S(2)}, u32[]{:S(2)}) collective-permute-start(f32[64,256]{1,0:T(8,128)S(1)} %add.24.refs_0_), channel_id=1, source_target_pairs={{0,2},{1,5},{2,0},{3,7},{4,6},{5,1},{6,4},{7,3},{8,10},{9,13},{10,... | collective-permute-start | bytes 196616 | tf_op jit(solution)/shard_map/ppermute | solution.py:283
  60.3 2.3 %collective-permute-done.11.refs_3_ = f32[64,256]{1,0:T(8,128)S(1)} collective-permute-done((f32[64,256]{1,0:T(8,128)S(1)}, f32[64,256]{1,0:T(8,128)S(1)}, u32[]{:S(2)}, u32[]{:S(2)}) %collective-permute-start.11) | collective-permute-done | bytes 65568 | tf_op jit(solution)/shard_map/ppermute | solution.py:283
  62.8 1.2 collective-permute-done.12.refs_9_
  64.4 2.8 %collective-permute-start.15 = (bf16[128,896]{1,0:T(8,128)(2,1)S(1)}, bf16[128,896]{1,0:T(8,128)(2,1)S(1)}, u32[]{:S(2)}, u32[]{:S(2)}) collective-permute-start(bf16[128,896]{1,0:T(8,128)(2,1)S(1)} %shard_map.35.sent), channel_id=1, source_target_pairs={{0,8},{1,9},{2,10},{3,11},{4,12},{5,13},{6,14},{7,15},{8,0},{9,1},... | collective-permute-start | bytes 688136 | tf_op jit(solution)/shard_map/ppermute | solution.py:283
  68.0 2.8 %collective-permute-start.13 = (bf16[128,384]{1,0:T(8,128)(2,1)S(1)}, bf16[128,384]{1,0:T(8,128)(2,1)S(1)}, u32[]{:S(2)}, u32[]{:S(2)}) collective-permute-start(bf16[128,384]{1,0:T(8,128)(2,1)S(1)} %shard_map.33.sent), channel_id=1, source_target_pairs={{0,8},{1,9},{2,10},{3,11},{4,12},{5,13},{6,14},{7,15},{8,0},{9,1},... | collective-permute-start | bytes 294920 | tf_op jit(solution)/shard_map/ppermute | solution.py:283
  70.8 13.3 %collective-permute-done.15.received = bf16[128,896]{1,0:T(8,128)(2,1)S(1)} collective-permute-done((bf16[128,896]{1,0:T(8,128)(2,1)S(1)}, bf16[128,896]{1,0:T(8,128)(2,1)S(1)}, u32[]{:S(2)}, u32[]{:S(2)}) %collective-permute-start.15) | collective-permute-done | bytes 229408 | tf_op jit(solution)/shard_map/ppermute | solution.py:283
  85.4 2.2 %collective-permute-done.14.received = bf16[128,640]{1,0:T(8,128)(2,1)S(1)} collective-permute-done((bf16[128,640]{1,0:T(8,128)(2,1)S(1)}, bf16[128,640]{1,0:T(8,128)(2,1)S(1)}, u32[]{:S(2)}, u32[]{:S(2)}) %collective-permute-start.14) | collective-permute-done | bytes 163872 | tf_op jit(solution)/shard_map/ppermute | solution.py:283
  91.4 1.2 collective-permute-start.17
  93.1 1.9 %collective-permute-start.19 = (f32[80,256]{1,0:T(8,128)S(1)}, f32[80,256]{1,0:T(8,128)S(1)}, u32[]{:S(2)}, u32[]{:S(2)}) collective-permute-start(f32[80,256]{1,0:T(8,128)S(1)} %add.25.refs_0_), channel_id=1, source_target_pairs={{0,6},{1,7},{2,4},{3,5},{4,2},{5,3},{6,0},{7,1},{8,14},{9,15},{10,... | collective-permute-start | bytes 245768 | tf_op jit(solution)/shard_map/ppermute | solution.py:283
  96.1 1.2 collective-permute-done.18.refs_2_
  97.3 1.6 %collective-permute-done.19.refs_3_ = f32[80,256]{1,0:T(8,128)S(1)} collective-permute-done((f32[80,256]{1,0:T(8,128)S(1)}, f32[80,256]{1,0:T(8,128)S(1)}, u32[]{:S(2)}, u32[]{:S(2)}) %collective-permute-start.19) | collective-permute-done | bytes 81952 | tf_op jit(solution)/shard_map/ppermute | solution.py:283
  98.8 2.0 %shard_map.43.refs_8_ = bf16[64,256]{1,0:T(8,128)(2,1)S(1)} custom-call(f32[80,256]{1,0:T(8,128)S(1)} %add.25.refs_0_, f32[80,256]{1,0:T(8,128)S(1)} %collective-permute-done.17.refs_1_, f32[80,256]{1,0:T(8,128)S(1)} %collective-permute-done.18.refs_2_, f32[80,256]{1,0:T(8,128)S(1)} %collective-permute-done.19.refs_3_), custom_call_target="tpu_custom_call" | custom-call | flops 15728640 | bytes 327680 | tf_op jit(solution)/shard_map/pallas_call | solution.py:99
  101.0 1.2 collective-permute-done.20.refs_9_
  102.5 3.1 %collective-permute-start.22 = (bf16[64,1152]{1,0:T(8,128)(2,1)S(1)}, bf16[64,1152]{1,0:T(8,128)(2,1)S(1)}, u32[]{:S(2)}, u32[]{:S(2)}) collective-permute-start(bf16[64,1152]{1,0:T(8,128)(2,1)S(1)} %shard_map.46), channel_id=1, source_target_pairs={{0,8},{1,9},{2,10},{3,11},{4,12},{5,13},{6,14},{7,15},{8,0},{9,1},... | collective-permute-start | bytes 442376 | tf_op jit(solution)/shard_map/ppermute | solution.py:283
  106.4 8.9 %collective-permute-done.22.received = bf16[64,1152]{1,0:T(8,128)(2,1)S(1)} collective-permute-done((bf16[64,1152]{1,0:T(8,128)(2,1)S(1)}, bf16[64,1152]{1,0:T(8,128)(2,1)S(1)}, u32[]{:S(2)}, u32[]{:S(2)}) %collective-permute-start.22) | collective-permute-done | bytes 147488 | tf_op jit(solution)/shard_map/ppermute | solution.py:283
  115.8 1.3 collective-permute-done.21.received
  117.6 2.3 %collective-permute-start.24 = (f32[64,64]{1,0:T(8,128)S(1)}, f32[64,64]{1,0:T(8,128)S(1)}, u32[]{:S(2)}, u32[]{:S(2)}) collective-permute-start(f32[64,64]{1,0:T(8,128)S(1)} %get-tuple-element.68), channel_id=1, source_target_pairs={{0,8},{1,9},{2,10},{3,11},{4,12},{5,13},{6,14},{7,15},{8,0},{9,1},... | collective-permute-start | bytes 49160 | tf_op jit(solution)/shard_map/ppermute | solution.py:283
  120.4 2.2 %collective-permute-done.23 = f32[64,64]{1,0:T(8,128)S(1)} collective-permute-done((f32[64,64]{1,0:T(8,128)S(1)}, f32[64,64]{1,0:T(8,128)S(1)}, u32[]{:S(2)}, u32[]{:S(2)}) %collective-permute-start.23) | collective-permute-done | bytes 16416 | tf_op jit(solution)/shard_map/ppermute | solution.py:283
  123.2 2.1 %collective-permute-start.26 = (f32[64,64]{1,0:T(8,128)S(1)}, f32[64,64]{1,0:T(8,128)S(1)}, u32[]{:S(2)}, u32[]{:S(2)}) collective-permute-start(f32[64,64]{1,0:T(8,128)S(1)} %add_add_fusion.1), channel_id=1, source_target_pairs={{0,6},{1,7},{2,4},{3,5},{4,2},{5,3},{6,0},{7,1},{8,14},{9,15},{10,... | collective-permute-start | bytes 49160 | tf_op jit(solution)/shard_map/ppermute | solution.py:283
  125.3 1.1 collective-permute-start.27
  126.7 1.4 %collective-permute-done.26 = f32[64,64]{1,0:T(8,128)S(1)} collective-permute-done((f32[64,64]{1,0:T(8,128)S(1)}, f32[64,64]{1,0:T(8,128)S(1)}, u32[]{:S(2)}, u32[]{:S(2)}) %collective-permute-start.26) | collective-permute-done | bytes 16416 | tf_op jit(solution)/shard_map/ppermute | solution.py:283
  130.4 3.2 %shard_map.50 = f32[64,1920]{1,0:T(8,128)} custom-call(f32[64,64]{1,0:T(8,128)S(1)} %add_add_fusion.gram, f32[64,1152]{1,0:T(8,128)S(1)} %get-tuple-element.69.refs_0_, f32[64,768]{1,0:T(8,128)S(1)} %get-tuple-element.70.refs_1_), custom_call_target="tpu_custom_call" | custom-call | flops 94371840 | bytes 983040 | tf_op jit(solution)/shard_map/pallas_call | solution.py:99
  (55 shorter events, 20.1 us)
Async XLA Ops:
  0.0 5.4 %copy-start = (bf16[1920,64]{0,1:T(8,128)(2,1)S(1)}, bf16[1920,64]{0,1:T(8,128)(2,1)}, u32[]{:S(2)}) copy-start(bf16[1920,64]{0,1:T(8,128)(2,1)} %param.3) | copy-start | bytes 737284
  2.2 22.5 %collective-permute-start = (bf16[64,3840]{1,0:T(8,128)(2,1)S(1)}, bf16[64,3840]{1,0:T(8,128)(2,1)S(1)}, u32[]{:S(2)}, u32[]{:S(2)}) collective-permute-start(bf16[64,3840]{1,0:T(8,128)(2,1)S(1)} %get-tuple-element.39), channel_id=1, source_target_pairs={{0,1},{1,0},{2,3},{3,2},{4,5},{5,4},{6,7},{7,6},{8,9},{9,8},{10,11... | collective-permute-start | bytes 1474568 | tf_op jit(solution)/shard_map/ppermute | solution.py:283
  2.8 22.0 %collective-permute-start.1 = (bf16[64,3840]{1,0:T(8,128)(2,1)S(1)}, bf16[64,3840]{1,0:T(8,128)(2,1)S(1)}, u32[]{:S(2)}, u32[]{:S(2)}) collective-permute-start(bf16[64,3840]{1,0:T(8,128)(2,1)S(1)} %get-tuple-element.40), channel_id=1, source_target_pairs={{0,2},{1,5},{2,0},{3,7},{4,6},{5,1},{6,4},{7,3},{8,10},{9,13},{10,... | collective-permute-start | bytes 1474568 | tf_op jit(solution)/shard_map/ppermute | solution.py:283
  5.4 11.7 %collective-permute-start.7 = (bf16[64,1920]{1,0:T(8,128)(2,1)S(1)}, bf16[64,1920]{1,0:T(8,128)(2,1)S(1)}, u32[]{:S(2)}, u32[]{:S(2)}) collective-permute-start(bf16[64,1920]{1,0:T(8,128)(2,1)S(1)} %bitcast.2), channel_id=1, source_target_pairs={{0,8},{1,9},{2,10},{3,11},{4,12},{5,13},{6,14},{7,15},{8,0},{9,1},... | collective-permute-start | bytes 737288 | tf_op jit(solution)/shard_map/ppermute | solution.py:283
  7.9 21.6 %collective-permute-start.2 = (bf16[64,3840]{1,0:T(8,128)(2,1)S(1)}, bf16[64,3840]{1,0:T(8,128)(2,1)S(1)}, u32[]{:S(2)}, u32[]{:S(2)}) collective-permute-start(bf16[64,3840]{1,0:T(8,128)(2,1)S(1)} %get-tuple-element.41), channel_id=1, source_target_pairs={{0,3},{1,4},{2,1},{3,6},{4,7},{5,0},{6,5},{7,2},{8,11},{9,12},{10,... | collective-permute-start | bytes 1474568 | tf_op jit(solution)/shard_map/ppermute | solution.py:283
  9.0 21.3 %collective-permute-start.4 = (bf16[64,3840]{1,0:T(8,128)(2,1)S(1)}, bf16[64,3840]{1,0:T(8,128)(2,1)S(1)}, u32[]{:S(2)}, u32[]{:S(2)}) collective-permute-start(bf16[64,3840]{1,0:T(8,128)(2,1)S(1)} %get-tuple-element.43), channel_id=1, source_target_pairs={{0,5},{1,2},{2,7},{3,0},{4,1},{5,6},{6,3},{7,4},{8,13},{9,10},{10,... | collective-permute-start | bytes 1474568 | tf_op jit(solution)/shard_map/ppermute | solution.py:283
  17.1 24.9 %collective-permute-start.6 = (bf16[64,3840]{1,0:T(8,128)(2,1)S(1)}, bf16[64,3840]{1,0:T(8,128)(2,1)S(1)}, u32[]{:S(2)}, u32[]{:S(2)}) collective-permute-start(bf16[64,3840]{1,0:T(8,128)(2,1)S(1)} %get-tuple-element.45), channel_id=1, source_target_pairs={{0,7},{1,6},{2,5},{3,4},{4,3},{5,2},{6,1},{7,0},{8,15},{9,14},{10,... | collective-permute-start | bytes 1474568 | tf_op jit(solution)/shard_map/ppermute | solution.py:283
  24.7 22.3 %collective-permute-start.3 = (bf16[64,3840]{1,0:T(8,128)(2,1)S(1)}, bf16[64,3840]{1,0:T(8,128)(2,1)S(1)}, u32[]{:S(2)}, u32[]{:S(2)}) collective-permute-start(bf16[64,3840]{1,0:T(8,128)(2,1)S(1)} %get-tuple-element.42), channel_id=1, source_target_pairs={{0,4},{1,3},{2,6},{3,1},{4,0},{5,7},{6,2},{7,5},{8,12},{9,11},{10,... | collective-permute-start | bytes 1474568 | tf_op jit(solution)/shard_map/ppermute | solution.py:283
  24.7 30.5 %collective-permute-start.5 = (bf16[64,3840]{1,0:T(8,128)(2,1)S(1)}, bf16[64,3840]{1,0:T(8,128)(2,1)S(1)}, u32[]{:S(2)}, u32[]{:S(2)}) collective-permute-start(bf16[64,3840]{1,0:T(8,128)(2,1)S(1)} %get-tuple-element.44), channel_id=1, source_target_pairs={{0,6},{1,7},{2,4},{3,5},{4,2},{5,3},{6,0},{7,1},{8,14},{9,15},{10,... | collective-permute-start | bytes 1474568 | tf_op jit(solution)/shard_map/ppermute | solution.py:283
  42.4 13.3 %collective-permute-start.8 = (f32[64,256]{1,0:T(8,128)S(1)}, f32[64,256]{1,0:T(8,128)S(1)}, u32[]{:S(2)}, u32[]{:S(2)}) collective-permute-start(f32[64,256]{1,0:T(8,128)S(1)} %shard_map.31), channel_id=1, source_target_pairs={{0,1},{1,0},{2,3},{3,2},{4,5},{5,4},{6,7},{7,6},{8,9},{9,8},{10,11... | collective-permute-start | bytes 196616 | tf_op jit(solution)/shard_map/ppermute | solution.py:283
  55.7 4.6 %collective-permute-start.10 = (f32[64,256]{1,0:T(8,128)S(1)}, f32[64,256]{1,0:T(8,128)S(1)}, u32[]{:S(2)}, u32[]{:S(2)}) collective-permute-start(f32[64,256]{1,0:T(8,128)S(1)} %add.24.refs_0_), channel_id=1, source_target_pairs={{0,4},{1,3},{2,6},{3,1},{4,0},{5,7},{6,2},{7,5},{8,12},{9,11},{10,... | collective-permute-start | bytes 196616 | tf_op jit(solution)/shard_map/ppermute | solution.py:283
  57.4 5.2 %collective-permute-start.11 = (f32[64,256]{1,0:T(8,128)S(1)}, f32[64,256]{1,0:T(8,128)S(1)}, u32[]{:S(2)}, u32[]{:S(2)}) collective-permute-start(f32[64,256]{1,0:T(8,128)S(1)} %add.24.refs_0_), channel_id=1, source_target_pairs={{0,6},{1,7},{2,4},{3,5},{4,2},{5,3},{6,0},{7,1},{8,14},{9,15},{10,... | collective-permute-start | bytes 196616 | tf_op jit(solution)/shard_map/ppermute | solution.py:283
  57.6 5.0 %collective-permute-start.9 = (f32[64,256]{1,0:T(8,128)S(1)}, f32[64,256]{1,0:T(8,128)S(1)}, u32[]{:S(2)}, u32[]{:S(2)}) collective-permute-start(f32[64,256]{1,0:T(8,128)S(1)} %add.24.refs_0_), channel_id=1, source_target_pairs={{0,2},{1,5},{2,0},{3,7},{4,6},{5,1},{6,4},{7,3},{8,10},{9,13},{10,... | collective-permute-start | bytes 196616 | tf_op jit(solution)/shard_map/ppermute | solution.py:283
  62.7 1.3 collective-permute-start.12
  64.4 19.8 %collective-permute-start.15 = (bf16[128,896]{1,0:T(8,128)(2,1)S(1)}, bf16[128,896]{1,0:T(8,128)(2,1)S(1)}, u32[]{:S(2)}, u32[]{:S(2)}) collective-permute-start(bf16[128,896]{1,0:T(8,128)(2,1)S(1)} %shard_map.35.sent), channel_id=1, source_target_pairs={{0,8},{1,9},{2,10},{3,11},{4,12},{5,13},{6,14},{7,15},{8,0},{9,1},... | collective-permute-start | bytes 688136 | tf_op jit(solution)/shard_map/ppermute | solution.py:283
  67.5 20.1 %collective-permute-start.14 = (bf16[128,640]{1,0:T(8,128)(2,1)S(1)}, bf16[128,640]{1,0:T(8,128)(2,1)S(1)}, u32[]{:S(2)}, u32[]{:S(2)}) collective-permute-start(bf16[128,640]{1,0:T(8,128)(2,1)S(1)} %shard_map.34.sent), channel_id=1, source_target_pairs={{0,8},{1,9},{2,10},{3,11},{4,12},{5,13},{6,14},{7,15},{8,0},{9,1},... | collective-permute-start | bytes 491528 | tf_op jit(solution)/shard_map/ppermute | solution.py:283
  68.0 21.3 %collective-permute-start.13 = (bf16[128,384]{1,0:T(8,128)(2,1)S(1)}, bf16[128,384]{1,0:T(8,128)(2,1)S(1)}, u32[]{:S(2)}, u32[]{:S(2)}) collective-permute-start(bf16[128,384]{1,0:T(8,128)(2,1)S(1)} %shard_map.33.sent), channel_id=1, source_target_pairs={{0,8},{1,9},{2,10},{3,11},{4,12},{5,13},{6,14},{7,15},{8,0},{9,1},... | collective-permute-start | bytes 294920 | tf_op jit(solution)/shard_map/ppermute | solution.py:283
  90.1 1.3 %collective-permute-start.16 = (f32[80,256]{1,0:T(8,128)S(1)}, f32[80,256]{1,0:T(8,128)S(1)}, u32[]{:S(2)}, u32[]{:S(2)}) collective-permute-start(f32[80,256]{1,0:T(8,128)S(1)} %shard_map.42), channel_id=1, source_target_pairs={{0,1},{1,0},{2,3},{3,2},{4,5},{5,4},{6,7},{7,6},{8,9},{9,8},{10,11... | collective-permute-start | bytes 245768 | tf_op jit(solution)/shard_map/ppermute | solution.py:283
  91.4 4.6 %collective-permute-start.17 = (f32[80,256]{1,0:T(8,128)S(1)}, f32[80,256]{1,0:T(8,128)S(1)}, u32[]{:S(2)}, u32[]{:S(2)}) collective-permute-start(f32[80,256]{1,0:T(8,128)S(1)} %add.25.refs_0_), channel_id=1, source_target_pairs={{0,2},{1,5},{2,0},{3,7},{4,6},{5,1},{6,4},{7,3},{8,10},{9,13},{10,... | collective-permute-start | bytes 245768 | tf_op jit(solution)/shard_map/ppermute | solution.py:283
  92.6 4.6 %collective-permute-start.18 = (f32[80,256]{1,0:T(8,128)S(1)}, f32[80,256]{1,0:T(8,128)S(1)}, u32[]{:S(2)}, u32[]{:S(2)}) collective-permute-start(f32[80,256]{1,0:T(8,128)S(1)} %add.25.refs_0_), channel_id=1, source_target_pairs={{0,4},{1,3},{2,6},{3,1},{4,0},{5,7},{6,2},{7,5},{8,12},{9,11},{10,... | collective-permute-start | bytes 245768 | tf_op jit(solution)/shard_map/ppermute | solution.py:283
  93.1 5.7 %collective-permute-start.19 = (f32[80,256]{1,0:T(8,128)S(1)}, f32[80,256]{1,0:T(8,128)S(1)}, u32[]{:S(2)}, u32[]{:S(2)}) collective-permute-start(f32[80,256]{1,0:T(8,128)S(1)} %add.25.refs_0_), channel_id=1, source_target_pairs={{0,6},{1,7},{2,4},{3,5},{4,2},{5,3},{6,0},{7,1},{8,14},{9,15},{10,... | collective-permute-start | bytes 245768 | tf_op jit(solution)/shard_map/ppermute | solution.py:283
  100.9 1.3 collective-permute-start.20
  102.5 12.8 %collective-permute-start.22 = (bf16[64,1152]{1,0:T(8,128)(2,1)S(1)}, bf16[64,1152]{1,0:T(8,128)(2,1)S(1)}, u32[]{:S(2)}, u32[]{:S(2)}) collective-permute-start(bf16[64,1152]{1,0:T(8,128)(2,1)S(1)} %shard_map.46), channel_id=1, source_target_pairs={{0,8},{1,9},{2,10},{3,11},{4,12},{5,13},{6,14},{7,15},{8,0},{9,1},... | collective-permute-start | bytes 442376 | tf_op jit(solution)/shard_map/ppermute | solution.py:283
  105.8 11.3 %collective-permute-start.21 = (bf16[64,768]{1,0:T(8,128)(2,1)S(1)}, bf16[64,768]{1,0:T(8,128)(2,1)S(1)}, u32[]{:S(2)}, u32[]{:S(2)}) collective-permute-start(bf16[64,768]{1,0:T(8,128)(2,1)S(1)} %shard_map.44), channel_id=1, source_target_pairs={{0,8},{1,9},{2,10},{3,11},{4,12},{5,13},{6,14},{7,15},{8,0},{9,1},... | collective-permute-start | bytes 294920 | tf_op jit(solution)/shard_map/ppermute | solution.py:283
  117.5 5.0 %collective-permute-start.23 = (f32[64,64]{1,0:T(8,128)S(1)}, f32[64,64]{1,0:T(8,128)S(1)}, u32[]{:S(2)}, u32[]{:S(2)}) collective-permute-start(f32[64,64]{1,0:T(8,128)S(1)} %get-tuple-element.68), channel_id=1, source_target_pairs={{0,9},{1,8},{2,11},{3,10},{4,13},{5,12},{6,15},{7,14},{8,1},{9,0},... | collective-permute-start | bytes 49160 | tf_op jit(solution)/shard_map/ppermute | solution.py:283
  117.6 5.5 %collective-permute-start.24 = (f32[64,64]{1,0:T(8,128)S(1)}, f32[64,64]{1,0:T(8,128)S(1)}, u32[]{:S(2)}, u32[]{:S(2)}) collective-permute-start(f32[64,64]{1,0:T(8,128)S(1)} %get-tuple-element.68), channel_id=1, source_target_pairs={{0,8},{1,9},{2,10},{3,11},{4,12},{5,13},{6,14},{7,15},{8,0},{9,1},... | collective-permute-start | bytes 49160 | tf_op jit(solution)/shard_map/ppermute | solution.py:283
  119.9 3.3 %collective-permute-start.25 = (f32[64,64]{1,0:T(8,128)S(1)}, f32[64,64]{1,0:T(8,128)S(1)}, u32[]{:S(2)}, u32[]{:S(2)}) collective-permute-start(f32[64,64]{1,0:T(8,128)S(1)} %get-tuple-element.68), channel_id=1, source_target_pairs={{0,1},{1,0},{2,3},{3,2},{4,5},{5,4},{6,7},{7,6},{8,9},{9,8},{10,11... | collective-permute-start | bytes 49160 | tf_op jit(solution)/shard_map/ppermute | solution.py:283
  123.2 4.9 %collective-permute-start.26 = (f32[64,64]{1,0:T(8,128)S(1)}, f32[64,64]{1,0:T(8,128)S(1)}, u32[]{:S(2)}, u32[]{:S(2)}) collective-permute-start(f32[64,64]{1,0:T(8,128)S(1)} %add_add_fusion.1), channel_id=1, source_target_pairs={{0,6},{1,7},{2,4},{3,5},{4,2},{5,3},{6,0},{7,1},{8,14},{9,15},{10,... | collective-permute-start | bytes 49160 | tf_op jit(solution)/shard_map/ppermute | solution.py:283
  125.3 3.9 %collective-permute-start.27 = (f32[64,64]{1,0:T(8,128)S(1)}, f32[64,64]{1,0:T(8,128)S(1)}, u32[]{:S(2)}, u32[]{:S(2)}) collective-permute-start(f32[64,64]{1,0:T(8,128)S(1)} %add_add_fusion.1), channel_id=1, source_target_pairs={{0,2},{1,5},{2,0},{3,7},{4,6},{5,1},{6,4},{7,3},{8,10},{9,13},{10,... | collective-permute-start | bytes 49160 | tf_op jit(solution)/shard_map/ppermute | solution.py:283
  126.4 3.9 %collective-permute-start.28 = (f32[64,64]{1,0:T(8,128)S(1)}, f32[64,64]{1,0:T(8,128)S(1)}, u32[]{:S(2)}, u32[]{:S(2)}) collective-permute-start(f32[64,64]{1,0:T(8,128)S(1)} %add_add_fusion.1), channel_id=1, source_target_pairs={{0,4},{1,3},{2,6},{3,1},{4,0},{5,7},{6,2},{7,5},{8,12},{9,11},{10,... | collective-permute-start | bytes 49160 | tf_op jit(solution)/shard_map/ppermute | solution.py:283

commit v13 on v12

--- a/solution.py
+++ b/solution.py
@@ -33,14 +33,9 @@
 
 
 def exact_nn(a, b):
-    size = a.shape[0]
-    parts = three(a)
-    total = 0.0
-    for count, part in zip((1, 2, 3), reversed(three(b))):
-        product = nn(jnp.concatenate(parts[:count], axis=0), part)
-        for i in reversed(range(count)):
-            total = total + product[i * size:(i + 1) * size]
-    return total
+    a1, a2, a3 = three(a)
+    b1, b2, b3 = three(b)
+    return nn(jnp.concatenate([a3, a2, a1, a2, a1, a1], axis=1), jnp.concatenate([b1, b2, b3, b1, b2, b1], axis=0))
 
 
 def exact_gram(a):
@@ -160,10 +155,10 @@
 
     rank = out.shape[0]
     top = [x[:rank] for x in values]
-    value = (top[0] + turned(top[3], 3)) + (turned(top[1], 1) + turned(top[2], 2))
+    value = (top[0] + turned(top[1], 1)) + (turned(top[2], 2) + turned(top[3], 3))
     if normalised:
         below = [x[rank:] for x in values]
-        below = (below[0] + below[3]) + (below[1] + below[2])
+        below = (below[0] + below[1]) + (below[2] + below[3])
         gram = jnp.concatenate([below[:, j * rank:(j + 1) * rank] for j in range(cells // rank)], axis=0)
         value = exact_nn(inverse_factor(gram), value)
     out[...] = value.astype(bf16)
@@ -284,13 +279,13 @@
 
 
 def legs(value, cells):
-    return [mate(value, cells, 2, 4), mate(value, cells, 4, 2), mate(value, cells, 6)]
+    return [mate(value, cells, 6), mate(value, cells, 2, 4), mate(value, cells, 4, 2)]
 
 
 def total_over_cells(value, cells):
     value = (value + mate(value, cells, GROUP | 1)) + (mate(value, cells, GROUP) + mate(value, cells, 1))
-    one, two, both_ways = legs(value, cells)
-    return (value + both_ways) + (one + two)
+    across, one, two = legs(value, cells)
+    return (value + across) + (one + two)
 
 
 def cuts(width, *percents):
@@ -303,7 +298,7 @@
 
 def square_program(cells, expression, start_basis):
     width, rank = start_basis.shape
-    masks = ((0, 0), (1, 1), (2, 4), (3, 5), (4, 2), (5, 3), (6, 6), (7, 7))
+    masks = ((0, 0), (1, 1), (6, 6), (7, 7), (2, 4), (3, 5), (4, 2), (5, 3))
     packs = pack(expression, masks, width)
     slots = [mate(x, cells, *pair) if k else x for k, (x, pair) in enumerate(zip(packs, masks))]
 

time: 134 us -> 133 us (level)
  starting transfers between devices: 38.7 us -> 35.5 us
  waiting for transfers between devices: 78.9 us -> 82.1 us
    ppermute x29, waiting for transfers between devices: 78.9 us -> 82.1 us  [mate(): lax.ppermute(value, 'cell', [(i, i ^ masks[i % 2]) for i in range(cells)])]
    ppermute x29, starting transfers between devices: 38.7 us -> 35.5 us  [mate(): lax.ppermute(value, 'cell', [(i, i ^ masks[i % 2]) for i in range(cells)])]
  transfers between devices with their start and end apart: 29 -> 29, of which waited for: 23 -> 24; matrix products, arithmetic and copies ran while one was open for 0% -> 0% of each run, Pallas kernels for 5% -> 5%
where the time goes in v13:
time: 133 us
  waiting for transfers between devices  82.1 us (62%)
  starting transfers between devices  35.5 us (27%)
  Pallas kernels  15.4 us (12%)
    ppermute x29, waiting for transfers between devices, mate(): lax.ppermute(value, 'cell', [(i, i ^ masks[i % 2]) for i in range(cells)])  82.1 us
    ppermute x29, starting transfers between devices, mate(): lax.ppermute(value, 'cell', [(i, i ^ masks[i % 2]) for i in range(cells)])  35.5 us
    pallas_call x22, Pallas kernels, call(): pl.pallas_call(kernel, in_specs=[VMEM] * len(args), out_specs=[VMEM] * le...  13.2 us
  transfers between devices with their start and end apart: 29, of which 24 were waited for; matrix products, arithmetic and copies ran while one was open for 0% of the time, Pallas kernels for 5%

profile of v13, /device:TPU:0, one launch (start us, length us, event | category | flops | bytes accessed | tf_op | source)
XLA Modules:
  0.0 133.3 jit_solution(15776314810135407056)
XLA Ops:
  0.0 2.2 %shard_map.28 = (bf16[64,3840]{1,0:T(8,128)(2,1)S(1)}, bf16[64,3840]{1,0:T(8,128)(2,1)S(1)}, bf16[64,3840]{1,0:T(8,128)(2,1)S(1)}, bf16[64,3840]{1,0:T(8,128)(2,...) custom-call(bf16[64,30720]{1,0:T(8,128)(2,1)} %matrix.1), custom_call_target="tpu_custom_call" | custom-call | bytes 7864320 | tf_op jit(solution)/shard_map/pallas_call | solution.py:82
  2.8 3.6 %collective-permute-start.1 = (bf16[64,3840]{1,0:T(8,128)(2,1)S(1)}, bf16[64,3840]{1,0:T(8,128)(2,1)S(1)}, u32[]{:S(2)}, u32[]{:S(2)}) collective-permute-start(bf16[64,3840]{1,0:T(8,128)(2,1)S(1)} %get-tuple-element.40), channel_id=1, source_target_pairs={{0,6},{1,7},{2,4},{3,5},{4,2},{5,3},{6,0},{7,1},{8,14},{9,15},{10,... | collective-permute-start | bytes 1474568 | tf_op jit(solution)/shard_map/ppermute | solution.py:278
  6.4 2.6 %collective-permute-start.7 = (bf16[64,1920]{1,0:T(8,128)(2,1)S(1)}, bf16[64,1920]{1,0:T(8,128)(2,1)S(1)}, u32[]{:S(2)}, u32[]{:S(2)}) collective-permute-start(bf16[64,1920]{1,0:T(8,128)(2,1)S(1)} %bitcast.2), channel_id=1, source_target_pairs={{0,8},{1,9},{2,10},{3,11},{4,12},{5,13},{6,14},{7,15},{8,0},{9,1},... | collective-permute-start | bytes 737288 | tf_op jit(solution)/shard_map/ppermute | solution.py:278
  9.0 1.6 %collective-permute-start.4 = (bf16[64,3840]{1,0:T(8,128)(2,1)S(1)}, bf16[64,3840]{1,0:T(8,128)(2,1)S(1)}, u32[]{:S(2)}, u32[]{:S(2)}) collective-permute-start(bf16[64,3840]{1,0:T(8,128)(2,1)S(1)} %get-tuple-element.43), channel_id=1, source_target_pairs={{0,3},{1,4},{2,1},{3,6},{4,7},{5,0},{6,5},{7,2},{8,11},{9,12},{10,... | collective-permute-start | bytes 1474568 | tf_op jit(solution)/shard_map/ppermute | solution.py:278
  10.6 12.6 %collective-permute-done.7.refs_1_ = bf16[64,1920]{1,0:T(8,128)(2,1)S(1)} collective-permute-done((bf16[64,1920]{1,0:T(8,128)(2,1)S(1)}, bf16[64,1920]{1,0:T(8,128)(2,1)S(1)}, u32[]{:S(2)}, u32[]{:S(2)}) %collective-permute-start.7) | collective-permute-done | bytes 245792 | tf_op jit(solution)/shard_map/ppermute | solution.py:278
  23.2 2.3 %collective-permute-start.6 = (bf16[64,3840]{1,0:T(8,128)(2,1)S(1)}, bf16[64,3840]{1,0:T(8,128)(2,1)S(1)}, u32[]{:S(2)}, u32[]{:S(2)}) collective-permute-start(bf16[64,3840]{1,0:T(8,128)(2,1)S(1)} %get-tuple-element.45), channel_id=1, source_target_pairs={{0,5},{1,2},{2,7},{3,0},{4,1},{5,6},{6,3},{7,4},{8,13},{9,10},{10,... | collective-permute-start | bytes 1474568 | tf_op jit(solution)/shard_map/ppermute | solution.py:278
  26.0 1.2 collective-permute-start.5
  27.3 6.6 %collective-permute-done.2.refs_5_.refs_3_ = bf16[64,3840]{1,0:T(8,128)(2,1)S(1)} collective-permute-done((bf16[64,3840]{1,0:T(8,128)(2,1)S(1)}, bf16[64,3840]{1,0:T(8,128)(2,1)S(1)}, u32[]{:S(2)}, u32[]{:S(2)}) %collective-permute-start.2) | collective-permute-done | bytes 491552 | tf_op jit(solution)/shard_map/ppermute | solution.py:278
  34.5 9.8 %collective-permute-done.4.refs_2_.refs_5_.refs_7_.refs_4_ = bf16[64,3840]{1,0:T(8,128)(2,1)S(1)} collective-permute-done((bf16[64,3840]{1,0:T(8,128)(2,1)S(1)}, bf16[64,3840]{1,0:T(8,128)(2,1)S(1)}, u32[]{:S(2)}, u32[]{:S(2)}) %collective-permute-start.4) | collective-permute-done | bytes 491552 | tf_op jit(solution)/shard_map/ppermute | solution.py:278
  45.8 3.7 %collective-permute-done.3.refs_2_.refs_4_.refs_6_ = bf16[64,3840]{1,0:T(8,128)(2,1)S(1)} collective-permute-done((bf16[64,3840]{1,0:T(8,128)(2,1)S(1)}, bf16[64,3840]{1,0:T(8,128)(2,1)S(1)}, u32[]{:S(2)}, u32[]{:S(2)}) %collective-permute-start.3) | collective-permute-done | bytes 491552 | tf_op jit(solution)/shard_map/ppermute | solution.py:278
  49.5 5.8 %collective-permute-done.5.refs_3_.refs_6_.refs_8_.refs_5_ = bf16[64,3840]{1,0:T(8,128)(2,1)S(1)} collective-permute-done((bf16[64,3840]{1,0:T(8,128)(2,1)S(1)}, bf16[64,3840]{1,0:T(8,128)(2,1)S(1)}, u32[]{:S(2)}, u32[]{:S(2)}) %collective-permute-start.5) | collective-permute-done | bytes 491552 | tf_op jit(solution)/shard_map/ppermute | solution.py:278
  56.2 1.7 %collective-permute-start.11 = (f32[64,256]{1,0:T(8,128)S(1)}, f32[64,256]{1,0:T(8,128)S(1)}, u32[]{:S(2)}, u32[]{:S(2)}) collective-permute-start(f32[64,256]{1,0:T(8,128)S(1)} %add.24.refs_0_), channel_id=1, source_target_pairs={{0,4},{1,3},{2,6},{3,1},{4,0},{5,7},{6,2},{7,5},{8,12},{9,11},{10,... | collective-permute-start | bytes 196616 | tf_op jit(solution)/shard_map/ppermute | solution.py:278
  58.0 1.4 %collective-permute-start.9 = (f32[64,256]{1,0:T(8,128)S(1)}, f32[64,256]{1,0:T(8,128)S(1)}, u32[]{:S(2)}, u32[]{:S(2)}) collective-permute-start(f32[64,256]{1,0:T(8,128)S(1)} %add.24.refs_0_), channel_id=1, source_target_pairs={{0,6},{1,7},{2,4},{3,5},{4,2},{5,3},{6,0},{7,1},{8,14},{9,15},{10,... | collective-permute-start | bytes 196616 | tf_op jit(solution)/shard_map/ppermute | solution.py:278
  59.3 1.9 %collective-permute-done.10.refs_2_ = f32[64,256]{1,0:T(8,128)S(1)} collective-permute-done((f32[64,256]{1,0:T(8,128)S(1)}, f32[64,256]{1,0:T(8,128)S(1)}, u32[]{:S(2)}, u32[]{:S(2)}) %collective-permute-start.10) | collective-permute-done | bytes 65568 | tf_op jit(solution)/shard_map/ppermute | solution.py:278
  61.3 1.9 %collective-permute-done.9.refs_1_ = f32[64,256]{1,0:T(8,128)S(1)} collective-permute-done((f32[64,256]{1,0:T(8,128)S(1)}, f32[64,256]{1,0:T(8,128)S(1)}, u32[]{:S(2)}, u32[]{:S(2)}) %collective-permute-start.9) | collective-permute-done | bytes 65568 | tf_op jit(solution)/shard_map/ppermute | solution.py:278
  63.3 1.2 collective-permute-done.12.refs_9_
  64.9 2.6 %collective-permute-start.15 = (bf16[128,896]{1,0:T(8,128)(2,1)S(1)}, bf16[128,896]{1,0:T(8,128)(2,1)S(1)}, u32[]{:S(2)}, u32[]{:S(2)}) collective-permute-start(bf16[128,896]{1,0:T(8,128)(2,1)S(1)} %shard_map.35.sent), channel_id=1, source_target_pairs={{0,8},{1,9},{2,10},{3,11},{4,12},{5,13},{6,14},{7,15},{8,0},{9,1},... | collective-permute-start | bytes 688136 | tf_op jit(solution)/shard_map/ppermute | solution.py:278
  68.6 2.6 %collective-permute-start.13 = (bf16[128,384]{1,0:T(8,128)(2,1)S(1)}, bf16[128,384]{1,0:T(8,128)(2,1)S(1)}, u32[]{:S(2)}, u32[]{:S(2)}) collective-permute-start(bf16[128,384]{1,0:T(8,128)(2,1)S(1)} %shard_map.33.sent), channel_id=1, source_target_pairs={{0,8},{1,9},{2,10},{3,11},{4,12},{5,13},{6,14},{7,15},{8,0},{9,1},... | collective-permute-start | bytes 294920 | tf_op jit(solution)/shard_map/ppermute | solution.py:278
  71.2 13.2 %collective-permute-done.15.received = bf16[128,896]{1,0:T(8,128)(2,1)S(1)} collective-permute-done((bf16[128,896]{1,0:T(8,128)(2,1)S(1)}, bf16[128,896]{1,0:T(8,128)(2,1)S(1)}, u32[]{:S(2)}, u32[]{:S(2)}) %collective-permute-start.15) | collective-permute-done | bytes 229408 | tf_op jit(solution)/shard_map/ppermute | solution.py:278
  85.6 2.2 %collective-permute-done.14.received = bf16[128,640]{1,0:T(8,128)(2,1)S(1)} collective-permute-done((bf16[128,640]{1,0:T(8,128)(2,1)S(1)}, bf16[128,640]{1,0:T(8,128)(2,1)S(1)}, u32[]{:S(2)}, u32[]{:S(2)}) %collective-permute-start.14) | collective-permute-done | bytes 163872 | tf_op jit(solution)/shard_map/ppermute | solution.py:278
  93.4 2.0 %collective-permute-start.19 = (f32[80,256]{1,0:T(8,128)S(1)}, f32[80,256]{1,0:T(8,128)S(1)}, u32[]{:S(2)}, u32[]{:S(2)}) collective-permute-start(f32[80,256]{1,0:T(8,128)S(1)} %add.25.refs_0_), channel_id=1, source_target_pairs={{0,4},{1,3},{2,6},{3,1},{4,0},{5,7},{6,2},{7,5},{8,12},{9,11},{10,... | collective-permute-start | bytes 245768 | tf_op jit(solution)/shard_map/ppermute | solution.py:278
  95.4 2.7 %collective-permute-done.17.refs_1_ = f32[80,256]{1,0:T(8,128)S(1)} collective-permute-done((f32[80,256]{1,0:T(8,128)S(1)}, f32[80,256]{1,0:T(8,128)S(1)}, u32[]{:S(2)}, u32[]{:S(2)}) %collective-permute-start.17) | collective-permute-done | bytes 81952 | tf_op jit(solution)/shard_map/ppermute | solution.py:278
  99.0 2.0 %shard_map.43.refs_8_ = bf16[64,256]{1,0:T(8,128)(2,1)S(1)} custom-call(f32[80,256]{1,0:T(8,128)S(1)} %add.25.refs_0_, f32[80,256]{1,0:T(8,128)S(1)} %collective-permute-done.17.refs_1_, f32[80,256]{1,0:T(8,128)S(1)} %collective-permute-done.18.refs_2_, f32[80,256]{1,0:T(8,128)S(1)} %collective-permute-done.19.refs_3_), custom_call_target="tpu_custom_call" | custom-call | flops 15728640 | bytes 327680 | tf_op jit(solution)/shard_map/pallas_call | solution.py:94
  102.5 2.2 %collective-permute-start.22 = (bf16[64,1152]{1,0:T(8,128)(2,1)S(1)}, bf16[64,1152]{1,0:T(8,128)(2,1)S(1)}, u32[]{:S(2)}, u32[]{:S(2)}) collective-permute-start(bf16[64,1152]{1,0:T(8,128)(2,1)S(1)} %shard_map.46), channel_id=1, source_target_pairs={{0,8},{1,9},{2,10},{3,11},{4,12},{5,13},{6,14},{7,15},{8,0},{9,1},... | collective-permute-start | bytes 442376 | tf_op jit(solution)/shard_map/ppermute | solution.py:278
  106.4 8.6 %collective-permute-done.22.received = bf16[64,1152]{1,0:T(8,128)(2,1)S(1)} collective-permute-done((bf16[64,1152]{1,0:T(8,128)(2,1)S(1)}, bf16[64,1152]{1,0:T(8,128)(2,1)S(1)}, u32[]{:S(2)}, u32[]{:S(2)}) %collective-permute-start.22) | collective-permute-done | bytes 147488 | tf_op jit(solution)/shard_map/ppermute | solution.py:278
  115.5 1.3 collective-permute-done.21.received
  117.3 2.3 %collective-permute-start.24 = (f32[64,64]{1,0:T(8,128)S(1)}, f32[64,64]{1,0:T(8,128)S(1)}, u32[]{:S(2)}, u32[]{:S(2)}) collective-permute-start(f32[64,64]{1,0:T(8,128)S(1)} %get-tuple-element.68), channel_id=1, source_target_pairs={{0,8},{1,9},{2,10},{3,11},{4,12},{5,13},{6,14},{7,15},{8,0},{9,1},... | collective-permute-start | bytes 49160 | tf_op jit(solution)/shard_map/ppermute | solution.py:278
  120.1 2.2 %collective-permute-done.23 = f32[64,64]{1,0:T(8,128)S(1)} collective-permute-done((f32[64,64]{1,0:T(8,128)S(1)}, f32[64,64]{1,0:T(8,128)S(1)}, u32[]{:S(2)}, u32[]{:S(2)}) %collective-permute-start.23) | collective-permute-done | bytes 16416 | tf_op jit(solution)/shard_map/ppermute | solution.py:278
  122.9 2.8 %collective-permute-start.26 = (f32[64,64]{1,0:T(8,128)S(1)}, f32[64,64]{1,0:T(8,128)S(1)}, u32[]{:S(2)}, u32[]{:S(2)}) collective-permute-start(f32[64,64]{1,0:T(8,128)S(1)} %add_add_fusion.1), channel_id=1, source_target_pairs={{0,6},{1,7},{2,4},{3,5},{4,2},{5,3},{6,0},{7,1},{8,14},{9,15},{10,... | collective-permute-start | bytes 49160 | tf_op jit(solution)/shard_map/ppermute | solution.py:278
  126.4 1.3 collective-permute-done.26
  127.8 1.8 %collective-permute-done.27 = f32[64,64]{1,0:T(8,128)S(1)} collective-permute-done((f32[64,64]{1,0:T(8,128)S(1)}, f32[64,64]{1,0:T(8,128)S(1)}, u32[]{:S(2)}, u32[]{:S(2)}) %collective-permute-start.27) | collective-permute-done | bytes 16416 | tf_op jit(solution)/shard_map/ppermute | solution.py:278
  130.3 3.0 %shard_map.50 = f32[64,1920]{1,0:T(8,128)} custom-call(f32[64,64]{1,0:T(8,128)S(1)} %add_add_fusion.gram, f32[64,1152]{1,0:T(8,128)S(1)} %get-tuple-element.69.refs_0_, f32[64,768]{1,0:T(8,128)S(1)} %get-tuple-element.70.refs_1_), custom_call_target="tpu_custom_call" | custom-call | flops 94371840 | bytes 983040 | tf_op jit(solution)/shard_map/pallas_call | solution.py:94
  (55 shorter events, 20.2 us)
Async XLA Ops:
  0.0 6.4 %copy-start = (bf16[1920,64]{0,1:T(8,128)(2,1)S(1)}, bf16[1920,64]{0,1:T(8,128)(2,1)}, u32[]{:S(2)}) copy-start(bf16[1920,64]{0,1:T(8,128)(2,1)} %param.3) | copy-start | bytes 737284
  2.2 23.3 %collective-permute-start = (bf16[64,3840]{1,0:T(8,128)(2,1)S(1)}, bf16[64,3840]{1,0:T(8,128)(2,1)S(1)}, u32[]{:S(2)}, u32[]{:S(2)}) collective-permute-start(bf16[64,3840]{1,0:T(8,128)(2,1)S(1)} %get-tuple-element.39), channel_id=1, source_target_pairs={{0,1},{1,0},{2,3},{3,2},{4,5},{5,4},{6,7},{7,6},{8,9},{9,8},{10,11... | collective-permute-start | bytes 1474568 | tf_op jit(solution)/shard_map/ppermute | solution.py:278
  2.8 23.3 %collective-permute-start.1 = (bf16[64,3840]{1,0:T(8,128)(2,1)S(1)}, bf16[64,3840]{1,0:T(8,128)(2,1)S(1)}, u32[]{:S(2)}, u32[]{:S(2)}) collective-permute-start(bf16[64,3840]{1,0:T(8,128)(2,1)S(1)} %get-tuple-element.40), channel_id=1, source_target_pairs={{0,6},{1,7},{2,4},{3,5},{4,2},{5,3},{6,0},{7,1},{8,14},{9,15},{10,... | collective-permute-start | bytes 1474568 | tf_op jit(solution)/shard_map/ppermute | solution.py:278
  6.4 16.8 %collective-permute-start.7 = (bf16[64,1920]{1,0:T(8,128)(2,1)S(1)}, bf16[64,1920]{1,0:T(8,128)(2,1)S(1)}, u32[]{:S(2)}, u32[]{:S(2)}) collective-permute-start(bf16[64,1920]{1,0:T(8,128)(2,1)S(1)} %bitcast.2), channel_id=1, source_target_pairs={{0,8},{1,9},{2,10},{3,11},{4,12},{5,13},{6,14},{7,15},{8,0},{9,1},... | collective-permute-start | bytes 737288 | tf_op jit(solution)/shard_map/ppermute | solution.py:278
  9.0 24.9 %collective-permute-start.2 = (bf16[64,3840]{1,0:T(8,128)(2,1)S(1)}, bf16[64,3840]{1,0:T(8,128)(2,1)S(1)}, u32[]{:S(2)}, u32[]{:S(2)}) collective-permute-start(bf16[64,3840]{1,0:T(8,128)(2,1)S(1)} %get-tuple-element.41), channel_id=1, source_target_pairs={{0,7},{1,6},{2,5},{3,4},{4,3},{5,2},{6,1},{7,0},{8,15},{9,14},{10,... | collective-permute-start | bytes 1474568 | tf_op jit(solution)/shard_map/ppermute | solution.py:278
  9.0 35.3 %collective-permute-start.4 = (bf16[64,3840]{1,0:T(8,128)(2,1)S(1)}, bf16[64,3840]{1,0:T(8,128)(2,1)S(1)}, u32[]{:S(2)}, u32[]{:S(2)}) collective-permute-start(bf16[64,3840]{1,0:T(8,128)(2,1)S(1)} %get-tuple-element.43), channel_id=1, source_target_pairs={{0,3},{1,4},{2,1},{3,6},{4,7},{5,0},{6,5},{7,2},{8,11},{9,12},{10,... | collective-permute-start | bytes 1474568 | tf_op jit(solution)/shard_map/ppermute | solution.py:278
  23.2 21.5 %collective-permute-start.6 = (bf16[64,3840]{1,0:T(8,128)(2,1)S(1)}, bf16[64,3840]{1,0:T(8,128)(2,1)S(1)}, u32[]{:S(2)}, u32[]{:S(2)}) collective-permute-start(bf16[64,3840]{1,0:T(8,128)(2,1)S(1)} %get-tuple-element.45), channel_id=1, source_target_pairs={{0,5},{1,2},{2,7},{3,0},{4,1},{5,6},{6,3},{7,4},{8,13},{9,10},{10,... | collective-permute-start | bytes 1474568 | tf_op jit(solution)/shard_map/ppermute | solution.py:278
  25.5 23.9 %collective-permute-start.3 = (bf16[64,3840]{1,0:T(8,128)(2,1)S(1)}, bf16[64,3840]{1,0:T(8,128)(2,1)S(1)}, u32[]{:S(2)}, u32[]{:S(2)}) collective-permute-start(bf16[64,3840]{1,0:T(8,128)(2,1)S(1)} %get-tuple-element.42), channel_id=1, source_target_pairs={{0,2},{1,5},{2,0},{3,7},{4,6},{5,1},{6,4},{7,3},{8,10},{9,13},{10,... | collective-permute-start | bytes 1474568 | tf_op jit(solution)/shard_map/ppermute | solution.py:278
  26.0 29.2 %collective-permute-start.5 = (bf16[64,3840]{1,0:T(8,128)(2,1)S(1)}, bf16[64,3840]{1,0:T(8,128)(2,1)S(1)}, u32[]{:S(2)}, u32[]{:S(2)}) collective-permute-start(bf16[64,3840]{1,0:T(8,128)(2,1)S(1)} %get-tuple-element.44), channel_id=1, source_target_pairs={{0,4},{1,3},{2,6},{3,1},{4,0},{5,7},{6,2},{7,5},{8,12},{9,11},{10,... | collective-permute-start | bytes 1474568 | tf_op jit(solution)/shard_map/ppermute | solution.py:278
  45.1 10.6 %collective-permute-start.8 = (f32[64,256]{1,0:T(8,128)S(1)}, f32[64,256]{1,0:T(8,128)S(1)}, u32[]{:S(2)}, u32[]{:S(2)}) collective-permute-start(f32[64,256]{1,0:T(8,128)S(1)} %shard_map.31), channel_id=1, source_target_pairs={{0,1},{1,0},{2,3},{3,2},{4,5},{5,4},{6,7},{7,6},{8,9},{9,8},{10,11... | collective-permute-start | bytes 196616 | tf_op jit(solution)/shard_map/ppermute | solution.py:278
  55.8 5.5 %collective-permute-start.10 = (f32[64,256]{1,0:T(8,128)S(1)}, f32[64,256]{1,0:T(8,128)S(1)}, u32[]{:S(2)}, u32[]{:S(2)}) collective-permute-start(f32[64,256]{1,0:T(8,128)S(1)} %add.24.refs_0_), channel_id=1, source_target_pairs={{0,2},{1,5},{2,0},{3,7},{4,6},{5,1},{6,4},{7,3},{8,10},{9,13},{10,... | collective-permute-start | bytes 196616 | tf_op jit(solution)/shard_map/ppermute | solution.py:278
  56.2 5.0 %collective-permute-start.11 = (f32[64,256]{1,0:T(8,128)S(1)}, f32[64,256]{1,0:T(8,128)S(1)}, u32[]{:S(2)}, u32[]{:S(2)}) collective-permute-start(f32[64,256]{1,0:T(8,128)S(1)} %add.24.refs_0_), channel_id=1, source_target_pairs={{0,4},{1,3},{2,6},{3,1},{4,0},{5,7},{6,2},{7,5},{8,12},{9,11},{10,... | collective-permute-start | bytes 196616 | tf_op jit(solution)/shard_map/ppermute | solution.py:278
  58.0 5.2 %collective-permute-start.9 = (f32[64,256]{1,0:T(8,128)S(1)}, f32[64,256]{1,0:T(8,128)S(1)}, u32[]{:S(2)}, u32[]{:S(2)}) collective-permute-start(f32[64,256]{1,0:T(8,128)S(1)} %add.24.refs_0_), channel_id=1, source_target_pairs={{0,6},{1,7},{2,4},{3,5},{4,2},{5,3},{6,0},{7,1},{8,14},{9,15},{10,... | collective-permute-start | bytes 196616 | tf_op jit(solution)/shard_map/ppermute | solution.py:278
  63.2 1.3 collective-permute-start.12
  64.9 19.5 %collective-permute-start.15 = (bf16[128,896]{1,0:T(8,128)(2,1)S(1)}, bf16[128,896]{1,0:T(8,128)(2,1)S(1)}, u32[]{:S(2)}, u32[]{:S(2)}) collective-permute-start(bf16[128,896]{1,0:T(8,128)(2,1)S(1)} %shard_map.35.sent), channel_id=1, source_target_pairs={{0,8},{1,9},{2,10},{3,11},{4,12},{5,13},{6,14},{7,15},{8,0},{9,1},... | collective-permute-start | bytes 688136 | tf_op jit(solution)/shard_map/ppermute | solution.py:278
  67.9 20.0 %collective-permute-start.14 = (bf16[128,640]{1,0:T(8,128)(2,1)S(1)}, bf16[128,640]{1,0:T(8,128)(2,1)S(1)}, u32[]{:S(2)}, u32[]{:S(2)}) collective-permute-start(bf16[128,640]{1,0:T(8,128)(2,1)S(1)} %shard_map.34.sent), channel_id=1, source_target_pairs={{0,8},{1,9},{2,10},{3,11},{4,12},{5,13},{6,14},{7,15},{8,0},{9,1},... | collective-permute-start | bytes 491528 | tf_op jit(solution)/shard_map/ppermute | solution.py:278
  68.6 21.1 %collective-permute-start.13 = (bf16[128,384]{1,0:T(8,128)(2,1)S(1)}, bf16[128,384]{1,0:T(8,128)(2,1)S(1)}, u32[]{:S(2)}, u32[]{:S(2)}) collective-permute-start(bf16[128,384]{1,0:T(8,128)(2,1)S(1)} %shard_map.33.sent), channel_id=1, source_target_pairs={{0,8},{1,9},{2,10},{3,11},{4,12},{5,13},{6,14},{7,15},{8,0},{9,1},... | collective-permute-start | bytes 294920 | tf_op jit(solution)/shard_map/ppermute | solution.py:278
  90.5 1.3 %collective-permute-start.16 = (f32[80,256]{1,0:T(8,128)S(1)}, f32[80,256]{1,0:T(8,128)S(1)}, u32[]{:S(2)}, u32[]{:S(2)}) collective-permute-start(f32[80,256]{1,0:T(8,128)S(1)} %shard_map.42), channel_id=1, source_target_pairs={{0,1},{1,0},{2,3},{3,2},{4,5},{5,4},{6,7},{7,6},{8,9},{9,8},{10,11... | collective-permute-start | bytes 245768 | tf_op jit(solution)/shard_map/ppermute | solution.py:278
  91.9 6.3 %collective-permute-start.17 = (f32[80,256]{1,0:T(8,128)S(1)}, f32[80,256]{1,0:T(8,128)S(1)}, u32[]{:S(2)}, u32[]{:S(2)}) collective-permute-start(f32[80,256]{1,0:T(8,128)S(1)} %add.25.refs_0_), channel_id=1, source_target_pairs={{0,6},{1,7},{2,4},{3,5},{4,2},{5,3},{6,0},{7,1},{8,14},{9,15},{10,... | collective-permute-start | bytes 245768 | tf_op jit(solution)/shard_map/ppermute | solution.py:278
  92.5 6.3 %collective-permute-start.18 = (f32[80,256]{1,0:T(8,128)S(1)}, f32[80,256]{1,0:T(8,128)S(1)}, u32[]{:S(2)}, u32[]{:S(2)}) collective-permute-start(f32[80,256]{1,0:T(8,128)S(1)} %add.25.refs_0_), channel_id=1, source_target_pairs={{0,2},{1,5},{2,0},{3,7},{4,6},{5,1},{6,4},{7,3},{8,10},{9,13},{10,... | collective-permute-start | bytes 245768 | tf_op jit(solution)/shard_map/ppermute | solution.py:278
  93.4 5.7 %collective-permute-start.19 = (f32[80,256]{1,0:T(8,128)S(1)}, f32[80,256]{1,0:T(8,128)S(1)}, u32[]{:S(2)}, u32[]{:S(2)}) collective-permute-start(f32[80,256]{1,0:T(8,128)S(1)} %add.25.refs_0_), channel_id=1, source_target_pairs={{0,4},{1,3},{2,6},{3,1},{4,0},{5,7},{6,2},{7,5},{8,12},{9,11},{10,... | collective-permute-start | bytes 245768 | tf_op jit(solution)/shard_map/ppermute | solution.py:278
  101.0 1.2 collective-permute-start.20
  102.5 12.5 %collective-permute-start.22 = (bf16[64,1152]{1,0:T(8,128)(2,1)S(1)}, bf16[64,1152]{1,0:T(8,128)(2,1)S(1)}, u32[]{:S(2)}, u32[]{:S(2)}) collective-permute-start(bf16[64,1152]{1,0:T(8,128)(2,1)S(1)} %shard_map.46), channel_id=1, source_target_pairs={{0,8},{1,9},{2,10},{3,11},{4,12},{5,13},{6,14},{7,15},{8,0},{9,1},... | collective-permute-start | bytes 442376 | tf_op jit(solution)/shard_map/ppermute | solution.py:278
  105.0 11.8 %collective-permute-start.21 = (bf16[64,768]{1,0:T(8,128)(2,1)S(1)}, bf16[64,768]{1,0:T(8,128)(2,1)S(1)}, u32[]{:S(2)}, u32[]{:S(2)}) collective-permute-start(bf16[64,768]{1,0:T(8,128)(2,1)S(1)} %shard_map.44), channel_id=1, source_target_pairs={{0,8},{1,9},{2,10},{3,11},{4,12},{5,13},{6,14},{7,15},{8,0},{9,1},... | collective-permute-start | bytes 294920 | tf_op jit(solution)/shard_map/ppermute | solution.py:278
  117.3 5.0 %collective-permute-start.23 = (f32[64,64]{1,0:T(8,128)S(1)}, f32[64,64]{1,0:T(8,128)S(1)}, u32[]{:S(2)}, u32[]{:S(2)}) collective-permute-start(f32[64,64]{1,0:T(8,128)S(1)} %get-tuple-element.68), channel_id=1, source_target_pairs={{0,9},{1,8},{2,11},{3,10},{4,13},{5,12},{6,15},{7,14},{8,1},{9,0},... | collective-permute-start | bytes 49160 | tf_op jit(solution)/shard_map/ppermute | solution.py:278
  117.3 5.5 %collective-permute-start.24 = (f32[64,64]{1,0:T(8,128)S(1)}, f32[64,64]{1,0:T(8,128)S(1)}, u32[]{:S(2)}, u32[]{:S(2)}) collective-permute-start(f32[64,64]{1,0:T(8,128)S(1)} %get-tuple-element.68), channel_id=1, source_target_pairs={{0,8},{1,9},{2,10},{3,11},{4,12},{5,13},{6,14},{7,15},{8,0},{9,1},... | collective-permute-start | bytes 49160 | tf_op jit(solution)/shard_map/ppermute | solution.py:278
  119.6 3.2 %collective-permute-start.25 = (f32[64,64]{1,0:T(8,128)S(1)}, f32[64,64]{1,0:T(8,128)S(1)}, u32[]{:S(2)}, u32[]{:S(2)}) collective-permute-start(f32[64,64]{1,0:T(8,128)S(1)} %get-tuple-element.68), channel_id=1, source_target_pairs={{0,1},{1,0},{2,3},{3,2},{4,5},{5,4},{6,7},{7,6},{8,9},{9,8},{10,11... | collective-permute-start | bytes 49160 | tf_op jit(solution)/shard_map/ppermute | solution.py:278
  122.9 4.9 %collective-permute-start.26 = (f32[64,64]{1,0:T(8,128)S(1)}, f32[64,64]{1,0:T(8,128)S(1)}, u32[]{:S(2)}, u32[]{:S(2)}) collective-permute-start(f32[64,64]{1,0:T(8,128)S(1)} %add_add_fusion.1), channel_id=1, source_target_pairs={{0,6},{1,7},{2,4},{3,5},{4,2},{5,3},{6,0},{7,1},{8,14},{9,15},{10,... | collective-permute-start | bytes 49160 | tf_op jit(solution)/shard_map/ppermute | solution.py:278
  125.7 3.9 %collective-permute-start.27 = (f32[64,64]{1,0:T(8,128)S(1)}, f32[64,64]{1,0:T(8,128)S(1)}, u32[]{:S(2)}, u32[]{:S(2)}) collective-permute-start(f32[64,64]{1,0:T(8,128)S(1)} %add_add_fusion.1), channel_id=1, source_target_pairs={{0,2},{1,5},{2,0},{3,7},{4,6},{5,1},{6,4},{7,3},{8,10},{9,13},{10,... | collective-permute-start | bytes 49160 | tf_op jit(solution)/shard_map/ppermute | solution.py:278
  126.4 3.9 %collective-permute-start.28 = (f32[64,64]{1,0:T(8,128)S(1)}, f32[64,64]{1,0:T(8,128)S(1)}, u32[]{:S(2)}, u32[]{:S(2)}) collective-permute-start(f32[64,64]{1,0:T(8,128)S(1)} %add_add_fusion.1), channel_id=1, source_target_pairs={{0,4},{1,3},{2,6},{3,1},{4,0},{5,7},{6,2},{7,5},{8,12},{9,11},{10,... | collective-permute-start | bytes 49160 | tf_op jit(solution)/shard_map/ppermute | solution.py:278

commit v14 on v13

--- a/solution.py
+++ b/solution.py
@@ -36,6 +36,20 @@
     a1, a2, a3 = three(a)
     b1, b2, b3 = three(b)
     return nn(jnp.concatenate([a3, a2, a1, a2, a1, a1], axis=1), jnp.concatenate([b1, b2, b3, b1, b2, b1], axis=0))
+
+
+def exact_nt(a, b):
+    a1, a2, a3 = three(a)
+    b1, b2, b3 = three(b)
+    return nt(jnp.concatenate([a3, a2, a1, a2, a1, a1], axis=1), jnp.concatenate([b1, b2, b3, b1, b2, b1], axis=1))
+
+
+def exact_by_bf16(a, b):
+    return nn(jnp.concatenate(three(a), axis=1), jnp.concatenate([b] * 3, axis=0))
+
+
+def first_half():
+    return lax.axis_index("cell") & GROUP == 0
 
 
 def exact_gram(a):
@@ -160,7 +174,7 @@
         below = [x[rank:] for x in values]
         below = (below[0] + below[1]) + (below[2] + below[3])
         gram = jnp.concatenate([below[:, j * rank:(j + 1) * rank] for j in range(cells // rank)], axis=0)
-        value = exact_nn(inverse_factor(gram), value)
+        value = exact_nn(factors(gram)[1], value)
     out[...] = value.astype(bf16)
 
 
@@ -168,6 +182,42 @@
     cells = value.shape[1]
     return call(functools.partial(image_kernel, normalised), [value, *mates], [struct((rank, cells), bf16)],
                 cost(12 * value.size * rank, 16 * value.size))[0]
+
+
+def whiten_kernel(even, odd, even_out, odd_out, factor):
+    rank = even.shape[0]
+    size = even.shape[1] // (GROUP // 2)
+    chips = []
+    for j in range(GROUP // 2):
+        one, two = (ref[:, j * size:(j + 1) * size] for ref in (even, odd))
+        chips.append(nt(one, one) + nt(two, two))
+    gram = (chips[0] + chips[1]) + (chips[2] + chips[3])
+    diagonal = lax.broadcasted_iota(jnp.int32, gram.shape, 0) == lax.broadcasted_iota(jnp.int32, gram.shape, 1)
+    shift = jnp.sum(jnp.where(diagonal, gram, 0.0), keepdims=True) * (1e-5 / rank) + 1e-12
+    upper, inverse = factors(gram + jnp.where(diagonal, shift, 0.0))
+    for source, out in ((even, even_out), (odd, odd_out)):
+        value = exact_by_bf16(inverse, source[...])
+        high = value.astype(bf16)
+        out[:rank] = high
+        out[rank:] = (value - high.astype(f32)).astype(bf16)
+    factor[...] = jnp.where(first_half(), inverse, upper)
+
+
+def whiten(even, odd):
+    rank = even.shape[0]
+    return call(whiten_kernel, [even, odd], [struct((2 * rank, even.shape[1]), bf16)] * 2 + [struct((rank, rank), f32)],
+                cost(12 * even.size * rank, 8 * even.size))
+
+
+def change_kernel(mine, theirs, out):
+    first = first_half()
+    inverse = jnp.where(first, mine[...], theirs[...])
+    upper = jnp.where(first, theirs[...], mine[...])
+    out[...] = exact_nt(inverse, upper)
+
+
+def change_of(mine, theirs):
+    return call(change_kernel, [mine, theirs], [struct(mine.shape, f32)], cost(12 * mine.size, 12 * mine.size))[0]
 
 
 def terms_kernel(starts, *refs):
@@ -181,23 +231,25 @@
             for odd in range(2):
                 big = jnp.concatenate([ref[:, start + left:start + left + step] for ref in slots[odd::2]], axis=0)
                 total = total + nn(images[odd][...], big)
-            out[part * rank:(part + 1) * rank, left:left + step] = total.astype(out.dtype)
+            out[part * rank:(part + 1) * rank, left:left + step] = (total[:rank] + total[rank:]).astype(out.dtype)
 
 
 def terms(slots, starts, width, images, dtype):
-    rank, cells = images[0].shape[0], slots[0].shape[0] * GROUP
+    rank, cells = images[0].shape[0] // 2, slots[0].shape[0] * GROUP
     size = cells * width * len(starts)
     return call(functools.partial(terms_kernel, starts), [*slots, *images],
-                [struct((rank * len(starts), width), dtype)], cost(2 * rank * size, 2 * size))[0]
-
-
-def both_kernel(sent, received, *refs):
+                [struct((rank * len(starts), width), dtype)], cost(4 * rank * size, 2 * size))[0]
+
+
+def both_kernel(sent, received, change, *refs):
     before, rows, gram = refs[:-3], refs[-3:-1], refs[-1]
     rank = rows[0].shape[0]
+    first = first_half()
     grams = []
     for block in range(2):
         mine, theirs = slice(block * rank, (block + 1) * rank), slice((1 - block) * rank, (2 - block) * rank)
-        value = sent[mine].astype(f32) + received[theirs].astype(f32)
+        one, two = sent[mine].astype(f32), received[theirs].astype(f32)
+        value = jnp.where(first, one, two) + exact_by_bf16(change[...], jnp.where(first, two, one).astype(bf16))
         rows[block][...] = value.astype(bf16)
         grams.append(exact_gram(value))
     total = grams[0] + grams[1]
@@ -206,15 +258,17 @@
     gram[...] = total
 
 
-def both(sent, received, before):
+def both(sent, received, change, before):
     rank, width = sent.shape[0] // 2, sent.shape[1]
-    return call(both_kernel, [sent, received, *before], [struct((rank, width), bf16)] * 2 + [struct((rank, rank), f32)],
+    return call(both_kernel, [sent, received, change, *before], [struct((rank, width), bf16)] * 2 + [struct((rank, rank), f32)],
                 cost(24 * rank * rank * width, 24 * rank * width))
 
 
-def loading_kernel(received, own, *refs):
+def loading_kernel(received, own, change, *refs):
     before, loading, gram = refs[:-2], refs[-2], refs[-1]
-    value = own[...] + received[...].astype(f32)
+    first = first_half()
+    one, two = own[...], received[...].astype(f32)
+    value = jnp.where(first, one, two) + exact_nn(change[...], jnp.where(first, two, one))
     loading[...] = value
     total = exact_gram(value)
     for ref in before:
@@ -222,13 +276,13 @@
     gram[...] = total
 
 
-def loading_and_gram(received, own, before):
+def loading_and_gram(received, own, change, before):
     rank, width = own.shape
-    return call(loading_kernel, [received, own, *before], [struct((rank, width), f32), struct((rank, rank), f32)],
+    return call(loading_kernel, [received, own, change, *before], [struct((rank, width), f32), struct((rank, rank), f32)],
                 cost(12 * rank * rank * width, 12 * rank * width))
 
 
-def inverse_factor(gram):
+def factors(gram):
     size = gram.shape[0]
     row = lax.broadcasted_iota(jnp.int32, (size, size), 0)
     column = lax.broadcasted_iota(jnp.int32, (size, size), 1)
@@ -255,12 +309,13 @@
             for k in range(b, panels):
                 factor = jnp.where(inner > t, scaled[k], 0.0) if k == b else scaled[k]
                 blocks[k] = blocks[k] - factor * pivot
-    return jnp.concatenate(done, axis=0)[:, size:]
+    rows = jnp.concatenate(done, axis=0)
+    return jnp.where(row <= column, rows[:, :size], 0.0), rows[:, size:]
 
 
 def output_kernel(scale, gram, *refs):
     parts, out = refs[:-1], refs[-1]
-    inverse = inverse_factor(gram[...]) * scale
+    inverse = factors(gram[...])[1] * scale
     start = 0
     for part in parts:
         out[:, start:start + part.shape[1]] = exact_nn(inverse, part[...])
@@ -307,12 +362,13 @@
         (even,) = scores(slots, work, bases, before[:1], *rest, odds=(0,))
         even = even + mate(odd, cells, 1)
         image = image_of(even, legs(even, cells), rank, normalised)
-        return image, mate(image, cells, 1)
+        *images, factor = whiten(image, mate(image, cells, 1))
+        return images, change_of(factor, mate(factor, cells, GROUP))
 
     basis = start_basis.T
     bases = {0: [basis], 1: [mate(basis, cells, GROUP)]}
     early = scores(slots, [(0, (0, 1))], bases)
-    images = image_from([(0, ()), (1, (0, 1))], bases, early, False)
+    images, change = image_from([(0, ()), (1, (0, 1))], bases, early, False)
     everything = [(0, (0, 1)), (1, (0, 1))]
     for _ in range(1, ITERS):
         total, before = [], ()
@@ -323,15 +379,15 @@
         for start, stop, sent, received in arrived:
             if before:
                 received, *before = lax.optimization_barrier((received, *before))
-            own, other, gram = both(sent, received, total)
+            own, other, gram = both(sent, received, change, total)
             total, rows = [gram], {0: [own], 1: [other]}
             if stop < width:
                 before = scores(slots, everything, rows, before, offset=start)
-        images = image_from(everything, rows, before, True, gram, start)
+        images, change = image_from(everything, rows, before, True, gram, start)
     parts, total = [], []
     for start, stop in cuts(width, 60):
         received = mate(terms(slots, (width + start,), stop - start, images, bf16), cells, GROUP)
-        rows, gram = loading_and_gram(received, terms(slots, (start,), stop - start, images, f32), total)
+        rows, gram = loading_and_gram(received, terms(slots, (start,), stop - start, images, f32), change, total)
         parts.append(rows)
         total = [gram]
     return output_call(total_over_cells(gram, cells), parts).T

time: 133 us -> 146 us (1.098)
  Pallas kernels: 15.4 us -> 22.1 us
  waiting for transfers between devices: 82.1 us -> 85.1 us
  starting transfers between devices: 35.5 us -> 38 us
    pallas_call x22 -> x26, Pallas kernels: 13.2 us -> 19.9 us  [call(): pl.pallas_call(kernel, in_specs=[VMEM] * len(args), out_specs=[VMEM] * le...]
    ppermute x29 -> x31, waiting for transfers between devices: 82.1 us -> 85.1 us  [mate(): lax.ppermute(value, 'cell', [(i, i ^ masks[i % 2]) for i in range(cells)])]
    ppermute x29 -> x31, starting transfers between devices: 35.5 us -> 38 us  [mate(): lax.ppermute(value, 'cell', [(i, i ^ masks[i % 2]) for i in range(cells)])]
  transfers between devices with their start and end apart: 29 -> 31, of which waited for: 24 -> 21; matrix products, arithmetic and copies ran while one was open for 0% -> 0% of each run, Pallas kernels for 5% -> 5%
where the time goes in v14:
time: 146 us
  waiting for transfers between devices  85.1 us (58%)
  starting transfers between devices  38 us (26%)
  Pallas kernels  22.1 us (15%)
    ppermute x31, waiting for transfers between devices, mate(): lax.ppermute(value, 'cell', [(i, i ^ masks[i % 2]) for i in range(cells)])  85.1 us
    ppermute x31, starting transfers between devices, mate(): lax.ppermute(value, 'cell', [(i, i ^ masks[i % 2]) for i in range(cells)])  38 us
    pallas_call x26, Pallas kernels, call(): pl.pallas_call(kernel, in_specs=[VMEM] * len(args), out_specs=[VMEM] * le...  19.9 us
  transfers between devices with their start and end apart: 31, of which 21 were waited for; matrix products, arithmetic and copies ran while one was open for 0% of the time, Pallas kernels for 5%

profile of v14, /device:TPU:0, one launch (start us, length us, event | category | flops | bytes accessed | tf_op | source)
XLA Modules:
  0.0 145.5 jit_solution(12170042621441108638)
XLA Ops:
  0.0 2.2 %shard_map.28 = (bf16[64,3840]{1,0:T(8,128)(2,1)S(1)}, bf16[64,3840]{1,0:T(8,128)(2,1)S(1)}, bf16[64,3840]{1,0:T(8,128)(2,1)S(1)}, bf16[64,3840]{1,0:T(8,128)(2,...) custom-call(bf16[64,30720]{1,0:T(8,128)(2,1)} %matrix.1), custom_call_target="tpu_custom_call" | custom-call | bytes 7864320 | tf_op jit(solution)/shard_map/pallas_call | solution.py:96
  2.8 3.6 %collective-permute-start.1 = (bf16[64,3840]{1,0:T(8,128)(2,1)S(1)}, bf16[64,3840]{1,0:T(8,128)(2,1)S(1)}, u32[]{:S(2)}, u32[]{:S(2)}) collective-permute-start(bf16[64,3840]{1,0:T(8,128)(2,1)S(1)} %get-tuple-element.46), channel_id=1, source_target_pairs={{0,6},{1,7},{2,4},{3,5},{4,2},{5,3},{6,0},{7,1},{8,14},{9,15},{10,... | collective-permute-start | bytes 1474568 | tf_op jit(solution)/shard_map/ppermute | solution.py:333
  6.4 2.6 %collective-permute-start.7 = (bf16[64,1920]{1,0:T(8,128)(2,1)S(1)}, bf16[64,1920]{1,0:T(8,128)(2,1)S(1)}, u32[]{:S(2)}, u32[]{:S(2)}) collective-permute-start(bf16[64,1920]{1,0:T(8,128)(2,1)S(1)} %bitcast.2), channel_id=1, source_target_pairs={{0,8},{1,9},{2,10},{3,11},{4,12},{5,13},{6,14},{7,15},{8,0},{9,1},... | collective-permute-start | bytes 737288 | tf_op jit(solution)/shard_map/ppermute | solution.py:333
  9.0 1.6 %collective-permute-start.4 = (bf16[64,3840]{1,0:T(8,128)(2,1)S(1)}, bf16[64,3840]{1,0:T(8,128)(2,1)S(1)}, u32[]{:S(2)}, u32[]{:S(2)}) collective-permute-start(bf16[64,3840]{1,0:T(8,128)(2,1)S(1)} %get-tuple-element.49), channel_id=1, source_target_pairs={{0,3},{1,4},{2,1},{3,6},{4,7},{5,0},{6,5},{7,2},{8,11},{9,12},{10,... | collective-permute-start | bytes 1474568 | tf_op jit(solution)/shard_map/ppermute | solution.py:333
  10.6 12.6 %collective-permute-done.7.refs_1_ = bf16[64,1920]{1,0:T(8,128)(2,1)S(1)} collective-permute-done((bf16[64,1920]{1,0:T(8,128)(2,1)S(1)}, bf16[64,1920]{1,0:T(8,128)(2,1)S(1)}, u32[]{:S(2)}, u32[]{:S(2)}) %collective-permute-start.7) | collective-permute-done | bytes 245792 | tf_op jit(solution)/shard_map/ppermute | solution.py:333
  23.2 2.3 %collective-permute-start.6 = (bf16[64,3840]{1,0:T(8,128)(2,1)S(1)}, bf16[64,3840]{1,0:T(8,128)(2,1)S(1)}, u32[]{:S(2)}, u32[]{:S(2)}) collective-permute-start(bf16[64,3840]{1,0:T(8,128)(2,1)S(1)} %get-tuple-element.51), channel_id=1, source_target_pairs={{0,5},{1,2},{2,7},{3,0},{4,1},{5,6},{6,3},{7,4},{8,13},{9,10},{10,... | collective-permute-start | bytes 1474568 | tf_op jit(solution)/shard_map/ppermute | solution.py:333
  26.0 1.2 collective-permute-start.5
  27.3 6.6 %collective-permute-done.2.refs_5_.refs_3_ = bf16[64,3840]{1,0:T(8,128)(2,1)S(1)} collective-permute-done((bf16[64,3840]{1,0:T(8,128)(2,1)S(1)}, bf16[64,3840]{1,0:T(8,128)(2,1)S(1)}, u32[]{:S(2)}, u32[]{:S(2)}) %collective-permute-start.2) | collective-permute-done | bytes 491552 | tf_op jit(solution)/shard_map/ppermute | solution.py:333
  34.5 9.8 %collective-permute-done.4.refs_2_.refs_5_.refs_7_.refs_4_ = bf16[64,3840]{1,0:T(8,128)(2,1)S(1)} collective-permute-done((bf16[64,3840]{1,0:T(8,128)(2,1)S(1)}, bf16[64,3840]{1,0:T(8,128)(2,1)S(1)}, u32[]{:S(2)}, u32[]{:S(2)}) %collective-permute-start.4) | collective-permute-done | bytes 491552 | tf_op jit(solution)/shard_map/ppermute | solution.py:333
  45.8 3.7 %collective-permute-done.3.refs_2_.refs_4_.refs_6_ = bf16[64,3840]{1,0:T(8,128)(2,1)S(1)} collective-permute-done((bf16[64,3840]{1,0:T(8,128)(2,1)S(1)}, bf16[64,3840]{1,0:T(8,128)(2,1)S(1)}, u32[]{:S(2)}, u32[]{:S(2)}) %collective-permute-start.3) | collective-permute-done | bytes 491552 | tf_op jit(solution)/shard_map/ppermute | solution.py:333
  49.5 5.8 %collective-permute-done.5.refs_3_.refs_6_.refs_8_.refs_5_ = bf16[64,3840]{1,0:T(8,128)(2,1)S(1)} collective-permute-done((bf16[64,3840]{1,0:T(8,128)(2,1)S(1)}, bf16[64,3840]{1,0:T(8,128)(2,1)S(1)}, u32[]{:S(2)}, u32[]{:S(2)}) %collective-permute-start.5) | collective-permute-done | bytes 491552 | tf_op jit(solution)/shard_map/ppermute | solution.py:333
  56.2 1.7 %collective-permute-start.11 = (f32[64,256]{1,0:T(8,128)S(1)}, f32[64,256]{1,0:T(8,128)S(1)}, u32[]{:S(2)}, u32[]{:S(2)}) collective-permute-start(f32[64,256]{1,0:T(8,128)S(1)} %add.24.refs_0_), channel_id=1, source_target_pairs={{0,4},{1,3},{2,6},{3,1},{4,0},{5,7},{6,2},{7,5},{8,12},{9,11},{10,... | collective-permute-start | bytes 196616 | tf_op jit(solution)/shard_map/ppermute | solution.py:333
  58.0 1.4 collective-permute-start.9
  59.3 1.9 %collective-permute-done.10.refs_2_ = f32[64,256]{1,0:T(8,128)S(1)} collective-permute-done((f32[64,256]{1,0:T(8,128)S(1)}, f32[64,256]{1,0:T(8,128)S(1)}, u32[]{:S(2)}, u32[]{:S(2)}) %collective-permute-start.10) | collective-permute-done | bytes 65568 | tf_op jit(solution)/shard_map/ppermute | solution.py:333
  61.3 1.9 %collective-permute-done.9.refs_1_ = f32[64,256]{1,0:T(8,128)S(1)} collective-permute-done((f32[64,256]{1,0:T(8,128)S(1)}, f32[64,256]{1,0:T(8,128)S(1)}, u32[]{:S(2)}, u32[]{:S(2)}) %collective-permute-start.9) | collective-permute-done | bytes 65568 | tf_op jit(solution)/shard_map/ppermute | solution.py:333
  64.5 2.4 %shard_map.33 = (bf16[128,256]{1,0:T(8,128)(2,1)S(1)}, bf16[128,256]{1,0:T(8,128)(2,1)S(1)}, f32[64,64]{1,0:T(8,128)S(1)}) custom-call(bf16[64,256]{1,0:T(8,128)(2,1)S(1)} %shard_map.32.even, bf16[64,256]{1,0:T(8,128)(2,1)S(1)} %collective-permute-done.12.odd), custom_call_target="tpu_custom_call" | custom-call | flops 12582912 | bytes 131072 | tf_op jit(solution)/shard_map/pallas_call | solution.py:108
  67.3 2.6 %collective-permute-start.15 = (bf16[128,896]{1,0:T(8,128)(2,1)S(1)}, bf16[128,896]{1,0:T(8,128)(2,1)S(1)}, u32[]{:S(2)}, u32[]{:S(2)}) collective-permute-start(bf16[128,896]{1,0:T(8,128)(2,1)S(1)} %shard_map.36.sent), channel_id=1, source_target_pairs={{0,8},{1,9},{2,10},{3,11},{4,12},{5,13},{6,14},{7,15},{8,0},{9,1},... | collective-permute-start | bytes 688136 | tf_op jit(solution)/shard_map/ppermute | solution.py:333
  71.1 2.6 %collective-permute-start.13 = (bf16[128,384]{1,0:T(8,128)(2,1)S(1)}, bf16[128,384]{1,0:T(8,128)(2,1)S(1)}, u32[]{:S(2)}, u32[]{:S(2)}) collective-permute-start(bf16[128,384]{1,0:T(8,128)(2,1)S(1)} %shard_map.34.sent), channel_id=1, source_target_pairs={{0,8},{1,9},{2,10},{3,11},{4,12},{5,13},{6,14},{7,15},{8,0},{9,1},... | collective-permute-start | bytes 294920 | tf_op jit(solution)/shard_map/ppermute | solution.py:333
  74.1 19.5 %collective-permute-done.16.theirs = f32[64,64]{1,0:T(8,128)S(1)} collective-permute-done((f32[64,64]{1,0:T(8,128)S(1)}, f32[64,64]{1,0:T(8,128)S(1)}, u32[]{:S(2)}, u32[]{:S(2)}) %collective-permute-start.16) | collective-permute-done | bytes 16416 | tf_op jit(solution)/shard_map/ppermute | solution.py:333
  100.5 2.1 %collective-permute-start.20 = (f32[80,256]{1,0:T(8,128)S(1)}, f32[80,256]{1,0:T(8,128)S(1)}, u32[]{:S(2)}, u32[]{:S(2)}) collective-permute-start(f32[80,256]{1,0:T(8,128)S(1)} %add.25.refs_0_), channel_id=1, source_target_pairs={{0,4},{1,3},{2,6},{3,1},{4,0},{5,7},{6,2},{7,5},{8,12},{9,11},{10,... | collective-permute-start | bytes 245768 | tf_op jit(solution)/shard_map/ppermute | solution.py:333
  102.6 2.7 %collective-permute-done.18.refs_1_ = f32[80,256]{1,0:T(8,128)S(1)} collective-permute-done((f32[80,256]{1,0:T(8,128)S(1)}, f32[80,256]{1,0:T(8,128)S(1)}, u32[]{:S(2)}, u32[]{:S(2)}) %collective-permute-start.18) | collective-permute-done | bytes 81952 | tf_op jit(solution)/shard_map/ppermute | solution.py:333
  106.2 2.0 %shard_map.45.even = bf16[64,256]{1,0:T(8,128)(2,1)S(1)} custom-call(f32[80,256]{1,0:T(8,128)S(1)} %add.25.refs_0_, f32[80,256]{1,0:T(8,128)S(1)} %collective-permute-done.18.refs_1_, f32[80,256]{1,0:T(8,128)S(1)} %collective-permute-done.19.refs_2_, f32[80,256]{1,0:T(8,128)S(1)} %collective-permute-done.20.refs_3_), custom_call_target="tpu_custom_call" | custom-call | flops 15728640 | bytes 327680 | tf_op jit(solution)/shard_map/pallas_call | solution.py:108
  109.4 2.4 %shard_map.46 = (bf16[128,256]{1,0:T(8,128)(2,1)S(1)}, bf16[128,256]{1,0:T(8,128)(2,1)S(1)}, f32[64,64]{1,0:T(8,128)S(1)}) custom-call(bf16[64,256]{1,0:T(8,128)(2,1)S(1)} %shard_map.45.even, bf16[64,256]{1,0:T(8,128)(2,1)S(1)} %collective-permute-done.21.odd), custom_call_target="tpu_custom_call" | custom-call | flops 12582912 | bytes 131072 | tf_op jit(solution)/shard_map/pallas_call | solution.py:108
  112.1 2.2 %collective-permute-start.24 = (bf16[64,1152]{1,0:T(8,128)(2,1)S(1)}, bf16[64,1152]{1,0:T(8,128)(2,1)S(1)}, u32[]{:S(2)}, u32[]{:S(2)}) collective-permute-start(bf16[64,1152]{1,0:T(8,128)(2,1)S(1)} %shard_map.50), channel_id=1, source_target_pairs={{0,8},{1,9},{2,10},{3,11},{4,12},{5,13},{6,14},{7,15},{8,0},{9,1},... | collective-permute-start | bytes 442376 | tf_op jit(solution)/shard_map/ppermute | solution.py:333
  115.5 2.1 %collective-permute-start.23 = (f32[64,64]{1,0:T(8,128)S(1)}, f32[64,64]{1,0:T(8,128)S(1)}, u32[]{:S(2)}, u32[]{:S(2)}) collective-permute-start(f32[64,64]{1,0:T(8,128)S(1)} %get-tuple-element.78.mine), channel_id=1, source_target_pairs={{0,8},{1,9},{2,10},{3,11},{4,12},{5,13},{6,14},{7,15},{8,0},{9,1},... | collective-permute-start | bytes 49160 | tf_op jit(solution)/shard_map/ppermute | solution.py:333
  118.2 9.5 %collective-permute-done.23.theirs = f32[64,64]{1,0:T(8,128)S(1)} collective-permute-done((f32[64,64]{1,0:T(8,128)S(1)}, f32[64,64]{1,0:T(8,128)S(1)}, u32[]{:S(2)}, u32[]{:S(2)}) %collective-permute-start.23) | collective-permute-done | bytes 16416 | tf_op jit(solution)/shard_map/ppermute | solution.py:333
  129.6 2.3 %collective-permute-start.26 = (f32[64,64]{1,0:T(8,128)S(1)}, f32[64,64]{1,0:T(8,128)S(1)}, u32[]{:S(2)}, u32[]{:S(2)}) collective-permute-start(f32[64,64]{1,0:T(8,128)S(1)} %get-tuple-element.80), channel_id=1, source_target_pairs={{0,8},{1,9},{2,10},{3,11},{4,12},{5,13},{6,14},{7,15},{8,0},{9,1},... | collective-permute-start | bytes 49160 | tf_op jit(solution)/shard_map/ppermute | solution.py:333
  132.3 2.2 %collective-permute-done.25 = f32[64,64]{1,0:T(8,128)S(1)} collective-permute-done((f32[64,64]{1,0:T(8,128)S(1)}, f32[64,64]{1,0:T(8,128)S(1)}, u32[]{:S(2)}, u32[]{:S(2)}) %collective-permute-start.25) | collective-permute-done | bytes 16416 | tf_op jit(solution)/shard_map/ppermute | solution.py:333
  135.1 2.8 %collective-permute-start.28 = (f32[64,64]{1,0:T(8,128)S(1)}, f32[64,64]{1,0:T(8,128)S(1)}, u32[]{:S(2)}, u32[]{:S(2)}) collective-permute-start(f32[64,64]{1,0:T(8,128)S(1)} %add_add_fusion.1), channel_id=1, source_target_pairs={{0,6},{1,7},{2,4},{3,5},{4,2},{5,3},{6,0},{7,1},{8,14},{9,15},{10,... | collective-permute-start | bytes 49160 | tf_op jit(solution)/shard_map/ppermute | solution.py:333
  138.7 1.3 collective-permute-done.28
  140.0 1.8 %collective-permute-done.29 = f32[64,64]{1,0:T(8,128)S(1)} collective-permute-done((f32[64,64]{1,0:T(8,128)S(1)}, f32[64,64]{1,0:T(8,128)S(1)}, u32[]{:S(2)}, u32[]{:S(2)}) %collective-permute-start.29) | collective-permute-done | bytes 16416 | tf_op jit(solution)/shard_map/ppermute | solution.py:333
  142.6 3.0 %shard_map.54 = f32[64,1920]{1,0:T(8,128)} custom-call(f32[64,64]{1,0:T(8,128)S(1)} %add_add_fusion.gram, f32[64,1152]{1,0:T(8,128)S(1)} %get-tuple-element.81.refs_0_, f32[64,768]{1,0:T(8,128)S(1)} %get-tuple-element.82.refs_1_), custom_call_target="tpu_custom_call" | custom-call | flops 94371840 | bytes 983040 | tf_op jit(solution)/shard_map/pallas_call | solution.py:108
  (63 shorter events, 23.0 us)
Async XLA Ops:
  0.0 6.4 %copy-start = (bf16[1920,64]{0,1:T(8,128)(2,1)S(1)}, bf16[1920,64]{0,1:T(8,128)(2,1)}, u32[]{:S(2)}) copy-start(bf16[1920,64]{0,1:T(8,128)(2,1)} %param.3) | copy-start | bytes 737284
  2.2 23.3 %collective-permute-start = (bf16[64,3840]{1,0:T(8,128)(2,1)S(1)}, bf16[64,3840]{1,0:T(8,128)(2,1)S(1)}, u32[]{:S(2)}, u32[]{:S(2)}) collective-permute-start(bf16[64,3840]{1,0:T(8,128)(2,1)S(1)} %get-tuple-element.45), channel_id=1, source_target_pairs={{0,1},{1,0},{2,3},{3,2},{4,5},{5,4},{6,7},{7,6},{8,9},{9,8},{10,11... | collective-permute-start | bytes 1474568 | tf_op jit(solution)/shard_map/ppermute | solution.py:333
  2.8 23.3 %collective-permute-start.1 = (bf16[64,3840]{1,0:T(8,128)(2,1)S(1)}, bf16[64,3840]{1,0:T(8,128)(2,1)S(1)}, u32[]{:S(2)}, u32[]{:S(2)}) collective-permute-start(bf16[64,3840]{1,0:T(8,128)(2,1)S(1)} %get-tuple-element.46), channel_id=1, source_target_pairs={{0,6},{1,7},{2,4},{3,5},{4,2},{5,3},{6,0},{7,1},{8,14},{9,15},{10,... | collective-permute-start | bytes 1474568 | tf_op jit(solution)/shard_map/ppermute | solution.py:333
  6.4 16.8 %collective-permute-start.7 = (bf16[64,1920]{1,0:T(8,128)(2,1)S(1)}, bf16[64,1920]{1,0:T(8,128)(2,1)S(1)}, u32[]{:S(2)}, u32[]{:S(2)}) collective-permute-start(bf16[64,1920]{1,0:T(8,128)(2,1)S(1)} %bitcast.2), channel_id=1, source_target_pairs={{0,8},{1,9},{2,10},{3,11},{4,12},{5,13},{6,14},{7,15},{8,0},{9,1},... | collective-permute-start | bytes 737288 | tf_op jit(solution)/shard_map/ppermute | solution.py:333
  9.0 24.9 %collective-permute-start.2 = (bf16[64,3840]{1,0:T(8,128)(2,1)S(1)}, bf16[64,3840]{1,0:T(8,128)(2,1)S(1)}, u32[]{:S(2)}, u32[]{:S(2)}) collective-permute-start(bf16[64,3840]{1,0:T(8,128)(2,1)S(1)} %get-tuple-element.47), channel_id=1, source_target_pairs={{0,7},{1,6},{2,5},{3,4},{4,3},{5,2},{6,1},{7,0},{8,15},{9,14},{10,... | collective-permute-start | bytes 1474568 | tf_op jit(solution)/shard_map/ppermute | solution.py:333
  9.0 35.3 %collective-permute-start.4 = (bf16[64,3840]{1,0:T(8,128)(2,1)S(1)}, bf16[64,3840]{1,0:T(8,128)(2,1)S(1)}, u32[]{:S(2)}, u32[]{:S(2)}) collective-permute-start(bf16[64,3840]{1,0:T(8,128)(2,1)S(1)} %get-tuple-element.49), channel_id=1, source_target_pairs={{0,3},{1,4},{2,1},{3,6},{4,7},{5,0},{6,5},{7,2},{8,11},{9,12},{10,... | collective-permute-start | bytes 1474568 | tf_op jit(solution)/shard_map/ppermute | solution.py:333
  23.2 21.5 %collective-permute-start.6 = (bf16[64,3840]{1,0:T(8,128)(2,1)S(1)}, bf16[64,3840]{1,0:T(8,128)(2,1)S(1)}, u32[]{:S(2)}, u32[]{:S(2)}) collective-permute-start(bf16[64,3840]{1,0:T(8,128)(2,1)S(1)} %get-tuple-element.51), channel_id=1, source_target_pairs={{0,5},{1,2},{2,7},{3,0},{4,1},{5,6},{6,3},{7,4},{8,13},{9,10},{10,... | collective-permute-start | bytes 1474568 | tf_op jit(solution)/shard_map/ppermute | solution.py:333
  25.5 23.9 %collective-permute-start.3 = (bf16[64,3840]{1,0:T(8,128)(2,1)S(1)}, bf16[64,3840]{1,0:T(8,128)(2,1)S(1)}, u32[]{:S(2)}, u32[]{:S(2)}) collective-permute-start(bf16[64,3840]{1,0:T(8,128)(2,1)S(1)} %get-tuple-element.48), channel_id=1, source_target_pairs={{0,2},{1,5},{2,0},{3,7},{4,6},{5,1},{6,4},{7,3},{8,10},{9,13},{10,... | collective-permute-start | bytes 1474568 | tf_op jit(solution)/shard_map/ppermute | solution.py:333
  26.0 29.2 %collective-permute-start.5 = (bf16[64,3840]{1,0:T(8,128)(2,1)S(1)}, bf16[64,3840]{1,0:T(8,128)(2,1)S(1)}, u32[]{:S(2)}, u32[]{:S(2)}) collective-permute-start(bf16[64,3840]{1,0:T(8,128)(2,1)S(1)} %get-tuple-element.50), channel_id=1, source_target_pairs={{0,4},{1,3},{2,6},{3,1},{4,0},{5,7},{6,2},{7,5},{8,12},{9,11},{10,... | collective-permute-start | bytes 1474568 | tf_op jit(solution)/shard_map/ppermute | solution.py:333
  45.1 10.6 %collective-permute-start.8 = (f32[64,256]{1,0:T(8,128)S(1)}, f32[64,256]{1,0:T(8,128)S(1)}, u32[]{:S(2)}, u32[]{:S(2)}) collective-permute-start(f32[64,256]{1,0:T(8,128)S(1)} %shard_map.31), channel_id=1, source_target_pairs={{0,1},{1,0},{2,3},{3,2},{4,5},{5,4},{6,7},{7,6},{8,9},{9,8},{10,11... | collective-permute-start | bytes 196616 | tf_op jit(solution)/shard_map/ppermute | solution.py:333
  55.8 5.5 %collective-permute-start.10 = (f32[64,256]{1,0:T(8,128)S(1)}, f32[64,256]{1,0:T(8,128)S(1)}, u32[]{:S(2)}, u32[]{:S(2)}) collective-permute-start(f32[64,256]{1,0:T(8,128)S(1)} %add.24.refs_0_), channel_id=1, source_target_pairs={{0,2},{1,5},{2,0},{3,7},{4,6},{5,1},{6,4},{7,3},{8,10},{9,13},{10,... | collective-permute-start | bytes 196616 | tf_op jit(solution)/shard_map/ppermute | solution.py:333
  56.2 5.0 %collective-permute-start.11 = (f32[64,256]{1,0:T(8,128)S(1)}, f32[64,256]{1,0:T(8,128)S(1)}, u32[]{:S(2)}, u32[]{:S(2)}) collective-permute-start(f32[64,256]{1,0:T(8,128)S(1)} %add.24.refs_0_), channel_id=1, source_target_pairs={{0,4},{1,3},{2,6},{3,1},{4,0},{5,7},{6,2},{7,5},{8,12},{9,11},{10,... | collective-permute-start | bytes 196616 | tf_op jit(solution)/shard_map/ppermute | solution.py:333
  58.0 5.2 %collective-permute-start.9 = (f32[64,256]{1,0:T(8,128)S(1)}, f32[64,256]{1,0:T(8,128)S(1)}, u32[]{:S(2)}, u32[]{:S(2)}) collective-permute-start(f32[64,256]{1,0:T(8,128)S(1)} %add.24.refs_0_), channel_id=1, source_target_pairs={{0,6},{1,7},{2,4},{3,5},{4,2},{5,3},{6,0},{7,1},{8,14},{9,15},{10,... | collective-permute-start | bytes 196616 | tf_op jit(solution)/shard_map/ppermute | solution.py:333
  63.2 1.3 collective-permute-start.12
  67.3 26.4 %collective-permute-start.15 = (bf16[128,896]{1,0:T(8,128)(2,1)S(1)}, bf16[128,896]{1,0:T(8,128)(2,1)S(1)}, u32[]{:S(2)}, u32[]{:S(2)}) collective-permute-start(bf16[128,896]{1,0:T(8,128)(2,1)S(1)} %shard_map.36.sent), channel_id=1, source_target_pairs={{0,8},{1,9},{2,10},{3,11},{4,12},{5,13},{6,14},{7,15},{8,0},{9,1},... | collective-permute-start | bytes 688136 | tf_op jit(solution)/shard_map/ppermute | solution.py:333
  70.3 25.0 %collective-permute-start.14 = (bf16[128,640]{1,0:T(8,128)(2,1)S(1)}, bf16[128,640]{1,0:T(8,128)(2,1)S(1)}, u32[]{:S(2)}, u32[]{:S(2)}) collective-permute-start(bf16[128,640]{1,0:T(8,128)(2,1)S(1)} %shard_map.35.sent), channel_id=1, source_target_pairs={{0,8},{1,9},{2,10},{3,11},{4,12},{5,13},{6,14},{7,15},{8,0},{9,1},... | collective-permute-start | bytes 491528 | tf_op jit(solution)/shard_map/ppermute | solution.py:333
  71.1 25.6 %collective-permute-start.13 = (bf16[128,384]{1,0:T(8,128)(2,1)S(1)}, bf16[128,384]{1,0:T(8,128)(2,1)S(1)}, u32[]{:S(2)}, u32[]{:S(2)}) collective-permute-start(bf16[128,384]{1,0:T(8,128)(2,1)S(1)} %shard_map.34.sent), channel_id=1, source_target_pairs={{0,8},{1,9},{2,10},{3,11},{4,12},{5,13},{6,14},{7,15},{8,0},{9,1},... | collective-permute-start | bytes 294920 | tf_op jit(solution)/shard_map/ppermute | solution.py:333
  73.7 19.8 %collective-permute-start.16 = (f32[64,64]{1,0:T(8,128)S(1)}, f32[64,64]{1,0:T(8,128)S(1)}, u32[]{:S(2)}, u32[]{:S(2)}) collective-permute-start(f32[64,64]{1,0:T(8,128)S(1)} %get-tuple-element.56.mine), channel_id=1, source_target_pairs={{0,8},{1,9},{2,10},{3,11},{4,12},{5,13},{6,14},{7,15},{8,0},{9,1},... | collective-permute-start | bytes 49160 | tf_op jit(solution)/shard_map/ppermute | solution.py:333
  97.7 1.3 collective-permute-start.17
  99.0 6.3 %collective-permute-start.18 = (f32[80,256]{1,0:T(8,128)S(1)}, f32[80,256]{1,0:T(8,128)S(1)}, u32[]{:S(2)}, u32[]{:S(2)}) collective-permute-start(f32[80,256]{1,0:T(8,128)S(1)} %add.25.refs_0_), channel_id=1, source_target_pairs={{0,6},{1,7},{2,4},{3,5},{4,2},{5,3},{6,0},{7,1},{8,14},{9,15},{10,... | collective-permute-start | bytes 245768 | tf_op jit(solution)/shard_map/ppermute | solution.py:333
  99.7 6.3 %collective-permute-start.19 = (f32[80,256]{1,0:T(8,128)S(1)}, f32[80,256]{1,0:T(8,128)S(1)}, u32[]{:S(2)}, u32[]{:S(2)}) collective-permute-start(f32[80,256]{1,0:T(8,128)S(1)} %add.25.refs_0_), channel_id=1, source_target_pairs={{0,2},{1,5},{2,0},{3,7},{4,6},{5,1},{6,4},{7,3},{8,10},{9,13},{10,... | collective-permute-start | bytes 245768 | tf_op jit(solution)/shard_map/ppermute | solution.py:333
  100.5 5.7 %collective-permute-start.20 = (f32[80,256]{1,0:T(8,128)S(1)}, f32[80,256]{1,0:T(8,128)S(1)}, u32[]{:S(2)}, u32[]{:S(2)}) collective-permute-start(f32[80,256]{1,0:T(8,128)S(1)} %add.25.refs_0_), channel_id=1, source_target_pairs={{0,4},{1,3},{2,6},{3,1},{4,0},{5,7},{6,2},{7,5},{8,12},{9,11},{10,... | collective-permute-start | bytes 245768 | tf_op jit(solution)/shard_map/ppermute | solution.py:333
  108.2 1.2 collective-permute-start.21
  112.1 15.9 %collective-permute-start.24 = (bf16[64,1152]{1,0:T(8,128)(2,1)S(1)}, bf16[64,1152]{1,0:T(8,128)(2,1)S(1)}, u32[]{:S(2)}, u32[]{:S(2)}) collective-permute-start(bf16[64,1152]{1,0:T(8,128)(2,1)S(1)} %shard_map.50), channel_id=1, source_target_pairs={{0,8},{1,9},{2,10},{3,11},{4,12},{5,13},{6,14},{7,15},{8,0},{9,1},... | collective-permute-start | bytes 442376 | tf_op jit(solution)/shard_map/ppermute | solution.py:333
  114.6 14.2 %collective-permute-start.22 = (bf16[64,768]{1,0:T(8,128)(2,1)S(1)}, bf16[64,768]{1,0:T(8,128)(2,1)S(1)}, u32[]{:S(2)}, u32[]{:S(2)}) collective-permute-start(bf16[64,768]{1,0:T(8,128)(2,1)S(1)} %shard_map.47), channel_id=1, source_target_pairs={{0,8},{1,9},{2,10},{3,11},{4,12},{5,13},{6,14},{7,15},{8,0},{9,1},... | collective-permute-start | bytes 294920 | tf_op jit(solution)/shard_map/ppermute | solution.py:333
  115.5 12.3 %collective-permute-start.23 = (f32[64,64]{1,0:T(8,128)S(1)}, f32[64,64]{1,0:T(8,128)S(1)}, u32[]{:S(2)}, u32[]{:S(2)}) collective-permute-start(f32[64,64]{1,0:T(8,128)S(1)} %get-tuple-element.78.mine), channel_id=1, source_target_pairs={{0,8},{1,9},{2,10},{3,11},{4,12},{5,13},{6,14},{7,15},{8,0},{9,1},... | collective-permute-start | bytes 49160 | tf_op jit(solution)/shard_map/ppermute | solution.py:333
  129.5 5.0 %collective-permute-start.25 = (f32[64,64]{1,0:T(8,128)S(1)}, f32[64,64]{1,0:T(8,128)S(1)}, u32[]{:S(2)}, u32[]{:S(2)}) collective-permute-start(f32[64,64]{1,0:T(8,128)S(1)} %get-tuple-element.80), channel_id=1, source_target_pairs={{0,9},{1,8},{2,11},{3,10},{4,13},{5,12},{6,15},{7,14},{8,1},{9,0},... | collective-permute-start | bytes 49160 | tf_op jit(solution)/shard_map/ppermute | solution.py:333
  129.6 5.5 %collective-permute-start.26 = (f32[64,64]{1,0:T(8,128)S(1)}, f32[64,64]{1,0:T(8,128)S(1)}, u32[]{:S(2)}, u32[]{:S(2)}) collective-permute-start(f32[64,64]{1,0:T(8,128)S(1)} %get-tuple-element.80), channel_id=1, source_target_pairs={{0,8},{1,9},{2,10},{3,11},{4,12},{5,13},{6,14},{7,15},{8,0},{9,1},... | collective-permute-start | bytes 49160 | tf_op jit(solution)/shard_map/ppermute | solution.py:333
  131.9 3.2 %collective-permute-start.27 = (f32[64,64]{1,0:T(8,128)S(1)}, f32[64,64]{1,0:T(8,128)S(1)}, u32[]{:S(2)}, u32[]{:S(2)}) collective-permute-start(f32[64,64]{1,0:T(8,128)S(1)} %get-tuple-element.80), channel_id=1, source_target_pairs={{0,1},{1,0},{2,3},{3,2},{4,5},{5,4},{6,7},{7,6},{8,9},{9,8},{10,11... | collective-permute-start | bytes 49160 | tf_op jit(solution)/shard_map/ppermute | solution.py:333
  135.1 4.9 %collective-permute-start.28 = (f32[64,64]{1,0:T(8,128)S(1)}, f32[64,64]{1,0:T(8,128)S(1)}, u32[]{:S(2)}, u32[]{:S(2)}) collective-permute-start(f32[64,64]{1,0:T(8,128)S(1)} %add_add_fusion.1), channel_id=1, source_target_pairs={{0,6},{1,7},{2,4},{3,5},{4,2},{5,3},{6,0},{7,1},{8,14},{9,15},{10,... | collective-permute-start | bytes 49160 | tf_op jit(solution)/shard_map/ppermute | solution.py:333
  137.9 3.9 %collective-permute-start.29 = (f32[64,64]{1,0:T(8,128)S(1)}, f32[64,64]{1,0:T(8,128)S(1)}, u32[]{:S(2)}, u32[]{:S(2)}) collective-permute-start(f32[64,64]{1,0:T(8,128)S(1)} %add_add_fusion.1), channel_id=1, source_target_pairs={{0,2},{1,5},{2,0},{3,7},{4,6},{5,1},{6,4},{7,3},{8,10},{9,13},{10,... | collective-permute-start | bytes 49160 | tf_op jit(solution)/shard_map/ppermute | solution.py:333
  138.6 3.9 %collective-permute-start.30 = (f32[64,64]{1,0:T(8,128)S(1)}, f32[64,64]{1,0:T(8,128)S(1)}, u32[]{:S(2)}, u32[]{:S(2)}) collective-permute-start(f32[64,64]{1,0:T(8,128)S(1)} %add_add_fusion.1), channel_id=1, source_target_pairs={{0,4},{1,3},{2,6},{3,1},{4,0},{5,7},{6,2},{7,5},{8,12},{9,11},{10,... | collective-permute-start | bytes 49160 | tf_op jit(solution)/shard_map/ppermute | solution.py:333

commit v15 on v14

--- a/solution.py
+++ b/solution.py
@@ -209,20 +209,27 @@
                 cost(12 * even.size * rank, 8 * even.size))
 
 
-def change_kernel(mine, theirs, out):
+def change_kernel(mine, message, out):
+    rank = out.shape[0]
+    rows, lanes = message.shape[0], message.shape[1]
+    if rows == rank:
+        places = [(0, lanes - 3 * rank), (0, lanes - 2 * rank), (0, lanes - rank)]
+    else:
+        places = [(0, lanes - 2 * rank), (0, lanes - rank), (rank, lanes - 2 * rank)]
+    high, middle, low = (message[top:top + rank, left:left + rank].astype(f32) for top, left in places)
+    theirs = (high + middle) + low
     first = first_half()
-    inverse = jnp.where(first, mine[...], theirs[...])
-    upper = jnp.where(first, theirs[...], mine[...])
+    inverse = jnp.where(first, mine[...], theirs)
+    upper = jnp.where(first, theirs, mine[...])
     out[...] = exact_nt(inverse, upper)
 
 
-def change_of(mine, theirs):
-    return call(change_kernel, [mine, theirs], [struct(mine.shape, f32)], cost(12 * mine.size, 12 * mine.size))[0]
-
-
-def terms_kernel(starts, *refs):
+def change_of(mine, message):
+    return call(change_kernel, [mine, message], [struct(mine.shape, f32)], cost(12 * mine.size, 12 * mine.size))[0]
+
+
+def terms_kernel(starts, width, with_factor, *refs):
     slots, images, out = refs[:GROUP], refs[GROUP:GROUP + 2], refs[-1]
-    width = out.shape[1]
     rank = out.shape[0] // len(starts)
     step = width // 2 if width % 256 == 0 else width
     for part, start in enumerate(starts):
@@ -232,23 +239,32 @@
                 big = jnp.concatenate([ref[:, start + left:start + left + step] for ref in slots[odd::2]], axis=0)
                 total = total + nn(images[odd][...], big)
             out[part * rank:(part + 1) * rank, left:left + step] = (total[:rank] + total[rank:]).astype(out.dtype)
-
-
-def terms(slots, starts, width, images, dtype):
+    if with_factor:
+        tail = list(three(refs[GROUP + 2][...]))
+        if len(starts) == 2:
+            tail.append(jnp.zeros_like(tail[0]))
+        across = len(tail) // len(starts)
+        for part in range(len(starts)):
+            out[part * rank:(part + 1) * rank, width:] = jnp.concatenate(tail[part * across:(part + 1) * across], axis=1)
+
+
+def terms(slots, starts, width, images, dtype, factor=None):
     rank, cells = images[0].shape[0] // 2, slots[0].shape[0] * GROUP
     size = cells * width * len(starts)
-    return call(functools.partial(terms_kernel, starts), [*slots, *images],
-                [struct((rank * len(starts), width), dtype)], cost(4 * rank * size, 2 * size))[0]
+    tail = 0 if factor is None else (3 if len(starts) == 1 else 2) * rank
+    args = [*slots, *images] + ([] if factor is None else [factor])
+    return call(functools.partial(terms_kernel, starts, width, factor is not None), args,
+                [struct((rank * len(starts), width + tail), dtype)], cost(4 * rank * size, 2 * size))[0]
 
 
 def both_kernel(sent, received, change, *refs):
     before, rows, gram = refs[:-3], refs[-3:-1], refs[-1]
-    rank = rows[0].shape[0]
+    rank, width = rows[0].shape
     first = first_half()
     grams = []
     for block in range(2):
         mine, theirs = slice(block * rank, (block + 1) * rank), slice((1 - block) * rank, (2 - block) * rank)
-        one, two = sent[mine].astype(f32), received[theirs].astype(f32)
+        one, two = sent[mine, :width].astype(f32), received[theirs, :width].astype(f32)
         value = jnp.where(first, one, two) + exact_by_bf16(change[...], jnp.where(first, two, one).astype(bf16))
         rows[block][...] = value.astype(bf16)
         grams.append(exact_gram(value))
@@ -258,8 +274,8 @@
     gram[...] = total
 
 
-def both(sent, received, change, before):
-    rank, width = sent.shape[0] // 2, sent.shape[1]
+def both(sent, received, width, change, before):
+    rank = sent.shape[0] // 2
     return call(both_kernel, [sent, received, change, *before], [struct((rank, width), bf16)] * 2 + [struct((rank, rank), f32)],
                 cost(24 * rank * rank * width, 24 * rank * width))
 
@@ -267,7 +283,7 @@
 def loading_kernel(received, own, change, *refs):
     before, loading, gram = refs[:-2], refs[-2], refs[-1]
     first = first_half()
-    one, two = own[...], received[...].astype(f32)
+    one, two = own[...], received[:, :own.shape[1]].astype(f32)
     value = jnp.where(first, one, two) + exact_nn(change[...], jnp.where(first, two, one))
     loading[...] = value
     total = exact_gram(value)
@@ -362,31 +378,35 @@
         (even,) = scores(slots, work, bases, before[:1], *rest, odds=(0,))
         even = even + mate(odd, cells, 1)
         image = image_of(even, legs(even, cells), rank, normalised)
-        *images, factor = whiten(image, mate(image, cells, 1))
-        return images, change_of(factor, mate(factor, cells, GROUP))
+        return whiten(image, mate(image, cells, 1))
 
     basis = start_basis.T
     bases = {0: [basis], 1: [mate(basis, cells, GROUP)]}
     early = scores(slots, [(0, (0, 1))], bases)
-    images, change = image_from([(0, ()), (1, (0, 1))], bases, early, False)
+    *images, factor = image_from([(0, ()), (1, (0, 1))], bases, early, False)
     everything = [(0, (0, 1)), (1, (0, 1))]
     for _ in range(1, ITERS):
         total, before = [], ()
         arrived = []
         for start, stop in cuts(width, 45, 33):
-            sent = terms(slots, (start, width + start), stop - start, images, bf16)
+            sent = terms(slots, (start, width + start), stop - start, images, bf16, None if start else factor)
             arrived.append((start, stop, sent, mate(sent, cells, GROUP)))
         for start, stop, sent, received in arrived:
+            if not start:
+                change = change_of(factor, received)
             if before:
                 received, *before = lax.optimization_barrier((received, *before))
-            own, other, gram = both(sent, received, change, total)
+            own, other, gram = both(sent, received, stop - start, change, total)
             total, rows = [gram], {0: [own], 1: [other]}
             if stop < width:
                 before = scores(slots, everything, rows, before, offset=start)
-        images, change = image_from(everything, rows, before, True, gram, start)
+        *images, factor = image_from(everything, rows, before, True, gram, start)
     parts, total = [], []
     for start, stop in cuts(width, 60):
-        received = mate(terms(slots, (width + start,), stop - start, images, bf16), cells, GROUP)
+        sent = terms(slots, (width + start,), stop - start, images, bf16, None if start else factor)
+        received = mate(sent, cells, GROUP)
+        if not start:
+            change = change_of(factor, received)
         rows, gram = loading_and_gram(received, terms(slots, (start,), stop - start, images, f32), change, total)
         parts.append(rows)
         total = [gram]

time: 146 us -> 142 us (0.973)
  starting transfers between devices: 38 us -> 35.5 us
  waiting for transfers between devices: 85.1 us -> 83.3 us
    ppermute x31 -> x29, starting transfers between devices: 38 us -> 35.5 us  [mate(): lax.ppermute(value, 'cell', [(i, i ^ masks[i % 2]) for i in range(cells)])]
    ppermute x31 -> x29, waiting for transfers between devices: 85.1 us -> 83.3 us  [mate(): lax.ppermute(value, 'cell', [(i, i ^ masks[i % 2]) for i in range(cells)])]
  transfers between devices with their start and end apart: 31 -> 29, of which waited for: 21 -> 24; matrix products, arithmetic and copies ran while one was open for 0% -> 0% of each run, Pallas kernels for 5% -> 5%
where the time goes in v15:
time: 142 us; the launch traced here: 141 us
  waiting for transfers between devices  83.3 us (59%)
  starting transfers between devices  35.5 us (25%)
  Pallas kernels  22.2 us (16%)
    ppermute x29, waiting for transfers between devices, mate(): lax.ppermute(value, 'cell', [(i, i ^ masks[i % 2]) for i in range(cells)])  83.3 us
    ppermute x29, starting transfers between devices, mate(): lax.ppermute(value, 'cell', [(i, i ^ masks[i % 2]) for i in range(cells)])  35.5 us
    pallas_call x26, Pallas kernels, call(): pl.pallas_call(kernel, in_specs=[VMEM] * len(args), out_specs=[VMEM] * le...  20 us
  transfers between devices with their start and end apart: 29, of which 24 were waited for; matrix products, arithmetic and copies ran while one was open for 0% of the time, Pallas kernels for 5%

profile of v15, /device:TPU:0, one launch (start us, length us, event | category | flops | bytes accessed | tf_op | source)
XLA Modules:
  0.0 141.4 jit_solution(14783525072179164109)
XLA Ops:
  0.0 2.2 %shard_map.28 = (bf16[64,3840]{1,0:T(8,128)(2,1)S(1)}, bf16[64,3840]{1,0:T(8,128)(2,1)S(1)}, bf16[64,3840]{1,0:T(8,128)(2,1)S(1)}, bf16[64,3840]{1,0:T(8,128)(2,...) custom-call(bf16[64,30720]{1,0:T(8,128)(2,1)} %matrix.1), custom_call_target="tpu_custom_call" | custom-call | bytes 7864320 | tf_op jit(solution)/shard_map/pallas_call | solution.py:96
  2.8 3.6 %collective-permute-start.1 = (bf16[64,3840]{1,0:T(8,128)(2,1)S(1)}, bf16[64,3840]{1,0:T(8,128)(2,1)S(1)}, u32[]{:S(2)}, u32[]{:S(2)}) collective-permute-start(bf16[64,3840]{1,0:T(8,128)(2,1)S(1)} %get-tuple-element.46), channel_id=1, source_target_pairs={{0,6},{1,7},{2,4},{3,5},{4,2},{5,3},{6,0},{7,1},{8,14},{9,15},{10,... | collective-permute-start | bytes 1474568 | tf_op jit(solution)/shard_map/ppermute | solution.py:349
  6.4 2.6 %collective-permute-start.7 = (bf16[64,1920]{1,0:T(8,128)(2,1)S(1)}, bf16[64,1920]{1,0:T(8,128)(2,1)S(1)}, u32[]{:S(2)}, u32[]{:S(2)}) collective-permute-start(bf16[64,1920]{1,0:T(8,128)(2,1)S(1)} %bitcast.2), channel_id=1, source_target_pairs={{0,8},{1,9},{2,10},{3,11},{4,12},{5,13},{6,14},{7,15},{8,0},{9,1},... | collective-permute-start | bytes 737288 | tf_op jit(solution)/shard_map/ppermute | solution.py:349
  9.0 1.6 %collective-permute-start.4 = (bf16[64,3840]{1,0:T(8,128)(2,1)S(1)}, bf16[64,3840]{1,0:T(8,128)(2,1)S(1)}, u32[]{:S(2)}, u32[]{:S(2)}) collective-permute-start(bf16[64,3840]{1,0:T(8,128)(2,1)S(1)} %get-tuple-element.49), channel_id=1, source_target_pairs={{0,3},{1,4},{2,1},{3,6},{4,7},{5,0},{6,5},{7,2},{8,11},{9,12},{10,... | collective-permute-start | bytes 1474568 | tf_op jit(solution)/shard_map/ppermute | solution.py:349
  10.6 12.6 %collective-permute-done.7.refs_1_ = bf16[64,1920]{1,0:T(8,128)(2,1)S(1)} collective-permute-done((bf16[64,1920]{1,0:T(8,128)(2,1)S(1)}, bf16[64,1920]{1,0:T(8,128)(2,1)S(1)}, u32[]{:S(2)}, u32[]{:S(2)}) %collective-permute-start.7) | collective-permute-done | bytes 245792 | tf_op jit(solution)/shard_map/ppermute | solution.py:349
  23.2 2.3 %collective-permute-start.6 = (bf16[64,3840]{1,0:T(8,128)(2,1)S(1)}, bf16[64,3840]{1,0:T(8,128)(2,1)S(1)}, u32[]{:S(2)}, u32[]{:S(2)}) collective-permute-start(bf16[64,3840]{1,0:T(8,128)(2,1)S(1)} %get-tuple-element.51), channel_id=1, source_target_pairs={{0,5},{1,2},{2,7},{3,0},{4,1},{5,6},{6,3},{7,4},{8,13},{9,10},{10,... | collective-permute-start | bytes 1474568 | tf_op jit(solution)/shard_map/ppermute | solution.py:349
  26.0 1.2 collective-permute-start.5
  27.3 6.6 %collective-permute-done.2.refs_5_.refs_3_ = bf16[64,3840]{1,0:T(8,128)(2,1)S(1)} collective-permute-done((bf16[64,3840]{1,0:T(8,128)(2,1)S(1)}, bf16[64,3840]{1,0:T(8,128)(2,1)S(1)}, u32[]{:S(2)}, u32[]{:S(2)}) %collective-permute-start.2) | collective-permute-done | bytes 491552 | tf_op jit(solution)/shard_map/ppermute | solution.py:349
  34.5 9.8 %collective-permute-done.4.refs_2_.refs_5_.refs_7_.refs_4_ = bf16[64,3840]{1,0:T(8,128)(2,1)S(1)} collective-permute-done((bf16[64,3840]{1,0:T(8,128)(2,1)S(1)}, bf16[64,3840]{1,0:T(8,128)(2,1)S(1)}, u32[]{:S(2)}, u32[]{:S(2)}) %collective-permute-start.4) | collective-permute-done | bytes 491552 | tf_op jit(solution)/shard_map/ppermute | solution.py:349
  45.8 3.7 %collective-permute-done.3.refs_2_.refs_4_.refs_6_ = bf16[64,3840]{1,0:T(8,128)(2,1)S(1)} collective-permute-done((bf16[64,3840]{1,0:T(8,128)(2,1)S(1)}, bf16[64,3840]{1,0:T(8,128)(2,1)S(1)}, u32[]{:S(2)}, u32[]{:S(2)}) %collective-permute-start.3) | collective-permute-done | bytes 491552 | tf_op jit(solution)/shard_map/ppermute | solution.py:349
  49.5 5.8 %collective-permute-done.5.refs_3_.refs_6_.refs_8_.refs_5_ = bf16[64,3840]{1,0:T(8,128)(2,1)S(1)} collective-permute-done((bf16[64,3840]{1,0:T(8,128)(2,1)S(1)}, bf16[64,3840]{1,0:T(8,128)(2,1)S(1)}, u32[]{:S(2)}, u32[]{:S(2)}) %collective-permute-start.5) | collective-permute-done | bytes 491552 | tf_op jit(solution)/shard_map/ppermute | solution.py:349
  56.2 1.7 %collective-permute-start.11 = (f32[64,256]{1,0:T(8,128)S(1)}, f32[64,256]{1,0:T(8,128)S(1)}, u32[]{:S(2)}, u32[]{:S(2)}) collective-permute-start(f32[64,256]{1,0:T(8,128)S(1)} %add.24.refs_0_), channel_id=1, source_target_pairs={{0,4},{1,3},{2,6},{3,1},{4,0},{5,7},{6,2},{7,5},{8,12},{9,11},{10,... | collective-permute-start | bytes 196616 | tf_op jit(solution)/shard_map/ppermute | solution.py:349
  58.0 1.4 collective-permute-start.9
  59.3 1.9 %collective-permute-done.10.refs_2_ = f32[64,256]{1,0:T(8,128)S(1)} collective-permute-done((f32[64,256]{1,0:T(8,128)S(1)}, f32[64,256]{1,0:T(8,128)S(1)}, u32[]{:S(2)}, u32[]{:S(2)}) %collective-permute-start.10) | collective-permute-done | bytes 65568 | tf_op jit(solution)/shard_map/ppermute | solution.py:349
  61.3 1.9 %collective-permute-done.9.refs_1_ = f32[64,256]{1,0:T(8,128)S(1)} collective-permute-done((f32[64,256]{1,0:T(8,128)S(1)}, f32[64,256]{1,0:T(8,128)S(1)}, u32[]{:S(2)}, u32[]{:S(2)}) %collective-permute-start.9) | collective-permute-done | bytes 65568 | tf_op jit(solution)/shard_map/ppermute | solution.py:349
  64.5 2.4 %shard_map.33 = (bf16[128,256]{1,0:T(8,128)(2,1)S(1)}, bf16[128,256]{1,0:T(8,128)(2,1)S(1)}, f32[64,64]{1,0:T(8,128)S(1)}) custom-call(bf16[64,256]{1,0:T(8,128)(2,1)S(1)} %shard_map.32.even, bf16[64,256]{1,0:T(8,128)(2,1)S(1)} %collective-permute-done.12.odd), custom_call_target="tpu_custom_call" | custom-call | flops 12582912 | bytes 131072 | tf_op jit(solution)/shard_map/pallas_call | solution.py:108
  67.3 2.6 %collective-permute-start.15 = (bf16[128,1024]{1,0:T(8,128)(2,1)S(1)}, bf16[128,1024]{1,0:T(8,128)(2,1)S(1)}, u32[]{:S(2)}, u32[]{:S(2)}) collective-permute-start(bf16[128,1024]{1,0:T(8,128)(2,1)S(1)} %shard_map.36.sent), channel_id=1, source_target_pairs={{0,8},{1,9},{2,10},{3,11},{4,12},{5,13},{6,14},{7,15},{8,0},{9,1},... | collective-permute-start | bytes 786440 | tf_op jit(solution)/shard_map/ppermute | solution.py:349
  71.1 2.6 %collective-permute-start.13 = (bf16[128,384]{1,0:T(8,128)(2,1)S(1)}, bf16[128,384]{1,0:T(8,128)(2,1)S(1)}, u32[]{:S(2)}, u32[]{:S(2)}) collective-permute-start(bf16[128,384]{1,0:T(8,128)(2,1)S(1)} %shard_map.34.sent), channel_id=1, source_target_pairs={{0,8},{1,9},{2,10},{3,11},{4,12},{5,13},{6,14},{7,15},{8,0},{9,1},... | collective-permute-start | bytes 294920 | tf_op jit(solution)/shard_map/ppermute | solution.py:349
  73.7 14.5 %collective-permute-done.15.message.received = bf16[128,1024]{1,0:T(8,128)(2,1)S(1)} collective-permute-done((bf16[128,1024]{1,0:T(8,128)(2,1)S(1)}, bf16[128,1024]{1,0:T(8,128)(2,1)S(1)}, u32[]{:S(2)}, u32[]{:S(2)}) %collective-permute-start.15) | collective-permute-done | bytes 262176 | tf_op jit(solution)/shard_map/ppermute | solution.py:349
  90.0 1.7 %collective-permute-done.14.received = bf16[128,640]{1,0:T(8,128)(2,1)S(1)} collective-permute-done((bf16[128,640]{1,0:T(8,128)(2,1)S(1)}, bf16[128,640]{1,0:T(8,128)(2,1)S(1)}, u32[]{:S(2)}, u32[]{:S(2)}) %collective-permute-start.14) | collective-permute-done | bytes 163872 | tf_op jit(solution)/shard_map/ppermute | solution.py:349
  97.4 2.1 %collective-permute-start.19 = (f32[80,256]{1,0:T(8,128)S(1)}, f32[80,256]{1,0:T(8,128)S(1)}, u32[]{:S(2)}, u32[]{:S(2)}) collective-permute-start(f32[80,256]{1,0:T(8,128)S(1)} %add.25.refs_0_), channel_id=1, source_target_pairs={{0,4},{1,3},{2,6},{3,1},{4,0},{5,7},{6,2},{7,5},{8,12},{9,11},{10,... | collective-permute-start | bytes 245768 | tf_op jit(solution)/shard_map/ppermute | solution.py:349
  99.4 2.7 %collective-permute-done.17.refs_1_ = f32[80,256]{1,0:T(8,128)S(1)} collective-permute-done((f32[80,256]{1,0:T(8,128)S(1)}, f32[80,256]{1,0:T(8,128)S(1)}, u32[]{:S(2)}, u32[]{:S(2)}) %collective-permute-start.17) | collective-permute-done | bytes 81952 | tf_op jit(solution)/shard_map/ppermute | solution.py:349
  103.1 2.0 %shard_map.45.even = bf16[64,256]{1,0:T(8,128)(2,1)S(1)} custom-call(f32[80,256]{1,0:T(8,128)S(1)} %add.25.refs_0_, f32[80,256]{1,0:T(8,128)S(1)} %collective-permute-done.17.refs_1_, f32[80,256]{1,0:T(8,128)S(1)} %collective-permute-done.18.refs_2_, f32[80,256]{1,0:T(8,128)S(1)} %collective-permute-done.19.refs_3_), custom_call_target="tpu_custom_call" | custom-call | flops 15728640 | bytes 327680 | tf_op jit(solution)/shard_map/pallas_call | solution.py:108
  106.3 2.4 %shard_map.46 = (bf16[128,256]{1,0:T(8,128)(2,1)S(1)}, bf16[128,256]{1,0:T(8,128)(2,1)S(1)}, f32[64,64]{1,0:T(8,128)S(1)}) custom-call(bf16[64,256]{1,0:T(8,128)(2,1)S(1)} %shard_map.45.even, bf16[64,256]{1,0:T(8,128)(2,1)S(1)} %collective-permute-done.20.odd), custom_call_target="tpu_custom_call" | custom-call | flops 12582912 | bytes 131072 | tf_op jit(solution)/shard_map/pallas_call | solution.py:108
  109.0 2.2 %collective-permute-start.22 = (bf16[64,1344]{1,0:T(8,128)(2,1)S(1)}, bf16[64,1344]{1,0:T(8,128)(2,1)S(1)}, u32[]{:S(2)}, u32[]{:S(2)}) collective-permute-start(bf16[64,1344]{1,0:T(8,128)(2,1)S(1)} %shard_map.49), channel_id=1, source_target_pairs={{0,8},{1,9},{2,10},{3,11},{4,12},{5,13},{6,14},{7,15},{8,0},{9,1},... | collective-permute-start | bytes 516104 | tf_op jit(solution)/shard_map/ppermute | solution.py:349
  113.0 9.9 %collective-permute-done.22.message.received = bf16[64,1344]{1,0:T(8,128)(2,1)S(1)} collective-permute-done((bf16[64,1344]{1,0:T(8,128)(2,1)S(1)}, bf16[64,1344]{1,0:T(8,128)(2,1)S(1)}, u32[]{:S(2)}, u32[]{:S(2)}) %collective-permute-start.22) | collective-permute-done | bytes 172064 | tf_op jit(solution)/shard_map/ppermute | solution.py:349
  125.4 2.3 %collective-permute-start.24 = (f32[64,64]{1,0:T(8,128)S(1)}, f32[64,64]{1,0:T(8,128)S(1)}, u32[]{:S(2)}, u32[]{:S(2)}) collective-permute-start(f32[64,64]{1,0:T(8,128)S(1)} %get-tuple-element.80), channel_id=1, source_target_pairs={{0,8},{1,9},{2,10},{3,11},{4,12},{5,13},{6,14},{7,15},{8,0},{9,1},... | collective-permute-start | bytes 49160 | tf_op jit(solution)/shard_map/ppermute | solution.py:349
  128.2 2.2 %collective-permute-done.23 = f32[64,64]{1,0:T(8,128)S(1)} collective-permute-done((f32[64,64]{1,0:T(8,128)S(1)}, f32[64,64]{1,0:T(8,128)S(1)}, u32[]{:S(2)}, u32[]{:S(2)}) %collective-permute-start.23) | collective-permute-done | bytes 16416 | tf_op jit(solution)/shard_map/ppermute | solution.py:349
  131.0 2.8 %collective-permute-start.26 = (f32[64,64]{1,0:T(8,128)S(1)}, f32[64,64]{1,0:T(8,128)S(1)}, u32[]{:S(2)}, u32[]{:S(2)}) collective-permute-start(f32[64,64]{1,0:T(8,128)S(1)} %add_add_fusion.1), channel_id=1, source_target_pairs={{0,6},{1,7},{2,4},{3,5},{4,2},{5,3},{6,0},{7,1},{8,14},{9,15},{10,... | collective-permute-start | bytes 49160 | tf_op jit(solution)/shard_map/ppermute | solution.py:349
  134.5 1.3 collective-permute-done.26
  135.9 1.8 %collective-permute-done.27 = f32[64,64]{1,0:T(8,128)S(1)} collective-permute-done((f32[64,64]{1,0:T(8,128)S(1)}, f32[64,64]{1,0:T(8,128)S(1)}, u32[]{:S(2)}, u32[]{:S(2)}) %collective-permute-start.27) | collective-permute-done | bytes 16416 | tf_op jit(solution)/shard_map/ppermute | solution.py:349
  138.4 3.0 %shard_map.54 = f32[64,1920]{1,0:T(8,128)} custom-call(f32[64,64]{1,0:T(8,128)S(1)} %add_add_fusion.gram, f32[64,1152]{1,0:T(8,128)S(1)} %get-tuple-element.81.refs_0_, f32[64,768]{1,0:T(8,128)S(1)} %get-tuple-element.82.refs_1_), custom_call_target="tpu_custom_call" | custom-call | flops 94371840 | bytes 983040 | tf_op jit(solution)/shard_map/pallas_call | solution.py:108
  (59 shorter events, 23.9 us)
Async XLA Ops:
  0.0 6.4 %copy-start = (bf16[1920,64]{0,1:T(8,128)(2,1)S(1)}, bf16[1920,64]{0,1:T(8,128)(2,1)}, u32[]{:S(2)}) copy-start(bf16[1920,64]{0,1:T(8,128)(2,1)} %param.3) | copy-start | bytes 737284
  2.2 23.3 %collective-permute-start = (bf16[64,3840]{1,0:T(8,128)(2,1)S(1)}, bf16[64,3840]{1,0:T(8,128)(2,1)S(1)}, u32[]{:S(2)}, u32[]{:S(2)}) collective-permute-start(bf16[64,3840]{1,0:T(8,128)(2,1)S(1)} %get-tuple-element.45), channel_id=1, source_target_pairs={{0,1},{1,0},{2,3},{3,2},{4,5},{5,4},{6,7},{7,6},{8,9},{9,8},{10,11... | collective-permute-start | bytes 1474568 | tf_op jit(solution)/shard_map/ppermute | solution.py:349
  2.8 23.3 %collective-permute-start.1 = (bf16[64,3840]{1,0:T(8,128)(2,1)S(1)}, bf16[64,3840]{1,0:T(8,128)(2,1)S(1)}, u32[]{:S(2)}, u32[]{:S(2)}) collective-permute-start(bf16[64,3840]{1,0:T(8,128)(2,1)S(1)} %get-tuple-element.46), channel_id=1, source_target_pairs={{0,6},{1,7},{2,4},{3,5},{4,2},{5,3},{6,0},{7,1},{8,14},{9,15},{10,... | collective-permute-start | bytes 1474568 | tf_op jit(solution)/shard_map/ppermute | solution.py:349
  6.4 16.8 %collective-permute-start.7 = (bf16[64,1920]{1,0:T(8,128)(2,1)S(1)}, bf16[64,1920]{1,0:T(8,128)(2,1)S(1)}, u32[]{:S(2)}, u32[]{:S(2)}) collective-permute-start(bf16[64,1920]{1,0:T(8,128)(2,1)S(1)} %bitcast.2), channel_id=1, source_target_pairs={{0,8},{1,9},{2,10},{3,11},{4,12},{5,13},{6,14},{7,15},{8,0},{9,1},... | collective-permute-start | bytes 737288 | tf_op jit(solution)/shard_map/ppermute | solution.py:349
  9.0 24.9 %collective-permute-start.2 = (bf16[64,3840]{1,0:T(8,128)(2,1)S(1)}, bf16[64,3840]{1,0:T(8,128)(2,1)S(1)}, u32[]{:S(2)}, u32[]{:S(2)}) collective-permute-start(bf16[64,3840]{1,0:T(8,128)(2,1)S(1)} %get-tuple-element.47), channel_id=1, source_target_pairs={{0,7},{1,6},{2,5},{3,4},{4,3},{5,2},{6,1},{7,0},{8,15},{9,14},{10,... | collective-permute-start | bytes 1474568 | tf_op jit(solution)/shard_map/ppermute | solution.py:349
  9.0 35.3 %collective-permute-start.4 = (bf16[64,3840]{1,0:T(8,128)(2,1)S(1)}, bf16[64,3840]{1,0:T(8,128)(2,1)S(1)}, u32[]{:S(2)}, u32[]{:S(2)}) collective-permute-start(bf16[64,3840]{1,0:T(8,128)(2,1)S(1)} %get-tuple-element.49), channel_id=1, source_target_pairs={{0,3},{1,4},{2,1},{3,6},{4,7},{5,0},{6,5},{7,2},{8,11},{9,12},{10,... | collective-permute-start | bytes 1474568 | tf_op jit(solution)/shard_map/ppermute | solution.py:349
  23.2 21.5 %collective-permute-start.6 = (bf16[64,3840]{1,0:T(8,128)(2,1)S(1)}, bf16[64,3840]{1,0:T(8,128)(2,1)S(1)}, u32[]{:S(2)}, u32[]{:S(2)}) collective-permute-start(bf16[64,3840]{1,0:T(8,128)(2,1)S(1)} %get-tuple-element.51), channel_id=1, source_target_pairs={{0,5},{1,2},{2,7},{3,0},{4,1},{5,6},{6,3},{7,4},{8,13},{9,10},{10,... | collective-permute-start | bytes 1474568 | tf_op jit(solution)/shard_map/ppermute | solution.py:349
  25.5 23.9 %collective-permute-start.3 = (bf16[64,3840]{1,0:T(8,128)(2,1)S(1)}, bf16[64,3840]{1,0:T(8,128)(2,1)S(1)}, u32[]{:S(2)}, u32[]{:S(2)}) collective-permute-start(bf16[64,3840]{1,0:T(8,128)(2,1)S(1)} %get-tuple-element.48), channel_id=1, source_target_pairs={{0,2},{1,5},{2,0},{3,7},{4,6},{5,1},{6,4},{7,3},{8,10},{9,13},{10,... | collective-permute-start | bytes 1474568 | tf_op jit(solution)/shard_map/ppermute | solution.py:349
  26.0 29.2 %collective-permute-start.5 = (bf16[64,3840]{1,0:T(8,128)(2,1)S(1)}, bf16[64,3840]{1,0:T(8,128)(2,1)S(1)}, u32[]{:S(2)}, u32[]{:S(2)}) collective-permute-start(bf16[64,3840]{1,0:T(8,128)(2,1)S(1)} %get-tuple-element.50), channel_id=1, source_target_pairs={{0,4},{1,3},{2,6},{3,1},{4,0},{5,7},{6,2},{7,5},{8,12},{9,11},{10,... | collective-permute-start | bytes 1474568 | tf_op jit(solution)/shard_map/ppermute | solution.py:349
  45.1 10.6 %collective-permute-start.8 = (f32[64,256]{1,0:T(8,128)S(1)}, f32[64,256]{1,0:T(8,128)S(1)}, u32[]{:S(2)}, u32[]{:S(2)}) collective-permute-start(f32[64,256]{1,0:T(8,128)S(1)} %shard_map.31), channel_id=1, source_target_pairs={{0,1},{1,0},{2,3},{3,2},{4,5},{5,4},{6,7},{7,6},{8,9},{9,8},{10,11... | collective-permute-start | bytes 196616 | tf_op jit(solution)/shard_map/ppermute | solution.py:349
  55.8 5.5 %collective-permute-start.10 = (f32[64,256]{1,0:T(8,128)S(1)}, f32[64,256]{1,0:T(8,128)S(1)}, u32[]{:S(2)}, u32[]{:S(2)}) collective-permute-start(f32[64,256]{1,0:T(8,128)S(1)} %add.24.refs_0_), channel_id=1, source_target_pairs={{0,2},{1,5},{2,0},{3,7},{4,6},{5,1},{6,4},{7,3},{8,10},{9,13},{10,... | collective-permute-start | bytes 196616 | tf_op jit(solution)/shard_map/ppermute | solution.py:349
  56.2 5.0 %collective-permute-start.11 = (f32[64,256]{1,0:T(8,128)S(1)}, f32[64,256]{1,0:T(8,128)S(1)}, u32[]{:S(2)}, u32[]{:S(2)}) collective-permute-start(f32[64,256]{1,0:T(8,128)S(1)} %add.24.refs_0_), channel_id=1, source_target_pairs={{0,4},{1,3},{2,6},{3,1},{4,0},{5,7},{6,2},{7,5},{8,12},{9,11},{10,... | collective-permute-start | bytes 196616 | tf_op jit(solution)/shard_map/ppermute | solution.py:349
  58.0 5.2 %collective-permute-start.9 = (f32[64,256]{1,0:T(8,128)S(1)}, f32[64,256]{1,0:T(8,128)S(1)}, u32[]{:S(2)}, u32[]{:S(2)}) collective-permute-start(f32[64,256]{1,0:T(8,128)S(1)} %add.24.refs_0_), channel_id=1, source_target_pairs={{0,6},{1,7},{2,4},{3,5},{4,2},{5,3},{6,0},{7,1},{8,14},{9,15},{10,... | collective-permute-start | bytes 196616 | tf_op jit(solution)/shard_map/ppermute | solution.py:349
  63.2 1.3 collective-permute-start.12
  67.3 20.9 %collective-permute-start.15 = (bf16[128,1024]{1,0:T(8,128)(2,1)S(1)}, bf16[128,1024]{1,0:T(8,128)(2,1)S(1)}, u32[]{:S(2)}, u32[]{:S(2)}) collective-permute-start(bf16[128,1024]{1,0:T(8,128)(2,1)S(1)} %shard_map.36.sent), channel_id=1, source_target_pairs={{0,8},{1,9},{2,10},{3,11},{4,12},{5,13},{6,14},{7,15},{8,0},{9,1},... | collective-permute-start | bytes 786440 | tf_op jit(solution)/shard_map/ppermute | solution.py:349
  70.3 21.4 %collective-permute-start.14 = (bf16[128,640]{1,0:T(8,128)(2,1)S(1)}, bf16[128,640]{1,0:T(8,128)(2,1)S(1)}, u32[]{:S(2)}, u32[]{:S(2)}) collective-permute-start(bf16[128,640]{1,0:T(8,128)(2,1)S(1)} %shard_map.35.sent), channel_id=1, source_target_pairs={{0,8},{1,9},{2,10},{3,11},{4,12},{5,13},{6,14},{7,15},{8,0},{9,1},... | collective-permute-start | bytes 491528 | tf_op jit(solution)/shard_map/ppermute | solution.py:349
  71.1 22.5 %collective-permute-start.13 = (bf16[128,384]{1,0:T(8,128)(2,1)S(1)}, bf16[128,384]{1,0:T(8,128)(2,1)S(1)}, u32[]{:S(2)}, u32[]{:S(2)}) collective-permute-start(bf16[128,384]{1,0:T(8,128)(2,1)S(1)} %shard_map.34.sent), channel_id=1, source_target_pairs={{0,8},{1,9},{2,10},{3,11},{4,12},{5,13},{6,14},{7,15},{8,0},{9,1},... | collective-permute-start | bytes 294920 | tf_op jit(solution)/shard_map/ppermute | solution.py:349
  94.5 1.3 collective-permute-start.16
  95.9 6.3 %collective-permute-start.17 = (f32[80,256]{1,0:T(8,128)S(1)}, f32[80,256]{1,0:T(8,128)S(1)}, u32[]{:S(2)}, u32[]{:S(2)}) collective-permute-start(f32[80,256]{1,0:T(8,128)S(1)} %add.25.refs_0_), channel_id=1, source_target_pairs={{0,6},{1,7},{2,4},{3,5},{4,2},{5,3},{6,0},{7,1},{8,14},{9,15},{10,... | collective-permute-start | bytes 245768 | tf_op jit(solution)/shard_map/ppermute | solution.py:349
  96.6 6.3 %collective-permute-start.18 = (f32[80,256]{1,0:T(8,128)S(1)}, f32[80,256]{1,0:T(8,128)S(1)}, u32[]{:S(2)}, u32[]{:S(2)}) collective-permute-start(f32[80,256]{1,0:T(8,128)S(1)} %add.25.refs_0_), channel_id=1, source_target_pairs={{0,2},{1,5},{2,0},{3,7},{4,6},{5,1},{6,4},{7,3},{8,10},{9,13},{10,... | collective-permute-start | bytes 245768 | tf_op jit(solution)/shard_map/ppermute | solution.py:349
  97.4 5.7 %collective-permute-start.19 = (f32[80,256]{1,0:T(8,128)S(1)}, f32[80,256]{1,0:T(8,128)S(1)}, u32[]{:S(2)}, u32[]{:S(2)}) collective-permute-start(f32[80,256]{1,0:T(8,128)S(1)} %add.25.refs_0_), channel_id=1, source_target_pairs={{0,4},{1,3},{2,6},{3,1},{4,0},{5,7},{6,2},{7,5},{8,12},{9,11},{10,... | collective-permute-start | bytes 245768 | tf_op jit(solution)/shard_map/ppermute | solution.py:349
  105.0 1.2 collective-permute-start.20
  109.0 13.9 %collective-permute-start.22 = (bf16[64,1344]{1,0:T(8,128)(2,1)S(1)}, bf16[64,1344]{1,0:T(8,128)(2,1)S(1)}, u32[]{:S(2)}, u32[]{:S(2)}) collective-permute-start(bf16[64,1344]{1,0:T(8,128)(2,1)S(1)} %shard_map.49), channel_id=1, source_target_pairs={{0,8},{1,9},{2,10},{3,11},{4,12},{5,13},{6,14},{7,15},{8,0},{9,1},... | collective-permute-start | bytes 516104 | tf_op jit(solution)/shard_map/ppermute | solution.py:349
  111.5 13.2 %collective-permute-start.21 = (bf16[64,768]{1,0:T(8,128)(2,1)S(1)}, bf16[64,768]{1,0:T(8,128)(2,1)S(1)}, u32[]{:S(2)}, u32[]{:S(2)}) collective-permute-start(bf16[64,768]{1,0:T(8,128)(2,1)S(1)} %shard_map.47), channel_id=1, source_target_pairs={{0,8},{1,9},{2,10},{3,11},{4,12},{5,13},{6,14},{7,15},{8,0},{9,1},... | collective-permute-start | bytes 294920 | tf_op jit(solution)/shard_map/ppermute | solution.py:349
  125.4 5.0 %collective-permute-start.23 = (f32[64,64]{1,0:T(8,128)S(1)}, f32[64,64]{1,0:T(8,128)S(1)}, u32[]{:S(2)}, u32[]{:S(2)}) collective-permute-start(f32[64,64]{1,0:T(8,128)S(1)} %get-tuple-element.80), channel_id=1, source_target_pairs={{0,9},{1,8},{2,11},{3,10},{4,13},{5,12},{6,15},{7,14},{8,1},{9,0},... | collective-permute-start | bytes 49160 | tf_op jit(solution)/shard_map/ppermute | solution.py:349
  125.4 5.5 %collective-permute-start.24 = (f32[64,64]{1,0:T(8,128)S(1)}, f32[64,64]{1,0:T(8,128)S(1)}, u32[]{:S(2)}, u32[]{:S(2)}) collective-permute-start(f32[64,64]{1,0:T(8,128)S(1)} %get-tuple-element.80), channel_id=1, source_target_pairs={{0,8},{1,9},{2,10},{3,11},{4,12},{5,13},{6,14},{7,15},{8,0},{9,1},... | collective-permute-start | bytes 49160 | tf_op jit(solution)/shard_map/ppermute | solution.py:349
  127.7 3.2 %collective-permute-start.25 = (f32[64,64]{1,0:T(8,128)S(1)}, f32[64,64]{1,0:T(8,128)S(1)}, u32[]{:S(2)}, u32[]{:S(2)}) collective-permute-start(f32[64,64]{1,0:T(8,128)S(1)} %get-tuple-element.80), channel_id=1, source_target_pairs={{0,1},{1,0},{2,3},{3,2},{4,5},{5,4},{6,7},{7,6},{8,9},{9,8},{10,11... | collective-permute-start | bytes 49160 | tf_op jit(solution)/shard_map/ppermute | solution.py:349
  131.0 4.9 %collective-permute-start.26 = (f32[64,64]{1,0:T(8,128)S(1)}, f32[64,64]{1,0:T(8,128)S(1)}, u32[]{:S(2)}, u32[]{:S(2)}) collective-permute-start(f32[64,64]{1,0:T(8,128)S(1)} %add_add_fusion.1), channel_id=1, source_target_pairs={{0,6},{1,7},{2,4},{3,5},{4,2},{5,3},{6,0},{7,1},{8,14},{9,15},{10,... | collective-permute-start | bytes 49160 | tf_op jit(solution)/shard_map/ppermute | solution.py:349
  133.8 3.9 %collective-permute-start.27 = (f32[64,64]{1,0:T(8,128)S(1)}, f32[64,64]{1,0:T(8,128)S(1)}, u32[]{:S(2)}, u32[]{:S(2)}) collective-permute-start(f32[64,64]{1,0:T(8,128)S(1)} %add_add_fusion.1), channel_id=1, source_target_pairs={{0,2},{1,5},{2,0},{3,7},{4,6},{5,1},{6,4},{7,3},{8,10},{9,13},{10,... | collective-permute-start | bytes 49160 | tf_op jit(solution)/shard_map/ppermute | solution.py:349
  134.5 3.9 %collective-permute-start.28 = (f32[64,64]{1,0:T(8,128)S(1)}, f32[64,64]{1,0:T(8,128)S(1)}, u32[]{:S(2)}, u32[]{:S(2)}) collective-permute-start(f32[64,64]{1,0:T(8,128)S(1)} %add_add_fusion.1), channel_id=1, source_target_pairs={{0,4},{1,3},{2,6},{3,1},{4,0},{5,7},{6,2},{7,5},{8,12},{9,11},{10,... | collective-permute-start | bytes 49160 | tf_op jit(solution)/shard_map/ppermute | solution.py:349

commit v16 on v15

--- a/solution.py
+++ b/solution.py
@@ -193,7 +193,7 @@
         chips.append(nt(one, one) + nt(two, two))
     gram = (chips[0] + chips[1]) + (chips[2] + chips[3])
     diagonal = lax.broadcasted_iota(jnp.int32, gram.shape, 0) == lax.broadcasted_iota(jnp.int32, gram.shape, 1)
-    shift = jnp.sum(jnp.where(diagonal, gram, 0.0), keepdims=True) * (1e-5 / rank) + 1e-12
+    shift = jnp.sum(jnp.where(diagonal, gram, 0.0), keepdims=True) * (1e-3 / rank) + 1e-12
     upper, inverse = factors(gram + jnp.where(diagonal, shift, 0.0))
     for source, out in ((even, even_out), (odd, odd_out)):
         value = exact_by_bf16(inverse, source[...])

time: 142 us -> 142 us (level)
  no operation moved by 1% of the time
where the time goes in v16:
time: 142 us; the launch traced here: 141 us
  waiting for transfers between devices  83.3 us (59%)
  starting transfers between devices  35.5 us (25%)
  Pallas kernels  22.2 us (16%)
    ppermute x29, waiting for transfers between devices, mate(): lax.ppermute(value, 'cell', [(i, i ^ masks[i % 2]) for i in range(cells)])  83.3 us
    ppermute x29, starting transfers between devices, mate(): lax.ppermute(value, 'cell', [(i, i ^ masks[i % 2]) for i in range(cells)])  35.5 us
    pallas_call x26, Pallas kernels, call(): pl.pallas_call(kernel, in_specs=[VMEM] * len(args), out_specs=[VMEM] * le...  20 us
  transfers between devices with their start and end apart: 29, of which 24 were waited for; matrix products, arithmetic and copies ran while one was open for 0% of the time, Pallas kernels for 5%

profile of v16, /device:TPU:0, one launch (start us, length us, event | category | flops | bytes accessed | tf_op | source)
XLA Modules:
  0.0 141.4 jit_solution(2900809239614196283)
XLA Ops:
  0.0 2.2 %shard_map.28 = (bf16[64,3840]{1,0:T(8,128)(2,1)S(1)}, bf16[64,3840]{1,0:T(8,128)(2,1)S(1)}, bf16[64,3840]{1,0:T(8,128)(2,1)S(1)}, bf16[64,3840]{1,0:T(8,128)(2,...) custom-call(bf16[64,30720]{1,0:T(8,128)(2,1)} %matrix.1), custom_call_target="tpu_custom_call" | custom-call | bytes 7864320 | tf_op jit(solution)/shard_map/pallas_call | solution.py:96
  2.8 3.6 %collective-permute-start.1 = (bf16[64,3840]{1,0:T(8,128)(2,1)S(1)}, bf16[64,3840]{1,0:T(8,128)(2,1)S(1)}, u32[]{:S(2)}, u32[]{:S(2)}) collective-permute-start(bf16[64,3840]{1,0:T(8,128)(2,1)S(1)} %get-tuple-element.46), channel_id=1, source_target_pairs={{0,6},{1,7},{2,4},{3,5},{4,2},{5,3},{6,0},{7,1},{8,14},{9,15},{10,... | collective-permute-start | bytes 1474568 | tf_op jit(solution)/shard_map/ppermute | solution.py:349
  6.4 2.6 %collective-permute-start.7 = (bf16[64,1920]{1,0:T(8,128)(2,1)S(1)}, bf16[64,1920]{1,0:T(8,128)(2,1)S(1)}, u32[]{:S(2)}, u32[]{:S(2)}) collective-permute-start(bf16[64,1920]{1,0:T(8,128)(2,1)S(1)} %bitcast.2), channel_id=1, source_target_pairs={{0,8},{1,9},{2,10},{3,11},{4,12},{5,13},{6,14},{7,15},{8,0},{9,1},... | collective-permute-start | bytes 737288 | tf_op jit(solution)/shard_map/ppermute | solution.py:349
  9.0 1.6 %collective-permute-start.4 = (bf16[64,3840]{1,0:T(8,128)(2,1)S(1)}, bf16[64,3840]{1,0:T(8,128)(2,1)S(1)}, u32[]{:S(2)}, u32[]{:S(2)}) collective-permute-start(bf16[64,3840]{1,0:T(8,128)(2,1)S(1)} %get-tuple-element.49), channel_id=1, source_target_pairs={{0,3},{1,4},{2,1},{3,6},{4,7},{5,0},{6,5},{7,2},{8,11},{9,12},{10,... | collective-permute-start | bytes 1474568 | tf_op jit(solution)/shard_map/ppermute | solution.py:349
  10.6 12.6 %collective-permute-done.7.refs_1_ = bf16[64,1920]{1,0:T(8,128)(2,1)S(1)} collective-permute-done((bf16[64,1920]{1,0:T(8,128)(2,1)S(1)}, bf16[64,1920]{1,0:T(8,128)(2,1)S(1)}, u32[]{:S(2)}, u32[]{:S(2)}) %collective-permute-start.7) | collective-permute-done | bytes 245792 | tf_op jit(solution)/shard_map/ppermute | solution.py:349
  23.2 2.3 %collective-permute-start.6 = (bf16[64,3840]{1,0:T(8,128)(2,1)S(1)}, bf16[64,3840]{1,0:T(8,128)(2,1)S(1)}, u32[]{:S(2)}, u32[]{:S(2)}) collective-permute-start(bf16[64,3840]{1,0:T(8,128)(2,1)S(1)} %get-tuple-element.51), channel_id=1, source_target_pairs={{0,5},{1,2},{2,7},{3,0},{4,1},{5,6},{6,3},{7,4},{8,13},{9,10},{10,... | collective-permute-start | bytes 1474568 | tf_op jit(solution)/shard_map/ppermute | solution.py:349
  26.0 1.2 collective-permute-start.5
  27.3 6.6 %collective-permute-done.2.refs_5_.refs_3_ = bf16[64,3840]{1,0:T(8,128)(2,1)S(1)} collective-permute-done((bf16[64,3840]{1,0:T(8,128)(2,1)S(1)}, bf16[64,3840]{1,0:T(8,128)(2,1)S(1)}, u32[]{:S(2)}, u32[]{:S(2)}) %collective-permute-start.2) | collective-permute-done | bytes 491552 | tf_op jit(solution)/shard_map/ppermute | solution.py:349
  34.5 9.8 %collective-permute-done.4.refs_2_.refs_5_.refs_7_.refs_4_ = bf16[64,3840]{1,0:T(8,128)(2,1)S(1)} collective-permute-done((bf16[64,3840]{1,0:T(8,128)(2,1)S(1)}, bf16[64,3840]{1,0:T(8,128)(2,1)S(1)}, u32[]{:S(2)}, u32[]{:S(2)}) %collective-permute-start.4) | collective-permute-done | bytes 491552 | tf_op jit(solution)/shard_map/ppermute | solution.py:349
  45.8 3.7 %collective-permute-done.3.refs_2_.refs_4_.refs_6_ = bf16[64,3840]{1,0:T(8,128)(2,1)S(1)} collective-permute-done((bf16[64,3840]{1,0:T(8,128)(2,1)S(1)}, bf16[64,3840]{1,0:T(8,128)(2,1)S(1)}, u32[]{:S(2)}, u32[]{:S(2)}) %collective-permute-start.3) | collective-permute-done | bytes 491552 | tf_op jit(solution)/shard_map/ppermute | solution.py:349
  49.5 5.8 %collective-permute-done.5.refs_3_.refs_6_.refs_8_.refs_5_ = bf16[64,3840]{1,0:T(8,128)(2,1)S(1)} collective-permute-done((bf16[64,3840]{1,0:T(8,128)(2,1)S(1)}, bf16[64,3840]{1,0:T(8,128)(2,1)S(1)}, u32[]{:S(2)}, u32[]{:S(2)}) %collective-permute-start.5) | collective-permute-done | bytes 491552 | tf_op jit(solution)/shard_map/ppermute | solution.py:349
  56.2 1.7 %collective-permute-start.11 = (f32[64,256]{1,0:T(8,128)S(1)}, f32[64,256]{1,0:T(8,128)S(1)}, u32[]{:S(2)}, u32[]{:S(2)}) collective-permute-start(f32[64,256]{1,0:T(8,128)S(1)} %add.24.refs_0_), channel_id=1, source_target_pairs={{0,4},{1,3},{2,6},{3,1},{4,0},{5,7},{6,2},{7,5},{8,12},{9,11},{10,... | collective-permute-start | bytes 196616 | tf_op jit(solution)/shard_map/ppermute | solution.py:349
  58.0 1.4 collective-permute-start.9
  59.3 1.9 %collective-permute-done.10.refs_2_ = f32[64,256]{1,0:T(8,128)S(1)} collective-permute-done((f32[64,256]{1,0:T(8,128)S(1)}, f32[64,256]{1,0:T(8,128)S(1)}, u32[]{:S(2)}, u32[]{:S(2)}) %collective-permute-start.10) | collective-permute-done | bytes 65568 | tf_op jit(solution)/shard_map/ppermute | solution.py:349
  61.3 1.9 %collective-permute-done.9.refs_1_ = f32[64,256]{1,0:T(8,128)S(1)} collective-permute-done((f32[64,256]{1,0:T(8,128)S(1)}, f32[64,256]{1,0:T(8,128)S(1)}, u32[]{:S(2)}, u32[]{:S(2)}) %collective-permute-start.9) | collective-permute-done | bytes 65568 | tf_op jit(solution)/shard_map/ppermute | solution.py:349
  64.5 2.4 %shard_map.33 = (bf16[128,256]{1,0:T(8,128)(2,1)S(1)}, bf16[128,256]{1,0:T(8,128)(2,1)S(1)}, f32[64,64]{1,0:T(8,128)S(1)}) custom-call(bf16[64,256]{1,0:T(8,128)(2,1)S(1)} %shard_map.32.even, bf16[64,256]{1,0:T(8,128)(2,1)S(1)} %collective-permute-done.12.odd), custom_call_target="tpu_custom_call" | custom-call | flops 12582912 | bytes 131072 | tf_op jit(solution)/shard_map/pallas_call | solution.py:108
  67.3 2.6 %collective-permute-start.15 = (bf16[128,1024]{1,0:T(8,128)(2,1)S(1)}, bf16[128,1024]{1,0:T(8,128)(2,1)S(1)}, u32[]{:S(2)}, u32[]{:S(2)}) collective-permute-start(bf16[128,1024]{1,0:T(8,128)(2,1)S(1)} %shard_map.36.sent), channel_id=1, source_target_pairs={{0,8},{1,9},{2,10},{3,11},{4,12},{5,13},{6,14},{7,15},{8,0},{9,1},... | collective-permute-start | bytes 786440 | tf_op jit(solution)/shard_map/ppermute | solution.py:349
  71.1 2.6 %collective-permute-start.13 = (bf16[128,384]{1,0:T(8,128)(2,1)S(1)}, bf16[128,384]{1,0:T(8,128)(2,1)S(1)}, u32[]{:S(2)}, u32[]{:S(2)}) collective-permute-start(bf16[128,384]{1,0:T(8,128)(2,1)S(1)} %shard_map.34.sent), channel_id=1, source_target_pairs={{0,8},{1,9},{2,10},{3,11},{4,12},{5,13},{6,14},{7,15},{8,0},{9,1},... | collective-permute-start | bytes 294920 | tf_op jit(solution)/shard_map/ppermute | solution.py:349
  73.7 14.5 %collective-permute-done.15.message.received = bf16[128,1024]{1,0:T(8,128)(2,1)S(1)} collective-permute-done((bf16[128,1024]{1,0:T(8,128)(2,1)S(1)}, bf16[128,1024]{1,0:T(8,128)(2,1)S(1)}, u32[]{:S(2)}, u32[]{:S(2)}) %collective-permute-start.15) | collective-permute-done | bytes 262176 | tf_op jit(solution)/shard_map/ppermute | solution.py:349
  90.0 1.7 %collective-permute-done.14.received = bf16[128,640]{1,0:T(8,128)(2,1)S(1)} collective-permute-done((bf16[128,640]{1,0:T(8,128)(2,1)S(1)}, bf16[128,640]{1,0:T(8,128)(2,1)S(1)}, u32[]{:S(2)}, u32[]{:S(2)}) %collective-permute-start.14) | collective-permute-done | bytes 163872 | tf_op jit(solution)/shard_map/ppermute | solution.py:349
  97.4 2.1 %collective-permute-start.19 = (f32[80,256]{1,0:T(8,128)S(1)}, f32[80,256]{1,0:T(8,128)S(1)}, u32[]{:S(2)}, u32[]{:S(2)}) collective-permute-start(f32[80,256]{1,0:T(8,128)S(1)} %add.25.refs_0_), channel_id=1, source_target_pairs={{0,4},{1,3},{2,6},{3,1},{4,0},{5,7},{6,2},{7,5},{8,12},{9,11},{10,... | collective-permute-start | bytes 245768 | tf_op jit(solution)/shard_map/ppermute | solution.py:349
  99.4 2.7 %collective-permute-done.17.refs_1_ = f32[80,256]{1,0:T(8,128)S(1)} collective-permute-done((f32[80,256]{1,0:T(8,128)S(1)}, f32[80,256]{1,0:T(8,128)S(1)}, u32[]{:S(2)}, u32[]{:S(2)}) %collective-permute-start.17) | collective-permute-done | bytes 81952 | tf_op jit(solution)/shard_map/ppermute | solution.py:349
  103.1 2.0 %shard_map.45.even = bf16[64,256]{1,0:T(8,128)(2,1)S(1)} custom-call(f32[80,256]{1,0:T(8,128)S(1)} %add.25.refs_0_, f32[80,256]{1,0:T(8,128)S(1)} %collective-permute-done.17.refs_1_, f32[80,256]{1,0:T(8,128)S(1)} %collective-permute-done.18.refs_2_, f32[80,256]{1,0:T(8,128)S(1)} %collective-permute-done.19.refs_3_), custom_call_target="tpu_custom_call" | custom-call | flops 15728640 | bytes 327680 | tf_op jit(solution)/shard_map/pallas_call | solution.py:108
  106.3 2.4 %shard_map.46 = (bf16[128,256]{1,0:T(8,128)(2,1)S(1)}, bf16[128,256]{1,0:T(8,128)(2,1)S(1)}, f32[64,64]{1,0:T(8,128)S(1)}) custom-call(bf16[64,256]{1,0:T(8,128)(2,1)S(1)} %shard_map.45.even, bf16[64,256]{1,0:T(8,128)(2,1)S(1)} %collective-permute-done.20.odd), custom_call_target="tpu_custom_call" | custom-call | flops 12582912 | bytes 131072 | tf_op jit(solution)/shard_map/pallas_call | solution.py:108
  109.0 2.2 %collective-permute-start.22 = (bf16[64,1344]{1,0:T(8,128)(2,1)S(1)}, bf16[64,1344]{1,0:T(8,128)(2,1)S(1)}, u32[]{:S(2)}, u32[]{:S(2)}) collective-permute-start(bf16[64,1344]{1,0:T(8,128)(2,1)S(1)} %shard_map.49), channel_id=1, source_target_pairs={{0,8},{1,9},{2,10},{3,11},{4,12},{5,13},{6,14},{7,15},{8,0},{9,1},... | collective-permute-start | bytes 516104 | tf_op jit(solution)/shard_map/ppermute | solution.py:349
  113.0 9.9 %collective-permute-done.22.message.received = bf16[64,1344]{1,0:T(8,128)(2,1)S(1)} collective-permute-done((bf16[64,1344]{1,0:T(8,128)(2,1)S(1)}, bf16[64,1344]{1,0:T(8,128)(2,1)S(1)}, u32[]{:S(2)}, u32[]{:S(2)}) %collective-permute-start.22) | collective-permute-done | bytes 172064 | tf_op jit(solution)/shard_map/ppermute | solution.py:349
  125.4 2.3 %collective-permute-start.24 = (f32[64,64]{1,0:T(8,128)S(1)}, f32[64,64]{1,0:T(8,128)S(1)}, u32[]{:S(2)}, u32[]{:S(2)}) collective-permute-start(f32[64,64]{1,0:T(8,128)S(1)} %get-tuple-element.80), channel_id=1, source_target_pairs={{0,8},{1,9},{2,10},{3,11},{4,12},{5,13},{6,14},{7,15},{8,0},{9,1},... | collective-permute-start | bytes 49160 | tf_op jit(solution)/shard_map/ppermute | solution.py:349
  128.2 2.2 %collective-permute-done.23 = f32[64,64]{1,0:T(8,128)S(1)} collective-permute-done((f32[64,64]{1,0:T(8,128)S(1)}, f32[64,64]{1,0:T(8,128)S(1)}, u32[]{:S(2)}, u32[]{:S(2)}) %collective-permute-start.23) | collective-permute-done | bytes 16416 | tf_op jit(solution)/shard_map/ppermute | solution.py:349
  131.0 2.8 %collective-permute-start.26 = (f32[64,64]{1,0:T(8,128)S(1)}, f32[64,64]{1,0:T(8,128)S(1)}, u32[]{:S(2)}, u32[]{:S(2)}) collective-permute-start(f32[64,64]{1,0:T(8,128)S(1)} %add_add_fusion.1), channel_id=1, source_target_pairs={{0,6},{1,7},{2,4},{3,5},{4,2},{5,3},{6,0},{7,1},{8,14},{9,15},{10,... | collective-permute-start | bytes 49160 | tf_op jit(solution)/shard_map/ppermute | solution.py:349
  134.5 1.3 collective-permute-done.26
  135.9 1.8 %collective-permute-done.27 = f32[64,64]{1,0:T(8,128)S(1)} collective-permute-done((f32[64,64]{1,0:T(8,128)S(1)}, f32[64,64]{1,0:T(8,128)S(1)}, u32[]{:S(2)}, u32[]{:S(2)}) %collective-permute-start.27) | collective-permute-done | bytes 16416 | tf_op jit(solution)/shard_map/ppermute | solution.py:349
  138.4 3.0 %shard_map.54 = f32[64,1920]{1,0:T(8,128)} custom-call(f32[64,64]{1,0:T(8,128)S(1)} %add_add_fusion.gram, f32[64,1152]{1,0:T(8,128)S(1)} %get-tuple-element.81.refs_0_, f32[64,768]{1,0:T(8,128)S(1)} %get-tuple-element.82.refs_1_), custom_call_target="tpu_custom_call" | custom-call | flops 94371840 | bytes 983040 | tf_op jit(solution)/shard_map/pallas_call | solution.py:108
  (59 shorter events, 23.9 us)
Async XLA Ops:
  0.0 6.4 %copy-start = (bf16[1920,64]{0,1:T(8,128)(2,1)S(1)}, bf16[1920,64]{0,1:T(8,128)(2,1)}, u32[]{:S(2)}) copy-start(bf16[1920,64]{0,1:T(8,128)(2,1)} %param.3) | copy-start | bytes 737284
  2.2 23.3 %collective-permute-start = (bf16[64,3840]{1,0:T(8,128)(2,1)S(1)}, bf16[64,3840]{1,0:T(8,128)(2,1)S(1)}, u32[]{:S(2)}, u32[]{:S(2)}) collective-permute-start(bf16[64,3840]{1,0:T(8,128)(2,1)S(1)} %get-tuple-element.45), channel_id=1, source_target_pairs={{0,1},{1,0},{2,3},{3,2},{4,5},{5,4},{6,7},{7,6},{8,9},{9,8},{10,11... | collective-permute-start | bytes 1474568 | tf_op jit(solution)/shard_map/ppermute | solution.py:349
  2.8 23.3 %collective-permute-start.1 = (bf16[64,3840]{1,0:T(8,128)(2,1)S(1)}, bf16[64,3840]{1,0:T(8,128)(2,1)S(1)}, u32[]{:S(2)}, u32[]{:S(2)}) collective-permute-start(bf16[64,3840]{1,0:T(8,128)(2,1)S(1)} %get-tuple-element.46), channel_id=1, source_target_pairs={{0,6},{1,7},{2,4},{3,5},{4,2},{5,3},{6,0},{7,1},{8,14},{9,15},{10,... | collective-permute-start | bytes 1474568 | tf_op jit(solution)/shard_map/ppermute | solution.py:349
  6.4 16.8 %collective-permute-start.7 = (bf16[64,1920]{1,0:T(8,128)(2,1)S(1)}, bf16[64,1920]{1,0:T(8,128)(2,1)S(1)}, u32[]{:S(2)}, u32[]{:S(2)}) collective-permute-start(bf16[64,1920]{1,0:T(8,128)(2,1)S(1)} %bitcast.2), channel_id=1, source_target_pairs={{0,8},{1,9},{2,10},{3,11},{4,12},{5,13},{6,14},{7,15},{8,0},{9,1},... | collective-permute-start | bytes 737288 | tf_op jit(solution)/shard_map/ppermute | solution.py:349
  9.0 24.9 %collective-permute-start.2 = (bf16[64,3840]{1,0:T(8,128)(2,1)S(1)}, bf16[64,3840]{1,0:T(8,128)(2,1)S(1)}, u32[]{:S(2)}, u32[]{:S(2)}) collective-permute-start(bf16[64,3840]{1,0:T(8,128)(2,1)S(1)} %get-tuple-element.47), channel_id=1, source_target_pairs={{0,7},{1,6},{2,5},{3,4},{4,3},{5,2},{6,1},{7,0},{8,15},{9,14},{10,... | collective-permute-start | bytes 1474568 | tf_op jit(solution)/shard_map/ppermute | solution.py:349
  9.0 35.3 %collective-permute-start.4 = (bf16[64,3840]{1,0:T(8,128)(2,1)S(1)}, bf16[64,3840]{1,0:T(8,128)(2,1)S(1)}, u32[]{:S(2)}, u32[]{:S(2)}) collective-permute-start(bf16[64,3840]{1,0:T(8,128)(2,1)S(1)} %get-tuple-element.49), channel_id=1, source_target_pairs={{0,3},{1,4},{2,1},{3,6},{4,7},{5,0},{6,5},{7,2},{8,11},{9,12},{10,... | collective-permute-start | bytes 1474568 | tf_op jit(solution)/shard_map/ppermute | solution.py:349
  23.2 21.5 %collective-permute-start.6 = (bf16[64,3840]{1,0:T(8,128)(2,1)S(1)}, bf16[64,3840]{1,0:T(8,128)(2,1)S(1)}, u32[]{:S(2)}, u32[]{:S(2)}) collective-permute-start(bf16[64,3840]{1,0:T(8,128)(2,1)S(1)} %get-tuple-element.51), channel_id=1, source_target_pairs={{0,5},{1,2},{2,7},{3,0},{4,1},{5,6},{6,3},{7,4},{8,13},{9,10},{10,... | collective-permute-start | bytes 1474568 | tf_op jit(solution)/shard_map/ppermute | solution.py:349
  25.5 23.9 %collective-permute-start.3 = (bf16[64,3840]{1,0:T(8,128)(2,1)S(1)}, bf16[64,3840]{1,0:T(8,128)(2,1)S(1)}, u32[]{:S(2)}, u32[]{:S(2)}) collective-permute-start(bf16[64,3840]{1,0:T(8,128)(2,1)S(1)} %get-tuple-element.48), channel_id=1, source_target_pairs={{0,2},{1,5},{2,0},{3,7},{4,6},{5,1},{6,4},{7,3},{8,10},{9,13},{10,... | collective-permute-start | bytes 1474568 | tf_op jit(solution)/shard_map/ppermute | solution.py:349
  26.0 29.2 %collective-permute-start.5 = (bf16[64,3840]{1,0:T(8,128)(2,1)S(1)}, bf16[64,3840]{1,0:T(8,128)(2,1)S(1)}, u32[]{:S(2)}, u32[]{:S(2)}) collective-permute-start(bf16[64,3840]{1,0:T(8,128)(2,1)S(1)} %get-tuple-element.50), channel_id=1, source_target_pairs={{0,4},{1,3},{2,6},{3,1},{4,0},{5,7},{6,2},{7,5},{8,12},{9,11},{10,... | collective-permute-start | bytes 1474568 | tf_op jit(solution)/shard_map/ppermute | solution.py:349
  45.1 10.6 %collective-permute-start.8 = (f32[64,256]{1,0:T(8,128)S(1)}, f32[64,256]{1,0:T(8,128)S(1)}, u32[]{:S(2)}, u32[]{:S(2)}) collective-permute-start(f32[64,256]{1,0:T(8,128)S(1)} %shard_map.31), channel_id=1, source_target_pairs={{0,1},{1,0},{2,3},{3,2},{4,5},{5,4},{6,7},{7,6},{8,9},{9,8},{10,11... | collective-permute-start | bytes 196616 | tf_op jit(solution)/shard_map/ppermute | solution.py:349
  55.8 5.5 %collective-permute-start.10 = (f32[64,256]{1,0:T(8,128)S(1)}, f32[64,256]{1,0:T(8,128)S(1)}, u32[]{:S(2)}, u32[]{:S(2)}) collective-permute-start(f32[64,256]{1,0:T(8,128)S(1)} %add.24.refs_0_), channel_id=1, source_target_pairs={{0,2},{1,5},{2,0},{3,7},{4,6},{5,1},{6,4},{7,3},{8,10},{9,13},{10,... | collective-permute-start | bytes 196616 | tf_op jit(solution)/shard_map/ppermute | solution.py:349
  56.2 5.0 %collective-permute-start.11 = (f32[64,256]{1,0:T(8,128)S(1)}, f32[64,256]{1,0:T(8,128)S(1)}, u32[]{:S(2)}, u32[]{:S(2)}) collective-permute-start(f32[64,256]{1,0:T(8,128)S(1)} %add.24.refs_0_), channel_id=1, source_target_pairs={{0,4},{1,3},{2,6},{3,1},{4,0},{5,7},{6,2},{7,5},{8,12},{9,11},{10,... | collective-permute-start | bytes 196616 | tf_op jit(solution)/shard_map/ppermute | solution.py:349
  58.0 5.2 %collective-permute-start.9 = (f32[64,256]{1,0:T(8,128)S(1)}, f32[64,256]{1,0:T(8,128)S(1)}, u32[]{:S(2)}, u32[]{:S(2)}) collective-permute-start(f32[64,256]{1,0:T(8,128)S(1)} %add.24.refs_0_), channel_id=1, source_target_pairs={{0,6},{1,7},{2,4},{3,5},{4,2},{5,3},{6,0},{7,1},{8,14},{9,15},{10,... | collective-permute-start | bytes 196616 | tf_op jit(solution)/shard_map/ppermute | solution.py:349
  63.2 1.3 collective-permute-start.12
  67.3 20.9 %collective-permute-start.15 = (bf16[128,1024]{1,0:T(8,128)(2,1)S(1)}, bf16[128,1024]{1,0:T(8,128)(2,1)S(1)}, u32[]{:S(2)}, u32[]{:S(2)}) collective-permute-start(bf16[128,1024]{1,0:T(8,128)(2,1)S(1)} %shard_map.36.sent), channel_id=1, source_target_pairs={{0,8},{1,9},{2,10},{3,11},{4,12},{5,13},{6,14},{7,15},{8,0},{9,1},... | collective-permute-start | bytes 786440 | tf_op jit(solution)/shard_map/ppermute | solution.py:349
  70.3 21.4 %collective-permute-start.14 = (bf16[128,640]{1,0:T(8,128)(2,1)S(1)}, bf16[128,640]{1,0:T(8,128)(2,1)S(1)}, u32[]{:S(2)}, u32[]{:S(2)}) collective-permute-start(bf16[128,640]{1,0:T(8,128)(2,1)S(1)} %shard_map.35.sent), channel_id=1, source_target_pairs={{0,8},{1,9},{2,10},{3,11},{4,12},{5,13},{6,14},{7,15},{8,0},{9,1},... | collective-permute-start | bytes 491528 | tf_op jit(solution)/shard_map/ppermute | solution.py:349
  71.1 22.5 %collective-permute-start.13 = (bf16[128,384]{1,0:T(8,128)(2,1)S(1)}, bf16[128,384]{1,0:T(8,128)(2,1)S(1)}, u32[]{:S(2)}, u32[]{:S(2)}) collective-permute-start(bf16[128,384]{1,0:T(8,128)(2,1)S(1)} %shard_map.34.sent), channel_id=1, source_target_pairs={{0,8},{1,9},{2,10},{3,11},{4,12},{5,13},{6,14},{7,15},{8,0},{9,1},... | collective-permute-start | bytes 294920 | tf_op jit(solution)/shard_map/ppermute | solution.py:349
  94.5 1.3 collective-permute-start.16
  95.9 6.3 %collective-permute-start.17 = (f32[80,256]{1,0:T(8,128)S(1)}, f32[80,256]{1,0:T(8,128)S(1)}, u32[]{:S(2)}, u32[]{:S(2)}) collective-permute-start(f32[80,256]{1,0:T(8,128)S(1)} %add.25.refs_0_), channel_id=1, source_target_pairs={{0,6},{1,7},{2,4},{3,5},{4,2},{5,3},{6,0},{7,1},{8,14},{9,15},{10,... | collective-permute-start | bytes 245768 | tf_op jit(solution)/shard_map/ppermute | solution.py:349
  96.6 6.3 %collective-permute-start.18 = (f32[80,256]{1,0:T(8,128)S(1)}, f32[80,256]{1,0:T(8,128)S(1)}, u32[]{:S(2)}, u32[]{:S(2)}) collective-permute-start(f32[80,256]{1,0:T(8,128)S(1)} %add.25.refs_0_), channel_id=1, source_target_pairs={{0,2},{1,5},{2,0},{3,7},{4,6},{5,1},{6,4},{7,3},{8,10},{9,13},{10,... | collective-permute-start | bytes 245768 | tf_op jit(solution)/shard_map/ppermute | solution.py:349
  97.4 5.7 %collective-permute-start.19 = (f32[80,256]{1,0:T(8,128)S(1)}, f32[80,256]{1,0:T(8,128)S(1)}, u32[]{:S(2)}, u32[]{:S(2)}) collective-permute-start(f32[80,256]{1,0:T(8,128)S(1)} %add.25.refs_0_), channel_id=1, source_target_pairs={{0,4},{1,3},{2,6},{3,1},{4,0},{5,7},{6,2},{7,5},{8,12},{9,11},{10,... | collective-permute-start | bytes 245768 | tf_op jit(solution)/shard_map/ppermute | solution.py:349
  105.0 1.2 collective-permute-start.20
  109.0 13.9 %collective-permute-start.22 = (bf16[64,1344]{1,0:T(8,128)(2,1)S(1)}, bf16[64,1344]{1,0:T(8,128)(2,1)S(1)}, u32[]{:S(2)}, u32[]{:S(2)}) collective-permute-start(bf16[64,1344]{1,0:T(8,128)(2,1)S(1)} %shard_map.49), channel_id=1, source_target_pairs={{0,8},{1,9},{2,10},{3,11},{4,12},{5,13},{6,14},{7,15},{8,0},{9,1},... | collective-permute-start | bytes 516104 | tf_op jit(solution)/shard_map/ppermute | solution.py:349
  111.5 13.2 %collective-permute-start.21 = (bf16[64,768]{1,0:T(8,128)(2,1)S(1)}, bf16[64,768]{1,0:T(8,128)(2,1)S(1)}, u32[]{:S(2)}, u32[]{:S(2)}) collective-permute-start(bf16[64,768]{1,0:T(8,128)(2,1)S(1)} %shard_map.47), channel_id=1, source_target_pairs={{0,8},{1,9},{2,10},{3,11},{4,12},{5,13},{6,14},{7,15},{8,0},{9,1},... | collective-permute-start | bytes 294920 | tf_op jit(solution)/shard_map/ppermute | solution.py:349
  125.4 5.0 %collective-permute-start.23 = (f32[64,64]{1,0:T(8,128)S(1)}, f32[64,64]{1,0:T(8,128)S(1)}, u32[]{:S(2)}, u32[]{:S(2)}) collective-permute-start(f32[64,64]{1,0:T(8,128)S(1)} %get-tuple-element.80), channel_id=1, source_target_pairs={{0,9},{1,8},{2,11},{3,10},{4,13},{5,12},{6,15},{7,14},{8,1},{9,0},... | collective-permute-start | bytes 49160 | tf_op jit(solution)/shard_map/ppermute | solution.py:349
  125.4 5.5 %collective-permute-start.24 = (f32[64,64]{1,0:T(8,128)S(1)}, f32[64,64]{1,0:T(8,128)S(1)}, u32[]{:S(2)}, u32[]{:S(2)}) collective-permute-start(f32[64,64]{1,0:T(8,128)S(1)} %get-tuple-element.80), channel_id=1, source_target_pairs={{0,8},{1,9},{2,10},{3,11},{4,12},{5,13},{6,14},{7,15},{8,0},{9,1},... | collective-permute-start | bytes 49160 | tf_op jit(solution)/shard_map/ppermute | solution.py:349
  127.7 3.2 %collective-permute-start.25 = (f32[64,64]{1,0:T(8,128)S(1)}, f32[64,64]{1,0:T(8,128)S(1)}, u32[]{:S(2)}, u32[]{:S(2)}) collective-permute-start(f32[64,64]{1,0:T(8,128)S(1)} %get-tuple-element.80), channel_id=1, source_target_pairs={{0,1},{1,0},{2,3},{3,2},{4,5},{5,4},{6,7},{7,6},{8,9},{9,8},{10,11... | collective-permute-start | bytes 49160 | tf_op jit(solution)/shard_map/ppermute | solution.py:349
  131.0 4.9 %collective-permute-start.26 = (f32[64,64]{1,0:T(8,128)S(1)}, f32[64,64]{1,0:T(8,128)S(1)}, u32[]{:S(2)}, u32[]{:S(2)}) collective-permute-start(f32[64,64]{1,0:T(8,128)S(1)} %add_add_fusion.1), channel_id=1, source_target_pairs={{0,6},{1,7},{2,4},{3,5},{4,2},{5,3},{6,0},{7,1},{8,14},{9,15},{10,... | collective-permute-start | bytes 49160 | tf_op jit(solution)/shard_map/ppermute | solution.py:349
  133.8 3.9 %collective-permute-start.27 = (f32[64,64]{1,0:T(8,128)S(1)}, f32[64,64]{1,0:T(8,128)S(1)}, u32[]{:S(2)}, u32[]{:S(2)}) collective-permute-start(f32[64,64]{1,0:T(8,128)S(1)} %add_add_fusion.1), channel_id=1, source_target_pairs={{0,2},{1,5},{2,0},{3,7},{4,6},{5,1},{6,4},{7,3},{8,10},{9,13},{10,... | collective-permute-start | bytes 49160 | tf_op jit(solution)/shard_map/ppermute | solution.py:349
  134.5 3.9 %collective-permute-start.28 = (f32[64,64]{1,0:T(8,128)S(1)}, f32[64,64]{1,0:T(8,128)S(1)}, u32[]{:S(2)}, u32[]{:S(2)}) collective-permute-start(f32[64,64]{1,0:T(8,128)S(1)} %add_add_fusion.1), channel_id=1, source_target_pairs={{0,4},{1,3},{2,6},{3,1},{4,0},{5,7},{6,2},{7,5},{8,12},{9,11},{10,... | collective-permute-start | bytes 49160 | tf_op jit(solution)/shard_map/ppermute | solution.py:349
